TPU v7x, 32 devices: a whole 2x2x4 slice. The times are simulated.
32 devices in a mesh: sx: 8 (over y, x, core), sy: 4 (over z).
Axes of the slice: x: 2, y: 2, z: 4, core: 2. Of those that a mesh axis runs over, the one named last changes fastest.
Arguments:
- a_tiles: bfloat16 [8, 4, 32, 7, 128, 128], P('sx', 'sy'), may hold values from -3 to 3
- columns: int32 [8, 4, 32, 7], P('sx', 'sy'), may hold values from 0 to 1023, as said below
- ptent: bfloat16 [8, 4, 32, 128, 128], P('sx', 'sy'), may hold values from -0.125 to 0.125
- dinv: bfloat16 [8, 4, 32, 128, 128], P('sx', 'sy'), may hold values from -0.5 to 0.5
- agg: int32 [1024], replicated, may hold values from 0 to 63, as said below
Outputs:
- coarse_op: bfloat16 [8, 4, 2, 13, 2, 128, 128], P('sx')
Inputs may be any that keep to these rules, and one draw needn't show every extreme that they name: columns[i, j, l, 0] is the row's own global index; every entry is the global index of a fine tile of subdomain (i, j) or of a subdomain one step away along one of the two directions. `agg`: the aggregate of a fine tile is a coarse tile of the same subdomain, and every coarse tile is the aggregate of at least one fine tile.
All inputs are finite; a program needn't handle non-finite values.
Results may differ from a plain program's by a relative error of at most 0.0064.
Values may be sent and summed in bfloat16 or wider, within the bound.
No kernel may reach another device: no remote copies, remote signals or barrier semaphores. Data moves between devices by JAX's collectives and lax.ppermute only.
A program may use at most 192 MiB of HBM per device.

v0:
```python
import functools

import jax
import jax.numpy as jnp
from jax import lax
from jax.experimental import pallas as pl
from jax.experimental.pallas import tpu as pltpu
from jax.sharding import PartitionSpec as P

CROSS_SHIFTS = ((0, -1), (0, 1), (-1, 0), (1, 0), (0, 0))
OWN = 4
WINDOW_SHIFTS = (
    (-2, 0),
    (-1, -1),
    (-1, 0),
    (-1, 1),
    (0, -2),
    (0, -1),
    (0, 0),
    (0, 1),
    (0, 2),
    (1, -1),
    (1, 0),
    (1, 1),
    (2, 0),
)
ALONG_Y = (4, 5, 7, 8)
REST = (1, 9, 0, 2, 6, 10, 12, 3, 11)
GROUPS = (ALONG_Y, REST)
smoothing = 2.0 / 3.0
MEMBERS = 2
ROWS_PER_STEP = 4
NT = (((1,), (1,)), ((), ()))


def shifted(x, axis, by):
    length = lax.axis_size(axis)
    pairs = [(i, i + by) for i in range(length) if 0 <= i + by < length]
    return lax.ppermute(x, axis, pairs)


def lane_tiles(g, tile, count=1):
    return pl.ds(pl.multiple_of(g * tile, tile), count * tile)


def own_kernel(count_y, rows, members, taps, columns, agg, place, a_ref, dinv_ref, tent, *refs):
    right, left, tiles, sources, slots, ends, found = refs[:7]
    sums = refs[7:]
    tile = a_ref.shape[-1]
    step = pl.program_id(0)

    @pl.when(step == 0)
    def _():
        found[0] = 0

    listed = found[0]
    for u in range(ROWS_PER_STEP):
        g = step * ROWS_PER_STEP + u
        total = sums[u]
        total[...] = jnp.zeros_like(total)
        own_member = 0
        for k in range(taps):
            target = columns[g * taps + k]
            holder = target // rows
            step_x = holder // count_y - place[0]
            step_y = holder % count_y - place[1]
            direction = jnp.where(
                step_y == -1,
                0,
                jnp.where(step_y == 1, 1, jnp.where(step_x == -1, 2, jnp.where(step_x == 1, 3, OWN))),
            )
            member = agg[target] % members
            if k == 0:
                own_member = member
            else:
                tiles[listed] = g * taps + k
                sources[listed] = direction * rows + target % rows
                slots[listed] = direction * members + member
                listed += jnp.where(direction == OWN, 0, 1)
            z = lax.dot_general(
                tent[target % rows], a_ref[u, k], NT, preferred_element_type=jnp.float32
            )
            slot = jnp.where(direction == OWN, member, members)
            total[lane_tiles(slot, tile), :] += z.astype(jnp.bfloat16).astype(jnp.float32)
        here = slice(u * tile, (u + 1) * tile)
        applied = total[: members * tile, :].astype(jnp.bfloat16)
        right[:, here] = applied
        smooth = lax.dot_general(applied, dinv_ref[u], NT, preferred_element_type=jnp.float32)
        total[: members * tile, :] = -smoothing * smooth
        total[lane_tiles(own_member, tile), :] += tent[g].astype(jnp.float32)
        left[:, here] = total[: members * tile, :].astype(jnp.bfloat16)
    found[0] = listed
    ends[step] = listed


def own_slots(a_tiles, columns, dinv, tent, agg, place, count_y, members):
    rows, taps, tile = a_tiles.shape[0], a_tiles.shape[1], a_tiles.shape[-1]
    steps = rows // ROWS_PER_STEP
    span = ROWS_PER_STEP * tile
    scalars = pl.BlockSpec(memory_space=pltpu.SMEM)
    return pl.pallas_call(
        functools.partial(own_kernel, count_y, rows, members, taps),
        grid_spec=pltpu.PrefetchScalarGridSpec(
            num_scalar_prefetch=3,
            grid=(steps,),
            in_specs=[
                pl.BlockSpec((ROWS_PER_STEP, taps, tile, tile), lambda s, *_: (s, 0, 0, 0)),
                pl.BlockSpec((ROWS_PER_STEP, tile, tile), lambda s, *_: (s, 0, 0)),
                pl.BlockSpec((rows, tile, tile), lambda s, *_: (0, 0, 0)),
            ],
            out_specs=[pl.BlockSpec((members * tile, span), lambda s, *_: (0, s))] * 2
            + [scalars] * 4,
            scratch_shapes=[pltpu.SMEM((1,), jnp.int32)]
            + [pltpu.VMEM(((members + 1) * tile, tile), jnp.float32)] * ROWS_PER_STEP,
        ),
        out_shape=[jax.ShapeDtypeStruct((members * tile, rows * tile), jnp.bfloat16)] * 2
        + [jax.ShapeDtypeStruct((rows * taps,), jnp.int32)] * 3
        + [jax.ShapeDtypeStruct((steps,), jnp.int32)],
        compiler_params=pltpu.CompilerParams(vmem_limit_bytes=24 * 1024 * 1024),
        cost_estimate=pl.CostEstimate(
            flops=2 * tile**3 * rows * (taps + members),
            bytes_accessed=2 * (a_tiles.size + dinv.size * 6),
            transcendentals=0,
        ),
        name="own_slots",
    )(columns, agg, place, a_tiles, dinv, tent)


def product(left, right, outs, members, tile):
    width = members * tile

    def one(d2, carry):
        value = lax.dot_general(
            left[...],
            right[lane_tiles(d2, width), :],
            NT,
            preferred_element_type=jnp.float32,
        )
        for d1, out in enumerate(outs):
            for m in range(members):
                for m2 in range(members):
                    row = (d1 * members + m) * tile
                    block = value[row : row + tile, m2 * tile : (m2 + 1) * tile]
                    out[d2, m, m2] = block.astype(out.dtype)
        return carry

    lax.fori_loop(0, 5, one, 0)


def smoothed_rows(left, right, first, count, dinv, g, tile):
    lanes = lane_tiles(g, tile)
    smooth = lax.dot_general(
        right[first : first + count, lanes], dinv[g], NT, preferred_element_type=jnp.float32
    )
    left[:count, lanes] = (-smoothing * smooth).astype(jnp.bfloat16)


def neighbour_kernel(members, taps, tiles, sources, slots, ends, *refs):
    a_tiles, dinv_hbm, *tents = refs[:6]
    right_own, to_lower, to_upper, right_out = refs[6:10]
    a_held, dinv, tent, right, left, sums, sems = refs[10:]
    tile = dinv.shape[-1]
    rows = dinv.shape[0]
    chunks = rows // ROWS_PER_STEP
    outer = 4 * members
    per = ROWS_PER_STEP * taps

    def a_copy(c):
        part = pl.ds(c * per, per)
        return pltpu.make_async_copy(a_tiles.at[part], a_held.at[part], sems.at[c])

    def out_copy(c):
        lanes = lane_tiles(c, ROWS_PER_STEP * tile)
        here = right.at[pl.ds(0, outer * tile), lanes]
        return pltpu.make_async_copy(here, right_out.at[:, lanes], sems.at[chunks + c])

    others = [
        pltpu.make_async_copy(source, tent.at[pl.ds(d * rows, rows)], sems.at[2 * chunks + d])
        for d, source in enumerate(tents)
    ]
    others.append(pltpu.make_async_copy(dinv_hbm, dinv, sems.at[2 * chunks + 4]))
    own_rows = right.at[pl.ds(outer * tile, members * tile), :]
    own_copy = pltpu.make_async_copy(right_own, own_rows, sems.at[2 * chunks + 5])
    for copy in others:
        copy.start()
    for c in range(chunks):
        a_copy(c).start()
    own_copy.start()
    for copy in others:
        copy.wait()

    def one_chunk(c, first):
        sums[...] = jnp.zeros_like(sums)
        a_copy(c).wait()
        last = ends[c]

        def some(n, carry):
            found = []
            for u in range(4):
                at = first + 4 * n + u
                index = jnp.minimum(at, last - 1)
                number = tiles[index]
                slot = jnp.where(at < last, slots[index], outer)
                z = lax.dot_general(
                    tent[sources[index]], a_held[number], NT, preferred_element_type=jnp.float32
                )
                found.append((slot, number // taps - c * ROWS_PER_STEP, z))
            for slot, row, z in found:
                at = (lane_tiles(slot, tile), lane_tiles(row, tile))
                sums[at] += z.astype(jnp.bfloat16).astype(jnp.float32)
            return carry

        lax.fori_loop(0, (last - first + 3) // 4, some, 0)
        lanes = lane_tiles(c, ROWS_PER_STEP * tile)
        right[: outer * tile, lanes] = sums[: outer * tile, :].astype(jnp.bfloat16)
        out_copy(c).start()
        for u in range(ROWS_PER_STEP):
            smoothed_rows(left, right, 0, 2 * members * tile, dinv, c * ROWS_PER_STEP + u, tile)
        return last

    lax.fori_loop(0, chunks, one_chunk, 0)
    own_copy.wait()
    product(left, right, (to_lower, to_upper), members, tile)
    for c in range(chunks):
        out_copy(c).wait()


def neighbour_slots(a_tiles, dinv, tents, own_right, lists, members):
    rows, taps, tile = a_tiles.shape[0], a_tiles.shape[1], a_tiles.shape[-1]
    block = (5, members, members, tile, tile)
    whole = pl.BlockSpec(block, lambda s, *_: (0,) * 5)
    anywhere = pl.BlockSpec(memory_space=pl.ANY)
    outer = 4 * members * tile
    chunks = rows // ROWS_PER_STEP
    return pl.pallas_call(
        functools.partial(neighbour_kernel, members, taps),
        grid_spec=pltpu.PrefetchScalarGridSpec(
            num_scalar_prefetch=4,
            grid=(1,),
            in_specs=[anywhere] * 7,
            out_specs=[whole, whole, anywhere],
            scratch_shapes=[
                pltpu.VMEM((rows * taps, tile, tile), jnp.bfloat16),
                pltpu.VMEM((rows, tile, tile), jnp.bfloat16),
                pltpu.VMEM((4 * rows, tile, tile), jnp.bfloat16),
                pltpu.VMEM((outer + members * tile, rows * tile), jnp.bfloat16),
                pltpu.VMEM((2 * members * tile, rows * tile), jnp.bfloat16),
                pltpu.VMEM((outer + tile, ROWS_PER_STEP * tile), jnp.float32),
                pltpu.SemaphoreType.DMA((2 * chunks + 6,)),
            ],
        ),
        out_shape=[jax.ShapeDtypeStruct(block, jnp.bfloat16)] * 2
        + [jax.ShapeDtypeStruct((outer, rows * tile), jnp.bfloat16)],
        compiler_params=pltpu.CompilerParams(vmem_limit_bytes=48 * 1024 * 1024),
        cost_estimate=pl.CostEstimate(
            flops=2 * tile**3 * rows * 2 * members * (1 + 5 * members),
            bytes_accessed=2 * (a_tiles.size + 16 * dinv.size),
            transcendentals=0,
        ),
        name="neighbour_slots",
    )(*lists, a_tiles.reshape(rows * taps, tile, tile), dinv, *tents, own_right)


def other_rows_kernel(members, dinv, right_outer, right_own, left_own, *refs):
    to_lower, to_upper, own, right, left, sems = refs
    rows, tile = dinv.shape[0], dinv.shape[-1]
    chunks = rows // ROWS_PER_STEP
    half = 2 * members * tile

    def x_copy(c):
        at = (pl.ds(half, half), lane_tiles(c, ROWS_PER_STEP * tile))
        return pltpu.make_async_copy(right_outer.at[at], right.at[at], sems.at[c])

    y_part = (pl.ds(0, half), slice(None))
    own_part = (pl.ds(2 * half, members * tile), slice(None))
    left_part = (pl.ds(half, members * tile), slice(None))
    others = [
        pltpu.make_async_copy(right_outer.at[y_part], right.at[y_part], sems.at[chunks]),
        pltpu.make_async_copy(right_own, right.at[own_part], sems.at[chunks + 1]),
        pltpu.make_async_copy(left_own, left.at[left_part], sems.at[chunks + 2]),
    ]
    for c in range(chunks):
        x_copy(c).start()
    for copy in others:
        copy.start()

    def one_chunk(c, carry):
        x_copy(c).wait()
        for u in range(ROWS_PER_STEP):
            smoothed_rows(left, right, half, half, dinv, c * ROWS_PER_STEP + u, tile)
        return carry

    lax.fori_loop(0, chunks, one_chunk, 0)
    for copy in others:
        copy.wait()
    product(left, right, (to_lower, to_upper, own), members, tile)


def other_rows(dinv, right_outer, right_own, left_own, members):
    rows, tile = dinv.shape[0], dinv.shape[-1]
    block = (5, members, members, tile, tile)
    anywhere = pl.BlockSpec(memory_space=pl.ANY)
    return pl.pallas_call(
        functools.partial(other_rows_kernel, members),
        grid=(1,),
        in_specs=[pl.BlockSpec(dinv.shape, lambda s: (0, 0, 0))] + [anywhere] * 3,
        out_specs=[pl.BlockSpec(block, lambda s: (0,) * 5)] * 3,
        out_shape=[jax.ShapeDtypeStruct(block, jnp.bfloat16)] * 2
        + [jax.ShapeDtypeStruct(block, jnp.float32)],
        scratch_shapes=[
            pltpu.VMEM((5 * members * tile, rows * tile), jnp.bfloat16),
            pltpu.VMEM((3 * members * tile, rows * tile), jnp.bfloat16),
            pltpu.SemaphoreType.DMA((rows // ROWS_PER_STEP + 3,)),
        ],
        compiler_params=pltpu.CompilerParams(vmem_limit_bytes=56 * 1024 * 1024),
        cost_estimate=pl.CostEstimate(
            flops=2 * tile**3 * rows * members * (2 + 15 * members),
            bytes_accessed=2 * 14 * members * tile * rows * tile,
            transcendentals=0,
        ),
        name="other_rows",
    )(dinv, right_outer, right_own, left_own)


def window_kernel(group, shifts, *refs):
    out = refs[-1]
    for position, offset in enumerate(group):
        total = None
        for shift, values in zip(shifts, refs):
            for d, member in enumerate(CROSS_SHIFTS):
                if (shift[0] + member[0], shift[1] + member[1]) == WINDOW_SHIFTS[offset]:
                    term = values[d].astype(jnp.float32)
                    total = term if total is None else total + term
        out[position] = total.astype(out.dtype)


def finished(group, shifts, blocks, name):
    _, members, _, tile, _ = blocks[0].shape
    spec = lambda lead: pl.BlockSpec(
        (lead, 1, members, tile, tile), lambda m: (0, m, 0, 0, 0)
    )
    shape = (len(group), members, members, tile, tile)
    return pl.pallas_call(
        functools.partial(window_kernel, group, shifts),
        grid=(members,),
        in_specs=[spec(5)] * len(blocks),
        out_specs=spec(len(group)),
        out_shape=jax.ShapeDtypeStruct(shape, jnp.bfloat16),
        compiler_params=pltpu.CompilerParams(vmem_limit_bytes=32 * 1024 * 1024),
        cost_estimate=pl.CostEstimate(
            flops=5 * blocks[0].size, bytes_accessed=8 * blocks[0].size, transcendentals=0
        ),
        name=name,
    )(*blocks)


def place_kernel(sources, row, kind, *refs):
    out = refs[-1]
    entry = pl.program_id(1)
    for source, (held, lists) in enumerate(sources):

        @pl.when(kind[entry] == source)
        def _():
            written = set()
            for array, offsets in zip(held, lists):
                for p, offset in enumerate(offsets):
                    out[0, 0, offset] = refs[array][p, 0]
                    written.add(offset)
            for offset in range(13):
                if offset not in written:
                    out[0, 0, offset] = jnp.zeros(out.shape[3:], out.dtype)


def placed(out, arrays, sources, entries, count):
    rows, kinds = entries
    members, _, tile, _ = arrays[0].shape[1:]
    in_specs = [
        pl.BlockSpec((a.shape[0], 1, members, tile, tile), lambda m, e, *_: (0, m, 0, 0, 0))
        for a in arrays
    ]
    shape = (count, members, 13, members, tile, tile)
    operands = list(arrays)
    if out is not None:
        in_specs.append(pl.BlockSpec(memory_space=pl.ANY))
        operands.append(out)
    return pl.pallas_call(
        functools.partial(place_kernel, sources),
        grid_spec=pltpu.PrefetchScalarGridSpec(
            num_scalar_prefetch=2,
            grid=(members, len(rows)),
            in_specs=in_specs,
            out_specs=pl.BlockSpec(
                (1, 1, 13, members, tile, tile),
                lambda m, e, row, kind: (row[e], m, 0, 0, 0, 0),
            ),
        ),
        out_shape=jax.ShapeDtypeStruct(shape, jnp.bfloat16),
        input_output_aliases={2 + len(arrays): 0} if out is not None else {},
        compiler_params=pltpu.CompilerParams(vmem_limit_bytes=32 * 1024 * 1024),
        cost_estimate=pl.CostEstimate(
            flops=0, bytes_accessed=6 * 13 * members * members * tile * tile, transcendentals=0
        ),
        name="placed",
    )(jnp.stack(rows).astype(jnp.int32), jnp.stack(kinds).astype(jnp.int32), *operands)


def hopped(shard, lists, hop, count_y):
    limit = count_y - 1 - hop
    lower = tuple(o for o in lists[0] if -WINDOW_SHIFTS[o][1] <= limit)
    upper = tuple(o for o in lists[1] if WINDOW_SHIFTS[o][1] <= limit)
    cut = len(lists[0]) - len(lower)
    arrived = (
        shifted(shard[0][cut:], "sy", 1),
        shifted(shard[1][: len(upper)], "sy", -1),
    )
    return arrived, (lower, upper)


def end_to_end(shard, group, grid_y, count_y):
    lower = tuple(o for o in group if WINDOW_SHIFTS[o][1] >= 0)
    upper = tuple(o for o in group if WINDOW_SHIFTS[o][1] <= 0)
    first = jnp.where(grid_y == 0, len(group) - len(lower), 0)
    sent = lax.dynamic_slice_in_dim(shard, first, len(lower), axis=0)
    last = count_y - 1
    return lax.ppermute(sent, "sy", [(0, last), (last, 0)]), (lower, upper)


def gathered_rows(along_y, rest_of, inputs, grid_y, count_y):
    first = hopped((along_y, along_y), (ALONG_Y, ALONG_Y), 1, count_y)
    inputs, moved = lax.optimization_barrier((inputs, first[0]))
    first = (moved, first[1])
    rest = rest_of(inputs)
    shards = [along_y, rest]
    ends = [end_to_end(shard, group, grid_y, count_y) for shard, group in zip(shards, GROUPS)]
    own = ((0, 1), GROUPS)
    out = None
    arrays, sources, entries = shards, (own,), ([grid_y], [jnp.zeros_like(grid_y)])
    chains = [None, ((rest, rest), (REST, REST))]
    ahead = first
    for hop in range(1, count_y - 1):
        chains[0] = ahead
        if hop + 2 < count_y:
            ahead = hopped(*ahead, hop + 1, count_y)
        chains[1] = hopped(*chains[1], hop, count_y)
        out = placed(out, arrays, sources, entries, count_y)
        behind = [chains[1][0], ahead[0]] + ([moved for moved, _ in ends] if hop == 1 else [])
        behind, out = lax.optimization_barrier((behind, out))
        chains[1], ahead = (behind[0], chains[1][1]), (behind[1], ahead[1])
        if hop == 1:
            ends = [(moved, lists) for moved, (_, lists) in zip(behind[2:], ends)]
        arrays = [chain[0][side] for side in (0, 1) for chain in chains]
        sources = tuple(
            ((2 * side, 2 * side + 1), tuple(chain[1][side] for chain in chains))
            for side in (0, 1)
        )
        has_lower, has_upper = grid_y >= hop, grid_y + hop < count_y
        lower, upper = (grid_y - hop, 0), (grid_y + hop, 1)
        spare = (lower, upper)
        if 2 * hop > count_y:
            arrays, sources = arrays + shards, sources + (((4, 5), GROUPS),)
            spare = ((grid_y, 2), (grid_y, 2))
        chosen = [
            tuple(jnp.where(has_lower, a, b) for a, b in zip(lower, spare[1])),
            tuple(jnp.where(has_upper, a, b) for a, b in zip(upper, spare[0])),
        ]
        if hop == 1:
            base, kind = len(arrays), len(sources)
            arrays = arrays + [moved for moved, _ in ends]
            sources = sources + tuple(
                ((base, base + 1), tuple(lists[side] for _, lists in ends)) for side in (0, 1)
            )
            at_end = [
                jnp.where(grid_y == 0, a, jnp.where(grid_y == count_y - 1, b, c))
                for a, b, c in zip((count_y - 1, kind + 1), (0, kind), chosen[1])
            ]
            chosen.append(tuple(at_end))
        entries = ([row for row, _ in chosen], [kind for _, kind in chosen])
    return placed(out, arrays, sources, entries, count_y)


def local(a_tiles, columns, ptent, dinv, agg):
    grid_x = lax.axis_index("sx")
    grid_y = lax.axis_index("sy")
    count_y = lax.axis_size("sy")
    rows, taps, tile = a_tiles.shape[2], a_tiles.shape[3], a_tiles.shape[-1]
    coupling = a_tiles.reshape(rows, taps, tile, tile)
    inverse = dinv.reshape(rows, tile, tile)
    tent = jnp.swapaxes(ptent.reshape(rows, tile, tile), 1, 2)
    tents = (
        shifted(tent, "sy", 1),
        shifted(tent, "sy", -1),
        shifted(tent, "sx", 1),
        shifted(tent, "sx", -1),
    )
    own_right, own_left, *lists = own_slots(
        coupling,
        columns.reshape(rows * taps),
        inverse,
        tent,
        agg,
        jnp.stack([grid_x, grid_y]).astype(jnp.int32),
        count_y,
        MEMBERS,
    )
    to_lower_y, to_upper_y, outer_right = neighbour_slots(
        coupling, inverse, tents, own_right, lists, MEMBERS
    )
    from_lower_y, from_upper_y = shifted(to_upper_y, "sy", 1), shifted(to_lower_y, "sy", -1)
    to_lower_x, to_upper_x, own = other_rows(inverse, outer_right, own_right, own_left, MEMBERS)
    from_lower_x, from_upper_x = shifted(to_upper_x, "sx", 1), shifted(to_lower_x, "sx", -1)
    along_y = finished(
        ALONG_Y, ((0, -1), (0, 1), (0, 0)), (from_lower_y, from_upper_y, own), "along_y"
    )
    rest_of = functools.partial(finished, REST, CROSS_SHIFTS, name="rest")
    inputs = (from_lower_y, from_upper_y, from_lower_x, from_upper_x, own)
    return gathered_rows(along_y, rest_of, inputs, grid_y, count_y)[None]


def solution(mesh):
    return jax.shard_map(
        local,
        mesh=mesh,
        in_specs=(
            P("sx", "sy", None, None, None, None),
            P("sx", "sy", None, None),
            P("sx", "sy", None, None, None),
            P("sx", "sy", None, None, None),
            P(),
        ),
        out_specs=P("sx", None, None, None, None, None, None),
        check_vma=False,
    )
```

profile of v0, /device:TPU:0, one launch (start us, length us, event | category | flops | bytes accessed | tf_op | source)
XLA Modules:
  0.0 211.2 jit_solution(12186164631261248705)
XLA Ops:
  0.0 1.7 copy.10
  1.7 5.0 %collective-permute-start = (bf16[32,128,128]{2,1,0:T(8,128)(2,1)S(1)}, bf16[32,128,128]{2,1,0:T(8,128)(2,1)S(1)}, u32[]{:S(2)}, u32[]{:S(2)}) collective-permute-start(bf16[32,128,128]{2,1,0:T(8,128)(2,1)S(1)} %bitcast.23), channel_id=1, source_target_pairs={{0,1},{1,2},{2,3},{4,5},{5,6},{6,7},{8,9},{9,10},{10,11},{12,13},{... | collective-permute-start | bytes 3145736 | tf_op jit(solution)/shard_map/ppermute | solution.py:39
  6.7 1.3 collective-permute-start.1
  8.0 2.5 %collective-permute-start.2 = (bf16[32,128,128]{2,1,0:T(8,128)(2,1)S(1)}, bf16[32,128,128]{2,1,0:T(8,128)(2,1)}, u32[]{:S(2)}, u32[]{:S(2)}) collective-permute-start(bf16[32,128,128]{2,1,0:T(8,128)(2,1)S(1)} %bitcast.25), channel_id=1, source_target_pairs={{0,4},{4,8},{8,12},{12,16},{16,20},{20,24},{24,28},{1,5},{5,9},{9,... | collective-permute-start | bytes 3145736 | tf_op jit(solution)/shard_map/ppermute | solution.py:39
  10.5 1.3 collective-permute-start.3
  11.8 0.0 copy-done.10
  11.8 0.1 copy.9
  11.9 0.1 reshape.12.columns
  12.0 0.1 pad_add_fusion.2.place
  12.1 0.0 copy-done.2
  12.1 0.0 copy-done.7
  12.1 3.1 %copy-done = bf16[1,1,32,7,128,128]{5,4,3,2,1,0:T(8,128)(2,1)S(1)} copy-done((bf16[1,1,32,7,128,128]{5,4,3,2,1,0:T(8,128)(2,1)S(1)}, bf16[1,1,32,7,128,128]{5,4,3,2,1,0:T(8,128)(2,1)}, u32[]{:S(2)}) %copy-start) | copy-done | bytes 7340056
  15.2 13.0 %own_slots.1 = (bf16[256,4096]{1,0:T(8,128)(2,1)S(1)}, bf16[256,4096]{1,0:T(8,128)(2,1)S(1)}, s32[224]{0:T(256)S(1)}, s32[224]{0:T(256)S(1)}, s32[224]{0:T(256)S(1)}, /*index=5*/s32[8]{0:T(128)S(1)}) custom-call(s32[224]{0:T(256)S(1)} %reshape.12.columns, s32[1024]{0:T(1024)S(1)} %copy-done.7, s32[2]{0:T(128)S(1)} %pad_add_fusion.2.place, ...), custom_call_target="tpu_custom_call" | custom-call | flops 1207959552 | bytes 13631488 | tf_op jit(solution)/shard_map/own_slots/pallas_call | solution.py:101
  28.1 0.0 copy-start.8
  28.2 1.3 copy-done.8
  29.5 1.4 copy-done.9
  30.8 0.0 collective-permute-done.refs_2_
  30.8 2.5 %collective-permute-done.1.refs_3_ = bf16[32,128,128]{2,1,0:T(8,128)(2,1)} collective-permute-done((bf16[32,128,128]{2,1,0:T(8,128)(2,1)S(1)}, bf16[32,128,128]{2,1,0:T(8,128)(2,1)}, u32[]{:S(2)}, u32[]{:S(2)}) %collective-permute-start.1) | collective-permute-done | bytes 1048608 | tf_op jit(solution)/shard_map/ppermute | solution.py:39
  33.3 0.0 collective-permute-done.2.refs_4_
  33.4 0.0 collective-permute-done.3.refs_5_
  33.4 17.4 %neighbour_slots.1 = (bf16[5,2,2,128,128]{4,3,2,1,0:T(8,128)(2,1)S(1)}, bf16[5,2,2,128,128]{4,3,2,1,0:T(8,128)(2,1)S(1)}, bf16[1024,4096]{1,0:T(8,128)(2,1)}) custom-call(s32[224]{0:T(256)S(1)} %get-tuple-element.34.tiles, s32[224]{0:T(256)S(1)} %get-tuple-element.35.sources, s32[224]{0:T(256)S(1)} %get-tuple-element.36.slots, s32[8]{0:T(128)S(1)} %get-tuple-element.37.ends, ...), custom_call_target="tpu_custom_call" | custom-call | flops 5905580032 | bytes 24117248 | tf_op jit(solution)/shard_map/neighbour_slots/pallas_call | solution.py:235
  50.7 4.6 %collective-permute-start.4 = (bf16[5,2,2,128,128]{4,3,2,1,0:T(8,128)(2,1)S(1)}, bf16[5,2,2,128,128]{4,3,2,1,0:T(8,128)(2,1)S(1)}, u32[]{:S(2)}, u32[]{:S(2)}) collective-permute-start(bf16[5,2,2,128,128]{4,3,2,1,0:T(8,128)(2,1)S(1)} %get-tuple-element.39), channel_id=1, source_target_pairs={{0,1},{1,2},{2,3},{4,5},{5,6},{6,7},{8,9},{9,10},{10,11},{12,13},{... | collective-permute-start | bytes 1966088 | tf_op jit(solution)/shard_map/ppermute | solution.py:39
  55.3 1.3 collective-permute-start.5
  56.6 16.5 %other_rows.1 = (bf16[5,2,2,128,128]{4,3,2,1,0:T(8,128)(2,1)}, bf16[5,2,2,128,128]{4,3,2,1,0:T(8,128)(2,1)}, f32[5,2,2,128,128]{4,3,2,1,0:T(8,128)}) custom-call(bf16[32,128,128]{2,1,0:T(8,128)(2,1)} %bitcast.28, bf16[1024,4096]{1,0:T(8,128)(2,1)} %get-tuple-element.41.right_outer, bf16[256,4096]{1,0:T(8,128)(2,1)} %copy-done.8, bf16[256,4096]{1,0:T(8,128)(2,1)} %copy-done.9), custom_call_target="tpu_custom_call" | custom-call | flops 8589934592 | bytes 29360128 | tf_op jit(solution)/shard_map/other_rows/pallas_call | solution.py:303
  73.2 6.8 %collective-permute-start.6 = (bf16[5,2,2,128,128]{4,3,2,1,0:T(8,128)(2,1)}, bf16[5,2,2,128,128]{4,3,2,1,0:T(8,128)(2,1)S(1)}, u32[]{:S(2)}, u32[]{:S(2)}) collective-permute-start(bf16[5,2,2,128,128]{4,3,2,1,0:T(8,128)(2,1)} %get-tuple-element.43), channel_id=1, source_target_pairs={{0,4},{4,8},{8,12},{12,16},{16,20},{20,24},{24,28},{1,5},{5,9},{9,... | collective-permute-start | bytes 1966088 | tf_op jit(solution)/shard_map/ppermute | solution.py:39
  80.0 1.3 collective-permute-start.7
  81.3 0.0 collective-permute-done.4.refs_0_
  81.3 0.0 collective-permute-done.5.refs_1_
  81.4 0.0 copy-start.1
  81.4 1.3 copy-done.1
  82.7 0.4 along_y.1.refs_0_
  83.0 5.2 %collective-permute-start.8 = (bf16[4,2,2,128,128]{4,3,2,1,0:T(8,128)(2,1)S(1)}, bf16[4,2,2,128,128]{4,3,2,1,0:T(8,128)(2,1)S(1)}, u32[]{:S(2)}, u32[]{:S(2)}) collective-permute-start(bf16[4,2,2,128,128]{4,3,2,1,0:T(8,128)(2,1)S(1)} %along_y.1.refs_0_), channel_id=1, source_target_pairs={{0,1},{1,2},{2,3},{4,5},{5,6},{6,7},{8,9},{9,10},{10,11},{12,13},{... | collective-permute-start | bytes 1572872 | tf_op jit(solution)/shard_map/ppermute | solution.py:39
  88.2 1.3 collective-permute-start.9
  89.5 0.0 collective-permute-done.6.refs_2_
  89.5 0.0 collective-permute-done.7.refs_3_
  89.5 10.8 %collective-permute-done.8.refs_0_ = bf16[4,2,2,128,128]{4,3,2,1,0:T(8,128)(2,1)S(1)} collective-permute-done((bf16[4,2,2,128,128]{4,3,2,1,0:T(8,128)(2,1)S(1)}, bf16[4,2,2,128,128]{4,3,2,1,0:T(8,128)(2,1)S(1)}, u32[]{:S(2)}, u32[]{:S(2)}) %collective-permute-start.8) | collective-permute-done | bytes 524320 | tf_op jit(solution)/shard_map/ppermute | solution.py:39
  100.3 4.5 %collective-permute-done.9.refs_2_ = bf16[4,2,2,128,128]{4,3,2,1,0:T(8,128)(2,1)S(1)} collective-permute-done((bf16[4,2,2,128,128]{4,3,2,1,0:T(8,128)(2,1)S(1)}, bf16[4,2,2,128,128]{4,3,2,1,0:T(8,128)(2,1)S(1)}, u32[]{:S(2)}, u32[]{:S(2)}) %collective-permute-start.9) | collective-permute-done | bytes 524320 | tf_op jit(solution)/shard_map/ppermute | solution.py:39
  104.8 0.6 rest.1.refs_1_
  105.4 4.6 %collective-permute-start.10 = (bf16[9,2,2,128,128]{4,3,2,1,0:T(8,128)(2,1)S(1)}, bf16[9,2,2,128,128]{4,3,2,1,0:T(8,128)(2,1)}, u32[]{:S(2)}, u32[]{:S(2)}) collective-permute-start(bf16[9,2,2,128,128]{4,3,2,1,0:T(8,128)(2,1)S(1)} %rest.1.refs_1_), channel_id=1, source_target_pairs={{0,1},{1,2},{2,3},{4,5},{5,6},{6,7},{8,9},{9,10},{10,11},{12,13},{... | collective-permute-start | bytes 3538952 | tf_op jit(solution)/shard_map/ppermute | solution.py:39
  110.1 1.3 collective-permute-start.11
  111.4 0.1 constant_dynamic-slice_fusion
  111.4 4.2 %collective-permute-start.15 = (bf16[7,2,2,128,128]{4,3,2,1,0:T(8,128)(2,1)S(1)}, bf16[7,2,2,128,128]{4,3,2,1,0:T(8,128)(2,1)S(1)}, u32[]{:S(2)}, u32[]{:S(2)}) collective-permute-start(bf16[7,2,2,128,128]{4,3,2,1,0:T(8,128)(2,1)S(1)} %constant_dynamic-slice_fusion), channel_id=1, source_target_pairs={{0,3},{3,0},{4,7},{7,4},{8,11},{11,8},{12,15},{15,12},{16,19},{19,... | collective-permute-start | bytes 2752520 | tf_op jit(solution)/shard_map/ppermute | solution.py:425
  115.7 3.4 %collective-permute-start.14 = (bf16[2,2,2,128,128]{4,3,2,1,0:T(8,128)(2,1)S(1)}, bf16[2,2,2,128,128]{4,3,2,1,0:T(8,128)(2,1)S(1)}, u32[]{:S(2)}, u32[]{:S(2)}) collective-permute-start(bf16[2,2,2,128,128]{4,3,2,1,0:T(8,128)(2,1)S(1)} %constant_dynamic-slice_fusion.1), channel_id=1, source_target_pairs={{0,3},{3,0},{4,7},{7,4},{8,11},{11,8},{12,15},{15,12},{16,19},{19,... | collective-permute-start | bytes 786440 | tf_op jit(solution)/shard_map/ppermute | solution.py:425
  119.2 1.3 collective-permute-start.12
  120.5 43.4 %collective-permute-done.14.refs_4_ = bf16[2,2,2,128,128]{4,3,2,1,0:T(8,128)(2,1)S(1)} collective-permute-done((bf16[2,2,2,128,128]{4,3,2,1,0:T(8,128)(2,1)S(1)}, bf16[2,2,2,128,128]{4,3,2,1,0:T(8,128)(2,1)S(1)}, u32[]{:S(2)}, u32[]{:S(2)}) %collective-permute-start.14) | collective-permute-done | bytes 262176 | tf_op jit(solution)/shard_map/ppermute | solution.py:425
  163.9 0.7 copy-done.5
  164.6 1.3 collective-permute-start.13
  165.9 1.4 placed.3.refs_6_
  167.3 0.9 collective-permute-done.12.refs_0_
  168.2 8.4 %collective-permute-done.13.refs_2_ = bf16[3,2,2,128,128]{4,3,2,1,0:T(8,128)(2,1)S(1)} collective-permute-done((bf16[3,2,2,128,128]{4,3,2,1,0:T(8,128)(2,1)S(1)}, bf16[3,2,2,128,128]{4,3,2,1,0:T(8,128)(2,1)S(1)}, u32[]{:S(2)}, u32[]{:S(2)}) %collective-permute-start.13) | collective-permute-done | bytes 393248 | tf_op jit(solution)/shard_map/ppermute | solution.py:39
  176.5 0.0 collective-permute-done.15.refs_5_
  176.5 0.9 copy-done.3
  177.5 0.0 collective-permute-done.10.refs_1_
  177.5 0.0 collective-permute-done.11.refs_3_
  177.5 1.5 collective-permute-start.16
  179.0 1.3 collective-permute-start.17
  180.3 0.1 pad_add_fusion
  180.4 0.1 pad_add_fusion.3
  180.5 1.2 copy-done.4
  181.7 0.9 copy-done.6
  182.6 5.3 %placed.4.refs_4_ = bf16[4,2,13,2,128,128]{5,4,3,2,1,0:T(8,128)(2,1)} custom-call(s32[3]{0:T(128)S(1)} %get-tuple-element.63.row, s32[3]{0:T(128)S(1)} %get-tuple-element.64.kind, bf16[4,2,2,128,128]{4,3,2,1,0:T(8,128)(2,1)S(1)} %collective-permute-done.8.refs_0_, ...), custom_call_target="tpu_custom_call", output_to_operand_aliasing={{}: (8, {})} | custom-call | bytes 5111808 | tf_op jit(solution)/shard_map/placed/pallas_call | solution.py:386
  187.9 14.9 %collective-permute-done.16.refs_1_ = bf16[9,2,2,128,128]{4,3,2,1,0:T(8,128)(2,1)S(1)} collective-permute-done((bf16[9,2,2,128,128]{4,3,2,1,0:T(8,128)(2,1)}, bf16[9,2,2,128,128]{4,3,2,1,0:T(8,128)(2,1)S(1)}, u32[]{:S(2)}, u32[]{:S(2)}) %collective-permute-start.16) | collective-permute-done | bytes 1179680 | tf_op jit(solution)/shard_map/ppermute | solution.py:39
  202.8 4.2 %collective-permute-done.17.refs_3_ = bf16[9,2,2,128,128]{4,3,2,1,0:T(8,128)(2,1)} collective-permute-done((bf16[9,2,2,128,128]{4,3,2,1,0:T(8,128)(2,1)}, bf16[9,2,2,128,128]{4,3,2,1,0:T(8,128)(2,1)}, u32[]{:S(2)}, u32[]{:S(2)}) %collective-permute-start.17) | collective-permute-done | bytes 1179680 | tf_op jit(solution)/shard_map/ppermute | solution.py:39
  207.0 4.2 %placed.5 = bf16[4,2,13,2,128,128]{5,4,3,2,1,0:T(8,128)(2,1)} custom-call(s32[2]{0:T(128)S(1)} %get-tuple-element.65.row, s32[2]{0:T(128)S(1)} %get-tuple-element.66.kind, bf16[3,2,2,128,128]{4,3,2,1,0:T(8,128)(2,1)S(1)} %collective-permute-done.12.refs_0_, ...), custom_call_target="tpu_custom_call", output_to_operand_aliasing={{}: (6, {})} | custom-call | bytes 5111808 | tf_op jit(solution)/shard_map/placed/pallas_call | solution.py:386
  (12 shorter events, 0.1 us)
Async XLA Ops:
  0.0 11.8 %copy-start.10 = (s32[1,1,32,7]{2,1,3,0:T(1,128)S(1)}, s32[1,1,32,7]{2,1,3,0:T(1,128)}, u32[]{:S(2)}) copy-start(s32[1,1,32,7]{2,1,3,0:T(1,128)} %param.6) | copy-start | bytes 2692
  0.0 12.1 %copy-start.2 = (bf16[1,1,32,128,128]{4,3,2,1,0:T(8,128)(2,1)S(1)}, bf16[1,1,32,128,128]{4,3,2,1,0:T(8,128)(2,1)}, u32[]{:S(2)}) copy-start(bf16[1,1,32,128,128]{4,3,2,1,0:T(8,128)(2,1)} %param.8) | copy-start | bytes 3145732
  0.0 12.1 %copy-start.7 = (s32[1024]{0:T(1024)S(1)}, s32[1024]{0:T(1024)}, u32[]{:S(2)}) copy-start(s32[1024]{0:T(1024)} %agg.1) | copy-start | bytes 12292
  1.7 29.1 %collective-permute-start = (bf16[32,128,128]{2,1,0:T(8,128)(2,1)S(1)}, bf16[32,128,128]{2,1,0:T(8,128)(2,1)S(1)}, u32[]{:S(2)}, u32[]{:S(2)}) collective-permute-start(bf16[32,128,128]{2,1,0:T(8,128)(2,1)S(1)} %bitcast.23), channel_id=1, source_target_pairs={{0,1},{1,2},{2,3},{4,5},{5,6},{6,7},{8,9},{9,10},{10,11},{12,13},{... | collective-permute-start | bytes 3145736 | tf_op jit(solution)/shard_map/ppermute | solution.py:39
  6.7 26.6 %collective-permute-start.1 = (bf16[32,128,128]{2,1,0:T(8,128)(2,1)S(1)}, bf16[32,128,128]{2,1,0:T(8,128)(2,1)}, u32[]{:S(2)}, u32[]{:S(2)}) collective-permute-start(bf16[32,128,128]{2,1,0:T(8,128)(2,1)S(1)} %bitcast.24), channel_id=1, source_target_pairs={{1,0},{2,1},{3,2},{5,4},{6,5},{7,6},{9,8},{10,9},{11,10},{13,12},{... | collective-permute-start | bytes 3145736 | tf_op jit(solution)/shard_map/ppermute | solution.py:39
  8.0 25.3 %collective-permute-start.2 = (bf16[32,128,128]{2,1,0:T(8,128)(2,1)S(1)}, bf16[32,128,128]{2,1,0:T(8,128)(2,1)}, u32[]{:S(2)}, u32[]{:S(2)}) collective-permute-start(bf16[32,128,128]{2,1,0:T(8,128)(2,1)S(1)} %bitcast.25), channel_id=1, source_target_pairs={{0,4},{4,8},{8,12},{12,16},{16,20},{20,24},{24,28},{1,5},{5,9},{9,... | collective-permute-start | bytes 3145736 | tf_op jit(solution)/shard_map/ppermute | solution.py:39
  10.5 22.9 %collective-permute-start.3 = (bf16[32,128,128]{2,1,0:T(8,128)(2,1)S(1)}, bf16[32,128,128]{2,1,0:T(8,128)(2,1)}, u32[]{:S(2)}, u32[]{:S(2)}) collective-permute-start(bf16[32,128,128]{2,1,0:T(8,128)(2,1)S(1)} %bitcast.26), channel_id=1, source_target_pairs={{4,0},{8,4},{12,8},{16,12},{20,16},{24,20},{28,24},{5,1},{9,5},{13... | collective-permute-start | bytes 3145736 | tf_op jit(solution)/shard_map/ppermute | solution.py:39
  12.1 3.1 %copy-start = (bf16[1,1,32,7,128,128]{5,4,3,2,1,0:T(8,128)(2,1)S(1)}, bf16[1,1,32,7,128,128]{5,4,3,2,1,0:T(8,128)(2,1)}, u32[]{:S(2)}) copy-start(bf16[1,1,32,7,128,128]{5,4,3,2,1,0:T(8,128)(2,1)} %param.5) | copy-start | bytes 22020100
  28.1 1.3 copy-start.8
  29.5 1.4 copy-start.9
  50.7 30.6 %collective-permute-start.4 = (bf16[5,2,2,128,128]{4,3,2,1,0:T(8,128)(2,1)S(1)}, bf16[5,2,2,128,128]{4,3,2,1,0:T(8,128)(2,1)S(1)}, u32[]{:S(2)}, u32[]{:S(2)}) collective-permute-start(bf16[5,2,2,128,128]{4,3,2,1,0:T(8,128)(2,1)S(1)} %get-tuple-element.39), channel_id=1, source_target_pairs={{0,1},{1,2},{2,3},{4,5},{5,6},{6,7},{8,9},{9,10},{10,11},{12,13},{... | collective-permute-start | bytes 1966088 | tf_op jit(solution)/shard_map/ppermute | solution.py:39
  55.3 26.0 %collective-permute-start.5 = (bf16[5,2,2,128,128]{4,3,2,1,0:T(8,128)(2,1)S(1)}, bf16[5,2,2,128,128]{4,3,2,1,0:T(8,128)(2,1)S(1)}, u32[]{:S(2)}, u32[]{:S(2)}) collective-permute-start(bf16[5,2,2,128,128]{4,3,2,1,0:T(8,128)(2,1)S(1)} %get-tuple-element.40), channel_id=1, source_target_pairs={{1,0},{2,1},{3,2},{5,4},{6,5},{7,6},{9,8},{10,9},{11,10},{13,12},{... | collective-permute-start | bytes 1966088 | tf_op jit(solution)/shard_map/ppermute | solution.py:39
  73.2 16.3 %collective-permute-start.6 = (bf16[5,2,2,128,128]{4,3,2,1,0:T(8,128)(2,1)}, bf16[5,2,2,128,128]{4,3,2,1,0:T(8,128)(2,1)S(1)}, u32[]{:S(2)}, u32[]{:S(2)}) collective-permute-start(bf16[5,2,2,128,128]{4,3,2,1,0:T(8,128)(2,1)} %get-tuple-element.43), channel_id=1, source_target_pairs={{0,4},{4,8},{8,12},{12,16},{16,20},{20,24},{24,28},{1,5},{5,9},{9,... | collective-permute-start | bytes 1966088 | tf_op jit(solution)/shard_map/ppermute | solution.py:39
  80.0 9.5 %collective-permute-start.7 = (bf16[5,2,2,128,128]{4,3,2,1,0:T(8,128)(2,1)}, bf16[5,2,2,128,128]{4,3,2,1,0:T(8,128)(2,1)S(1)}, u32[]{:S(2)}, u32[]{:S(2)}) collective-permute-start(bf16[5,2,2,128,128]{4,3,2,1,0:T(8,128)(2,1)} %get-tuple-element.44), channel_id=1, source_target_pairs={{4,0},{8,4},{12,8},{16,12},{20,16},{24,20},{28,24},{5,1},{9,5},{13... | collective-permute-start | bytes 1966088 | tf_op jit(solution)/shard_map/ppermute | solution.py:39
  81.4 1.3 copy-start.1
  83.0 17.3 %collective-permute-start.8 = (bf16[4,2,2,128,128]{4,3,2,1,0:T(8,128)(2,1)S(1)}, bf16[4,2,2,128,128]{4,3,2,1,0:T(8,128)(2,1)S(1)}, u32[]{:S(2)}, u32[]{:S(2)}) collective-permute-start(bf16[4,2,2,128,128]{4,3,2,1,0:T(8,128)(2,1)S(1)} %along_y.1.refs_0_), channel_id=1, source_target_pairs={{0,1},{1,2},{2,3},{4,5},{5,6},{6,7},{8,9},{9,10},{10,11},{12,13},{... | collective-permute-start | bytes 1572872 | tf_op jit(solution)/shard_map/ppermute | solution.py:39
  88.2 16.6 %collective-permute-start.9 = (bf16[4,2,2,128,128]{4,3,2,1,0:T(8,128)(2,1)S(1)}, bf16[4,2,2,128,128]{4,3,2,1,0:T(8,128)(2,1)S(1)}, u32[]{:S(2)}, u32[]{:S(2)}) collective-permute-start(bf16[4,2,2,128,128]{4,3,2,1,0:T(8,128)(2,1)S(1)} %along_y.1.refs_0_), channel_id=1, source_target_pairs={{1,0},{2,1},{3,2},{5,4},{6,5},{7,6},{9,8},{10,9},{11,10},{13,12},{... | collective-permute-start | bytes 1572872 | tf_op jit(solution)/shard_map/ppermute | solution.py:39
  105.4 72.0 %collective-permute-start.10 = (bf16[9,2,2,128,128]{4,3,2,1,0:T(8,128)(2,1)S(1)}, bf16[9,2,2,128,128]{4,3,2,1,0:T(8,128)(2,1)}, u32[]{:S(2)}, u32[]{:S(2)}) collective-permute-start(bf16[9,2,2,128,128]{4,3,2,1,0:T(8,128)(2,1)S(1)} %rest.1.refs_1_), channel_id=1, source_target_pairs={{0,1},{1,2},{2,3},{4,5},{5,6},{6,7},{8,9},{9,10},{10,11},{12,13},{... | collective-permute-start | bytes 3538952 | tf_op jit(solution)/shard_map/ppermute | solution.py:39
  110.1 67.4 %collective-permute-start.11 = (bf16[9,2,2,128,128]{4,3,2,1,0:T(8,128)(2,1)S(1)}, bf16[9,2,2,128,128]{4,3,2,1,0:T(8,128)(2,1)}, u32[]{:S(2)}, u32[]{:S(2)}) collective-permute-start(bf16[9,2,2,128,128]{4,3,2,1,0:T(8,128)(2,1)S(1)} %rest.1.refs_1_), channel_id=1, source_target_pairs={{1,0},{2,1},{3,2},{5,4},{6,5},{7,6},{9,8},{10,9},{11,10},{13,12},{... | collective-permute-start | bytes 3538952 | tf_op jit(solution)/shard_map/ppermute | solution.py:39
  111.4 65.1 %collective-permute-start.15 = (bf16[7,2,2,128,128]{4,3,2,1,0:T(8,128)(2,1)S(1)}, bf16[7,2,2,128,128]{4,3,2,1,0:T(8,128)(2,1)S(1)}, u32[]{:S(2)}, u32[]{:S(2)}) collective-permute-start(bf16[7,2,2,128,128]{4,3,2,1,0:T(8,128)(2,1)S(1)} %constant_dynamic-slice_fusion), channel_id=1, source_target_pairs={{0,3},{3,0},{4,7},{7,4},{8,11},{11,8},{12,15},{15,12},{16,19},{19,... | collective-permute-start | bytes 2752520 | tf_op jit(solution)/shard_map/ppermute | solution.py:425
  115.7 48.2 %collective-permute-start.14 = (bf16[2,2,2,128,128]{4,3,2,1,0:T(8,128)(2,1)S(1)}, bf16[2,2,2,128,128]{4,3,2,1,0:T(8,128)(2,1)S(1)}, u32[]{:S(2)}, u32[]{:S(2)}) collective-permute-start(bf16[2,2,2,128,128]{4,3,2,1,0:T(8,128)(2,1)S(1)} %constant_dynamic-slice_fusion.1), channel_id=1, source_target_pairs={{0,3},{3,0},{4,7},{7,4},{8,11},{11,8},{12,15},{15,12},{16,19},{19,... | collective-permute-start | bytes 786440 | tf_op jit(solution)/shard_map/ppermute | solution.py:425
  119.2 49.0 %collective-permute-start.12 = (bf16[3,2,2,128,128]{4,3,2,1,0:T(8,128)(2,1)S(1)}, bf16[3,2,2,128,128]{4,3,2,1,0:T(8,128)(2,1)S(1)}, u32[]{:S(2)}, u32[]{:S(2)}) collective-permute-start(bf16[3,2,2,128,128]{4,3,2,1,0:T(8,128)(2,1)S(1)} %slice.6), channel_id=1, source_target_pairs={{0,1},{1,2},{2,3},{4,5},{5,6},{6,7},{8,9},{9,10},{10,11},{12,13},{... | collective-permute-start | bytes 1179656 | tf_op jit(solution)/shard_map/ppermute | solution.py:39
  163.9 0.7 copy-start.5
  164.6 11.9 %collective-permute-start.13 = (bf16[3,2,2,128,128]{4,3,2,1,0:T(8,128)(2,1)S(1)}, bf16[3,2,2,128,128]{4,3,2,1,0:T(8,128)(2,1)S(1)}, u32[]{:S(2)}, u32[]{:S(2)}) collective-permute-start(bf16[3,2,2,128,128]{4,3,2,1,0:T(8,128)(2,1)S(1)} %slice.7), channel_id=1, source_target_pairs={{1,0},{2,1},{3,2},{5,4},{6,5},{7,6},{9,8},{10,9},{11,10},{13,12},{... | collective-permute-start | bytes 1179656 | tf_op jit(solution)/shard_map/ppermute | solution.py:39
  176.5 0.9 copy-start.3
  177.5 25.4 %collective-permute-start.16 = (bf16[9,2,2,128,128]{4,3,2,1,0:T(8,128)(2,1)}, bf16[9,2,2,128,128]{4,3,2,1,0:T(8,128)(2,1)S(1)}, u32[]{:S(2)}, u32[]{:S(2)}) collective-permute-start(bf16[9,2,2,128,128]{4,3,2,1,0:T(8,128)(2,1)} %collective-permute-done.10.refs_1_), channel_id=1, source_target_pairs={{0,1},{1,2},{2,3},{4,5},{5,6},{6,7},{8,9},{9,10},{10,11},{12,13},{... | collective-permute-start | bytes 3538952 | tf_op jit(solution)/shard_map/ppermute | solution.py:39
  179.0 28.0 %collective-permute-start.17 = (bf16[9,2,2,128,128]{4,3,2,1,0:T(8,128)(2,1)}, bf16[9,2,2,128,128]{4,3,2,1,0:T(8,128)(2,1)}, u32[]{:S(2)}, u32[]{:S(2)}) collective-permute-start(bf16[9,2,2,128,128]{4,3,2,1,0:T(8,128)(2,1)} %collective-permute-done.11.refs_3_), channel_id=1, source_target_pairs={{1,0},{2,1},{3,2},{5,4},{6,5},{7,6},{9,8},{10,9},{11,10},{13,12},{... | collective-permute-start | bytes 3538952 | tf_op jit(solution)/shard_map/ppermute | solution.py:39
  180.5 1.2 copy-start.4
  181.7 0.9 copy-start.6
where the time goes:
time: 212 us; the launch traced here: 211 us
  waiting for transfers between devices  89.4 us (42%)
  Pallas kernels  58.8 us (28%)
  starting transfers between devices  49.5 us (23%)
  local copies, waits for them, and re-layouts  12.9 us (6%)
    ppermute x16, waiting for transfers between devices, shifted(): return lax.ppermute(x, axis, pairs)  46.1 us
    ppermute x2, waiting for transfers between devices, end_to_end(): return (lax.ppermute(sent, 'sy', [(0, last), (last, 0)]), (lower, upper))  43.4 us
    ppermute x16, starting transfers between devices, shifted(): return lax.ppermute(x, axis, pairs)  41.9 us
    pallas_call x1, Pallas kernels, neighbour_slots(): pl.pallas_call(functools.partial(neighbour_kernel, members, taps), grid_s...  17.4 us
    pallas_call x1, Pallas kernels, other_rows(): pl.pallas_call(functools.partial(other_rows_kernel, members), grid=(1,),...  16.5 us
    pallas_call x1, Pallas kernels, own_slots(): pl.pallas_call(functools.partial(own_kernel, count_y, rows, members, taps...  13 us
    unnamed x24, local copies, waits for them, and re-layouts  12.7 us
    pallas_call x3, Pallas kernels, placed(): pl.pallas_call(functools.partial(place_kernel, sources), grid_spec=pltpu....  10.9 us
  transfers between devices with their start and end apart: 18, of which 8 were waited for; matrix products, arithmetic and copies ran while one was open for 0% of the time, Pallas kernels for 17%

commit v1 on v0

--- a/solution.py
+++ b/solution.py
@@ -30,6 +30,7 @@
 smoothing = 2.0 / 3.0
 MEMBERS = 2
 ROWS_PER_STEP = 4
+UNROLL = 8
 NT = (((1,), (1,)), ((), ()))
 
 
@@ -196,8 +197,8 @@
 
         def some(n, carry):
             found = []
-            for u in range(4):
-                at = first + 4 * n + u
+            for u in range(UNROLL):
+                at = first + UNROLL * n + u
                 index = jnp.minimum(at, last - 1)
                 number = tiles[index]
                 slot = jnp.where(at < last, slots[index], outer)
@@ -210,7 +211,7 @@
                 sums[at] += z.astype(jnp.bfloat16).astype(jnp.float32)
             return carry
 
-        lax.fori_loop(0, (last - first + 3) // 4, some, 0)
+        lax.fori_loop(0, (last - first + UNROLL - 1) // UNROLL, some, 0)
         lanes = lane_tiles(c, ROWS_PER_STEP * tile)
         right[: outer * tile, lanes] = sums[: outer * tile, :].astype(jnp.bfloat16)
         out_copy(c).start()
@@ -356,7 +357,7 @@
 
 def place_kernel(sources, row, kind, *refs):
     out = refs[-1]
-    entry = pl.program_id(1)
+    entry = pl.program_id(2)
     for source, (held, lists) in enumerate(sources):
 
         @pl.when(kind[entry] == source)
@@ -364,18 +365,18 @@
             written = set()
             for array, offsets in zip(held, lists):
                 for p, offset in enumerate(offsets):
-                    out[0, 0, offset] = refs[array][p, 0]
+                    out[0, 0, offset, 0] = refs[array][p, 0, 0]
                     written.add(offset)
             for offset in range(13):
                 if offset not in written:
-                    out[0, 0, offset] = jnp.zeros(out.shape[3:], out.dtype)
+                    out[0, 0, offset, 0] = jnp.zeros(out.shape[4:], out.dtype)
 
 
 def placed(out, arrays, sources, entries, count):
     rows, kinds = entries
     members, _, tile, _ = arrays[0].shape[1:]
     in_specs = [
-        pl.BlockSpec((a.shape[0], 1, members, tile, tile), lambda m, e, *_: (0, m, 0, 0, 0))
+        pl.BlockSpec((a.shape[0], 1, 1, tile, tile), lambda m, n, e, *_: (0, m, n, 0, 0))
         for a in arrays
     ]
     shape = (count, members, 13, members, tile, tile)
@@ -387,11 +388,11 @@
         functools.partial(place_kernel, sources),
         grid_spec=pltpu.PrefetchScalarGridSpec(
             num_scalar_prefetch=2,
-            grid=(members, len(rows)),
+            grid=(members, members, len(rows)),
             in_specs=in_specs,
             out_specs=pl.BlockSpec(
-                (1, 1, 13, members, tile, tile),
-                lambda m, e, row, kind: (row[e], m, 0, 0, 0, 0),
+                (1, 1, 13, 1, tile, tile),
+                lambda m, n, e, row, kind: (row[e], m, 0, n, 0, 0),
             ),
         ),
         out_shape=jax.ShapeDtypeStruct(shape, jnp.bfloat16),
@@ -416,41 +417,45 @@
     return arrived, (lower, upper)
 
 
-def end_to_end(shard, group, grid_y, count_y):
-    lower = tuple(o for o in group if WINDOW_SHIFTS[o][1] >= 0)
-    upper = tuple(o for o in group if WINDOW_SHIFTS[o][1] <= 0)
-    first = jnp.where(grid_y == 0, len(group) - len(lower), 0)
-    sent = lax.dynamic_slice_in_dim(shard, first, len(lower), axis=0)
+def end_to_end(shards, after, grid_y, count_y):
+    lower = tuple(tuple(o for o in group if WINDOW_SHIFTS[o][1] >= 0) for group in GROUPS)
+    upper = tuple(tuple(o for o in group if WINDOW_SHIFTS[o][1] <= 0) for group in GROUPS)
+    sent = [
+        lax.dynamic_slice_in_dim(
+            shard, jnp.where(grid_y == 0, len(group) - len(kept), 0), len(kept), axis=0
+        )
+        for shard, group, kept in zip(shards, GROUPS, lower)
+    ]
+    sent, after = lax.optimization_barrier((jnp.concatenate(sent, axis=0), after))
     last = count_y - 1
-    return lax.ppermute(sent, "sy", [(0, last), (last, 0)]), (lower, upper)
+    moved = lax.ppermute(sent, "sy", [(0, last), (last, 0)])
+    return moved, after, (sum(lower, ()), sum(upper, ()))
 
 
 def gathered_rows(along_y, rest_of, inputs, grid_y, count_y):
-    first = hopped((along_y, along_y), (ALONG_Y, ALONG_Y), 1, count_y)
-    inputs, moved = lax.optimization_barrier((inputs, first[0]))
-    first = (moved, first[1])
+    ahead = hopped((along_y, along_y), (ALONG_Y, ALONG_Y), 1, count_y)
+    inputs, moved = lax.optimization_barrier((inputs, ahead[0]))
+    ahead = (moved, ahead[1])
     rest = rest_of(inputs)
     shards = [along_y, rest]
-    ends = [end_to_end(shard, group, grid_y, count_y) for shard, group in zip(shards, GROUPS)]
+    behind = ((rest, rest), (REST, REST))
     own = ((0, 1), GROUPS)
     out = None
     arrays, sources, entries = shards, (own,), ([grid_y], [jnp.zeros_like(grid_y)])
-    chains = [None, ((rest, rest), (REST, REST))]
-    ahead = first
     for hop in range(1, count_y - 1):
-        chains[0] = ahead
+        now = ahead
+        behind = hopped(*behind, hop, count_y)
         if hop + 2 < count_y:
             ahead = hopped(*ahead, hop + 1, count_y)
-        chains[1] = hopped(*chains[1], hop, count_y)
+        if hop == 1:
+            direct, moved, direct_lists = end_to_end(shards, ahead[0], grid_y, count_y)
+            ahead = (moved, ahead[1])
         out = placed(out, arrays, sources, entries, count_y)
-        behind = [chains[1][0], ahead[0]] + ([moved for moved, _ in ends] if hop == 1 else [])
-        behind, out = lax.optimization_barrier((behind, out))
-        chains[1], ahead = (behind[0], chains[1][1]), (behind[1], ahead[1])
-        if hop == 1:
-            ends = [(moved, lists) for moved, (_, lists) in zip(behind[2:], ends)]
-        arrays = [chain[0][side] for side in (0, 1) for chain in chains]
+        moved, out = lax.optimization_barrier((behind[0], out))
+        behind = (moved, behind[1])
+        arrays = [chain[0][side] for side in (0, 1) for chain in (now, behind)]
         sources = tuple(
-            ((2 * side, 2 * side + 1), tuple(chain[1][side] for chain in chains))
+            ((2 * side, 2 * side + 1), tuple(chain[1][side] for chain in (now, behind)))
             for side in (0, 1)
         )
         has_lower, has_upper = grid_y >= hop, grid_y + hop < count_y
@@ -464,11 +469,9 @@
             tuple(jnp.where(has_upper, a, b) for a, b in zip(upper, spare[0])),
         ]
         if hop == 1:
-            base, kind = len(arrays), len(sources)
-            arrays = arrays + [moved for moved, _ in ends]
-            sources = sources + tuple(
-                ((base, base + 1), tuple(lists[side] for _, lists in ends)) for side in (0, 1)
-            )
+            kind = len(sources)
+            sources = sources + tuple(((len(arrays),), (held,)) for held in direct_lists)
+            arrays = arrays + [direct]
             at_end = [
                 jnp.where(grid_y == 0, a, jnp.where(grid_y == count_y - 1, b, c))
                 for a, b, c in zip((count_y - 1, kind + 1), (0, kind), chosen[1])
@@ -507,10 +510,10 @@
     )
     from_lower_y, from_upper_y = shifted(to_upper_y, "sy", 1), shifted(to_lower_y, "sy", -1)
     to_lower_x, to_upper_x, own = other_rows(inverse, outer_right, own_right, own_left, MEMBERS)
-    from_lower_x, from_upper_x = shifted(to_upper_x, "sx", 1), shifted(to_lower_x, "sx", -1)
     along_y = finished(
         ALONG_Y, ((0, -1), (0, 1), (0, 0)), (from_lower_y, from_upper_y, own), "along_y"
     )
+    from_lower_x, from_upper_x = shifted(to_upper_x, "sx", 1), shifted(to_lower_x, "sx", -1)
     rest_of = functools.partial(finished, REST, CROSS_SHIFTS, name="rest")
     inputs = (from_lower_y, from_upper_y, from_lower_x, from_upper_x, own)
     return gathered_rows(along_y, rest_of, inputs, grid_y, count_y)[None]

time: 212 us -> 210 us (level)
  Pallas kernels: 58.8 us -> 63.1 us
  local copies, waits for them, and re-layouts: 12.9 us -> 9.17 us
  starting transfers between devices: 49.5 us -> 46 us
    ppermute x2 -> x1, waiting for transfers between devices: 43.4 us -> 27.7 us  [end_to_end(): moved = lax.ppermute(sent, 'sy', [(0, last), (last, 0)])]
    ppermute x16, waiting for transfers between devices: 46.1 us -> 60.7 us  [shifted(): return lax.ppermute(x, axis, pairs)]
    ppermute x2 -> x1, starting transfers between devices: 7.64 us -> 1.91 us  [end_to_end(): moved = lax.ppermute(sent, 'sy', [(0, last), (last, 0)])]
    pallas_call x3, Pallas kernels: 10.9 us -> 15.5 us  [placed(): pl.pallas_call(functools.partial(place_kernel, sources), grid_spec=pltpu....]
    unnamed x24 -> x16, local copies, waits for them, and re-layouts: 12.7 us -> 8.92 us
    ppermute x16, starting transfers between devices: 41.9 us -> 44.1 us  [shifted(): return lax.ppermute(x, axis, pairs)]
  transfers between devices with their start and end apart: 18 -> 17, of which waited for: 8 -> 8; matrix products, arithmetic and copies ran while one was open for 0% -> 1% of each run, Pallas kernels for 17% -> 19%
where the time goes in v1:
time: 210 us; the launch traced here: 208 us
  waiting for transfers between devices  88.4 us (42%)
  Pallas kernels  63.1 us (30%)
  starting transfers between devices  46 us (22%)
  local copies, waits for them, and re-layouts  9.17 us (4%)
    ppermute x16, waiting for transfers between devices, shifted(): return lax.ppermute(x, axis, pairs)  60.7 us
    ppermute x16, starting transfers between devices, shifted(): return lax.ppermute(x, axis, pairs)  44.1 us
    ppermute x1, waiting for transfers between devices, end_to_end(): moved = lax.ppermute(sent, 'sy', [(0, last), (last, 0)])  27.7 us
    pallas_call x1, Pallas kernels, neighbour_slots(): pl.pallas_call(functools.partial(neighbour_kernel, members, taps), grid_s...  17.1 us
    pallas_call x1, Pallas kernels, other_rows(): pl.pallas_call(functools.partial(other_rows_kernel, members), grid=(1,),...  16.6 us
    pallas_call x3, Pallas kernels, placed(): pl.pallas_call(functools.partial(place_kernel, sources), grid_spec=pltpu....  15.5 us
    pallas_call x1, Pallas kernels, own_slots(): pl.pallas_call(functools.partial(own_kernel, count_y, rows, members, taps...  12.9 us
    unnamed x16, local copies, waits for them, and re-layouts  8.92 us
  transfers between devices with their start and end apart: 17, of which 8 were waited for; matrix products, arithmetic and copies ran while one was open for 1% of the time, Pallas kernels for 19%

profile of v1, /device:TPU:0, one launch (start us, length us, event | category | flops | bytes accessed | tf_op | source)
XLA Modules:
  0.0 208.4 jit_solution(1445525864736807471)
XLA Ops:
  0.0 0.0 copy-start.6
  0.0 0.0 copy-start.2
  0.0 0.0 copy-start.3
  0.0 1.7 copy.10
  1.7 5.0 %collective-permute-start = (bf16[32,128,128]{2,1,0:T(8,128)(2,1)S(1)}, bf16[32,128,128]{2,1,0:T(8,128)(2,1)S(1)}, u32[]{:S(2)}, u32[]{:S(2)}) collective-permute-start(bf16[32,128,128]{2,1,0:T(8,128)(2,1)S(1)} %bitcast.23), channel_id=1, source_target_pairs={{0,1},{1,2},{2,3},{4,5},{5,6},{6,7},{8,9},{9,10},{10,11},{12,13},{... | collective-permute-start | bytes 3145736 | tf_op jit(solution)/shard_map/ppermute | solution.py:40
  6.7 1.3 collective-permute-start.1
  8.0 2.5 %collective-permute-start.2 = (bf16[32,128,128]{2,1,0:T(8,128)(2,1)S(1)}, bf16[32,128,128]{2,1,0:T(8,128)(2,1)}, u32[]{:S(2)}, u32[]{:S(2)}) collective-permute-start(bf16[32,128,128]{2,1,0:T(8,128)(2,1)S(1)} %bitcast.25), channel_id=1, source_target_pairs={{0,4},{4,8},{8,12},{12,16},{16,20},{20,24},{24,28},{1,5},{5,9},{9,... | collective-permute-start | bytes 3145736 | tf_op jit(solution)/shard_map/ppermute | solution.py:40
  10.5 1.3 collective-permute-start.3
  11.8 0.0 copy-done.6
  11.8 0.1 copy.9
  11.9 0.1 reshape.12.columns
  12.0 0.1 pad_add_fusion.2.place
  12.1 0.0 copy-done.2
  12.1 0.0 copy-done.3
  12.1 0.0 copy-start
  12.1 3.1 %copy-done = bf16[1,1,32,7,128,128]{5,4,3,2,1,0:T(8,128)(2,1)S(1)} copy-done((bf16[1,1,32,7,128,128]{5,4,3,2,1,0:T(8,128)(2,1)S(1)}, bf16[1,1,32,7,128,128]{5,4,3,2,1,0:T(8,128)(2,1)}, u32[]{:S(2)}) %copy-start) | copy-done | bytes 7340056
  15.2 12.9 %own_slots.1 = (bf16[256,4096]{1,0:T(8,128)(2,1)S(1)}, bf16[256,4096]{1,0:T(8,128)(2,1)S(1)}, s32[224]{0:T(256)S(1)}, s32[224]{0:T(256)S(1)}, s32[224]{0:T(256)S(1)}, /*index=5*/s32[8]{0:T(128)S(1)}) custom-call(s32[224]{0:T(256)S(1)} %reshape.12.columns, s32[1024]{0:T(1024)S(1)} %copy-done.3, s32[2]{0:T(128)S(1)} %pad_add_fusion.2.place, ...), custom_call_target="tpu_custom_call" | custom-call | flops 1207959552 | bytes 13631488 | tf_op jit(solution)/shard_map/own_slots/pallas_call | solution.py:102
  28.1 0.0 copy-start.4
  28.1 1.3 copy-done.4
  29.5 0.0 copy-start.5
  29.5 1.4 copy-done.5
  30.8 0.0 collective-permute-done.refs_2_
  30.9 2.5 %collective-permute-done.1.refs_3_ = bf16[32,128,128]{2,1,0:T(8,128)(2,1)} collective-permute-done((bf16[32,128,128]{2,1,0:T(8,128)(2,1)S(1)}, bf16[32,128,128]{2,1,0:T(8,128)(2,1)}, u32[]{:S(2)}, u32[]{:S(2)}) %collective-permute-start.1) | collective-permute-done | bytes 1048608 | tf_op jit(solution)/shard_map/ppermute | solution.py:40
  33.3 0.0 collective-permute-done.2.refs_4_
  33.4 0.0 collective-permute-done.3.refs_5_
  33.4 17.1 %neighbour_slots.1 = (bf16[5,2,2,128,128]{4,3,2,1,0:T(8,128)(2,1)S(1)}, bf16[5,2,2,128,128]{4,3,2,1,0:T(8,128)(2,1)S(1)}, bf16[1024,4096]{1,0:T(8,128)(2,1)}) custom-call(s32[224]{0:T(256)S(1)} %get-tuple-element.33.tiles, s32[224]{0:T(256)S(1)} %get-tuple-element.34.sources, s32[224]{0:T(256)S(1)} %get-tuple-element.35.slots, s32[8]{0:T(128)S(1)} %get-tuple-element.36.ends, ...), custom_call_target="tpu_custom_call" | custom-call | flops 5905580032 | bytes 24117248 | tf_op jit(solution)/shard_map/neighbour_slots/pallas_call | solution.py:236
  50.5 4.4 %collective-permute-start.4 = (bf16[5,2,2,128,128]{4,3,2,1,0:T(8,128)(2,1)S(1)}, bf16[5,2,2,128,128]{4,3,2,1,0:T(8,128)(2,1)S(1)}, u32[]{:S(2)}, u32[]{:S(2)}) collective-permute-start(bf16[5,2,2,128,128]{4,3,2,1,0:T(8,128)(2,1)S(1)} %get-tuple-element.38), channel_id=1, source_target_pairs={{0,1},{1,2},{2,3},{4,5},{5,6},{6,7},{8,9},{9,10},{10,11},{12,13},{... | collective-permute-start | bytes 1966088 | tf_op jit(solution)/shard_map/ppermute | solution.py:40
  54.9 1.3 collective-permute-start.5
  56.2 16.6 %other_rows.1 = (bf16[5,2,2,128,128]{4,3,2,1,0:T(8,128)(2,1)}, bf16[5,2,2,128,128]{4,3,2,1,0:T(8,128)(2,1)}, f32[5,2,2,128,128]{4,3,2,1,0:T(8,128)}) custom-call(bf16[32,128,128]{2,1,0:T(8,128)(2,1)} %bitcast.28, bf16[1024,4096]{1,0:T(8,128)(2,1)} %get-tuple-element.40.right_outer, bf16[256,4096]{1,0:T(8,128)(2,1)} %copy-done.4, bf16[256,4096]{1,0:T(8,128)(2,1)} %copy-done.5), custom_call_target="tpu_custom_call" | custom-call | flops 8589934592 | bytes 29360128 | tf_op jit(solution)/shard_map/other_rows/pallas_call | solution.py:304
  72.8 7.0 %collective-permute-start.6 = (bf16[5,2,2,128,128]{4,3,2,1,0:T(8,128)(2,1)}, bf16[5,2,2,128,128]{4,3,2,1,0:T(8,128)(2,1)S(1)}, u32[]{:S(2)}, u32[]{:S(2)}) collective-permute-start(bf16[5,2,2,128,128]{4,3,2,1,0:T(8,128)(2,1)} %get-tuple-element.43), channel_id=1, source_target_pairs={{0,4},{4,8},{8,12},{12,16},{16,20},{20,24},{24,28},{1,5},{5,9},{9,... | collective-permute-start | bytes 1966088 | tf_op jit(solution)/shard_map/ppermute | solution.py:40
  79.8 1.3 collective-permute-start.7
  81.1 0.0 collective-permute-done.4.refs_0_
  81.1 0.0 collective-permute-done.5.refs_1_
  81.1 0.0 copy-start.1
  81.1 1.3 copy-done.1
  82.4 0.4 along_y.1.refs_0_
  82.8 4.3 %collective-permute-start.8 = (bf16[4,2,2,128,128]{4,3,2,1,0:T(8,128)(2,1)S(1)}, bf16[4,2,2,128,128]{4,3,2,1,0:T(8,128)(2,1)S(1)}, u32[]{:S(2)}, u32[]{:S(2)}) collective-permute-start(bf16[4,2,2,128,128]{4,3,2,1,0:T(8,128)(2,1)S(1)} %along_y.1.refs_0_), channel_id=1, source_target_pairs={{0,1},{1,2},{2,3},{4,5},{5,6},{6,7},{8,9},{9,10},{10,11},{12,13},{... | collective-permute-start | bytes 1572872 | tf_op jit(solution)/shard_map/ppermute | solution.py:40
  87.1 1.3 collective-permute-start.9
  88.4 0.0 collective-permute-done.6.refs_2_
  88.4 0.0 collective-permute-done.7.refs_3_
  88.4 10.8 %collective-permute-done.8.refs_0_ = bf16[4,2,2,128,128]{4,3,2,1,0:T(8,128)(2,1)S(1)} collective-permute-done((bf16[4,2,2,128,128]{4,3,2,1,0:T(8,128)(2,1)S(1)}, bf16[4,2,2,128,128]{4,3,2,1,0:T(8,128)(2,1)S(1)}, u32[]{:S(2)}, u32[]{:S(2)}) %collective-permute-start.8) | collective-permute-done | bytes 524320 | tf_op jit(solution)/shard_map/ppermute | solution.py:40
  99.2 4.5 %collective-permute-done.9.refs_2_ = bf16[4,2,2,128,128]{4,3,2,1,0:T(8,128)(2,1)S(1)} collective-permute-done((bf16[4,2,2,128,128]{4,3,2,1,0:T(8,128)(2,1)S(1)}, bf16[4,2,2,128,128]{4,3,2,1,0:T(8,128)(2,1)S(1)}, u32[]{:S(2)}, u32[]{:S(2)}) %collective-permute-start.9) | collective-permute-done | bytes 524320 | tf_op jit(solution)/shard_map/ppermute | solution.py:40
  103.7 0.6 rest.1.refs_1_
  104.3 4.2 %collective-permute-start.12 = (bf16[9,2,2,128,128]{4,3,2,1,0:T(8,128)(2,1)S(1)}, bf16[9,2,2,128,128]{4,3,2,1,0:T(8,128)(2,1)}, u32[]{:S(2)}, u32[]{:S(2)}) collective-permute-start(bf16[9,2,2,128,128]{4,3,2,1,0:T(8,128)(2,1)S(1)} %rest.1.refs_1_), channel_id=1, source_target_pairs={{0,1},{1,2},{2,3},{4,5},{5,6},{6,7},{8,9},{9,10},{10,11},{12,13},{... | collective-permute-start | bytes 3538952 | tf_op jit(solution)/shard_map/ppermute | solution.py:40
  108.5 1.3 collective-permute-start.13
  109.8 4.6 %collective-permute-start.10 = (bf16[3,2,2,128,128]{4,3,2,1,0:T(8,128)(2,1)S(1)}, bf16[3,2,2,128,128]{4,3,2,1,0:T(8,128)(2,1)S(1)}, u32[]{:S(2)}, u32[]{:S(2)}) collective-permute-start(bf16[3,2,2,128,128]{4,3,2,1,0:T(8,128)(2,1)S(1)} %slice.6), channel_id=1, source_target_pairs={{0,1},{1,2},{2,3},{4,5},{5,6},{6,7},{8,9},{9,10},{10,11},{12,13},{... | collective-permute-start | bytes 1179656 | tf_op jit(solution)/shard_map/ppermute | solution.py:40
  114.4 1.3 collective-permute-start.11
  115.8 1.9 placed.3.refs_5_
  117.6 0.1 constant_dynamic-slice_fusion
  117.7 1.1 pad_maximum_fusion
  118.8 22.5 %collective-permute-done.10.refs_0_ = bf16[3,2,2,128,128]{4,3,2,1,0:T(8,128)(2,1)S(1)} collective-permute-done((bf16[3,2,2,128,128]{4,3,2,1,0:T(8,128)(2,1)S(1)}, bf16[3,2,2,128,128]{4,3,2,1,0:T(8,128)(2,1)S(1)}, u32[]{:S(2)}, u32[]{:S(2)}) %collective-permute-start.10) | collective-permute-done | bytes 393248 | tf_op jit(solution)/shard_map/ppermute | solution.py:40
  141.3 5.2 %collective-permute-done.11.refs_2_ = bf16[3,2,2,128,128]{4,3,2,1,0:T(8,128)(2,1)S(1)} collective-permute-done((bf16[3,2,2,128,128]{4,3,2,1,0:T(8,128)(2,1)S(1)}, bf16[3,2,2,128,128]{4,3,2,1,0:T(8,128)(2,1)S(1)}, u32[]{:S(2)}, u32[]{:S(2)}) %collective-permute-start.11) | collective-permute-done | bytes 393248 | tf_op jit(solution)/shard_map/ppermute | solution.py:40
  146.5 1.9 collective-permute-start.16
  148.4 0.0 collective-permute-done.12.refs_1_
  148.4 0.0 collective-permute-done.13.refs_3_
  148.4 1.8 collective-permute-start.14
  150.2 1.3 collective-permute-start.15
  151.6 0.1 pad_add_fusion
  151.6 0.1 pad_add_fusion.3
  151.7 27.7 %collective-permute-done.16.refs_4_ = bf16[9,2,2,128,128]{4,3,2,1,0:T(8,128)(2,1)} collective-permute-done((bf16[9,2,2,128,128]{4,3,2,1,0:T(8,128)(2,1)}, bf16[9,2,2,128,128]{4,3,2,1,0:T(8,128)(2,1)}, u32[]{:S(2)}, u32[]{:S(2)}) %collective-permute-start.16) | collective-permute-done | bytes 1179680 | tf_op jit(solution)/shard_map/ppermute | solution.py:431
  179.5 7.8 %placed.4.refs_4_ = bf16[4,2,13,2,128,128]{5,4,3,2,1,0:T(8,128)(2,1)} custom-call(s32[3]{0:T(128)S(1)} %get-tuple-element.61.row, s32[3]{0:T(128)S(1)} %get-tuple-element.62.kind, bf16[4,2,2,128,128]{4,3,2,1,0:T(8,128)(2,1)S(1)} %collective-permute-done.8.refs_0_, ...), custom_call_target="tpu_custom_call", output_to_operand_aliasing={{}: (7, {})} | custom-call | bytes 5111808 | tf_op jit(solution)/shard_map/placed/pallas_call | solution.py:387
  187.3 11.4 %collective-permute-done.14.refs_1_ = bf16[9,2,2,128,128]{4,3,2,1,0:T(8,128)(2,1)S(1)} collective-permute-done((bf16[9,2,2,128,128]{4,3,2,1,0:T(8,128)(2,1)}, bf16[9,2,2,128,128]{4,3,2,1,0:T(8,128)(2,1)S(1)}, u32[]{:S(2)}, u32[]{:S(2)}) %collective-permute-start.14) | collective-permute-done | bytes 1179680 | tf_op jit(solution)/shard_map/ppermute | solution.py:40
  198.6 3.9 %collective-permute-done.15.refs_3_ = bf16[9,2,2,128,128]{4,3,2,1,0:T(8,128)(2,1)} collective-permute-done((bf16[9,2,2,128,128]{4,3,2,1,0:T(8,128)(2,1)}, bf16[9,2,2,128,128]{4,3,2,1,0:T(8,128)(2,1)}, u32[]{:S(2)}, u32[]{:S(2)}) %collective-permute-start.15) | collective-permute-done | bytes 1179680 | tf_op jit(solution)/shard_map/ppermute | solution.py:40
  202.5 5.8 %placed.5 = bf16[4,2,13,2,128,128]{5,4,3,2,1,0:T(8,128)(2,1)} custom-call(s32[2]{0:T(128)S(1)} %get-tuple-element.63.row, s32[2]{0:T(128)S(1)} %get-tuple-element.64.kind, bf16[3,2,2,128,128]{4,3,2,1,0:T(8,128)(2,1)S(1)} %collective-permute-done.10.refs_0_, ...), custom_call_target="tpu_custom_call", output_to_operand_aliasing={{}: (6, {})} | custom-call | bytes 5111808 | tf_op jit(solution)/shard_map/placed/pallas_call | solution.py:387
  (3 shorter events, 0.1 us)
Async XLA Ops:
  0.0 11.8 %copy-start.6 = (s32[1,1,32,7]{2,1,3,0:T(1,128)S(1)}, s32[1,1,32,7]{2,1,3,0:T(1,128)}, u32[]{:S(2)}) copy-start(s32[1,1,32,7]{2,1,3,0:T(1,128)} %param.6) | copy-start | bytes 2692
  0.0 12.1 %copy-start.2 = (bf16[1,1,32,128,128]{4,3,2,1,0:T(8,128)(2,1)S(1)}, bf16[1,1,32,128,128]{4,3,2,1,0:T(8,128)(2,1)}, u32[]{:S(2)}) copy-start(bf16[1,1,32,128,128]{4,3,2,1,0:T(8,128)(2,1)} %param.8) | copy-start | bytes 3145732
  0.0 12.1 %copy-start.3 = (s32[1024]{0:T(1024)S(1)}, s32[1024]{0:T(1024)}, u32[]{:S(2)}) copy-start(s32[1024]{0:T(1024)} %agg.1) | copy-start | bytes 12292
  1.7 29.1 %collective-permute-start = (bf16[32,128,128]{2,1,0:T(8,128)(2,1)S(1)}, bf16[32,128,128]{2,1,0:T(8,128)(2,1)S(1)}, u32[]{:S(2)}, u32[]{:S(2)}) collective-permute-start(bf16[32,128,128]{2,1,0:T(8,128)(2,1)S(1)} %bitcast.23), channel_id=1, source_target_pairs={{0,1},{1,2},{2,3},{4,5},{5,6},{6,7},{8,9},{9,10},{10,11},{12,13},{... | collective-permute-start | bytes 3145736 | tf_op jit(solution)/shard_map/ppermute | solution.py:40
  6.7 26.6 %collective-permute-start.1 = (bf16[32,128,128]{2,1,0:T(8,128)(2,1)S(1)}, bf16[32,128,128]{2,1,0:T(8,128)(2,1)}, u32[]{:S(2)}, u32[]{:S(2)}) collective-permute-start(bf16[32,128,128]{2,1,0:T(8,128)(2,1)S(1)} %bitcast.24), channel_id=1, source_target_pairs={{1,0},{2,1},{3,2},{5,4},{6,5},{7,6},{9,8},{10,9},{11,10},{13,12},{... | collective-permute-start | bytes 3145736 | tf_op jit(solution)/shard_map/ppermute | solution.py:40
  8.0 25.3 %collective-permute-start.2 = (bf16[32,128,128]{2,1,0:T(8,128)(2,1)S(1)}, bf16[32,128,128]{2,1,0:T(8,128)(2,1)}, u32[]{:S(2)}, u32[]{:S(2)}) collective-permute-start(bf16[32,128,128]{2,1,0:T(8,128)(2,1)S(1)} %bitcast.25), channel_id=1, source_target_pairs={{0,4},{4,8},{8,12},{12,16},{16,20},{20,24},{24,28},{1,5},{5,9},{9,... | collective-permute-start | bytes 3145736 | tf_op jit(solution)/shard_map/ppermute | solution.py:40
  10.5 22.9 %collective-permute-start.3 = (bf16[32,128,128]{2,1,0:T(8,128)(2,1)S(1)}, bf16[32,128,128]{2,1,0:T(8,128)(2,1)}, u32[]{:S(2)}, u32[]{:S(2)}) collective-permute-start(bf16[32,128,128]{2,1,0:T(8,128)(2,1)S(1)} %bitcast.26), channel_id=1, source_target_pairs={{4,0},{8,4},{12,8},{16,12},{20,16},{24,20},{28,24},{5,1},{9,5},{13... | collective-permute-start | bytes 3145736 | tf_op jit(solution)/shard_map/ppermute | solution.py:40
  12.1 3.1 %copy-start = (bf16[1,1,32,7,128,128]{5,4,3,2,1,0:T(8,128)(2,1)S(1)}, bf16[1,1,32,7,128,128]{5,4,3,2,1,0:T(8,128)(2,1)}, u32[]{:S(2)}) copy-start(bf16[1,1,32,7,128,128]{5,4,3,2,1,0:T(8,128)(2,1)} %param.5) | copy-start | bytes 22020100
  28.1 1.3 copy-start.4
  29.5 1.4 copy-start.5
  50.5 30.6 %collective-permute-start.4 = (bf16[5,2,2,128,128]{4,3,2,1,0:T(8,128)(2,1)S(1)}, bf16[5,2,2,128,128]{4,3,2,1,0:T(8,128)(2,1)S(1)}, u32[]{:S(2)}, u32[]{:S(2)}) collective-permute-start(bf16[5,2,2,128,128]{4,3,2,1,0:T(8,128)(2,1)S(1)} %get-tuple-element.38), channel_id=1, source_target_pairs={{0,1},{1,2},{2,3},{4,5},{5,6},{6,7},{8,9},{9,10},{10,11},{12,13},{... | collective-permute-start | bytes 1966088 | tf_op jit(solution)/shard_map/ppermute | solution.py:40
  54.9 26.2 %collective-permute-start.5 = (bf16[5,2,2,128,128]{4,3,2,1,0:T(8,128)(2,1)S(1)}, bf16[5,2,2,128,128]{4,3,2,1,0:T(8,128)(2,1)S(1)}, u32[]{:S(2)}, u32[]{:S(2)}) collective-permute-start(bf16[5,2,2,128,128]{4,3,2,1,0:T(8,128)(2,1)S(1)} %get-tuple-element.39), channel_id=1, source_target_pairs={{1,0},{2,1},{3,2},{5,4},{6,5},{7,6},{9,8},{10,9},{11,10},{13,12},{... | collective-permute-start | bytes 1966088 | tf_op jit(solution)/shard_map/ppermute | solution.py:40
  72.8 15.6 %collective-permute-start.6 = (bf16[5,2,2,128,128]{4,3,2,1,0:T(8,128)(2,1)}, bf16[5,2,2,128,128]{4,3,2,1,0:T(8,128)(2,1)S(1)}, u32[]{:S(2)}, u32[]{:S(2)}) collective-permute-start(bf16[5,2,2,128,128]{4,3,2,1,0:T(8,128)(2,1)} %get-tuple-element.43), channel_id=1, source_target_pairs={{0,4},{4,8},{8,12},{12,16},{16,20},{20,24},{24,28},{1,5},{5,9},{9,... | collective-permute-start | bytes 1966088 | tf_op jit(solution)/shard_map/ppermute | solution.py:40
  79.8 8.6 %collective-permute-start.7 = (bf16[5,2,2,128,128]{4,3,2,1,0:T(8,128)(2,1)}, bf16[5,2,2,128,128]{4,3,2,1,0:T(8,128)(2,1)S(1)}, u32[]{:S(2)}, u32[]{:S(2)}) collective-permute-start(bf16[5,2,2,128,128]{4,3,2,1,0:T(8,128)(2,1)} %get-tuple-element.44), channel_id=1, source_target_pairs={{4,0},{8,4},{12,8},{16,12},{20,16},{24,20},{28,24},{5,1},{9,5},{13... | collective-permute-start | bytes 1966088 | tf_op jit(solution)/shard_map/ppermute | solution.py:40
  81.1 1.3 copy-start.1
  82.8 16.4 %collective-permute-start.8 = (bf16[4,2,2,128,128]{4,3,2,1,0:T(8,128)(2,1)S(1)}, bf16[4,2,2,128,128]{4,3,2,1,0:T(8,128)(2,1)S(1)}, u32[]{:S(2)}, u32[]{:S(2)}) collective-permute-start(bf16[4,2,2,128,128]{4,3,2,1,0:T(8,128)(2,1)S(1)} %along_y.1.refs_0_), channel_id=1, source_target_pairs={{0,1},{1,2},{2,3},{4,5},{5,6},{6,7},{8,9},{9,10},{10,11},{12,13},{... | collective-permute-start | bytes 1572872 | tf_op jit(solution)/shard_map/ppermute | solution.py:40
  87.1 16.6 %collective-permute-start.9 = (bf16[4,2,2,128,128]{4,3,2,1,0:T(8,128)(2,1)S(1)}, bf16[4,2,2,128,128]{4,3,2,1,0:T(8,128)(2,1)S(1)}, u32[]{:S(2)}, u32[]{:S(2)}) collective-permute-start(bf16[4,2,2,128,128]{4,3,2,1,0:T(8,128)(2,1)S(1)} %along_y.1.refs_0_), channel_id=1, source_target_pairs={{1,0},{2,1},{3,2},{5,4},{6,5},{7,6},{9,8},{10,9},{11,10},{13,12},{... | collective-permute-start | bytes 1572872 | tf_op jit(solution)/shard_map/ppermute | solution.py:40
  104.3 44.1 %collective-permute-start.12 = (bf16[9,2,2,128,128]{4,3,2,1,0:T(8,128)(2,1)S(1)}, bf16[9,2,2,128,128]{4,3,2,1,0:T(8,128)(2,1)}, u32[]{:S(2)}, u32[]{:S(2)}) collective-permute-start(bf16[9,2,2,128,128]{4,3,2,1,0:T(8,128)(2,1)S(1)} %rest.1.refs_1_), channel_id=1, source_target_pairs={{0,1},{1,2},{2,3},{4,5},{5,6},{6,7},{8,9},{9,10},{10,11},{12,13},{... | collective-permute-start | bytes 3538952 | tf_op jit(solution)/shard_map/ppermute | solution.py:40
  108.5 39.9 %collective-permute-start.13 = (bf16[9,2,2,128,128]{4,3,2,1,0:T(8,128)(2,1)S(1)}, bf16[9,2,2,128,128]{4,3,2,1,0:T(8,128)(2,1)}, u32[]{:S(2)}, u32[]{:S(2)}) collective-permute-start(bf16[9,2,2,128,128]{4,3,2,1,0:T(8,128)(2,1)S(1)} %rest.1.refs_1_), channel_id=1, source_target_pairs={{1,0},{2,1},{3,2},{5,4},{6,5},{7,6},{9,8},{10,9},{11,10},{13,12},{... | collective-permute-start | bytes 3538952 | tf_op jit(solution)/shard_map/ppermute | solution.py:40
  109.8 31.5 %collective-permute-start.10 = (bf16[3,2,2,128,128]{4,3,2,1,0:T(8,128)(2,1)S(1)}, bf16[3,2,2,128,128]{4,3,2,1,0:T(8,128)(2,1)S(1)}, u32[]{:S(2)}, u32[]{:S(2)}) collective-permute-start(bf16[3,2,2,128,128]{4,3,2,1,0:T(8,128)(2,1)S(1)} %slice.6), channel_id=1, source_target_pairs={{0,1},{1,2},{2,3},{4,5},{5,6},{6,7},{8,9},{9,10},{10,11},{12,13},{... | collective-permute-start | bytes 1179656 | tf_op jit(solution)/shard_map/ppermute | solution.py:40
  114.4 32.0 %collective-permute-start.11 = (bf16[3,2,2,128,128]{4,3,2,1,0:T(8,128)(2,1)S(1)}, bf16[3,2,2,128,128]{4,3,2,1,0:T(8,128)(2,1)S(1)}, u32[]{:S(2)}, u32[]{:S(2)}) collective-permute-start(bf16[3,2,2,128,128]{4,3,2,1,0:T(8,128)(2,1)S(1)} %slice.7), channel_id=1, source_target_pairs={{1,0},{2,1},{3,2},{5,4},{6,5},{7,6},{9,8},{10,9},{11,10},{13,12},{... | collective-permute-start | bytes 1179656 | tf_op jit(solution)/shard_map/ppermute | solution.py:40
  146.5 33.0 %collective-permute-start.16 = (bf16[9,2,2,128,128]{4,3,2,1,0:T(8,128)(2,1)}, bf16[9,2,2,128,128]{4,3,2,1,0:T(8,128)(2,1)}, u32[]{:S(2)}, u32[]{:S(2)}) collective-permute-start(bf16[9,2,2,128,128]{4,3,2,1,0:T(8,128)(2,1)} %pad_maximum_fusion), channel_id=1, source_target_pairs={{0,3},{3,0},{4,7},{7,4},{8,11},{11,8},{12,15},{15,12},{16,19},{19,... | collective-permute-start | bytes 3538952 | tf_op jit(solution)/shard_map/ppermute | solution.py:431
  148.4 50.2 %collective-permute-start.14 = (bf16[9,2,2,128,128]{4,3,2,1,0:T(8,128)(2,1)}, bf16[9,2,2,128,128]{4,3,2,1,0:T(8,128)(2,1)S(1)}, u32[]{:S(2)}, u32[]{:S(2)}) collective-permute-start(bf16[9,2,2,128,128]{4,3,2,1,0:T(8,128)(2,1)} %collective-permute-done.12.refs_1_), channel_id=1, source_target_pairs={{0,1},{1,2},{2,3},{4,5},{5,6},{6,7},{8,9},{9,10},{10,11},{12,13},{... | collective-permute-start | bytes 3538952 | tf_op jit(solution)/shard_map/ppermute | solution.py:40
  150.2 52.3 %collective-permute-start.15 = (bf16[9,2,2,128,128]{4,3,2,1,0:T(8,128)(2,1)}, bf16[9,2,2,128,128]{4,3,2,1,0:T(8,128)(2,1)}, u32[]{:S(2)}, u32[]{:S(2)}) collective-permute-start(bf16[9,2,2,128,128]{4,3,2,1,0:T(8,128)(2,1)} %collective-permute-done.13.refs_3_), channel_id=1, source_target_pairs={{1,0},{2,1},{3,2},{5,4},{6,5},{7,6},{9,8},{10,9},{11,10},{13,12},{... | collective-permute-start | bytes 3538952 | tf_op jit(solution)/shard_map/ppermute | solution.py:40

commit v2 on v1

v2 whole, which is shorter than its diff:
```python
import functools

import jax
import jax.numpy as jnp
from jax import lax
from jax.experimental import pallas as pl
from jax.experimental.pallas import tpu as pltpu
from jax.sharding import PartitionSpec as P

CROSS_SHIFTS = ((0, -1), (0, 1), (-1, 0), (1, 0), (0, 0))
OWN = 4
WINDOW_SHIFTS = (
    (-2, 0),
    (-1, -1),
    (-1, 0),
    (-1, 1),
    (0, -2),
    (0, -1),
    (0, 0),
    (0, 1),
    (0, 2),
    (1, -1),
    (1, 0),
    (1, 1),
    (2, 0),
)
TRAVEL = (4, 1, 5, 9, 0, 2, 6, 10, 12, 3, 7, 11, 8)
smoothing = 2.0 / 3.0
MEMBERS = 2
ROWS_PER_STEP = 4
UNROLL = 8
NT = (((1,), (1,)), ((), ()))


def shifted(x, axis, by):
    length = lax.axis_size(axis)
    pairs = [(i, i + by) for i in range(length) if 0 <= i + by < length]
    return lax.ppermute(x, axis, pairs)


def lane_tiles(g, tile):
    return pl.ds(pl.multiple_of(g * tile, tile), tile)


def own_kernel(count_y, rows, members, taps, columns, agg, place, a_ref, dinv_ref, tent, *refs):
    right, left, tiles, sources, slots, ends, found = refs[:7]
    sums = refs[7:]
    tile = a_ref.shape[-1]
    step = pl.program_id(0)

    @pl.when(step == 0)
    def _():
        found[0] = 0

    listed = found[0]
    for u in range(ROWS_PER_STEP):
        g = step * ROWS_PER_STEP + u
        total = sums[u]
        total[...] = jnp.zeros_like(total)
        own_member = 0
        for k in range(taps):
            target = columns[g * taps + k]
            holder = target // rows
            step_x = holder // count_y - place[0]
            step_y = holder % count_y - place[1]
            direction = jnp.where(
                step_y == -1,
                0,
                jnp.where(step_y == 1, 1, jnp.where(step_x == -1, 2, jnp.where(step_x == 1, 3, OWN))),
            )
            member = agg[target] % members
            if k == 0:
                own_member = member
            else:
                tiles[listed] = g * taps + k
                sources[listed] = direction * rows + target % rows
                slots[listed] = direction * members + member
                listed += jnp.where(direction == OWN, 0, 1)
            z = lax.dot_general(
                tent[target % rows], a_ref[u, k], NT, preferred_element_type=jnp.float32
            )
            slot = jnp.where(direction == OWN, member, members)
            total[lane_tiles(slot, tile), :] += z.astype(jnp.bfloat16).astype(jnp.float32)
        here = slice(u * tile, (u + 1) * tile)
        applied = total[: members * tile, :].astype(jnp.bfloat16)
        right[:, here] = applied
        smooth = lax.dot_general(applied, dinv_ref[u], NT, preferred_element_type=jnp.float32)
        total[: members * tile, :] = -smoothing * smooth
        total[lane_tiles(own_member, tile), :] += tent[g].astype(jnp.float32)
        left[:, here] = total[: members * tile, :].astype(jnp.bfloat16)
    found[0] = listed
    ends[step] = listed


def own_slots(a_tiles, columns, dinv, tent, agg, place, count_y, members):
    rows, taps, tile = a_tiles.shape[0], a_tiles.shape[1], a_tiles.shape[-1]
    steps = rows // ROWS_PER_STEP
    span = ROWS_PER_STEP * tile
    scalars = pl.BlockSpec(memory_space=pltpu.SMEM)
    return pl.pallas_call(
        functools.partial(own_kernel, count_y, rows, members, taps),
        grid_spec=pltpu.PrefetchScalarGridSpec(
            num_scalar_prefetch=3,
            grid=(steps,),
            in_specs=[
                pl.BlockSpec((ROWS_PER_STEP, taps, tile, tile), lambda s, *_: (s, 0, 0, 0)),
                pl.BlockSpec((ROWS_PER_STEP, tile, tile), lambda s, *_: (s, 0, 0)),
                pl.BlockSpec((rows, tile, tile), lambda s, *_: (0, 0, 0)),
            ],
            out_specs=[pl.BlockSpec((members * tile, span), lambda s, *_: (0, s))] * 2
            + [scalars] * 4,
            scratch_shapes=[pltpu.SMEM((1,), jnp.int32)]
            + [pltpu.VMEM(((members + 1) * tile, tile), jnp.float32)] * ROWS_PER_STEP,
        ),
        out_shape=[jax.ShapeDtypeStruct((members * tile, rows * tile), jnp.bfloat16)] * 2
        + [jax.ShapeDtypeStruct((rows * taps,), jnp.int32)] * 3
        + [jax.ShapeDtypeStruct((steps,), jnp.int32)],
        compiler_params=pltpu.CompilerParams(vmem_limit_bytes=24 * 1024 * 1024),
        cost_estimate=pl.CostEstimate(
            flops=2 * tile**3 * rows * (taps + members),
            bytes_accessed=2 * (a_tiles.size + dinv.size * 6),
            transcendentals=0,
        ),
        name="own_slots",
    )(columns, agg, place, a_tiles, dinv, tent)


def product(left, right, outs, members, tile):
    width = members * tile

    def one(d2, carry):
        value = lax.dot_general(
            left[...],
            right[lane_tiles(d2, width), :],
            NT,
            preferred_element_type=jnp.float32,
        )
        for d1, out in enumerate(outs):
            for m in range(members):
                for m2 in range(members):
                    row = (d1 * members + m) * tile
                    block = value[row : row + tile, m2 * tile : (m2 + 1) * tile]
                    out[d2, m, m2] = block.astype(out.dtype)
        return carry

    lax.fori_loop(0, 5, one, 0)


def smoothed_rows(left, right, first, count, dinv, g, tile):
    lanes = lane_tiles(g, tile)
    smooth = lax.dot_general(
        right[first : first + count, lanes], dinv[g], NT, preferred_element_type=jnp.float32
    )
    left[:count, lanes] = (-smoothing * smooth).astype(jnp.bfloat16)


def partial_kernel(members, taps, tiles, sources, slots, ends, *refs):
    a_tiles, dinv_hbm, *tents = refs[:6]
    right_own, left_own, *outs = refs[6:13]
    a_held, dinv, tent, right, left, sums, sems = refs[13:]
    tile = dinv.shape[-1]
    rows = dinv.shape[0]
    chunks = rows // ROWS_PER_STEP
    outer = 4 * members
    per = ROWS_PER_STEP * taps

    def a_copy(c):
        part = pl.ds(c * per, per)
        return pltpu.make_async_copy(a_tiles.at[part], a_held.at[part], sems.at[c])

    others = [
        pltpu.make_async_copy(source, tent.at[pl.ds(d * rows, rows)], sems.at[chunks + d])
        for d, source in enumerate(tents)
    ]
    others.append(pltpu.make_async_copy(dinv_hbm, dinv, sems.at[chunks + 4]))
    own_part = (pl.ds(outer * tile, members * tile), slice(None))
    own_copies = [
        pltpu.make_async_copy(right_own, right.at[own_part], sems.at[chunks + 5]),
        pltpu.make_async_copy(left_own, left.at[own_part], sems.at[chunks + 6]),
    ]
    for copy in others:
        copy.start()
    for c in range(chunks):
        a_copy(c).start()
    for copy in own_copies:
        copy.start()
    for copy in others:
        copy.wait()

    def one_chunk(c, first):
        sums[...] = jnp.zeros_like(sums)
        a_copy(c).wait()
        last = ends[c]

        def some(n, carry):
            found = []
            for u in range(UNROLL):
                at = first + UNROLL * n + u
                index = jnp.minimum(at, last - 1)
                number = tiles[index]
                slot = jnp.where(at < last, slots[index], outer)
                z = lax.dot_general(
                    tent[sources[index]], a_held[number], NT, preferred_element_type=jnp.float32
                )
                found.append((slot, number // taps - c * ROWS_PER_STEP, z))
            for slot, row, z in found:
                at = (lane_tiles(slot, tile), lane_tiles(row, tile))
                sums[at] += z.astype(jnp.bfloat16).astype(jnp.float32)
            return carry

        lax.fori_loop(0, (last - first + UNROLL - 1) // UNROLL, some, 0)
        lanes = lane_tiles(c, ROWS_PER_STEP * tile)
        right[: outer * tile, lanes] = sums[: outer * tile, :].astype(jnp.bfloat16)
        for u in range(ROWS_PER_STEP):
            g = c * ROWS_PER_STEP + u
            lanes = lane_tiles(g, tile)
            smooth = lax.dot_general(
                right[: outer * tile, lanes], dinv[g], NT, preferred_element_type=jnp.float32
            )
            left[: outer * tile, lanes] = (-smoothing * smooth).astype(jnp.bfloat16)
        return last

    lax.fori_loop(0, chunks, one_chunk, 0)
    for copy in own_copies:
        copy.wait()
    width = members * tile

    def one_direction(d2, carry):
        value = lax.dot_general(
            left[...], right[lane_tiles(d2, width), :], NT, preferred_element_type=jnp.float32
        )
        for d1, out in enumerate(outs):
            for m in range(members):
                for m2 in range(members):
                    row = (d1 * members + m) * tile
                    block = value[row : row + tile, m2 * tile : (m2 + 1) * tile]
                    out[d2, m, m2] = block.astype(out.dtype)
        return carry

    lax.fori_loop(0, 5, one_direction, 0)


def partial_blocks(a_tiles, dinv, tents, own_right, own_left, lists, members):
    rows, taps, tile = a_tiles.shape[0], a_tiles.shape[1], a_tiles.shape[-1]
    block = (5, members, members, tile, tile)
    whole = pl.BlockSpec(block, lambda s, *_: (0,) * 5)
    outer = 4 * members * tile
    slots = outer + members * tile
    return pl.pallas_call(
        functools.partial(partial_kernel, members, taps),
        grid_spec=pltpu.PrefetchScalarGridSpec(
            num_scalar_prefetch=4,
            grid=(1,),
            in_specs=[pl.BlockSpec(memory_space=pl.ANY)] * 8,
            out_specs=[whole] * 5,
            scratch_shapes=[
                pltpu.VMEM((rows * taps, tile, tile), jnp.bfloat16),
                pltpu.VMEM((rows, tile, tile), jnp.bfloat16),
                pltpu.VMEM((4 * rows, tile, tile), jnp.bfloat16),
                pltpu.VMEM((slots, rows * tile), jnp.bfloat16),
                pltpu.VMEM((slots, rows * tile), jnp.bfloat16),
                pltpu.VMEM((outer + tile, ROWS_PER_STEP * tile), jnp.float32),
                pltpu.SemaphoreType.DMA((rows // ROWS_PER_STEP + 7,)),
            ],
        ),
        out_shape=[jax.ShapeDtypeStruct(block, jnp.bfloat16)] * 4
        + [jax.ShapeDtypeStruct(block, jnp.float32)],
        compiler_params=pltpu.CompilerParams(vmem_limit_bytes=50 * 1024 * 1024),
        cost_estimate=pl.CostEstimate(
            flops=2 * tile**3 * rows * members * (4 + 25 * members),
            bytes_accessed=2 * (a_tiles.size + 20 * dinv.size),
            transcendentals=0,
        ),
        name="partial_blocks",
    )(*lists, a_tiles.reshape(rows * taps, tile, tile), dinv, *tents, own_right, own_left)


def window_kernel(*refs):
    out = refs[-1]
    for position, offset in enumerate(TRAVEL):
        total = None
        for shift, values in zip(CROSS_SHIFTS, refs):
            for d, member in enumerate(CROSS_SHIFTS):
                if (shift[0] + member[0], shift[1] + member[1]) == WINDOW_SHIFTS[offset]:
                    term = values[d].astype(jnp.float32)
                    total = term if total is None else total + term
        out[position] = total.astype(out.dtype)


def finished_window(blocks):
    _, members, _, tile, _ = blocks[0].shape
    spec = lambda lead: pl.BlockSpec(
        (lead, 1, members, tile, tile), lambda m: (0, m, 0, 0, 0)
    )
    return pl.pallas_call(
        window_kernel,
        grid=(members,),
        in_specs=[spec(5)] * 5,
        out_specs=spec(13),
        out_shape=jax.ShapeDtypeStruct((13, members, members, tile, tile), jnp.bfloat16),
        compiler_params=pltpu.CompilerParams(vmem_limit_bytes=32 * 1024 * 1024),
        cost_estimate=pl.CostEstimate(
            flops=5 * blocks[0].size, bytes_accessed=16 * blocks[0].size, transcendentals=0
        ),
        name="finished_window",
    )(*blocks)


def place_kernel(lists, members, row, kind, *refs):
    arrays, (out, nothing, sems) = refs[: len(lists)], refs[-3:]
    nothing[...] = jnp.zeros_like(nothing)

    def each(act):
        for index, (array, held) in enumerate(zip(arrays, lists)):

            @pl.when(kind[index] == 1)
            def _():
                for offset in range(13):
                    for m in range(members):
                        source = array.at[held.index(offset), m] if offset in held else nothing
                        act(
                            pltpu.make_async_copy(
                                source,
                                out.at[row[index], m, offset],
                                sems.at[(index * 13 + offset) * members + m],
                            )
                        )

    each(lambda copy: copy.start())
    each(lambda copy: copy.wait())


def placed(out, pieces, count):
    arrays = [piece[0] for piece in pieces]
    members, _, tile, _ = arrays[0].shape[1:]
    in_specs = [pl.BlockSpec(a.shape, lambda s, *_: (0,) * 5) for a in arrays]
    shape = (count, members, 13, members, tile, tile)
    operands = list(arrays)
    if out is not None:
        in_specs.append(pl.BlockSpec(memory_space=pl.ANY))
        operands.append(out)
    rows = jnp.stack([jnp.asarray(jnp.where(p[3], p[2], 0), jnp.int32) for p in pieces])
    kinds = jnp.stack([jnp.asarray(p[3], jnp.int32) for p in pieces])
    return pl.pallas_call(
        functools.partial(place_kernel, tuple(p[1] for p in pieces), members),
        grid_spec=pltpu.PrefetchScalarGridSpec(
            num_scalar_prefetch=2,
            grid=(1,),
            in_specs=in_specs,
            out_specs=pl.BlockSpec(memory_space=pl.ANY),
            scratch_shapes=[
                pltpu.VMEM((members, tile, tile), jnp.bfloat16),
                pltpu.SemaphoreType.DMA((len(pieces) * 13 * members,)),
            ],
        ),
        out_shape=jax.ShapeDtypeStruct(shape, jnp.bfloat16),
        input_output_aliases={2 + len(arrays): 0} if out is not None else {},
        compiler_params=pltpu.CompilerParams(vmem_limit_bytes=32 * 1024 * 1024),
        cost_estimate=pl.CostEstimate(
            flops=0, bytes_accessed=6 * 13 * members * members * tile * tile, transcendentals=0
        ),
        name="placed",
    )(rows, kinds, *operands)


def hopped(shard, lists, hop, count_y):
    limit = count_y - 1 - hop
    lower = tuple(o for o in lists[0] if -WINDOW_SHIFTS[o][1] <= limit)
    upper = tuple(o for o in lists[1] if WINDOW_SHIFTS[o][1] <= limit)
    cut = len(lists[0]) - len(lower)
    arrived = (
        shifted(shard[0][cut:], "sy", 1),
        shifted(shard[1][: len(upper)], "sy", -1),
    )
    return arrived, (lower, upper)


def end_to_end(shard, grid_y, count_y):
    lower = tuple(o for o in TRAVEL if WINDOW_SHIFTS[o][1] >= 0)
    upper = tuple(o for o in TRAVEL if WINDOW_SHIFTS[o][1] <= 0)
    start = jnp.where(grid_y == 0, len(TRAVEL) - len(lower), 0)
    sent = lax.dynamic_slice_in_dim(shard, start, len(lower), axis=0)
    last = count_y - 1
    moved = lax.ppermute(sent, "sy", [(0, last), (last, 0)])
    return [(moved, lower, 0, grid_y == last), (moved, upper, last, grid_y == 0)]


def gathered_rows(shard, grid_y, count_y):
    arrived, lists = (shard, shard), (TRAVEL, TRAVEL)
    pieces = [(shard, TRAVEL, grid_y, True)]
    direct = end_to_end(shard, grid_y, count_y)
    out = None
    for hop in range(1, count_y - 1):
        arrived, lists = hopped(arrived, lists, hop, count_y)
        out = placed(out, pieces, count_y)
        arrived, out = lax.optimization_barrier((arrived, out))
        pieces = [
            (arrived[0], lists[0], grid_y - hop, grid_y >= hop),
            (arrived[1], lists[1], grid_y + hop, grid_y + hop < count_y),
        ]
        if hop == 1:
            pieces += direct
    return placed(out, pieces, count_y)


def local(a_tiles, columns, ptent, dinv, agg):
    grid_x = lax.axis_index("sx")
    grid_y = lax.axis_index("sy")
    count_y = lax.axis_size("sy")
    rows, taps, tile = a_tiles.shape[2], a_tiles.shape[3], a_tiles.shape[-1]
    coupling = a_tiles.reshape(rows, taps, tile, tile)
    inverse = dinv.reshape(rows, tile, tile)
    tent = jnp.swapaxes(ptent.reshape(rows, tile, tile), 1, 2)
    tents = (
        shifted(tent, "sy", 1),
        shifted(tent, "sy", -1),
        shifted(tent, "sx", 1),
        shifted(tent, "sx", -1),
    )
    own_right, own_left, *lists = own_slots(
        coupling,
        columns.reshape(rows * taps),
        inverse,
        tent,
        agg,
        jnp.stack([grid_x, grid_y]).astype(jnp.int32),
        count_y,
        MEMBERS,
    )
    to_lower_y, to_upper_y, to_lower_x, to_upper_x, own = partial_blocks(
        coupling, inverse, tents, own_right, own_left, lists, MEMBERS
    )
    shard = finished_window(
        (
            shifted(to_upper_y, "sy", 1),
            shifted(to_lower_y, "sy", -1),
            shifted(to_upper_x, "sx", 1),
            shifted(to_lower_x, "sx", -1),
            own,
        )
    )
    return gathered_rows(shard, grid_y, count_y)[None]


def solution(mesh):
    return jax.shard_map(
        local,
        mesh=mesh,
        in_specs=(
            P("sx", "sy", None, None, None, None),
            P("sx", "sy", None, None),
            P("sx", "sy", None, None, None),
            P("sx", "sy", None, None, None),
            P(),
        ),
        out_specs=P("sx", None, None, None, None, None, None),
        check_vma=False,
    )
```

time: 210 us -> 214 us (1.019)
  the two profiles are of different devices: /device:TPU:0 before, /device:TPU:2 now
where the time goes in v2:
time: 214 us
  waiting for transfers between devices  107 us (50%)
  Pallas kernels  51.8 us (24%)
  starting transfers between devices  39.3 us (18%)
  local copies, waits for them, and re-layouts  14.3 us (7%)
    ppermute x1, waiting for transfers between devices, end_to_end(): moved = lax.ppermute(sent, 'sy', [(0, last), (last, 0)])  54.4 us
    ppermute x12, waiting for transfers between devices, shifted(): return lax.ppermute(x, axis, pairs)  53.1 us
    ppermute x12, starting transfers between devices, shifted(): return lax.ppermute(x, axis, pairs)  34.9 us
    pallas_call x1, Pallas kernels, partial_blocks(): pl.pallas_call(functools.partial(partial_kernel, members, taps), grid_spe...  29.5 us
    pallas_call x1, Pallas kernels, own_slots(): pl.pallas_call(functools.partial(own_kernel, count_y, rows, members, taps...  12.9 us
    unnamed x22, local copies, waits for them, and re-layouts  10.3 us
    pallas_call x3, Pallas kernels, placed(): pl.pallas_call(functools.partial(place_kernel, tuple((p[1] for p in piece...  8.64 us
    ppermute x1, starting transfers between devices, end_to_end(): moved = lax.ppermute(sent, 'sy', [(0, last), (last, 0)])  4.39 us
  transfers between devices with their start and end apart: 13, of which 8 were waited for; matrix products, arithmetic and copies ran while one was open for 1% of the time, Pallas kernels for 8%

profile of v2, /device:TPU:2, one launch (start us, length us, event | category | flops | bytes accessed | tf_op | source)
XLA Modules:
  0.0 213.5 jit_solution(3174335634810309080)
XLA Ops:
  0.0 0.0 copy-start.8
  0.0 0.0 copy-start.4
  0.0 0.0 copy-start.5
  0.0 1.7 copy.10
  1.7 3.5 %collective-permute-start = (bf16[32,128,128]{2,1,0:T(8,128)(2,1)S(1)}, bf16[32,128,128]{2,1,0:T(8,128)(2,1)S(1)}, u32[]{:S(2)}, u32[]{:S(2)}) collective-permute-start(bf16[32,128,128]{2,1,0:T(8,128)(2,1)S(1)} %bitcast.24), channel_id=1, source_target_pairs={{0,1},{1,2},{2,3},{4,5},{5,6},{6,7},{8,9},{9,10},{10,11},{12,13},{... | collective-permute-start | bytes 3145736 | tf_op jit(solution)/shard_map/ppermute | solution.py:38
  5.3 1.3 collective-permute-start.1
  6.6 1.9 collective-permute-start.2
  8.5 3.6 %collective-permute-start.3 = (bf16[32,128,128]{2,1,0:T(8,128)(2,1)S(1)}, bf16[32,128,128]{2,1,0:T(8,128)(2,1)}, u32[]{:S(2)}, u32[]{:S(2)}) collective-permute-start(bf16[32,128,128]{2,1,0:T(8,128)(2,1)S(1)} %bitcast.27), channel_id=1, source_target_pairs={{4,0},{8,4},{12,8},{16,12},{20,16},{24,20},{28,24},{5,1},{9,5},{13... | collective-permute-start | bytes 3145736 | tf_op jit(solution)/shard_map/ppermute | solution.py:38
  12.2 0.0 copy-done.8
  12.2 0.1 copy.9
  12.3 0.1 reshape.12.columns
  12.4 0.1 pad_add_fusion.1.place
  12.4 0.0 copy-done.4
  12.5 0.0 copy-done.5
  12.5 0.0 copy-start
  12.5 3.1 %copy-done = bf16[1,1,32,7,128,128]{5,4,3,2,1,0:T(8,128)(2,1)S(1)} copy-done((bf16[1,1,32,7,128,128]{5,4,3,2,1,0:T(8,128)(2,1)S(1)}, bf16[1,1,32,7,128,128]{5,4,3,2,1,0:T(8,128)(2,1)}, u32[]{:S(2)}) %copy-start) | copy-done | bytes 7340056
  15.5 12.9 %own_slots.1 = (bf16[256,4096]{1,0:T(8,128)(2,1)S(1)}, bf16[256,4096]{1,0:T(8,128)(2,1)S(1)}, s32[224]{0:T(256)S(1)}, s32[224]{0:T(256)S(1)}, s32[224]{0:T(256)S(1)}, /*index=5*/s32[8]{0:T(128)S(1)}) custom-call(s32[224]{0:T(256)S(1)} %reshape.12.columns, s32[1024]{0:T(1024)S(1)} %copy-done.5, s32[2]{0:T(128)S(1)} %pad_add_fusion.1.place, ...), custom_call_target="tpu_custom_call" | custom-call | flops 1207959552 | bytes 13631488 | tf_op jit(solution)/shard_map/own_slots/pallas_call | solution.py:100
  28.5 0.0 copy-start.6
  28.5 1.3 copy-done.6
  29.8 0.0 copy-start.7
  29.8 1.3 copy-done.7
  31.2 0.0 collective-permute-done.refs_2_
  31.2 0.0 copy-start.9
  31.2 0.7 collective-permute-done.1.refs_3_
  31.9 0.0 collective-permute-done.2.refs_4_
  31.9 1.0 collective-permute-done.3.refs_5_
  32.9 0.0 copy-done.9
  32.9 29.5 %partial_blocks.1 = (bf16[5,2,2,128,128]{4,3,2,1,0:T(8,128)(2,1)S(1)}, bf16[5,2,2,128,128]{4,3,2,1,0:T(8,128)(2,1)S(1)}, bf16[5,2,2,128,128]{4,3,2,1,0:T(8,128)(...) custom-call(s32[224]{0:T(256)S(1)} %get-tuple-element.22.tiles, ...), custom_call_target="tpu_custom_call" | custom-call | flops 14495514624 | bytes 28311552 | tf_op jit(solution)/shard_map/partial_blocks/pallas_call | solution.py:249
  62.4 6.2 %collective-permute-start.4 = (bf16[5,2,2,128,128]{4,3,2,1,0:T(8,128)(2,1)S(1)}, bf16[5,2,2,128,128]{4,3,2,1,0:T(8,128)(2,1)S(1)}, u32[]{:S(2)}, u32[]{:S(2)}) collective-permute-start(bf16[5,2,2,128,128]{4,3,2,1,0:T(8,128)(2,1)S(1)} %get-tuple-element.28), channel_id=1, source_target_pairs={{0,1},{1,2},{2,3},{4,5},{5,6},{6,7},{8,9},{9,10},{10,11},{12,13},{... | collective-permute-start | bytes 1966088 | tf_op jit(solution)/shard_map/ppermute | solution.py:38
  68.7 1.3 collective-permute-start.5
  70.0 2.5 %collective-permute-start.6 = (bf16[5,2,2,128,128]{4,3,2,1,0:T(8,128)(2,1)S(1)}, bf16[5,2,2,128,128]{4,3,2,1,0:T(8,128)(2,1)S(1)}, u32[]{:S(2)}, u32[]{:S(2)}) collective-permute-start(bf16[5,2,2,128,128]{4,3,2,1,0:T(8,128)(2,1)S(1)} %get-tuple-element.30), channel_id=1, source_target_pairs={{0,4},{4,8},{8,12},{12,16},{16,20},{20,24},{24,28},{1,5},{5,9},{9,... | collective-permute-start | bytes 1966088 | tf_op jit(solution)/shard_map/ppermute | solution.py:38
  72.5 3.1 %collective-permute-start.7 = (bf16[5,2,2,128,128]{4,3,2,1,0:T(8,128)(2,1)S(1)}, bf16[5,2,2,128,128]{4,3,2,1,0:T(8,128)(2,1)S(1)}, u32[]{:S(2)}, u32[]{:S(2)}) collective-permute-start(bf16[5,2,2,128,128]{4,3,2,1,0:T(8,128)(2,1)S(1)} %get-tuple-element.31), channel_id=1, source_target_pairs={{4,0},{8,4},{12,8},{16,12},{20,16},{24,20},{28,24},{5,1},{9,5},{13... | collective-permute-start | bytes 1966088 | tf_op jit(solution)/shard_map/ppermute | solution.py:38
  75.6 8.1 %collective-permute-done.4.refs_0_ = bf16[5,2,2,128,128]{4,3,2,1,0:T(8,128)(2,1)S(1)} collective-permute-done((bf16[5,2,2,128,128]{4,3,2,1,0:T(8,128)(2,1)S(1)}, bf16[5,2,2,128,128]{4,3,2,1,0:T(8,128)(2,1)S(1)}, u32[]{:S(2)}, u32[]{:S(2)}) %collective-permute-start.4) | collective-permute-done | bytes 655392 | tf_op jit(solution)/shard_map/ppermute | solution.py:38
  83.7 4.2 %collective-permute-done.5.refs_1_ = bf16[5,2,2,128,128]{4,3,2,1,0:T(8,128)(2,1)S(1)} collective-permute-done((bf16[5,2,2,128,128]{4,3,2,1,0:T(8,128)(2,1)S(1)}, bf16[5,2,2,128,128]{4,3,2,1,0:T(8,128)(2,1)S(1)}, u32[]{:S(2)}, u32[]{:S(2)}) %collective-permute-start.5) | collective-permute-done | bytes 655392 | tf_op jit(solution)/shard_map/ppermute | solution.py:38
  87.9 0.0 collective-permute-done.6.refs_2_
  87.9 0.1 collective-permute-done.7.refs_3_
  88.0 0.0 copy-start.3
  88.0 1.3 copy-done.3
  89.3 0.7 finished_window.1.refs_0_
  90.1 4.7 %collective-permute-start.8 = (bf16[13,2,2,128,128]{4,3,2,1,0:T(8,128)(2,1)S(1)}, bf16[13,2,2,128,128]{4,3,2,1,0:T(8,128)(2,1)S(1)}, u32[]{:S(2)}, u32[]{:S(2)}) collective-permute-start(bf16[13,2,2,128,128]{4,3,2,1,0:T(8,128)(2,1)S(1)} %finished_window.1.refs_0_), channel_id=1, source_target_pairs={{0,1},{1,2},{2,3},{4,5},{5,6},{6,7},{8,9},{9,10},{10,11},{12,13},{... | collective-permute-start | bytes 5111816 | tf_op jit(solution)/shard_map/ppermute | solution.py:38
  94.7 1.3 collective-permute-start.9
  96.0 1.4 placed.3.refs_4_
  97.4 34.5 %collective-permute-done.8.refs_0_ = bf16[13,2,2,128,128]{4,3,2,1,0:T(8,128)(2,1)S(1)} collective-permute-done((bf16[13,2,2,128,128]{4,3,2,1,0:T(8,128)(2,1)S(1)}, bf16[13,2,2,128,128]{4,3,2,1,0:T(8,128)(2,1)S(1)}, u32[]{:S(2)}, u32[]{:S(2)}) %collective-permute-start.8) | collective-permute-done | bytes 1703968 | tf_op jit(solution)/shard_map/ppermute | solution.py:38
  131.9 4.4 %collective-permute-done.9.refs_1_ = bf16[13,2,2,128,128]{4,3,2,1,0:T(8,128)(2,1)S(1)} collective-permute-done((bf16[13,2,2,128,128]{4,3,2,1,0:T(8,128)(2,1)S(1)}, bf16[13,2,2,128,128]{4,3,2,1,0:T(8,128)(2,1)S(1)}, u32[]{:S(2)}, u32[]{:S(2)}) %collective-permute-start.9) | collective-permute-done | bytes 1703968 | tf_op jit(solution)/shard_map/ppermute | solution.py:38
  136.3 0.0 copy-start.1
  136.3 1.3 slice.6
  137.7 4.2 %collective-permute-start.10 = (bf16[12,2,2,128,128]{4,3,2,1,0:T(8,128)(2,1)}, bf16[12,2,2,128,128]{4,3,2,1,0:T(8,128)(2,1)}, u32[]{:S(2)}, u32[]{:S(2)}) collective-permute-start(bf16[12,2,2,128,128]{4,3,2,1,0:T(8,128)(2,1)} %slice.6), channel_id=1, source_target_pairs={{0,1},{1,2},{2,3},{4,5},{5,6},{6,7},{8,9},{9,10},{10,11},{12,13},{... | collective-permute-start | bytes 4718600 | tf_op jit(solution)/shard_map/ppermute | solution.py:38
  141.9 1.3 slice.7
  143.2 0.0 copy-done.1
  143.2 1.3 collective-permute-start.11
  144.5 1.2 constant_dynamic-slice_fusion
  145.7 4.4 %collective-permute-start.12 = (bf16[9,2,2,128,128]{4,3,2,1,0:T(8,128)(2,1)}, bf16[9,2,2,128,128]{4,3,2,1,0:T(8,128)(2,1)S(1)}, u32[]{:S(2)}, u32[]{:S(2)}) collective-permute-start(bf16[9,2,2,128,128]{4,3,2,1,0:T(8,128)(2,1)} %constant_dynamic-slice_fusion), channel_id=1, source_target_pairs={{0,3},{3,0},{4,7},{7,4},{8,11},{11,8},{12,15},{15,12},{16,19},{19,... | collective-permute-start | bytes 3538952 | tf_op jit(solution)/shard_map/ppermute | solution.py:384
  150.1 0.1 pad_add_fusion.row
  150.2 0.1 add_convert_fusion.kind
  150.3 0.1 pad_add_fusion.2.row
  150.4 0.1 add_convert_fusion.1.kind
  150.4 54.4 %collective-permute-done.12.refs_2_.refs_3_ = bf16[9,2,2,128,128]{4,3,2,1,0:T(8,128)(2,1)S(1)} collective-permute-done((bf16[9,2,2,128,128]{4,3,2,1,0:T(8,128)(2,1)}, bf16[9,2,2,128,128]{4,3,2,1,0:T(8,128)(2,1)S(1)}, u32[]{:S(2)}, u32[]{:S(2)}) %collective-permute-start.12) | collective-permute-done | bytes 1179680 | tf_op jit(solution)/shard_map/ppermute | solution.py:384
  204.8 0.0 copy-start.2
  204.8 1.5 copy-done.2
  206.3 3.2 %placed.4.refs_2_ = bf16[4,2,13,2,128,128]{5,4,3,2,1,0:T(8,128)(2,1)} custom-call(s32[4]{0:T(128)S(1)} %pad_add_fusion.2.row, s32[4]{0:T(128)S(1)} %add_convert_fusion.1.kind, bf16[13,2,2,128,128]{4,3,2,1,0:T(8,128)(2,1)S(1)} %collective-permute-done.8.refs_0_, bf16[13,2,2,128,128]{4,3,2,1,0:T(8,128)(2,1)S(1)} %copy-done.2, ...), custom_call_target="tpu_custom_call", output_to_operand_aliasing={{}: (6, {})} | custom-call | bytes 5111808 | tf_op jit(solution)/shard_map/placed/pallas_call | solution.py:344
  209.5 0.0 collective-permute-done.10.refs_0_
  209.5 0.0 collective-permute-done.11.refs_1_
  209.5 4.1 %placed.5 = bf16[4,2,13,2,128,128]{5,4,3,2,1,0:T(8,128)(2,1)} custom-call(s32[2]{0:T(128)S(1)} %pad_add_fusion.row, s32[2]{0:T(128)S(1)} %add_convert_fusion.kind, bf16[12,2,2,128,128]{4,3,2,1,0:T(8,128)(2,1)} %collective-permute-done.10.refs_0_, bf16[12,2,2,128,128]{4,3,2,1,0:T(8,128)(2,1)} %collective-permute-done.11.refs_1_, ...), custom_call_target="tpu_custom_call", output_to_operand_aliasing={{}: (4, {})} | custom-call | bytes 5111808 | tf_op jit(solution)/shard_map/placed/pallas_call | solution.py:344
Async XLA Ops:
  0.0 12.2 %copy-start.8 = (s32[1,1,32,7]{2,1,3,0:T(1,128)S(1)}, s32[1,1,32,7]{2,1,3,0:T(1,128)}, u32[]{:S(2)}) copy-start(s32[1,1,32,7]{2,1,3,0:T(1,128)} %param.6) | copy-start | bytes 2692
  0.0 12.4 %copy-start.4 = (bf16[1,1,32,128,128]{4,3,2,1,0:T(8,128)(2,1)S(1)}, bf16[1,1,32,128,128]{4,3,2,1,0:T(8,128)(2,1)}, u32[]{:S(2)}) copy-start(bf16[1,1,32,128,128]{4,3,2,1,0:T(8,128)(2,1)} %param.8) | copy-start | bytes 3145732
  0.0 12.4 %copy-start.5 = (s32[1024]{0:T(1024)S(1)}, s32[1024]{0:T(1024)}, u32[]{:S(2)}) copy-start(s32[1024]{0:T(1024)} %agg.1) | copy-start | bytes 12292
  1.7 29.4 %collective-permute-start = (bf16[32,128,128]{2,1,0:T(8,128)(2,1)S(1)}, bf16[32,128,128]{2,1,0:T(8,128)(2,1)S(1)}, u32[]{:S(2)}, u32[]{:S(2)}) collective-permute-start(bf16[32,128,128]{2,1,0:T(8,128)(2,1)S(1)} %bitcast.24), channel_id=1, source_target_pairs={{0,1},{1,2},{2,3},{4,5},{5,6},{6,7},{8,9},{9,10},{10,11},{12,13},{... | collective-permute-start | bytes 3145736 | tf_op jit(solution)/shard_map/ppermute | solution.py:38
  5.3 26.6 %collective-permute-start.1 = (bf16[32,128,128]{2,1,0:T(8,128)(2,1)S(1)}, bf16[32,128,128]{2,1,0:T(8,128)(2,1)}, u32[]{:S(2)}, u32[]{:S(2)}) collective-permute-start(bf16[32,128,128]{2,1,0:T(8,128)(2,1)S(1)} %bitcast.25), channel_id=1, source_target_pairs={{1,0},{2,1},{3,2},{5,4},{6,5},{7,6},{9,8},{10,9},{11,10},{13,12},{... | collective-permute-start | bytes 3145736 | tf_op jit(solution)/shard_map/ppermute | solution.py:38
  6.6 25.3 %collective-permute-start.2 = (bf16[32,128,128]{2,1,0:T(8,128)(2,1)S(1)}, bf16[32,128,128]{2,1,0:T(8,128)(2,1)}, u32[]{:S(2)}, u32[]{:S(2)}) collective-permute-start(bf16[32,128,128]{2,1,0:T(8,128)(2,1)S(1)} %bitcast.26), channel_id=1, source_target_pairs={{0,4},{4,8},{8,12},{12,16},{16,20},{20,24},{24,28},{1,5},{5,9},{9,... | collective-permute-start | bytes 3145736 | tf_op jit(solution)/shard_map/ppermute | solution.py:38
  8.5 24.4 %collective-permute-start.3 = (bf16[32,128,128]{2,1,0:T(8,128)(2,1)S(1)}, bf16[32,128,128]{2,1,0:T(8,128)(2,1)}, u32[]{:S(2)}, u32[]{:S(2)}) collective-permute-start(bf16[32,128,128]{2,1,0:T(8,128)(2,1)S(1)} %bitcast.27), channel_id=1, source_target_pairs={{4,0},{8,4},{12,8},{16,12},{20,16},{24,20},{28,24},{5,1},{9,5},{13... | collective-permute-start | bytes 3145736 | tf_op jit(solution)/shard_map/ppermute | solution.py:38
  12.5 3.1 %copy-start = (bf16[1,1,32,7,128,128]{5,4,3,2,1,0:T(8,128)(2,1)S(1)}, bf16[1,1,32,7,128,128]{5,4,3,2,1,0:T(8,128)(2,1)}, u32[]{:S(2)}) copy-start(bf16[1,1,32,7,128,128]{5,4,3,2,1,0:T(8,128)(2,1)} %param.5) | copy-start | bytes 22020100
  28.5 1.3 copy-start.6
  29.8 1.3 copy-start.7
  31.2 1.8 copy-start.9
  62.4 21.2 %collective-permute-start.4 = (bf16[5,2,2,128,128]{4,3,2,1,0:T(8,128)(2,1)S(1)}, bf16[5,2,2,128,128]{4,3,2,1,0:T(8,128)(2,1)S(1)}, u32[]{:S(2)}, u32[]{:S(2)}) collective-permute-start(bf16[5,2,2,128,128]{4,3,2,1,0:T(8,128)(2,1)S(1)} %get-tuple-element.28), channel_id=1, source_target_pairs={{0,1},{1,2},{2,3},{4,5},{5,6},{6,7},{8,9},{9,10},{10,11},{12,13},{... | collective-permute-start | bytes 1966088 | tf_op jit(solution)/shard_map/ppermute | solution.py:38
  68.7 19.2 %collective-permute-start.5 = (bf16[5,2,2,128,128]{4,3,2,1,0:T(8,128)(2,1)S(1)}, bf16[5,2,2,128,128]{4,3,2,1,0:T(8,128)(2,1)S(1)}, u32[]{:S(2)}, u32[]{:S(2)}) collective-permute-start(bf16[5,2,2,128,128]{4,3,2,1,0:T(8,128)(2,1)S(1)} %get-tuple-element.29), channel_id=1, source_target_pairs={{1,0},{2,1},{3,2},{5,4},{6,5},{7,6},{9,8},{10,9},{11,10},{13,12},{... | collective-permute-start | bytes 1966088 | tf_op jit(solution)/shard_map/ppermute | solution.py:38
  70.0 17.9 %collective-permute-start.6 = (bf16[5,2,2,128,128]{4,3,2,1,0:T(8,128)(2,1)S(1)}, bf16[5,2,2,128,128]{4,3,2,1,0:T(8,128)(2,1)S(1)}, u32[]{:S(2)}, u32[]{:S(2)}) collective-permute-start(bf16[5,2,2,128,128]{4,3,2,1,0:T(8,128)(2,1)S(1)} %get-tuple-element.30), channel_id=1, source_target_pairs={{0,4},{4,8},{8,12},{12,16},{16,20},{20,24},{24,28},{1,5},{5,9},{9,... | collective-permute-start | bytes 1966088 | tf_op jit(solution)/shard_map/ppermute | solution.py:38
  72.5 15.5 %collective-permute-start.7 = (bf16[5,2,2,128,128]{4,3,2,1,0:T(8,128)(2,1)S(1)}, bf16[5,2,2,128,128]{4,3,2,1,0:T(8,128)(2,1)S(1)}, u32[]{:S(2)}, u32[]{:S(2)}) collective-permute-start(bf16[5,2,2,128,128]{4,3,2,1,0:T(8,128)(2,1)S(1)} %get-tuple-element.31), channel_id=1, source_target_pairs={{4,0},{8,4},{12,8},{16,12},{20,16},{24,20},{28,24},{5,1},{9,5},{13... | collective-permute-start | bytes 1966088 | tf_op jit(solution)/shard_map/ppermute | solution.py:38
  88.0 1.3 copy-start.3
  90.1 41.8 %collective-permute-start.8 = (bf16[13,2,2,128,128]{4,3,2,1,0:T(8,128)(2,1)S(1)}, bf16[13,2,2,128,128]{4,3,2,1,0:T(8,128)(2,1)S(1)}, u32[]{:S(2)}, u32[]{:S(2)}) collective-permute-start(bf16[13,2,2,128,128]{4,3,2,1,0:T(8,128)(2,1)S(1)} %finished_window.1.refs_0_), channel_id=1, source_target_pairs={{0,1},{1,2},{2,3},{4,5},{5,6},{6,7},{8,9},{9,10},{10,11},{12,13},{... | collective-permute-start | bytes 5111816 | tf_op jit(solution)/shard_map/ppermute | solution.py:38
  94.7 41.6 %collective-permute-start.9 = (bf16[13,2,2,128,128]{4,3,2,1,0:T(8,128)(2,1)S(1)}, bf16[13,2,2,128,128]{4,3,2,1,0:T(8,128)(2,1)S(1)}, u32[]{:S(2)}, u32[]{:S(2)}) collective-permute-start(bf16[13,2,2,128,128]{4,3,2,1,0:T(8,128)(2,1)S(1)} %finished_window.1.refs_0_), channel_id=1, source_target_pairs={{1,0},{2,1},{3,2},{5,4},{6,5},{7,6},{9,8},{10,9},{11,10},{13,12},{... | collective-permute-start | bytes 5111816 | tf_op jit(solution)/shard_map/ppermute | solution.py:38
  136.3 6.9 %copy-start.1 = (bf16[13,2,2,128,128]{4,3,2,1,0:T(8,128)(2,1)}, bf16[13,2,2,128,128]{4,3,2,1,0:T(8,128)(2,1)S(1)}, u32[]{:S(2)}) copy-start(bf16[13,2,2,128,128]{4,3,2,1,0:T(8,128)(2,1)S(1)} %collective-permute-done.9.refs_1_) | copy-start | bytes 5111812
  137.7 71.8 %collective-permute-start.10 = (bf16[12,2,2,128,128]{4,3,2,1,0:T(8,128)(2,1)}, bf16[12,2,2,128,128]{4,3,2,1,0:T(8,128)(2,1)}, u32[]{:S(2)}, u32[]{:S(2)}) collective-permute-start(bf16[12,2,2,128,128]{4,3,2,1,0:T(8,128)(2,1)} %slice.6), channel_id=1, source_target_pairs={{0,1},{1,2},{2,3},{4,5},{5,6},{6,7},{8,9},{9,10},{10,11},{12,13},{... | collective-permute-start | bytes 4718600 | tf_op jit(solution)/shard_map/ppermute | solution.py:38
  143.2 66.3 %collective-permute-start.11 = (bf16[12,2,2,128,128]{4,3,2,1,0:T(8,128)(2,1)}, bf16[12,2,2,128,128]{4,3,2,1,0:T(8,128)(2,1)}, u32[]{:S(2)}, u32[]{:S(2)}) collective-permute-start(bf16[12,2,2,128,128]{4,3,2,1,0:T(8,128)(2,1)} %slice.7), channel_id=1, source_target_pairs={{1,0},{2,1},{3,2},{5,4},{6,5},{7,6},{9,8},{10,9},{11,10},{13,12},{... | collective-permute-start | bytes 4718600 | tf_op jit(solution)/shard_map/ppermute | solution.py:38
  145.7 59.1 %collective-permute-start.12 = (bf16[9,2,2,128,128]{4,3,2,1,0:T(8,128)(2,1)}, bf16[9,2,2,128,128]{4,3,2,1,0:T(8,128)(2,1)S(1)}, u32[]{:S(2)}, u32[]{:S(2)}) collective-permute-start(bf16[9,2,2,128,128]{4,3,2,1,0:T(8,128)(2,1)} %constant_dynamic-slice_fusion), channel_id=1, source_target_pairs={{0,3},{3,0},{4,7},{7,4},{8,11},{11,8},{12,15},{15,12},{16,19},{19,... | collective-permute-start | bytes 3538952 | tf_op jit(solution)/shard_map/ppermute | solution.py:384
  204.8 1.5 copy-start.2

commit v3 on v2

--- a/solution.py
+++ b/solution.py
@@ -25,6 +25,7 @@
     (2, 0),
 )
 TRAVEL = (4, 1, 5, 9, 0, 2, 6, 10, 12, 3, 7, 11, 8)
+HALVES = (TRAVEL[:6], TRAVEL[6:])
 smoothing = 2.0 / 3.0
 MEMBERS = 2
 ROWS_PER_STEP = 4
@@ -156,8 +157,8 @@
 
 def partial_kernel(members, taps, tiles, sources, slots, ends, *refs):
     a_tiles, dinv_hbm, *tents = refs[:6]
-    right_own, left_own, *outs = refs[6:13]
-    a_held, dinv, tent, right, left, sums, sems = refs[13:]
+    right_own, *outs, right_out = refs[6:12]
+    a_held, dinv, tent, right, left, sums, sems = refs[12:]
     tile = dinv.shape[-1]
     rows = dinv.shape[0]
     chunks = rows // ROWS_PER_STEP
@@ -174,16 +175,13 @@
     ]
     others.append(pltpu.make_async_copy(dinv_hbm, dinv, sems.at[chunks + 4]))
     own_part = (pl.ds(outer * tile, members * tile), slice(None))
-    own_copies = [
-        pltpu.make_async_copy(right_own, right.at[own_part], sems.at[chunks + 5]),
-        pltpu.make_async_copy(left_own, left.at[own_part], sems.at[chunks + 6]),
-    ]
+    own_copy = pltpu.make_async_copy(right_own, right.at[own_part], sems.at[chunks + 5])
+    out_copy = pltpu.make_async_copy(right, right_out, sems.at[chunks + 6])
     for copy in others:
         copy.start()
     for c in range(chunks):
         a_copy(c).start()
-    for copy in own_copies:
-        copy.start()
+    own_copy.start()
     for copy in others:
         copy.wait()
 
@@ -221,26 +219,13 @@
         return last
 
     lax.fori_loop(0, chunks, one_chunk, 0)
-    for copy in own_copies:
-        copy.wait()
-    width = members * tile
-
-    def one_direction(d2, carry):
-        value = lax.dot_general(
-            left[...], right[lane_tiles(d2, width), :], NT, preferred_element_type=jnp.float32
-        )
-        for d1, out in enumerate(outs):
-            for m in range(members):
-                for m2 in range(members):
-                    row = (d1 * members + m) * tile
-                    block = value[row : row + tile, m2 * tile : (m2 + 1) * tile]
-                    out[d2, m, m2] = block.astype(out.dtype)
-        return carry
-
-    lax.fori_loop(0, 5, one_direction, 0)
-
-
-def partial_blocks(a_tiles, dinv, tents, own_right, own_left, lists, members):
+    own_copy.wait()
+    out_copy.start()
+    product(left, right, outs, members, tile)
+    out_copy.wait()
+
+
+def partial_blocks(a_tiles, dinv, tents, own_right, lists, members):
     rows, taps, tile = a_tiles.shape[0], a_tiles.shape[1], a_tiles.shape[-1]
     block = (5, members, members, tile, tile)
     whole = pl.BlockSpec(block, lambda s, *_: (0,) * 5)
@@ -251,40 +236,76 @@
         grid_spec=pltpu.PrefetchScalarGridSpec(
             num_scalar_prefetch=4,
             grid=(1,),
-            in_specs=[pl.BlockSpec(memory_space=pl.ANY)] * 8,
-            out_specs=[whole] * 5,
+            in_specs=[pl.BlockSpec(memory_space=pl.ANY)] * 7,
+            out_specs=[whole] * 4 + [pl.BlockSpec(memory_space=pl.ANY)],
             scratch_shapes=[
                 pltpu.VMEM((rows * taps, tile, tile), jnp.bfloat16),
                 pltpu.VMEM((rows, tile, tile), jnp.bfloat16),
                 pltpu.VMEM((4 * rows, tile, tile), jnp.bfloat16),
                 pltpu.VMEM((slots, rows * tile), jnp.bfloat16),
-                pltpu.VMEM((slots, rows * tile), jnp.bfloat16),
+                pltpu.VMEM((outer, rows * tile), jnp.bfloat16),
                 pltpu.VMEM((outer + tile, ROWS_PER_STEP * tile), jnp.float32),
                 pltpu.SemaphoreType.DMA((rows // ROWS_PER_STEP + 7,)),
             ],
         ),
         out_shape=[jax.ShapeDtypeStruct(block, jnp.bfloat16)] * 4
-        + [jax.ShapeDtypeStruct(block, jnp.float32)],
-        compiler_params=pltpu.CompilerParams(vmem_limit_bytes=50 * 1024 * 1024),
+        + [jax.ShapeDtypeStruct((slots, rows * tile), jnp.bfloat16)],
+        compiler_params=pltpu.CompilerParams(vmem_limit_bytes=48 * 1024 * 1024),
         cost_estimate=pl.CostEstimate(
-            flops=2 * tile**3 * rows * members * (4 + 25 * members),
+            flops=2 * tile**3 * rows * members * (4 + 20 * members),
             bytes_accessed=2 * (a_tiles.size + 20 * dinv.size),
             transcendentals=0,
         ),
         name="partial_blocks",
-    )(*lists, a_tiles.reshape(rows * taps, tile, tile), dinv, *tents, own_right, own_left)
+    )(*lists, a_tiles.reshape(rows * taps, tile, tile), dinv, *tents, own_right)
+
+
+def own_rows_kernel(members, left_own, right_all, own, left, right, sems):
+    copies = [
+        pltpu.make_async_copy(left_own, left, sems.at[0]),
+        pltpu.make_async_copy(right_all, right, sems.at[1]),
+    ]
+    for copy in copies:
+        copy.start()
+    for copy in copies:
+        copy.wait()
+    product(left, right, (own,), members, own.shape[-1])
+
+
+def own_rows(left, right, members):
+    tile = left.shape[0] // members
+    block = (5, members, members, tile, tile)
+    return pl.pallas_call(
+        functools.partial(own_rows_kernel, members),
+        grid=(1,),
+        in_specs=[pl.BlockSpec(memory_space=pl.ANY)] * 2,
+        out_specs=pl.BlockSpec(block, lambda s: (0,) * 5),
+        out_shape=jax.ShapeDtypeStruct(block, jnp.float32),
+        scratch_shapes=[
+            pltpu.VMEM(left.shape, left.dtype),
+            pltpu.VMEM(right.shape, right.dtype),
+            pltpu.SemaphoreType.DMA((2,)),
+        ],
+        compiler_params=pltpu.CompilerParams(vmem_limit_bytes=32 * 1024 * 1024),
+        cost_estimate=pl.CostEstimate(
+            flops=2 * left.size * right.shape[0],
+            bytes_accessed=2 * (left.size + right.size),
+            transcendentals=0,
+        ),
+        name="own_rows",
+    )(left, right)
 
 
 def window_kernel(*refs):
-    out = refs[-1]
-    for position, offset in enumerate(TRAVEL):
-        total = None
-        for shift, values in zip(CROSS_SHIFTS, refs):
-            for d, member in enumerate(CROSS_SHIFTS):
-                if (shift[0] + member[0], shift[1] + member[1]) == WINDOW_SHIFTS[offset]:
-                    term = values[d].astype(jnp.float32)
-                    total = term if total is None else total + term
-        out[position] = total.astype(out.dtype)
+    for out, half in zip(refs[5:], HALVES):
+        for position, offset in enumerate(half):
+            total = None
+            for shift, values in zip(CROSS_SHIFTS, refs):
+                for d, member in enumerate(CROSS_SHIFTS):
+                    if (shift[0] + member[0], shift[1] + member[1]) == WINDOW_SHIFTS[offset]:
+                        term = values[d].astype(jnp.float32)
+                        total = term if total is None else total + term
+            out[position] = total.astype(out.dtype)
 
 
 def finished_window(blocks):
@@ -296,8 +317,11 @@
         window_kernel,
         grid=(members,),
         in_specs=[spec(5)] * 5,
-        out_specs=spec(13),
-        out_shape=jax.ShapeDtypeStruct((13, members, members, tile, tile), jnp.bfloat16),
+        out_specs=[spec(len(half)) for half in HALVES],
+        out_shape=[
+            jax.ShapeDtypeStruct((len(half), members, members, tile, tile), jnp.bfloat16)
+            for half in HALVES
+        ],
         compiler_params=pltpu.CompilerParams(vmem_limit_bytes=32 * 1024 * 1024),
         cost_estimate=pl.CostEstimate(
             flops=5 * blocks[0].size, bytes_accessed=16 * blocks[0].size, transcendentals=0
@@ -306,16 +330,16 @@
     )(*blocks)
 
 
-def place_kernel(lists, members, row, kind, *refs):
+def place_kernel(lists, members, row, valid, *refs):
     arrays, (out, nothing, sems) = refs[: len(lists)], refs[-3:]
     nothing[...] = jnp.zeros_like(nothing)
 
     def each(act):
-        for index, (array, held) in enumerate(zip(arrays, lists)):
-
-            @pl.when(kind[index] == 1)
+        for index, (array, (held, written)) in enumerate(zip(arrays, lists)):
+
+            @pl.when(valid[index] == 1)
             def _():
-                for offset in range(13):
+                for offset in written:
                     for m in range(members):
                         source = array.at[held.index(offset), m] if offset in held else nothing
                         act(
@@ -333,34 +357,32 @@
 def placed(out, pieces, count):
     arrays = [piece[0] for piece in pieces]
     members, _, tile, _ = arrays[0].shape[1:]
-    in_specs = [pl.BlockSpec(a.shape, lambda s, *_: (0,) * 5) for a in arrays]
-    shape = (count, members, 13, members, tile, tile)
+    scalars = pl.BlockSpec(memory_space=pltpu.SMEM)
+    in_specs = [scalars] * 2 + [pl.BlockSpec(memory_space=pltpu.VMEM)] * len(arrays)
     operands = list(arrays)
     if out is not None:
         in_specs.append(pl.BlockSpec(memory_space=pl.ANY))
         operands.append(out)
-    rows = jnp.stack([jnp.asarray(jnp.where(p[3], p[2], 0), jnp.int32) for p in pieces])
-    kinds = jnp.stack([jnp.asarray(p[3], jnp.int32) for p in pieces])
+    rows = jnp.stack([jnp.asarray(jnp.where(p[4], p[3], 0), jnp.int32) for p in pieces])
+    valid = jnp.stack([jnp.asarray(p[4], jnp.int32) for p in pieces])
     return pl.pallas_call(
-        functools.partial(place_kernel, tuple(p[1] for p in pieces), members),
-        grid_spec=pltpu.PrefetchScalarGridSpec(
-            num_scalar_prefetch=2,
-            grid=(1,),
-            in_specs=in_specs,
-            out_specs=pl.BlockSpec(memory_space=pl.ANY),
-            scratch_shapes=[
-                pltpu.VMEM((members, tile, tile), jnp.bfloat16),
-                pltpu.SemaphoreType.DMA((len(pieces) * 13 * members,)),
-            ],
-        ),
-        out_shape=jax.ShapeDtypeStruct(shape, jnp.bfloat16),
+        functools.partial(place_kernel, tuple(p[1:3] for p in pieces), members),
+        in_specs=in_specs,
+        out_specs=pl.BlockSpec(memory_space=pl.ANY),
+        scratch_shapes=[
+            pltpu.VMEM((members, tile, tile), jnp.bfloat16),
+            pltpu.SemaphoreType.DMA((len(pieces) * 13 * members,)),
+        ],
+        out_shape=jax.ShapeDtypeStruct(
+            (count, members, 13, members, tile, tile), jnp.bfloat16
+        ),
         input_output_aliases={2 + len(arrays): 0} if out is not None else {},
-        compiler_params=pltpu.CompilerParams(vmem_limit_bytes=32 * 1024 * 1024),
+        compiler_params=pltpu.CompilerParams(vmem_limit_bytes=24 * 1024 * 1024),
         cost_estimate=pl.CostEstimate(
             flops=0, bytes_accessed=6 * 13 * members * members * tile * tile, transcendentals=0
         ),
         name="placed",
-    )(rows, kinds, *operands)
+    )(rows, valid, *operands)
 
 
 def hopped(shard, lists, hop, count_y):
@@ -375,32 +397,40 @@
     return arrived, (lower, upper)
 
 
-def end_to_end(shard, grid_y, count_y):
+def end_to_end(halves, grid_y, count_y):
     lower = tuple(o for o in TRAVEL if WINDOW_SHIFTS[o][1] >= 0)
     upper = tuple(o for o in TRAVEL if WINDOW_SHIFTS[o][1] <= 0)
     start = jnp.where(grid_y == 0, len(TRAVEL) - len(lower), 0)
-    sent = lax.dynamic_slice_in_dim(shard, start, len(lower), axis=0)
+    sent = lax.dynamic_slice_in_dim(jnp.concatenate(halves, axis=0), start, len(lower), axis=0)
     last = count_y - 1
     moved = lax.ppermute(sent, "sy", [(0, last), (last, 0)])
-    return [(moved, lower, 0, grid_y == last), (moved, upper, last, grid_y == 0)]
-
-
-def gathered_rows(shard, grid_y, count_y):
-    arrived, lists = (shard, shard), (TRAVEL, TRAVEL)
-    pieces = [(shard, TRAVEL, grid_y, True)]
-    direct = end_to_end(shard, grid_y, count_y)
+    return [
+        (moved, lower, TRAVEL, 0, grid_y == last),
+        (moved, upper, TRAVEL, last, grid_y == 0),
+    ]
+
+
+def gathered_rows(halves, grid_y, count_y):
+    chains = [((half, half), (group, group)) for half, group in zip(halves, HALVES)]
+    pieces = [(half, group, group, grid_y, True) for half, group in zip(halves, HALVES)]
     out = None
     for hop in range(1, count_y - 1):
-        arrived, lists = hopped(arrived, lists, hop, count_y)
+        chains = [hopped(*chain, hop, count_y) for chain in chains]
+        if hop == 1:
+            direct = end_to_end(halves, grid_y, count_y)
         out = placed(out, pieces, count_y)
-        arrived, out = lax.optimization_barrier((arrived, out))
-        pieces = [
-            (arrived[0], lists[0], grid_y - hop, grid_y >= hop),
-            (arrived[1], lists[1], grid_y + hop, grid_y + hop < count_y),
-        ]
-        if hop == 1:
-            pieces += direct
-    return placed(out, pieces, count_y)
+        (first, lists), second = chains
+        second, out = (second[0], out) if hop > 1 else lax.optimization_barrier((second[0], out))
+        chains = [(first, lists), (second, chains[1][1])]
+        pieces = []
+        for (arrived, lists), group in zip(chains, HALVES):
+            has_lower, has_upper = grid_y >= hop, grid_y + hop < count_y
+            pieces += [
+                (arrived[0], lists[0], group, grid_y - hop, has_lower),
+                (arrived[1], lists[1], group, grid_y + hop, has_upper),
+            ]
+    out = placed(out, direct + pieces[:2], count_y)
+    return placed(out, pieces[2:], count_y)
 
 
 def local(a_tiles, columns, ptent, dinv, agg):
@@ -427,19 +457,19 @@
         count_y,
         MEMBERS,
     )
-    to_lower_y, to_upper_y, to_lower_x, to_upper_x, own = partial_blocks(
-        coupling, inverse, tents, own_right, own_left, lists, MEMBERS
-    )
-    shard = finished_window(
+    to_lower_y, to_upper_y, to_lower_x, to_upper_x, right = partial_blocks(
+        coupling, inverse, tents, own_right, lists, MEMBERS
+    )
+    halves = finished_window(
         (
             shifted(to_upper_y, "sy", 1),
             shifted(to_lower_y, "sy", -1),
             shifted(to_upper_x, "sx", 1),
             shifted(to_lower_x, "sx", -1),
-            own,
+            own_rows(own_left, right, MEMBERS),
         )
     )
-    return gathered_rows(shard, grid_y, count_y)[None]
+    return gathered_rows(halves, grid_y, count_y)[None]
 
 
 def solution(mesh):

time: 214 us -> 194 us (0.907)
  the two profiles are of different devices: /device:TPU:2 before, /device:TPU:3 now
where the time goes in v3:
time: 194 us; the launch traced here: 193 us
  waiting for transfers between devices  71.7 us (37%)
  Pallas kernels  57.2 us (29%)
  starting transfers between devices  47.6 us (25%)
  local copies, waits for them, and re-layouts  13.2 us (7%)
  other arithmetic  2.77 us (1%)
    ppermute x16, waiting for transfers between devices, shifted(): return lax.ppermute(x, axis, pairs)  63.2 us
    ppermute x16, starting transfers between devices, shifted(): return lax.ppermute(x, axis, pairs)  44.9 us
    pallas_call x1, Pallas kernels, partial_blocks(): pl.pallas_call(functools.partial(partial_kernel, members, taps), grid_spe...  25.4 us
    pallas_call x1, Pallas kernels, own_slots(): pl.pallas_call(functools.partial(own_kernel, count_y, rows, members, taps...  13 us
    pallas_call x4, Pallas kernels, placed(): pl.pallas_call(functools.partial(place_kernel, tuple((p[1:3] for p in pie...  12.8 us
    unnamed x14, local copies, waits for them, and re-layouts  10.2 us
    ppermute x1, waiting for transfers between devices, end_to_end(): moved = lax.ppermute(sent, 'sy', [(0, last), (last, 0)])  8.51 us
    pallas_call x1, Pallas kernels, own_rows(): pl.pallas_call(functools.partial(own_rows_kernel, members), grid=(1,), in...  4.57 us
  transfers between devices with their start and end apart: 17, of which 9 were waited for; matrix products, arithmetic and copies ran while one was open for 3% of the time, Pallas kernels for 14%

profile of v3, /device:TPU:3, one launch (start us, length us, event | category | flops | bytes accessed | tf_op | source)
XLA Modules:
  0.0 192.7 jit_solution(17222954561613817932)
XLA Ops:
  0.0 0.0 copy-start.5
  0.0 0.0 copy-start.2
  0.0 1.7 copy.11
  1.7 3.3 %collective-permute-start = (bf16[32,128,128]{2,1,0:T(8,128)(2,1)S(1)}, bf16[32,128,128]{2,1,0:T(8,128)(2,1)S(1)}, u32[]{:S(2)}, u32[]{:S(2)}) collective-permute-start(bf16[32,128,128]{2,1,0:T(8,128)(2,1)S(1)} %bitcast.24), channel_id=1, source_target_pairs={{0,1},{1,2},{2,3},{4,5},{5,6},{6,7},{8,9},{9,10},{10,11},{12,13},{... | collective-permute-start | bytes 3145736 | tf_op jit(solution)/shard_map/ppermute | solution.py:39
  5.0 1.3 collective-permute-start.1
  6.3 4.0 %collective-permute-start.2 = (bf16[32,128,128]{2,1,0:T(8,128)(2,1)S(1)}, bf16[32,128,128]{2,1,0:T(8,128)(2,1)}, u32[]{:S(2)}, u32[]{:S(2)}) collective-permute-start(bf16[32,128,128]{2,1,0:T(8,128)(2,1)S(1)} %bitcast.26), channel_id=1, source_target_pairs={{0,4},{4,8},{8,12},{12,16},{16,20},{20,24},{24,28},{1,5},{5,9},{9,... | collective-permute-start | bytes 3145736 | tf_op jit(solution)/shard_map/ppermute | solution.py:39
  10.3 1.9 collective-permute-start.3
  12.2 0.0 copy-done.5
  12.2 0.1 copy.10
  12.3 0.1 reshape.12.columns
  12.4 0.1 pad_add_fusion.2.place
  12.5 0.0 copy-done.2
  12.5 0.0 copy-done.3
  12.5 3.1 %copy-done.1 = bf16[1,1,32,7,128,128]{5,4,3,2,1,0:T(8,128)(2,1)S(1)} copy-done((bf16[1,1,32,7,128,128]{5,4,3,2,1,0:T(8,128)(2,1)S(1)}, bf16[1,1,32,7,128,128]{5,4,3,2,1,0:T(8,128)(2,1)}, u32[]{:S(2)}) %copy-start.1) | copy-done | bytes 7340056
  15.6 13.0 %own_slots.1 = (bf16[256,4096]{1,0:T(8,128)(2,1)S(1)}, bf16[256,4096]{1,0:T(8,128)(2,1)S(1)}, s32[224]{0:T(256)S(1)}, s32[224]{0:T(256)S(1)}, s32[224]{0:T(256)S(1)}, /*index=5*/s32[8]{0:T(128)S(1)}) custom-call(s32[224]{0:T(256)S(1)} %reshape.12.columns, s32[1024]{0:T(1024)S(1)} %copy-done.3, s32[2]{0:T(128)S(1)} %pad_add_fusion.2.place, ...), custom_call_target="tpu_custom_call" | custom-call | flops 1207959552 | bytes 13631488 | tf_op jit(solution)/shard_map/own_slots/pallas_call | solution.py:101
  28.6 0.0 copy-start.4
  28.6 1.3 copy-done.4
  29.9 0.0 collective-permute-done.refs_2_
  29.9 0.8 collective-permute-done.1.refs_3_
  30.7 0.0 collective-permute-done.2.refs_4_
  30.7 4.3 %collective-permute-done.3.refs_5_ = bf16[32,128,128]{2,1,0:T(8,128)(2,1)} collective-permute-done((bf16[32,128,128]{2,1,0:T(8,128)(2,1)S(1)}, bf16[32,128,128]{2,1,0:T(8,128)(2,1)}, u32[]{:S(2)}, u32[]{:S(2)}) %collective-permute-start.3) | collective-permute-done | bytes 1048608 | tf_op jit(solution)/shard_map/ppermute | solution.py:39
  35.0 25.4 %partial_blocks.1 = (bf16[5,2,2,128,128]{4,3,2,1,0:T(8,128)(2,1)S(1)}, bf16[5,2,2,128,128]{4,3,2,1,0:T(8,128)(2,1)S(1)}, bf16[5,2,2,128,128]{4,3,2,1,0:T(8,128)(...) custom-call(s32[224]{0:T(256)S(1)} %get-tuple-element.21.tiles, s32[224]{0:T(256)S(1)} %get-tuple-element.22.sources, ...), custom_call_target="tpu_custom_call" | custom-call | flops 11811160064 | bytes 28311552 | tf_op jit(solution)/shard_map/partial_blocks/pallas_call | solution.py:234
  60.4 5.6 %collective-permute-start.4 = (bf16[5,2,2,128,128]{4,3,2,1,0:T(8,128)(2,1)S(1)}, bf16[5,2,2,128,128]{4,3,2,1,0:T(8,128)(2,1)S(1)}, u32[]{:S(2)}, u32[]{:S(2)}) collective-permute-start(bf16[5,2,2,128,128]{4,3,2,1,0:T(8,128)(2,1)S(1)} %get-tuple-element.26), channel_id=1, source_target_pairs={{0,1},{1,2},{2,3},{4,5},{5,6},{6,7},{8,9},{9,10},{10,11},{12,13},{... | collective-permute-start | bytes 1966088 | tf_op jit(solution)/shard_map/ppermute | solution.py:39
  66.0 1.3 collective-permute-start.5
  67.3 1.9 collective-permute-start.6
  69.3 2.4 %collective-permute-start.7 = (bf16[5,2,2,128,128]{4,3,2,1,0:T(8,128)(2,1)S(1)}, bf16[5,2,2,128,128]{4,3,2,1,0:T(8,128)(2,1)S(1)}, u32[]{:S(2)}, u32[]{:S(2)}) collective-permute-start(bf16[5,2,2,128,128]{4,3,2,1,0:T(8,128)(2,1)S(1)} %get-tuple-element.29), channel_id=1, source_target_pairs={{4,0},{8,4},{12,8},{16,12},{20,16},{24,20},{28,24},{5,1},{9,5},{13... | collective-permute-start | bytes 1966088 | tf_op jit(solution)/shard_map/ppermute | solution.py:39
  71.7 0.0 copy-start
  71.7 4.0 %copy-done = bf16[1280,4096]{1,0:T(8,128)(2,1)S(1)} copy-done((bf16[1280,4096]{1,0:T(8,128)(2,1)S(1)}, bf16[1280,4096]{1,0:T(8,128)(2,1)}, u32[]{:S(2)}) %copy-start) | copy-done | bytes 10485784
  75.7 4.6 %own_rows.1.refs_4_ = f32[5,2,2,128,128]{4,3,2,1,0:T(8,128)S(1)} custom-call(bf16[256,4096]{1,0:T(8,128)(2,1)S(1)} %get-tuple-element.30.left_own, bf16[1280,4096]{1,0:T(8,128)(2,1)S(1)} %copy-done), custom_call_target="tpu_custom_call" | custom-call | flops 2684354560 | bytes 12582912 | tf_op jit(solution)/shard_map/own_rows/pallas_call | solution.py:278
  80.2 0.0 collective-permute-done.4.refs_0_
  80.2 3.5 %collective-permute-done.5.refs_1_ = bf16[5,2,2,128,128]{4,3,2,1,0:T(8,128)(2,1)S(1)} collective-permute-done((bf16[5,2,2,128,128]{4,3,2,1,0:T(8,128)(2,1)S(1)}, bf16[5,2,2,128,128]{4,3,2,1,0:T(8,128)(2,1)S(1)}, u32[]{:S(2)}, u32[]{:S(2)}) %collective-permute-start.5) | collective-permute-done | bytes 655392 | tf_op jit(solution)/shard_map/ppermute | solution.py:39
  83.8 0.0 collective-permute-done.6.refs_2_
  83.8 0.0 collective-permute-done.7.refs_3_
  83.8 1.4 finished_window.1
  85.2 4.7 %collective-permute-start.8 = (bf16[7,2,2,128,128]{4,3,2,1,0:T(8,128)(2,1)S(1)}, bf16[7,2,2,128,128]{4,3,2,1,0:T(8,128)(2,1)}, u32[]{:S(2)}, u32[]{:S(2)}) collective-permute-start(bf16[7,2,2,128,128]{4,3,2,1,0:T(8,128)(2,1)S(1)} %get-tuple-element.32.refs_1_), channel_id=1, source_target_pairs={{0,1},{1,2},{2,3},{4,5},{5,6},{6,7},{8,9},{9,10},{10,11},{12,13},{... | collective-permute-start | bytes 2752520 | tf_op jit(solution)/shard_map/ppermute | solution.py:39
  89.9 1.3 collective-permute-start.9
  91.2 1.3 collective-permute-start.15
  92.5 5.5 %collective-permute-start.13 = (bf16[6,2,2,128,128]{4,3,2,1,0:T(8,128)(2,1)}, bf16[6,2,2,128,128]{4,3,2,1,0:T(8,128)(2,1)}, u32[]{:S(2)}, u32[]{:S(2)}) collective-permute-start(bf16[6,2,2,128,128]{4,3,2,1,0:T(8,128)(2,1)} %get-tuple-element.33.refs_0_), channel_id=1, source_target_pairs={{0,1},{1,2},{2,3},{4,5},{5,6},{6,7},{8,9},{9,10},{10,11},{12,13},{... | collective-permute-start | bytes 2359304 | tf_op jit(solution)/shard_map/ppermute | solution.py:39
  98.0 2.3 %fusion = bf16[9,2,2,128,128]{4,3,2,1,0:T(8,128)(2,1)} fusion(s32[]{:T(128)S(6)} %select_n.32, bf16[6,2,2,128,128]{4,3,2,1,0:T(8,128)(2,1)} %get-tuple-element.33.refs_0_, bf16[7,2,2,128,128]{4,3,2,1,0:T(8,128)(2,1)S(1)} %get-tuple-element.32.refs_1_), kind=kLoop, calls=%fused_computation.2 | loop fusion | flops 589824 | bytes 2883588 | tf_op jit(solution)/shard_map/concatenate | solution.py:404
  100.3 2.7 %collective-permute-start.12 = (bf16[9,2,2,128,128]{4,3,2,1,0:T(8,128)(2,1)}, bf16[9,2,2,128,128]{4,3,2,1,0:T(8,128)(2,1)S(1)}, u32[]{:S(2)}, u32[]{:S(2)}) collective-permute-start(bf16[9,2,2,128,128]{4,3,2,1,0:T(8,128)(2,1)} %fusion), channel_id=1, source_target_pairs={{0,3},{3,0},{4,7},{7,4},{8,11},{11,8},{12,15},{15,12},{16,19},{19,... | collective-permute-start | bytes 3538952 | tf_op jit(solution)/shard_map/ppermute | solution.py:406
  103.0 0.1 pad_add_fusion.3.row
  103.1 2.8 %placed.4.refs_4_ = bf16[4,2,13,2,128,128]{5,4,3,2,1,0:T(8,128)(2,1)} custom-call(s32[2]{0:T(128)S(1)} %pad_add_fusion.3.row, s32[2]{0:T(128)S(1)} %broadcast_1_valid.2.valid, bf16[6,2,2,128,128]{4,3,2,1,0:T(8,128)(2,1)} %get-tuple-element.33.refs_0_, bf16[7,2,2,128,128]{4,3,2,1,0:T(8,128)(2,1)S(1)} %get-tuple-element.32.refs_1_), custom_call_target="tpu_custom_call" | custom-call | bytes 5111808 | tf_op jit(solution)/shard_map/placed/pallas_call | solution.py:368
  105.9 1.8 collective-permute-done.8.refs_2_
  107.7 4.7 %collective-permute-done.9.refs_3_ = bf16[7,2,2,128,128]{4,3,2,1,0:T(8,128)(2,1)S(1)} collective-permute-done((bf16[7,2,2,128,128]{4,3,2,1,0:T(8,128)(2,1)S(1)}, bf16[7,2,2,128,128]{4,3,2,1,0:T(8,128)(2,1)S(1)}, u32[]{:S(2)}, u32[]{:S(2)}) %collective-permute-start.9) | collective-permute-done | bytes 917536 | tf_op jit(solution)/shard_map/ppermute | solution.py:39
  112.4 2.4 %collective-permute-start.10 = (bf16[7,2,2,128,128]{4,3,2,1,0:T(8,128)(2,1)}, bf16[7,2,2,128,128]{4,3,2,1,0:T(8,128)(2,1)S(1)}, u32[]{:S(2)}, u32[]{:S(2)}) collective-permute-start(bf16[7,2,2,128,128]{4,3,2,1,0:T(8,128)(2,1)} %collective-permute-done.8.refs_2_), channel_id=1, source_target_pairs={{0,1},{1,2},{2,3},{4,5},{5,6},{6,7},{8,9},{9,10},{10,11},{12,13},{... | collective-permute-start | bytes 2752520 | tf_op jit(solution)/shard_map/ppermute | solution.py:39
  114.8 15.3 %collective-permute-done.15.refs_1_ = bf16[6,2,2,128,128]{4,3,2,1,0:T(8,128)(2,1)} collective-permute-done((bf16[6,2,2,128,128]{4,3,2,1,0:T(8,128)(2,1)}, bf16[6,2,2,128,128]{4,3,2,1,0:T(8,128)(2,1)}, u32[]{:S(2)}, u32[]{:S(2)}) %collective-permute-start.15) | collective-permute-done | bytes 786464 | tf_op jit(solution)/shard_map/ppermute | solution.py:39
  130.2 1.3 collective-permute-start.16
  131.5 0.9 slice.6
  132.4 1.3 collective-permute-start.11
  133.7 0.0 collective-permute-done.13.refs_0_
  133.7 2.0 %slice.8 = bf16[5,2,2,128,128]{4,3,2,1,0:T(8,128)(2,1)} slice(bf16[6,2,2,128,128]{4,3,2,1,0:T(8,128)(2,1)} %collective-permute-done.13.refs_0_), slice={[1:6], [0:2], [0:2], [0:128], [0:128]} | slice | bytes 1310720 | tf_op jit(solution)/shard_map/slice | solution.py:394
  135.7 5.4 %collective-permute-start.14 = (bf16[5,2,2,128,128]{4,3,2,1,0:T(8,128)(2,1)}, bf16[5,2,2,128,128]{4,3,2,1,0:T(8,128)(2,1)}, u32[]{:S(2)}, u32[]{:S(2)}) collective-permute-start(bf16[5,2,2,128,128]{4,3,2,1,0:T(8,128)(2,1)} %slice.8), channel_id=1, source_target_pairs={{0,1},{1,2},{2,3},{4,5},{5,6},{6,7},{8,9},{9,10},{10,11},{12,13},{... | collective-permute-start | bytes 1966088 | tf_op jit(solution)/shard_map/ppermute | solution.py:39
  141.1 0.1 pad_add_fusion.6.row
  141.2 0.1 add_convert_fusion.valid
  141.3 0.1 pad_add_fusion
  141.4 0.1 pad_add_fusion.4
  141.5 3.8 %placed.5.refs_4_ = bf16[4,2,13,2,128,128]{5,4,3,2,1,0:T(8,128)(2,1)} custom-call(s32[4]{0:T(128)S(1)} %pad_add_fusion.6.row, s32[4]{0:T(128)S(1)} %add_convert_fusion.valid, bf16[6,2,2,128,128]{4,3,2,1,0:T(8,128)(2,1)} %collective-permute-done.13.refs_0_, ...), custom_call_target="tpu_custom_call", output_to_operand_aliasing={{}: (6, {})} | custom-call | bytes 5111808 | tf_op jit(solution)/shard_map/placed/pallas_call | solution.py:368
  145.2 8.5 %collective-permute-done.12.refs_0_.refs_1_ = bf16[9,2,2,128,128]{4,3,2,1,0:T(8,128)(2,1)S(1)} collective-permute-done((bf16[9,2,2,128,128]{4,3,2,1,0:T(8,128)(2,1)}, bf16[9,2,2,128,128]{4,3,2,1,0:T(8,128)(2,1)S(1)}, u32[]{:S(2)}, u32[]{:S(2)}) %collective-permute-start.12) | collective-permute-done | bytes 1179680 | tf_op jit(solution)/shard_map/ppermute | solution.py:406
  153.7 29.9 %collective-permute-done.14.refs_2_ = bf16[5,2,2,128,128]{4,3,2,1,0:T(8,128)(2,1)} collective-permute-done((bf16[5,2,2,128,128]{4,3,2,1,0:T(8,128)(2,1)}, bf16[5,2,2,128,128]{4,3,2,1,0:T(8,128)(2,1)}, u32[]{:S(2)}, u32[]{:S(2)}) %collective-permute-start.14) | collective-permute-done | bytes 655392 | tf_op jit(solution)/shard_map/ppermute | solution.py:39
  183.7 0.0 collective-permute-done.16.refs_3_
  183.7 3.7 %placed.6.refs_2_ = bf16[4,2,13,2,128,128]{5,4,3,2,1,0:T(8,128)(2,1)} custom-call(s32[4]{0:T(128)S(1)} %get-tuple-element.37.row, s32[4]{0:T(128)S(1)} %get-tuple-element.38.valid, bf16[9,2,2,128,128]{4,3,2,1,0:T(8,128)(2,1)S(1)} %collective-permute-done.12.refs_0_.refs_1_, ...), custom_call_target="tpu_custom_call", output_to_operand_aliasing={{}: (6, {})} | custom-call | bytes 5111808 | tf_op jit(solution)/shard_map/placed/pallas_call | solution.py:368
  187.4 2.8 %collective-permute-done.11.refs_1_ = bf16[6,2,2,128,128]{4,3,2,1,0:T(8,128)(2,1)} collective-permute-done((bf16[6,2,2,128,128]{4,3,2,1,0:T(8,128)(2,1)}, bf16[6,2,2,128,128]{4,3,2,1,0:T(8,128)(2,1)}, u32[]{:S(2)}, u32[]{:S(2)}) %collective-permute-start.11) | collective-permute-done | bytes 786464 | tf_op jit(solution)/shard_map/ppermute | solution.py:39
  190.2 0.0 collective-permute-done.10.refs_0_
  190.2 2.5 %placed.7 = bf16[4,2,13,2,128,128]{5,4,3,2,1,0:T(8,128)(2,1)} custom-call(s32[2]{0:T(128)S(1)} %get-tuple-element.39.row, s32[2]{0:T(128)S(1)} %get-tuple-element.40.valid, bf16[7,2,2,128,128]{4,3,2,1,0:T(8,128)(2,1)S(1)} %collective-permute-done.10.refs_0_, ...), custom_call_target="tpu_custom_call", output_to_operand_aliasing={{}: (4, {})} | custom-call | bytes 5111808 | tf_op jit(solution)/shard_map/placed/pallas_call | solution.py:368
  (3 shorter events, 0.0 us)
Async XLA Ops:
  0.0 12.2 %copy-start.5 = (s32[1,1,32,7]{2,1,3,0:T(1,128)S(1)}, s32[1,1,32,7]{2,1,3,0:T(1,128)}, u32[]{:S(2)}) copy-start(s32[1,1,32,7]{2,1,3,0:T(1,128)} %param.6) | copy-start | bytes 2692
  0.0 12.5 %copy-start.2 = (bf16[1,1,32,128,128]{4,3,2,1,0:T(8,128)(2,1)S(1)}, bf16[1,1,32,128,128]{4,3,2,1,0:T(8,128)(2,1)}, u32[]{:S(2)}) copy-start(bf16[1,1,32,128,128]{4,3,2,1,0:T(8,128)(2,1)} %param.8) | copy-start | bytes 3145732
  0.0 12.5 %copy-start.3 = (s32[1024]{0:T(1024)S(1)}, s32[1024]{0:T(1024)}, u32[]{:S(2)}) copy-start(s32[1024]{0:T(1024)} %agg.1) | copy-start | bytes 12292
  1.7 28.2 %collective-permute-start = (bf16[32,128,128]{2,1,0:T(8,128)(2,1)S(1)}, bf16[32,128,128]{2,1,0:T(8,128)(2,1)S(1)}, u32[]{:S(2)}, u32[]{:S(2)}) collective-permute-start(bf16[32,128,128]{2,1,0:T(8,128)(2,1)S(1)} %bitcast.24), channel_id=1, source_target_pairs={{0,1},{1,2},{2,3},{4,5},{5,6},{6,7},{8,9},{9,10},{10,11},{12,13},{... | collective-permute-start | bytes 3145736 | tf_op jit(solution)/shard_map/ppermute | solution.py:39
  5.0 25.7 %collective-permute-start.1 = (bf16[32,128,128]{2,1,0:T(8,128)(2,1)S(1)}, bf16[32,128,128]{2,1,0:T(8,128)(2,1)}, u32[]{:S(2)}, u32[]{:S(2)}) collective-permute-start(bf16[32,128,128]{2,1,0:T(8,128)(2,1)S(1)} %bitcast.25), channel_id=1, source_target_pairs={{1,0},{2,1},{3,2},{5,4},{6,5},{7,6},{9,8},{10,9},{11,10},{13,12},{... | collective-permute-start | bytes 3145736 | tf_op jit(solution)/shard_map/ppermute | solution.py:39
  6.3 24.4 %collective-permute-start.2 = (bf16[32,128,128]{2,1,0:T(8,128)(2,1)S(1)}, bf16[32,128,128]{2,1,0:T(8,128)(2,1)}, u32[]{:S(2)}, u32[]{:S(2)}) collective-permute-start(bf16[32,128,128]{2,1,0:T(8,128)(2,1)S(1)} %bitcast.26), channel_id=1, source_target_pairs={{0,4},{4,8},{8,12},{12,16},{16,20},{20,24},{24,28},{1,5},{5,9},{9,... | collective-permute-start | bytes 3145736 | tf_op jit(solution)/shard_map/ppermute | solution.py:39
  10.3 24.7 %collective-permute-start.3 = (bf16[32,128,128]{2,1,0:T(8,128)(2,1)S(1)}, bf16[32,128,128]{2,1,0:T(8,128)(2,1)}, u32[]{:S(2)}, u32[]{:S(2)}) collective-permute-start(bf16[32,128,128]{2,1,0:T(8,128)(2,1)S(1)} %bitcast.27), channel_id=1, source_target_pairs={{4,0},{8,4},{12,8},{16,12},{20,16},{24,20},{28,24},{5,1},{9,5},{13... | collective-permute-start | bytes 3145736 | tf_op jit(solution)/shard_map/ppermute | solution.py:39
  12.5 3.1 %copy-start.1 = (bf16[1,1,32,7,128,128]{5,4,3,2,1,0:T(8,128)(2,1)S(1)}, bf16[1,1,32,7,128,128]{5,4,3,2,1,0:T(8,128)(2,1)}, u32[]{:S(2)}) copy-start(bf16[1,1,32,7,128,128]{5,4,3,2,1,0:T(8,128)(2,1)} %param.5) | copy-start | bytes 22020100
  28.6 1.3 copy-start.4
  60.4 19.8 %collective-permute-start.4 = (bf16[5,2,2,128,128]{4,3,2,1,0:T(8,128)(2,1)S(1)}, bf16[5,2,2,128,128]{4,3,2,1,0:T(8,128)(2,1)S(1)}, u32[]{:S(2)}, u32[]{:S(2)}) collective-permute-start(bf16[5,2,2,128,128]{4,3,2,1,0:T(8,128)(2,1)S(1)} %get-tuple-element.26), channel_id=1, source_target_pairs={{0,1},{1,2},{2,3},{4,5},{5,6},{6,7},{8,9},{9,10},{10,11},{12,13},{... | collective-permute-start | bytes 1966088 | tf_op jit(solution)/shard_map/ppermute | solution.py:39
  66.0 17.7 %collective-permute-start.5 = (bf16[5,2,2,128,128]{4,3,2,1,0:T(8,128)(2,1)S(1)}, bf16[5,2,2,128,128]{4,3,2,1,0:T(8,128)(2,1)S(1)}, u32[]{:S(2)}, u32[]{:S(2)}) collective-permute-start(bf16[5,2,2,128,128]{4,3,2,1,0:T(8,128)(2,1)S(1)} %get-tuple-element.27), channel_id=1, source_target_pairs={{1,0},{2,1},{3,2},{5,4},{6,5},{7,6},{9,8},{10,9},{11,10},{13,12},{... | collective-permute-start | bytes 1966088 | tf_op jit(solution)/shard_map/ppermute | solution.py:39
  67.3 16.4 %collective-permute-start.6 = (bf16[5,2,2,128,128]{4,3,2,1,0:T(8,128)(2,1)S(1)}, bf16[5,2,2,128,128]{4,3,2,1,0:T(8,128)(2,1)S(1)}, u32[]{:S(2)}, u32[]{:S(2)}) collective-permute-start(bf16[5,2,2,128,128]{4,3,2,1,0:T(8,128)(2,1)S(1)} %get-tuple-element.28), channel_id=1, source_target_pairs={{0,4},{4,8},{8,12},{12,16},{16,20},{20,24},{24,28},{1,5},{5,9},{9,... | collective-permute-start | bytes 1966088 | tf_op jit(solution)/shard_map/ppermute | solution.py:39
  69.3 14.5 %collective-permute-start.7 = (bf16[5,2,2,128,128]{4,3,2,1,0:T(8,128)(2,1)S(1)}, bf16[5,2,2,128,128]{4,3,2,1,0:T(8,128)(2,1)S(1)}, u32[]{:S(2)}, u32[]{:S(2)}) collective-permute-start(bf16[5,2,2,128,128]{4,3,2,1,0:T(8,128)(2,1)S(1)} %get-tuple-element.29), channel_id=1, source_target_pairs={{4,0},{8,4},{12,8},{16,12},{20,16},{24,20},{28,24},{5,1},{9,5},{13... | collective-permute-start | bytes 1966088 | tf_op jit(solution)/shard_map/ppermute | solution.py:39
  71.7 4.0 %copy-start = (bf16[1280,4096]{1,0:T(8,128)(2,1)S(1)}, bf16[1280,4096]{1,0:T(8,128)(2,1)}, u32[]{:S(2)}) copy-start(bf16[1280,4096]{1,0:T(8,128)(2,1)} %get-tuple-element.31.right_all) | copy-start | bytes 31457284
  85.2 22.5 %collective-permute-start.8 = (bf16[7,2,2,128,128]{4,3,2,1,0:T(8,128)(2,1)S(1)}, bf16[7,2,2,128,128]{4,3,2,1,0:T(8,128)(2,1)}, u32[]{:S(2)}, u32[]{:S(2)}) collective-permute-start(bf16[7,2,2,128,128]{4,3,2,1,0:T(8,128)(2,1)S(1)} %get-tuple-element.32.refs_1_), channel_id=1, source_target_pairs={{0,1},{1,2},{2,3},{4,5},{5,6},{6,7},{8,9},{9,10},{10,11},{12,13},{... | collective-permute-start | bytes 2752520 | tf_op jit(solution)/shard_map/ppermute | solution.py:39
  89.9 22.5 %collective-permute-start.9 = (bf16[7,2,2,128,128]{4,3,2,1,0:T(8,128)(2,1)S(1)}, bf16[7,2,2,128,128]{4,3,2,1,0:T(8,128)(2,1)S(1)}, u32[]{:S(2)}, u32[]{:S(2)}) collective-permute-start(bf16[7,2,2,128,128]{4,3,2,1,0:T(8,128)(2,1)S(1)} %get-tuple-element.32.refs_1_), channel_id=1, source_target_pairs={{1,0},{2,1},{3,2},{5,4},{6,5},{7,6},{9,8},{10,9},{11,10},{13,12},{... | collective-permute-start | bytes 2752520 | tf_op jit(solution)/shard_map/ppermute | solution.py:39
  91.2 39.0 %collective-permute-start.15 = (bf16[6,2,2,128,128]{4,3,2,1,0:T(8,128)(2,1)}, bf16[6,2,2,128,128]{4,3,2,1,0:T(8,128)(2,1)}, u32[]{:S(2)}, u32[]{:S(2)}) collective-permute-start(bf16[6,2,2,128,128]{4,3,2,1,0:T(8,128)(2,1)} %get-tuple-element.33.refs_0_), channel_id=1, source_target_pairs={{1,0},{2,1},{3,2},{5,4},{6,5},{7,6},{9,8},{10,9},{11,10},{13,12},{... | collective-permute-start | bytes 2359304 | tf_op jit(solution)/shard_map/ppermute | solution.py:39
  92.5 41.2 %collective-permute-start.13 = (bf16[6,2,2,128,128]{4,3,2,1,0:T(8,128)(2,1)}, bf16[6,2,2,128,128]{4,3,2,1,0:T(8,128)(2,1)}, u32[]{:S(2)}, u32[]{:S(2)}) collective-permute-start(bf16[6,2,2,128,128]{4,3,2,1,0:T(8,128)(2,1)} %get-tuple-element.33.refs_0_), channel_id=1, source_target_pairs={{0,1},{1,2},{2,3},{4,5},{5,6},{6,7},{8,9},{9,10},{10,11},{12,13},{... | collective-permute-start | bytes 2359304 | tf_op jit(solution)/shard_map/ppermute | solution.py:39
  100.3 53.5 %collective-permute-start.12 = (bf16[9,2,2,128,128]{4,3,2,1,0:T(8,128)(2,1)}, bf16[9,2,2,128,128]{4,3,2,1,0:T(8,128)(2,1)S(1)}, u32[]{:S(2)}, u32[]{:S(2)}) collective-permute-start(bf16[9,2,2,128,128]{4,3,2,1,0:T(8,128)(2,1)} %fusion), channel_id=1, source_target_pairs={{0,3},{3,0},{4,7},{7,4},{8,11},{11,8},{12,15},{15,12},{16,19},{19,... | collective-permute-start | bytes 3538952 | tf_op jit(solution)/shard_map/ppermute | solution.py:406
  112.4 77.8 %collective-permute-start.10 = (bf16[7,2,2,128,128]{4,3,2,1,0:T(8,128)(2,1)}, bf16[7,2,2,128,128]{4,3,2,1,0:T(8,128)(2,1)S(1)}, u32[]{:S(2)}, u32[]{:S(2)}) collective-permute-start(bf16[7,2,2,128,128]{4,3,2,1,0:T(8,128)(2,1)} %collective-permute-done.8.refs_2_), channel_id=1, source_target_pairs={{0,1},{1,2},{2,3},{4,5},{5,6},{6,7},{8,9},{9,10},{10,11},{12,13},{... | collective-permute-start | bytes 2752520 | tf_op jit(solution)/shard_map/ppermute | solution.py:39
  130.2 53.5 %collective-permute-start.16 = (bf16[6,2,2,128,128]{4,3,2,1,0:T(8,128)(2,1)}, bf16[6,2,2,128,128]{4,3,2,1,0:T(8,128)(2,1)}, u32[]{:S(2)}, u32[]{:S(2)}) collective-permute-start(bf16[6,2,2,128,128]{4,3,2,1,0:T(8,128)(2,1)} %collective-permute-done.15.refs_1_), channel_id=1, source_target_pairs={{1,0},{2,1},{3,2},{5,4},{6,5},{7,6},{9,8},{10,9},{11,10},{13,12},{... | collective-permute-start | bytes 2359304 | tf_op jit(solution)/shard_map/ppermute | solution.py:39
  132.4 57.8 %collective-permute-start.11 = (bf16[6,2,2,128,128]{4,3,2,1,0:T(8,128)(2,1)}, bf16[6,2,2,128,128]{4,3,2,1,0:T(8,128)(2,1)}, u32[]{:S(2)}, u32[]{:S(2)}) collective-permute-start(bf16[6,2,2,128,128]{4,3,2,1,0:T(8,128)(2,1)} %slice.6), channel_id=1, source_target_pairs={{1,0},{2,1},{3,2},{5,4},{6,5},{7,6},{9,8},{10,9},{11,10},{13,12},{... | collective-permute-start | bytes 2359304 | tf_op jit(solution)/shard_map/ppermute | solution.py:39
  135.7 48.0 %collective-permute-start.14 = (bf16[5,2,2,128,128]{4,3,2,1,0:T(8,128)(2,1)}, bf16[5,2,2,128,128]{4,3,2,1,0:T(8,128)(2,1)}, u32[]{:S(2)}, u32[]{:S(2)}) collective-permute-start(bf16[5,2,2,128,128]{4,3,2,1,0:T(8,128)(2,1)} %slice.8), channel_id=1, source_target_pairs={{0,1},{1,2},{2,3},{4,5},{5,6},{6,7},{8,9},{9,10},{10,11},{12,13},{... | collective-permute-start | bytes 1966088 | tf_op jit(solution)/shard_map/ppermute | solution.py:39

commit v4 on v3

--- a/solution.py
+++ b/solution.py
@@ -9,6 +9,7 @@
 
 CROSS_SHIFTS = ((0, -1), (0, 1), (-1, 0), (1, 0), (0, 0))
 OWN = 4
+DOWN, UP = CROSS_SHIFTS[:2]
 WINDOW_SHIFTS = (
     (-2, 0),
     (-1, -1),
@@ -24,6 +25,7 @@
     (1, 1),
     (2, 0),
 )
+AHEAD, BEHIND = 4, 8
 TRAVEL = (4, 1, 5, 9, 0, 2, 6, 10, 12, 3, 7, 11, 8)
 HALVES = (TRAVEL[:6], TRAVEL[6:])
 smoothing = 2.0 / 3.0
@@ -116,7 +118,7 @@
         out_shape=[jax.ShapeDtypeStruct((members * tile, rows * tile), jnp.bfloat16)] * 2
         + [jax.ShapeDtypeStruct((rows * taps,), jnp.int32)] * 3
         + [jax.ShapeDtypeStruct((steps,), jnp.int32)],
-        compiler_params=pltpu.CompilerParams(vmem_limit_bytes=24 * 1024 * 1024),
+        compiler_params=pltpu.CompilerParams(vmem_limit_bytes=44 * 1024 * 1024),
         cost_estimate=pl.CostEstimate(
             flops=2 * tile**3 * rows * (taps + members),
             bytes_accessed=2 * (a_tiles.size + dinv.size * 6),
@@ -126,7 +128,12 @@
     )(columns, agg, place, a_tiles, dinv, tent)
 
 
-def product(left, right, outs, members, tile):
+def kept_members(shift):
+    lone = CROSS_SHIFTS.index(shift)
+    return tuple((lone + 1 + p) % 5 for p in range(4))
+
+
+def product(left, right, outs, lone, members, tile):
     width = members * tile
 
     def one(d2, carry):
@@ -136,12 +143,28 @@
             NT,
             preferred_element_type=jnp.float32,
         )
-        for d1, out in enumerate(outs):
+
+        def write(out, at, d1):
             for m in range(members):
                 for m2 in range(members):
                     row = (d1 * members + m) * tile
                     block = value[row : row + tile, m2 * tile : (m2 + 1) * tile]
-                    out[d2, m, m2] = block.astype(out.dtype)
+                    out[at, m, m2] = block.astype(out.dtype)
+
+        for d1, out in enumerate(outs):
+            if d1 not in lone:
+                write(out, d2, d1)
+                continue
+            direction, single = lone[d1]
+
+            @pl.when(d2 == direction)
+            def _():
+                write(single, 0, d1)
+
+            @pl.when(d2 != direction)
+            def _():
+                write(out, (d2 + 4 - direction) % 5, d1)
+
         return carry
 
     lax.fori_loop(0, 5, one, 0)
@@ -157,8 +180,8 @@
 
 def partial_kernel(members, taps, tiles, sources, slots, ends, *refs):
     a_tiles, dinv_hbm, *tents = refs[:6]
-    right_own, *outs, right_out = refs[6:12]
-    a_held, dinv, tent, right, left, sums, sems = refs[12:]
+    right_own, *outs, behind, ahead, right_out = refs[6:14]
+    a_held, dinv, tent, right, left, sums, sems = refs[14:]
     tile = dinv.shape[-1]
     rows = dinv.shape[0]
     chunks = rows // ROWS_PER_STEP
@@ -182,11 +205,11 @@
     for c in range(chunks):
         a_copy(c).start()
     own_copy.start()
+    sums[...] = jnp.zeros_like(sums)
     for copy in others:
         copy.wait()
 
     def one_chunk(c, first):
-        sums[...] = jnp.zeros_like(sums)
         a_copy(c).wait()
         last = ends[c]
 
@@ -209,6 +232,7 @@
         lax.fori_loop(0, (last - first + UNROLL - 1) // UNROLL, some, 0)
         lanes = lane_tiles(c, ROWS_PER_STEP * tile)
         right[: outer * tile, lanes] = sums[: outer * tile, :].astype(jnp.bfloat16)
+        sums[...] = jnp.zeros_like(sums)
         for u in range(ROWS_PER_STEP):
             g = c * ROWS_PER_STEP + u
             lanes = lane_tiles(g, tile)
@@ -221,14 +245,15 @@
     lax.fori_loop(0, chunks, one_chunk, 0)
     own_copy.wait()
     out_copy.start()
-    product(left, right, outs, members, tile)
+    lone = {d: (CROSS_SHIFTS.index(t), out) for d, t, out in ((0, UP, behind), (1, DOWN, ahead))}
+    product(left, right, outs, lone, members, tile)
     out_copy.wait()
 
 
 def partial_blocks(a_tiles, dinv, tents, own_right, lists, members):
     rows, taps, tile = a_tiles.shape[0], a_tiles.shape[1], a_tiles.shape[-1]
-    block = (5, members, members, tile, tile)
-    whole = pl.BlockSpec(block, lambda s, *_: (0,) * 5)
+    whole = lambda lead: pl.BlockSpec((lead, members, members, tile, tile), lambda s, *_: (0,) * 5)
+    leads = (4, 4, 5, 5, 1, 1)
     outer = 4 * members * tile
     slots = outer + members * tile
     return pl.pallas_call(
@@ -237,7 +262,7 @@
             num_scalar_prefetch=4,
             grid=(1,),
             in_specs=[pl.BlockSpec(memory_space=pl.ANY)] * 7,
-            out_specs=[whole] * 4 + [pl.BlockSpec(memory_space=pl.ANY)],
+            out_specs=[whole(lead) for lead in leads] + [pl.BlockSpec(memory_space=pl.ANY)],
             scratch_shapes=[
                 pltpu.VMEM((rows * taps, tile, tile), jnp.bfloat16),
                 pltpu.VMEM((rows, tile, tile), jnp.bfloat16),
@@ -248,7 +273,10 @@
                 pltpu.SemaphoreType.DMA((rows // ROWS_PER_STEP + 7,)),
             ],
         ),
-        out_shape=[jax.ShapeDtypeStruct(block, jnp.bfloat16)] * 4
+        out_shape=[
+            jax.ShapeDtypeStruct((lead, members, members, tile, tile), jnp.bfloat16)
+            for lead in leads
+        ]
         + [jax.ShapeDtypeStruct((slots, rows * tile), jnp.bfloat16)],
         compiler_params=pltpu.CompilerParams(vmem_limit_bytes=48 * 1024 * 1024),
         cost_estimate=pl.CostEstimate(
@@ -269,7 +297,7 @@
         copy.start()
     for copy in copies:
         copy.wait()
-    product(left, right, (own,), members, own.shape[-1])
+    product(left, right, (own,), {}, members, own.shape[-1])
 
 
 def own_rows(left, right, members):
@@ -297,11 +325,18 @@
 
 
 def window_kernel(*refs):
-    for out, half in zip(refs[5:], HALVES):
+    every = tuple(range(5))
+    held = (kept_members(DOWN), kept_members(UP), every, every, every)
+    behind, ahead = refs[5:7]
+    for out, half in zip(refs[7:], HALVES):
         for position, offset in enumerate(half):
+            if offset in (AHEAD, BEHIND):
+                out[position] = (ahead if offset == AHEAD else behind)[0]
+                continue
             total = None
-            for shift, values in zip(CROSS_SHIFTS, refs):
-                for d, member in enumerate(CROSS_SHIFTS):
+            for shift, values, directions in zip(CROSS_SHIFTS, refs, held):
+                for d, direction in enumerate(directions):
+                    member = CROSS_SHIFTS[direction]
                     if (shift[0] + member[0], shift[1] + member[1]) == WINDOW_SHIFTS[offset]:
                         term = values[d].astype(jnp.float32)
                         total = term if total is None else total + term
@@ -316,7 +351,7 @@
     return pl.pallas_call(
         window_kernel,
         grid=(members,),
-        in_specs=[spec(5)] * 5,
+        in_specs=[spec(block.shape[0]) for block in blocks],
         out_specs=[spec(len(half)) for half in HALVES],
         out_shape=[
             jax.ShapeDtypeStruct((len(half), members, members, tile, tile), jnp.bfloat16)
@@ -324,31 +359,50 @@
         ],
         compiler_params=pltpu.CompilerParams(vmem_limit_bytes=32 * 1024 * 1024),
         cost_estimate=pl.CostEstimate(
-            flops=5 * blocks[0].size, bytes_accessed=16 * blocks[0].size, transcendentals=0
+            flops=5 * blocks[4].size, bytes_accessed=16 * blocks[4].size, transcendentals=0
         ),
         name="finished_window",
     )(*blocks)
 
 
-def place_kernel(lists, members, row, valid, *refs):
+def place_kernel(lists, edges, row, valid, *refs):
     arrays, (out, nothing, sems) = refs[: len(lists)], refs[-3:]
+    count = out.shape[0]
     nothing[...] = jnp.zeros_like(nothing)
 
     def each(act):
+        def move(source, target, offset, sem):
+            act(pltpu.make_async_copy(source, out.at[target, :, offset], sems.at[sem]))
+
         for index, (array, (held, written)) in enumerate(zip(arrays, lists)):
+
+            def write(offset, target):
+                source = array.at[held.index(offset)] if offset in held else nothing
+                move(source, target, offset, index * 13 + offset)
+
+            here = row[index]
 
             @pl.when(valid[index] == 1)
             def _():
                 for offset in written:
-                    for m in range(members):
-                        source = array.at[held.index(offset), m] if offset in held else nothing
-                        act(
-                            pltpu.make_async_copy(
-                                source,
-                                out.at[row[index], m, offset],
-                                sems.at[(index * 13 + offset) * members + m],
-                            )
-                        )
+                    if offset not in (AHEAD, BEHIND):
+                        write(offset, here)
+
+            if AHEAD in written:
+
+                @pl.when((valid[index] == 1) & (here + 1 < count))
+                def _():
+                    write(AHEAD, here + 1)
+
+            if BEHIND in written:
+
+                @pl.when((valid[index] == 1) & (here > 0))
+                def _():
+                    write(BEHIND, here - 1)
+
+        if edges:
+            move(nothing, 0, AHEAD, 13 * len(lists))
+            move(nothing, count - 1, BEHIND, 13 * len(lists) + 1)
 
     each(lambda copy: copy.start())
     each(lambda copy: copy.wait())
@@ -366,12 +420,12 @@
     rows = jnp.stack([jnp.asarray(jnp.where(p[4], p[3], 0), jnp.int32) for p in pieces])
     valid = jnp.stack([jnp.asarray(p[4], jnp.int32) for p in pieces])
     return pl.pallas_call(
-        functools.partial(place_kernel, tuple(p[1:3] for p in pieces), members),
+        functools.partial(place_kernel, tuple(p[1:3] for p in pieces), out is None),
         in_specs=in_specs,
         out_specs=pl.BlockSpec(memory_space=pl.ANY),
         scratch_shapes=[
-            pltpu.VMEM((members, tile, tile), jnp.bfloat16),
-            pltpu.SemaphoreType.DMA((len(pieces) * 13 * members,)),
+            pltpu.VMEM((members, members, tile, tile), jnp.bfloat16),
+            pltpu.SemaphoreType.DMA((len(pieces) * 13 + 2,)),
         ],
         out_shape=jax.ShapeDtypeStruct(
             (count, members, 13, members, tile, tile), jnp.bfloat16
@@ -385,22 +439,10 @@
     )(rows, valid, *operands)
 
 
-def hopped(shard, lists, hop, count_y):
-    limit = count_y - 1 - hop
-    lower = tuple(o for o in lists[0] if -WINDOW_SHIFTS[o][1] <= limit)
-    upper = tuple(o for o in lists[1] if WINDOW_SHIFTS[o][1] <= limit)
-    cut = len(lists[0]) - len(lower)
-    arrived = (
-        shifted(shard[0][cut:], "sy", 1),
-        shifted(shard[1][: len(upper)], "sy", -1),
-    )
-    return arrived, (lower, upper)
-
-
 def end_to_end(halves, grid_y, count_y):
-    lower = tuple(o for o in TRAVEL if WINDOW_SHIFTS[o][1] >= 0)
-    upper = tuple(o for o in TRAVEL if WINDOW_SHIFTS[o][1] <= 0)
-    start = jnp.where(grid_y == 0, len(TRAVEL) - len(lower), 0)
+    lower = tuple(o for o in TRAVEL if WINDOW_SHIFTS[o][1] in (0, 1))
+    upper = tuple(o for o in TRAVEL if WINDOW_SHIFTS[o][1] in (-1, 0))
+    start = jnp.where(grid_y == 0, TRAVEL.index(lower[0]), TRAVEL.index(upper[0]))
     sent = lax.dynamic_slice_in_dim(jnp.concatenate(halves, axis=0), start, len(lower), axis=0)
     last = count_y - 1
     moved = lax.ppermute(sent, "sy", [(0, last), (last, 0)])
@@ -411,23 +453,21 @@
 
 
 def gathered_rows(halves, grid_y, count_y):
-    chains = [((half, half), (group, group)) for half, group in zip(halves, HALVES)]
+    chains = [(half, half) for half in halves]
     pieces = [(half, group, group, grid_y, True) for half, group in zip(halves, HALVES)]
     out = None
     for hop in range(1, count_y - 1):
-        chains = [hopped(*chain, hop, count_y) for chain in chains]
+        chains = [(shifted(a, "sy", 1), shifted(b, "sy", -1)) for a, b in chains]
         if hop == 1:
             direct = end_to_end(halves, grid_y, count_y)
         out = placed(out, pieces, count_y)
-        (first, lists), second = chains
-        second, out = (second[0], out) if hop > 1 else lax.optimization_barrier((second[0], out))
-        chains = [(first, lists), (second, chains[1][1])]
+        if hop == 1:
+            chains[1], out = lax.optimization_barrier((chains[1], out))
         pieces = []
-        for (arrived, lists), group in zip(chains, HALVES):
-            has_lower, has_upper = grid_y >= hop, grid_y + hop < count_y
+        for (from_lower, from_upper), group in zip(chains, HALVES):
             pieces += [
-                (arrived[0], lists[0], group, grid_y - hop, has_lower),
-                (arrived[1], lists[1], group, grid_y + hop, has_upper),
+                (from_lower, group, group, grid_y - hop, grid_y >= hop),
+                (from_upper, group, group, grid_y + hop, grid_y + hop < count_y),
             ]
     out = placed(out, direct + pieces[:2], count_y)
     return placed(out, pieces[2:], count_y)
@@ -457,7 +497,7 @@
         count_y,
         MEMBERS,
     )
-    to_lower_y, to_upper_y, to_lower_x, to_upper_x, right = partial_blocks(
+    to_lower_y, to_upper_y, to_lower_x, to_upper_x, behind, ahead, right = partial_blocks(
         coupling, inverse, tents, own_right, lists, MEMBERS
     )
     halves = finished_window(
@@ -467,6 +507,8 @@
             shifted(to_upper_x, "sx", 1),
             shifted(to_lower_x, "sx", -1),
             own_rows(own_left, right, MEMBERS),
+            behind,
+            ahead,
         )
     )
     return gathered_rows(halves, grid_y, count_y)[None]

time: 194 us -> 199 us (1.026)
  the two profiles are of different devices: /device:TPU:3 before, /device:TPU:0 now
where the time goes in v4:
time: 199 us; the launch traced here: 198 us
  starting transfers between devices  73.1 us (37%)
  waiting for transfers between devices  58 us (29%)
  Pallas kernels  55.2 us (28%)
  local copies, waits for them, and re-layouts  9.77 us (5%)
    ppermute x16, starting transfers between devices, shifted(): return lax.ppermute(x, axis, pairs)  67.3 us
    ppermute x16, waiting for transfers between devices, shifted(): return lax.ppermute(x, axis, pairs)  58 us
    pallas_call x1, Pallas kernels, partial_blocks(): pl.pallas_call(functools.partial(partial_kernel, members, taps), grid_spe...  25 us
    pallas_call x1, Pallas kernels, own_slots(): pl.pallas_call(functools.partial(own_kernel, count_y, rows, members, taps...  14.2 us
    pallas_call x4, Pallas kernels, placed(): pl.pallas_call(functools.partial(place_kernel, tuple((p[1:3] for p in pie...  10.8 us
    unnamed x12, local copies, waits for them, and re-layouts  9.67 us
    ppermute x1, starting transfers between devices, end_to_end(): moved = lax.ppermute(sent, 'sy', [(0, last), (last, 0)])  5.79 us
    pallas_call x1, Pallas kernels, own_rows(): pl.pallas_call(functools.partial(own_rows_kernel, members), grid=(1,), in...  4.56 us
  transfers between devices with their start and end apart: 17, of which 9 were waited for; matrix products, arithmetic and copies ran while one was open for 1% of the time, Pallas kernels for 14%

profile of v4, /device:TPU:0, one launch (start us, length us, event | category | flops | bytes accessed | tf_op | source)
XLA Modules:
  0.0 198.1 jit_solution(12114555191665040598)
XLA Ops:
  0.0 0.0 copy-start.2
  0.0 1.7 copy.11
  1.7 5.0 %collective-permute-start = (bf16[32,128,128]{2,1,0:T(8,128)(2,1)S(1)}, bf16[32,128,128]{2,1,0:T(8,128)(2,1)S(1)}, u32[]{:S(2)}, u32[]{:S(2)}) collective-permute-start(bf16[32,128,128]{2,1,0:T(8,128)(2,1)S(1)} %bitcast.22), channel_id=1, source_target_pairs={{0,1},{1,2},{2,3},{4,5},{5,6},{6,7},{8,9},{9,10},{10,11},{12,13},{... | collective-permute-start | bytes 3145736 | tf_op jit(solution)/shard_map/ppermute | solution.py:41
  6.7 1.3 collective-permute-start.1
  8.0 2.5 %collective-permute-start.2 = (bf16[32,128,128]{2,1,0:T(8,128)(2,1)S(1)}, bf16[32,128,128]{2,1,0:T(8,128)(2,1)}, u32[]{:S(2)}, u32[]{:S(2)}) collective-permute-start(bf16[32,128,128]{2,1,0:T(8,128)(2,1)S(1)} %bitcast.24), channel_id=1, source_target_pairs={{0,4},{4,8},{8,12},{12,16},{16,20},{20,24},{24,28},{1,5},{5,9},{9,... | collective-permute-start | bytes 3145736 | tf_op jit(solution)/shard_map/ppermute | solution.py:41
  10.5 1.3 collective-permute-start.3
  11.8 0.8 copy.10
  12.5 0.1 reshape.12.columns
  12.6 0.1 pad_add_fusion.2.place
  12.7 0.0 copy-start.1
  12.7 1.2 copy-done.1
  14.0 0.0 copy-start.3
  14.0 0.7 copy-done.3
  14.6 14.2 %own_slots.1 = (bf16[256,4096]{1,0:T(8,128)(2,1)S(1)}, bf16[256,4096]{1,0:T(8,128)(2,1)S(1)}, s32[224]{0:T(256)S(1)}, s32[224]{0:T(256)S(1)}, s32[224]{0:T(256)S(1)}, /*index=5*/s32[8]{0:T(128)S(1)}) custom-call(s32[224]{0:T(256)S(1)} %reshape.12.columns, s32[1024]{0:T(1024)S(1)} %copy-done.3, s32[2]{0:T(128)S(1)} %pad_add_fusion.2.place, ...), custom_call_target="tpu_custom_call" | custom-call | flops 1207959552 | bytes 13631488 | tf_op jit(solution)/shard_map/own_slots/pallas_call | solution.py:103
  28.8 0.0 copy-start.4
  28.8 1.3 copy-done.4
  30.1 0.0 collective-permute-done.refs_2_
  30.1 3.2 %collective-permute-done.1.refs_3_ = bf16[32,128,128]{2,1,0:T(8,128)(2,1)} collective-permute-done((bf16[32,128,128]{2,1,0:T(8,128)(2,1)S(1)}, bf16[32,128,128]{2,1,0:T(8,128)(2,1)}, u32[]{:S(2)}, u32[]{:S(2)}) %collective-permute-start.1) | collective-permute-done | bytes 1048608 | tf_op jit(solution)/shard_map/ppermute | solution.py:41
  33.3 0.0 collective-permute-done.2.refs_4_
  33.3 0.0 collective-permute-done.3.refs_5_
  33.3 0.0 copy-done.2
  33.3 25.0 %partial_blocks.1 = (bf16[4,2,2,128,128]{4,3,2,1,0:T(8,128)(2,1)S(1)}, bf16[4,2,2,128,128]{4,3,2,1,0:T(8,128)(2,1)S(1)}, bf16[5,2,2,128,128]{4,3,2,1,0:T(8,128)(...) custom-call(s32[224]{0:T(256)S(1)} %get-tuple-element.23.tiles, ...), custom_call_target="tpu_custom_call" | custom-call | flops 11811160064 | bytes 28311552 | tf_op jit(solution)/shard_map/partial_blocks/pallas_call | solution.py:259
  58.3 5.5 %collective-permute-start.6 = (bf16[5,2,2,128,128]{4,3,2,1,0:T(8,128)(2,1)S(1)}, bf16[5,2,2,128,128]{4,3,2,1,0:T(8,128)(2,1)S(1)}, u32[]{:S(2)}, u32[]{:S(2)}) collective-permute-start(bf16[5,2,2,128,128]{4,3,2,1,0:T(8,128)(2,1)S(1)} %get-tuple-element.30), channel_id=1, source_target_pairs={{0,4},{4,8},{8,12},{12,16},{16,20},{20,24},{24,28},{1,5},{5,9},{9,... | collective-permute-start | bytes 1966088 | tf_op jit(solution)/shard_map/ppermute | solution.py:41
  63.8 1.3 collective-permute-start.7
  65.1 5.6 %collective-permute-start.4 = (bf16[4,2,2,128,128]{4,3,2,1,0:T(8,128)(2,1)S(1)}, bf16[4,2,2,128,128]{4,3,2,1,0:T(8,128)(2,1)S(1)}, u32[]{:S(2)}, u32[]{:S(2)}) collective-permute-start(bf16[4,2,2,128,128]{4,3,2,1,0:T(8,128)(2,1)S(1)} %get-tuple-element.28), channel_id=1, source_target_pairs={{0,1},{1,2},{2,3},{4,5},{5,6},{6,7},{8,9},{9,10},{10,11},{12,13},{... | collective-permute-start | bytes 1572872 | tf_op jit(solution)/shard_map/ppermute | solution.py:41
  70.7 1.3 collective-permute-start.5
  72.0 0.0 copy-start
  72.0 4.0 %copy-done = bf16[1280,4096]{1,0:T(8,128)(2,1)S(1)} copy-done((bf16[1280,4096]{1,0:T(8,128)(2,1)S(1)}, bf16[1280,4096]{1,0:T(8,128)(2,1)}, u32[]{:S(2)}) %copy-start) | copy-done | bytes 10485784
  76.0 4.6 %own_rows.1.refs_4_ = f32[5,2,2,128,128]{4,3,2,1,0:T(8,128)S(1)} custom-call(bf16[256,4096]{1,0:T(8,128)(2,1)S(1)} %get-tuple-element.32.left_own, bf16[1280,4096]{1,0:T(8,128)(2,1)S(1)} %copy-done), custom_call_target="tpu_custom_call" | custom-call | flops 2684354560 | bytes 12582912 | tf_op jit(solution)/shard_map/own_rows/pallas_call | solution.py:306
  80.5 2.3 %collective-permute-done.4.refs_0_ = bf16[4,2,2,128,128]{4,3,2,1,0:T(8,128)(2,1)S(1)} collective-permute-done((bf16[4,2,2,128,128]{4,3,2,1,0:T(8,128)(2,1)S(1)}, bf16[4,2,2,128,128]{4,3,2,1,0:T(8,128)(2,1)S(1)}, u32[]{:S(2)}, u32[]{:S(2)}) %collective-permute-start.4) | collective-permute-done | bytes 524320 | tf_op jit(solution)/shard_map/ppermute | solution.py:41
  82.8 4.5 %collective-permute-done.5.refs_1_ = bf16[4,2,2,128,128]{4,3,2,1,0:T(8,128)(2,1)S(1)} collective-permute-done((bf16[4,2,2,128,128]{4,3,2,1,0:T(8,128)(2,1)S(1)}, bf16[4,2,2,128,128]{4,3,2,1,0:T(8,128)(2,1)S(1)}, u32[]{:S(2)}, u32[]{:S(2)}) %collective-permute-start.5) | collective-permute-done | bytes 524320 | tf_op jit(solution)/shard_map/ppermute | solution.py:41
  87.3 0.0 collective-permute-done.6.refs_2_
  87.3 0.0 collective-permute-done.7.refs_3_
  87.3 0.7 finished_window.1
  88.0 4.9 %collective-permute-start.8 = (bf16[7,2,2,128,128]{4,3,2,1,0:T(8,128)(2,1)S(1)}, bf16[7,2,2,128,128]{4,3,2,1,0:T(8,128)(2,1)}, u32[]{:S(2)}, u32[]{:S(2)}) collective-permute-start(bf16[7,2,2,128,128]{4,3,2,1,0:T(8,128)(2,1)S(1)} %get-tuple-element.36.refs_1_), channel_id=1, source_target_pairs={{0,1},{1,2},{2,3},{4,5},{5,6},{6,7},{8,9},{9,10},{10,11},{12,13},{... | collective-permute-start | bytes 2752520 | tf_op jit(solution)/shard_map/ppermute | solution.py:41
  92.9 1.3 collective-permute-start.9
  94.2 4.6 %collective-permute-start.13 = (bf16[6,2,2,128,128]{4,3,2,1,0:T(8,128)(2,1)S(1)}, bf16[6,2,2,128,128]{4,3,2,1,0:T(8,128)(2,1)S(1)}, u32[]{:S(2)}, u32[]{:S(2)}) collective-permute-start(bf16[6,2,2,128,128]{4,3,2,1,0:T(8,128)(2,1)S(1)} %get-tuple-element.37.refs_0_), channel_id=1, source_target_pairs={{0,1},{1,2},{2,3},{4,5},{5,6},{6,7},{8,9},{9,10},{10,11},{12,13},{... | collective-permute-start | bytes 2359304 | tf_op jit(solution)/shard_map/ppermute | solution.py:41
  98.8 1.3 collective-permute-start.15
  100.1 1.3 fusion
  101.5 5.8 %collective-permute-start.12 = (bf16[8,2,2,128,128]{4,3,2,1,0:T(8,128)(2,1)}, bf16[8,2,2,128,128]{4,3,2,1,0:T(8,128)(2,1)S(1)}, u32[]{:S(2)}, u32[]{:S(2)}) collective-permute-start(bf16[8,2,2,128,128]{4,3,2,1,0:T(8,128)(2,1)} %fusion), channel_id=1, source_target_pairs={{0,3},{3,0},{4,7},{7,4},{8,11},{11,8},{12,15},{15,12},{16,19},{19,... | collective-permute-start | bytes 3145736 | tf_op jit(solution)/shard_map/ppermute | solution.py:448
  107.3 0.1 pad_add_fusion.3.row
  107.4 2.0 %placed.4.refs_4_ = bf16[4,2,13,2,128,128]{5,4,3,2,1,0:T(8,128)(2,1)} custom-call(s32[2]{0:T(128)S(1)} %pad_add_fusion.3.row, s32[2]{0:T(128)S(1)} %broadcast_1_valid.2.valid, bf16[6,2,2,128,128]{4,3,2,1,0:T(8,128)(2,1)S(1)} %get-tuple-element.37.refs_0_, bf16[7,2,2,128,128]{4,3,2,1,0:T(8,128)(2,1)S(1)} %get-tuple-element.36.refs_1_), custom_call_target="tpu_custom_call" | custom-call | bytes 5111808 | tf_op jit(solution)/shard_map/placed/pallas_call | solution.py:422
  109.4 3.4 %collective-permute-done.8.refs_2_ = bf16[7,2,2,128,128]{4,3,2,1,0:T(8,128)(2,1)} collective-permute-done((bf16[7,2,2,128,128]{4,3,2,1,0:T(8,128)(2,1)S(1)}, bf16[7,2,2,128,128]{4,3,2,1,0:T(8,128)(2,1)}, u32[]{:S(2)}, u32[]{:S(2)}) %collective-permute-start.8) | collective-permute-done | bytes 917536 | tf_op jit(solution)/shard_map/ppermute | solution.py:41
  112.7 5.5 %collective-permute-done.9.refs_3_ = bf16[7,2,2,128,128]{4,3,2,1,0:T(8,128)(2,1)} collective-permute-done((bf16[7,2,2,128,128]{4,3,2,1,0:T(8,128)(2,1)S(1)}, bf16[7,2,2,128,128]{4,3,2,1,0:T(8,128)(2,1)}, u32[]{:S(2)}, u32[]{:S(2)}) %collective-permute-start.9) | collective-permute-done | bytes 917536 | tf_op jit(solution)/shard_map/ppermute | solution.py:41
  118.2 2.6 %collective-permute-start.10 = (bf16[7,2,2,128,128]{4,3,2,1,0:T(8,128)(2,1)}, bf16[7,2,2,128,128]{4,3,2,1,0:T(8,128)(2,1)S(1)}, u32[]{:S(2)}, u32[]{:S(2)}) collective-permute-start(bf16[7,2,2,128,128]{4,3,2,1,0:T(8,128)(2,1)} %collective-permute-done.8.refs_2_), channel_id=1, source_target_pairs={{0,1},{1,2},{2,3},{4,5},{5,6},{6,7},{8,9},{9,10},{10,11},{12,13},{... | collective-permute-start | bytes 2752520 | tf_op jit(solution)/shard_map/ppermute | solution.py:41
  120.8 1.3 collective-permute-start.11
  122.1 7.5 %collective-permute-done.13.refs_0_ = bf16[6,2,2,128,128]{4,3,2,1,0:T(8,128)(2,1)S(1)} collective-permute-done((bf16[6,2,2,128,128]{4,3,2,1,0:T(8,128)(2,1)S(1)}, bf16[6,2,2,128,128]{4,3,2,1,0:T(8,128)(2,1)S(1)}, u32[]{:S(2)}, u32[]{:S(2)}) %collective-permute-start.13) | collective-permute-done | bytes 786464 | tf_op jit(solution)/shard_map/ppermute | solution.py:41
  129.6 26.4 %collective-permute-start.14 = (bf16[6,2,2,128,128]{4,3,2,1,0:T(8,128)(2,1)S(1)}, bf16[6,2,2,128,128]{4,3,2,1,0:T(8,128)(2,1)}, u32[]{:S(2)}, u32[]{:S(2)}) collective-permute-start(bf16[6,2,2,128,128]{4,3,2,1,0:T(8,128)(2,1)S(1)} %collective-permute-done.13.refs_0_), channel_id=1, source_target_pairs={{0,1},{1,2},{2,3},{4,5},{5,6},{6,7},{8,9},{9,10},{10,11},{12,13},{... | collective-permute-start | bytes 2359304 | tf_op jit(solution)/shard_map/ppermute | solution.py:41
  156.0 1.5 collective-permute-done.15.refs_1_
  157.5 1.3 collective-permute-start.16
  158.8 0.1 pad_add_fusion.6.row
  158.9 0.1 add_convert_fusion.valid
  159.0 0.1 pad_add_fusion
  159.1 0.1 pad_add_fusion.4
  159.1 3.4 %placed.5.refs_4_ = bf16[4,2,13,2,128,128]{5,4,3,2,1,0:T(8,128)(2,1)} custom-call(s32[4]{0:T(128)S(1)} %pad_add_fusion.6.row, s32[4]{0:T(128)S(1)} %add_convert_fusion.valid, bf16[6,2,2,128,128]{4,3,2,1,0:T(8,128)(2,1)S(1)} %collective-permute-done.13.refs_0_, ...), custom_call_target="tpu_custom_call", output_to_operand_aliasing={{}: (6, {})} | custom-call | bytes 5111808 | tf_op jit(solution)/shard_map/placed/pallas_call | solution.py:422
  162.5 0.0 collective-permute-done.12.refs_0_.refs_1_
  162.5 25.1 %collective-permute-done.14.refs_2_ = bf16[6,2,2,128,128]{4,3,2,1,0:T(8,128)(2,1)} collective-permute-done((bf16[6,2,2,128,128]{4,3,2,1,0:T(8,128)(2,1)S(1)}, bf16[6,2,2,128,128]{4,3,2,1,0:T(8,128)(2,1)}, u32[]{:S(2)}, u32[]{:S(2)}) %collective-permute-start.14) | collective-permute-done | bytes 786464 | tf_op jit(solution)/shard_map/ppermute | solution.py:41
  187.6 5.0 %collective-permute-done.16.refs_3_ = bf16[6,2,2,128,128]{4,3,2,1,0:T(8,128)(2,1)S(1)} collective-permute-done((bf16[6,2,2,128,128]{4,3,2,1,0:T(8,128)(2,1)}, bf16[6,2,2,128,128]{4,3,2,1,0:T(8,128)(2,1)S(1)}, u32[]{:S(2)}, u32[]{:S(2)}) %collective-permute-start.16) | collective-permute-done | bytes 786464 | tf_op jit(solution)/shard_map/ppermute | solution.py:41
  192.6 3.0 %placed.6.refs_2_ = bf16[4,2,13,2,128,128]{5,4,3,2,1,0:T(8,128)(2,1)} custom-call(s32[4]{0:T(128)S(1)} %get-tuple-element.41.row, s32[4]{0:T(128)S(1)} %get-tuple-element.42.valid, bf16[8,2,2,128,128]{4,3,2,1,0:T(8,128)(2,1)S(1)} %collective-permute-done.12.refs_0_.refs_1_, ...), custom_call_target="tpu_custom_call", output_to_operand_aliasing={{}: (6, {})} | custom-call | bytes 5111808 | tf_op jit(solution)/shard_map/placed/pallas_call | solution.py:422
  195.7 0.0 collective-permute-done.10.refs_0_
  195.7 0.0 collective-permute-done.11.refs_1_
  195.7 2.4 %placed.7 = bf16[4,2,13,2,128,128]{5,4,3,2,1,0:T(8,128)(2,1)} custom-call(s32[2]{0:T(128)S(1)} %get-tuple-element.43.row, s32[2]{0:T(128)S(1)} %get-tuple-element.44.valid, bf16[7,2,2,128,128]{4,3,2,1,0:T(8,128)(2,1)S(1)} %collective-permute-done.10.refs_0_, ...), custom_call_target="tpu_custom_call", output_to_operand_aliasing={{}: (4, {})} | custom-call | bytes 5111808 | tf_op jit(solution)/shard_map/placed/pallas_call | solution.py:422
  (1 shorter events, 0.0 us)
Async XLA Ops:
  0.0 33.3 %copy-start.2 = (bf16[1,1,32,128,128]{4,3,2,1,0:T(8,128)(2,1)S(1)}, bf16[1,1,32,128,128]{4,3,2,1,0:T(8,128)(2,1)}, u32[]{:S(2)}) copy-start(bf16[1,1,32,128,128]{4,3,2,1,0:T(8,128)(2,1)} %param.8) | copy-start | bytes 3145732
  1.7 28.4 %collective-permute-start = (bf16[32,128,128]{2,1,0:T(8,128)(2,1)S(1)}, bf16[32,128,128]{2,1,0:T(8,128)(2,1)S(1)}, u32[]{:S(2)}, u32[]{:S(2)}) collective-permute-start(bf16[32,128,128]{2,1,0:T(8,128)(2,1)S(1)} %bitcast.22), channel_id=1, source_target_pairs={{0,1},{1,2},{2,3},{4,5},{5,6},{6,7},{8,9},{9,10},{10,11},{12,13},{... | collective-permute-start | bytes 3145736 | tf_op jit(solution)/shard_map/ppermute | solution.py:41
  6.7 26.6 %collective-permute-start.1 = (bf16[32,128,128]{2,1,0:T(8,128)(2,1)S(1)}, bf16[32,128,128]{2,1,0:T(8,128)(2,1)}, u32[]{:S(2)}, u32[]{:S(2)}) collective-permute-start(bf16[32,128,128]{2,1,0:T(8,128)(2,1)S(1)} %bitcast.23), channel_id=1, source_target_pairs={{1,0},{2,1},{3,2},{5,4},{6,5},{7,6},{9,8},{10,9},{11,10},{13,12},{... | collective-permute-start | bytes 3145736 | tf_op jit(solution)/shard_map/ppermute | solution.py:41
  8.0 25.3 %collective-permute-start.2 = (bf16[32,128,128]{2,1,0:T(8,128)(2,1)S(1)}, bf16[32,128,128]{2,1,0:T(8,128)(2,1)}, u32[]{:S(2)}, u32[]{:S(2)}) collective-permute-start(bf16[32,128,128]{2,1,0:T(8,128)(2,1)S(1)} %bitcast.24), channel_id=1, source_target_pairs={{0,4},{4,8},{8,12},{12,16},{16,20},{20,24},{24,28},{1,5},{5,9},{9,... | collective-permute-start | bytes 3145736 | tf_op jit(solution)/shard_map/ppermute | solution.py:41
  10.5 22.9 %collective-permute-start.3 = (bf16[32,128,128]{2,1,0:T(8,128)(2,1)S(1)}, bf16[32,128,128]{2,1,0:T(8,128)(2,1)}, u32[]{:S(2)}, u32[]{:S(2)}) collective-permute-start(bf16[32,128,128]{2,1,0:T(8,128)(2,1)S(1)} %bitcast.25), channel_id=1, source_target_pairs={{4,0},{8,4},{12,8},{16,12},{20,16},{24,20},{28,24},{5,1},{9,5},{13... | collective-permute-start | bytes 3145736 | tf_op jit(solution)/shard_map/ppermute | solution.py:41
  12.7 1.2 copy-start.1
  14.0 0.7 copy-start.3
  28.8 1.3 copy-start.4
  58.3 29.0 %collective-permute-start.6 = (bf16[5,2,2,128,128]{4,3,2,1,0:T(8,128)(2,1)S(1)}, bf16[5,2,2,128,128]{4,3,2,1,0:T(8,128)(2,1)S(1)}, u32[]{:S(2)}, u32[]{:S(2)}) collective-permute-start(bf16[5,2,2,128,128]{4,3,2,1,0:T(8,128)(2,1)S(1)} %get-tuple-element.30), channel_id=1, source_target_pairs={{0,4},{4,8},{8,12},{12,16},{16,20},{20,24},{24,28},{1,5},{5,9},{9,... | collective-permute-start | bytes 1966088 | tf_op jit(solution)/shard_map/ppermute | solution.py:41
  63.8 23.5 %collective-permute-start.7 = (bf16[5,2,2,128,128]{4,3,2,1,0:T(8,128)(2,1)S(1)}, bf16[5,2,2,128,128]{4,3,2,1,0:T(8,128)(2,1)S(1)}, u32[]{:S(2)}, u32[]{:S(2)}) collective-permute-start(bf16[5,2,2,128,128]{4,3,2,1,0:T(8,128)(2,1)S(1)} %get-tuple-element.31), channel_id=1, source_target_pairs={{4,0},{8,4},{12,8},{16,12},{20,16},{24,20},{28,24},{5,1},{9,5},{13... | collective-permute-start | bytes 1966088 | tf_op jit(solution)/shard_map/ppermute | solution.py:41
  65.1 17.7 %collective-permute-start.4 = (bf16[4,2,2,128,128]{4,3,2,1,0:T(8,128)(2,1)S(1)}, bf16[4,2,2,128,128]{4,3,2,1,0:T(8,128)(2,1)S(1)}, u32[]{:S(2)}, u32[]{:S(2)}) collective-permute-start(bf16[4,2,2,128,128]{4,3,2,1,0:T(8,128)(2,1)S(1)} %get-tuple-element.28), channel_id=1, source_target_pairs={{0,1},{1,2},{2,3},{4,5},{5,6},{6,7},{8,9},{9,10},{10,11},{12,13},{... | collective-permute-start | bytes 1572872 | tf_op jit(solution)/shard_map/ppermute | solution.py:41
  70.7 16.7 %collective-permute-start.5 = (bf16[4,2,2,128,128]{4,3,2,1,0:T(8,128)(2,1)S(1)}, bf16[4,2,2,128,128]{4,3,2,1,0:T(8,128)(2,1)S(1)}, u32[]{:S(2)}, u32[]{:S(2)}) collective-permute-start(bf16[4,2,2,128,128]{4,3,2,1,0:T(8,128)(2,1)S(1)} %get-tuple-element.29), channel_id=1, source_target_pairs={{1,0},{2,1},{3,2},{5,4},{6,5},{7,6},{9,8},{10,9},{11,10},{13,12},{... | collective-permute-start | bytes 1572872 | tf_op jit(solution)/shard_map/ppermute | solution.py:41
  72.0 4.0 %copy-start = (bf16[1280,4096]{1,0:T(8,128)(2,1)S(1)}, bf16[1280,4096]{1,0:T(8,128)(2,1)}, u32[]{:S(2)}) copy-start(bf16[1280,4096]{1,0:T(8,128)(2,1)} %get-tuple-element.33.right_all) | copy-start | bytes 31457284
  88.0 24.7 %collective-permute-start.8 = (bf16[7,2,2,128,128]{4,3,2,1,0:T(8,128)(2,1)S(1)}, bf16[7,2,2,128,128]{4,3,2,1,0:T(8,128)(2,1)}, u32[]{:S(2)}, u32[]{:S(2)}) collective-permute-start(bf16[7,2,2,128,128]{4,3,2,1,0:T(8,128)(2,1)S(1)} %get-tuple-element.36.refs_1_), channel_id=1, source_target_pairs={{0,1},{1,2},{2,3},{4,5},{5,6},{6,7},{8,9},{9,10},{10,11},{12,13},{... | collective-permute-start | bytes 2752520 | tf_op jit(solution)/shard_map/ppermute | solution.py:41
  92.9 25.2 %collective-permute-start.9 = (bf16[7,2,2,128,128]{4,3,2,1,0:T(8,128)(2,1)S(1)}, bf16[7,2,2,128,128]{4,3,2,1,0:T(8,128)(2,1)}, u32[]{:S(2)}, u32[]{:S(2)}) collective-permute-start(bf16[7,2,2,128,128]{4,3,2,1,0:T(8,128)(2,1)S(1)} %get-tuple-element.36.refs_1_), channel_id=1, source_target_pairs={{1,0},{2,1},{3,2},{5,4},{6,5},{7,6},{9,8},{10,9},{11,10},{13,12},{... | collective-permute-start | bytes 2752520 | tf_op jit(solution)/shard_map/ppermute | solution.py:41
  94.2 35.3 %collective-permute-start.13 = (bf16[6,2,2,128,128]{4,3,2,1,0:T(8,128)(2,1)S(1)}, bf16[6,2,2,128,128]{4,3,2,1,0:T(8,128)(2,1)S(1)}, u32[]{:S(2)}, u32[]{:S(2)}) collective-permute-start(bf16[6,2,2,128,128]{4,3,2,1,0:T(8,128)(2,1)S(1)} %get-tuple-element.37.refs_0_), channel_id=1, source_target_pairs={{0,1},{1,2},{2,3},{4,5},{5,6},{6,7},{8,9},{9,10},{10,11},{12,13},{... | collective-permute-start | bytes 2359304 | tf_op jit(solution)/shard_map/ppermute | solution.py:41
  98.8 58.7 %collective-permute-start.15 = (bf16[6,2,2,128,128]{4,3,2,1,0:T(8,128)(2,1)S(1)}, bf16[6,2,2,128,128]{4,3,2,1,0:T(8,128)(2,1)}, u32[]{:S(2)}, u32[]{:S(2)}) collective-permute-start(bf16[6,2,2,128,128]{4,3,2,1,0:T(8,128)(2,1)S(1)} %get-tuple-element.37.refs_0_), channel_id=1, source_target_pairs={{1,0},{2,1},{3,2},{5,4},{6,5},{7,6},{9,8},{10,9},{11,10},{13,12},{... | collective-permute-start | bytes 2359304 | tf_op jit(solution)/shard_map/ppermute | solution.py:41
  101.5 61.0 %collective-permute-start.12 = (bf16[8,2,2,128,128]{4,3,2,1,0:T(8,128)(2,1)}, bf16[8,2,2,128,128]{4,3,2,1,0:T(8,128)(2,1)S(1)}, u32[]{:S(2)}, u32[]{:S(2)}) collective-permute-start(bf16[8,2,2,128,128]{4,3,2,1,0:T(8,128)(2,1)} %fusion), channel_id=1, source_target_pairs={{0,3},{3,0},{4,7},{7,4},{8,11},{11,8},{12,15},{15,12},{16,19},{19,... | collective-permute-start | bytes 3145736 | tf_op jit(solution)/shard_map/ppermute | solution.py:448
  118.2 77.5 %collective-permute-start.10 = (bf16[7,2,2,128,128]{4,3,2,1,0:T(8,128)(2,1)}, bf16[7,2,2,128,128]{4,3,2,1,0:T(8,128)(2,1)S(1)}, u32[]{:S(2)}, u32[]{:S(2)}) collective-permute-start(bf16[7,2,2,128,128]{4,3,2,1,0:T(8,128)(2,1)} %collective-permute-done.8.refs_2_), channel_id=1, source_target_pairs={{0,1},{1,2},{2,3},{4,5},{5,6},{6,7},{8,9},{9,10},{10,11},{12,13},{... | collective-permute-start | bytes 2752520 | tf_op jit(solution)/shard_map/ppermute | solution.py:41
  120.8 74.9 %collective-permute-start.11 = (bf16[7,2,2,128,128]{4,3,2,1,0:T(8,128)(2,1)}, bf16[7,2,2,128,128]{4,3,2,1,0:T(8,128)(2,1)}, u32[]{:S(2)}, u32[]{:S(2)}) collective-permute-start(bf16[7,2,2,128,128]{4,3,2,1,0:T(8,128)(2,1)} %collective-permute-done.9.refs_3_), channel_id=1, source_target_pairs={{1,0},{2,1},{3,2},{5,4},{6,5},{7,6},{9,8},{10,9},{11,10},{13,12},{... | collective-permute-start | bytes 2752520 | tf_op jit(solution)/shard_map/ppermute | solution.py:41
  129.6 58.1 %collective-permute-start.14 = (bf16[6,2,2,128,128]{4,3,2,1,0:T(8,128)(2,1)S(1)}, bf16[6,2,2,128,128]{4,3,2,1,0:T(8,128)(2,1)}, u32[]{:S(2)}, u32[]{:S(2)}) collective-permute-start(bf16[6,2,2,128,128]{4,3,2,1,0:T(8,128)(2,1)S(1)} %collective-permute-done.13.refs_0_), channel_id=1, source_target_pairs={{0,1},{1,2},{2,3},{4,5},{5,6},{6,7},{8,9},{9,10},{10,11},{12,13},{... | collective-permute-start | bytes 2359304 | tf_op jit(solution)/shard_map/ppermute | solution.py:41
  157.5 35.1 %collective-permute-start.16 = (bf16[6,2,2,128,128]{4,3,2,1,0:T(8,128)(2,1)}, bf16[6,2,2,128,128]{4,3,2,1,0:T(8,128)(2,1)S(1)}, u32[]{:S(2)}, u32[]{:S(2)}) collective-permute-start(bf16[6,2,2,128,128]{4,3,2,1,0:T(8,128)(2,1)} %collective-permute-done.15.refs_1_), channel_id=1, source_target_pairs={{1,0},{2,1},{3,2},{5,4},{6,5},{7,6},{9,8},{10,9},{11,10},{13,12},{... | collective-permute-start | bytes 2359304 | tf_op jit(solution)/shard_map/ppermute | solution.py:41

commit v5 on v4

--- a/solution.py
+++ b/solution.py
@@ -31,6 +31,7 @@
 smoothing = 2.0 / 3.0
 MEMBERS = 2
 ROWS_PER_STEP = 4
+ROWS_PER_CHUNK = 8
 UNROLL = 8
 NT = (((1,), (1,)), ((), ()))
 
@@ -184,34 +185,36 @@
     a_held, dinv, tent, right, left, sums, sems = refs[14:]
     tile = dinv.shape[-1]
     rows = dinv.shape[0]
-    chunks = rows // ROWS_PER_STEP
+    chunks = rows // ROWS_PER_CHUNK
     outer = 4 * members
-    per = ROWS_PER_STEP * taps
+    per = ROWS_PER_CHUNK * taps
 
     def a_copy(c):
         part = pl.ds(c * per, per)
         return pltpu.make_async_copy(a_tiles.at[part], a_held.at[part], sems.at[c])
 
-    others = [
+    tent_copies = [
         pltpu.make_async_copy(source, tent.at[pl.ds(d * rows, rows)], sems.at[chunks + d])
         for d, source in enumerate(tents)
     ]
-    others.append(pltpu.make_async_copy(dinv_hbm, dinv, sems.at[chunks + 4]))
+    dinv_copy = pltpu.make_async_copy(dinv_hbm, dinv, sems.at[chunks + 4])
     own_part = (pl.ds(outer * tile, members * tile), slice(None))
     own_copy = pltpu.make_async_copy(right_own, right.at[own_part], sems.at[chunks + 5])
     out_copy = pltpu.make_async_copy(right, right_out, sems.at[chunks + 6])
-    for copy in others:
+    for copy in tent_copies:
         copy.start()
-    for c in range(chunks):
+    a_copy(0).start()
+    sums[...] = jnp.zeros_like(sums)
+    for copy in tent_copies:
+        copy.wait()
+    dinv_copy.start()
+    for c in range(1, chunks):
         a_copy(c).start()
     own_copy.start()
-    sums[...] = jnp.zeros_like(sums)
-    for copy in others:
-        copy.wait()
 
     def one_chunk(c, first):
         a_copy(c).wait()
-        last = ends[c]
+        last = ends[(c + 1) * (ROWS_PER_CHUNK // ROWS_PER_STEP) - 1]
 
         def some(n, carry):
             found = []
@@ -223,18 +226,23 @@
                 z = lax.dot_general(
                     tent[sources[index]], a_held[number], NT, preferred_element_type=jnp.float32
                 )
-                found.append((slot, number // taps - c * ROWS_PER_STEP, z))
+                found.append((slot, number // taps - c * ROWS_PER_CHUNK, z))
             for slot, row, z in found:
                 at = (lane_tiles(slot, tile), lane_tiles(row, tile))
                 sums[at] += z.astype(jnp.bfloat16).astype(jnp.float32)
             return carry
 
         lax.fori_loop(0, (last - first + UNROLL - 1) // UNROLL, some, 0)
-        lanes = lane_tiles(c, ROWS_PER_STEP * tile)
+        lanes = lane_tiles(c, ROWS_PER_CHUNK * tile)
         right[: outer * tile, lanes] = sums[: outer * tile, :].astype(jnp.bfloat16)
         sums[...] = jnp.zeros_like(sums)
-        for u in range(ROWS_PER_STEP):
-            g = c * ROWS_PER_STEP + u
+
+        @pl.when(c == 0)
+        def _():
+            dinv_copy.wait()
+
+        for u in range(ROWS_PER_CHUNK):
+            g = c * ROWS_PER_CHUNK + u
             lanes = lane_tiles(g, tile)
             smooth = lax.dot_general(
                 right[: outer * tile, lanes], dinv[g], NT, preferred_element_type=jnp.float32
@@ -269,8 +277,8 @@
                 pltpu.VMEM((4 * rows, tile, tile), jnp.bfloat16),
                 pltpu.VMEM((slots, rows * tile), jnp.bfloat16),
                 pltpu.VMEM((outer, rows * tile), jnp.bfloat16),
-                pltpu.VMEM((outer + tile, ROWS_PER_STEP * tile), jnp.float32),
-                pltpu.SemaphoreType.DMA((rows // ROWS_PER_STEP + 7,)),
+                pltpu.VMEM((outer + tile, ROWS_PER_CHUNK * tile), jnp.float32),
+                pltpu.SemaphoreType.DMA((rows // ROWS_PER_CHUNK + 7,)),
             ],
         ),
         out_shape=[
@@ -469,8 +477,8 @@
                 (from_lower, group, group, grid_y - hop, grid_y >= hop),
                 (from_upper, group, group, grid_y + hop, grid_y + hop < count_y),
             ]
-    out = placed(out, direct + pieces[:2], count_y)
-    return placed(out, pieces[2:], count_y)
+    out = placed(out, direct + pieces[2:], count_y)
+    return placed(out, pieces[:2], count_y)
 
 
 def local(a_tiles, columns, ptent, dinv, agg):

time: 199 us -> 195 us (0.980)
  starting transfers between devices: 73.1 us -> 48.2 us
  waiting for transfers between devices: 58 us -> 80.2 us
    ppermute x16, waiting for transfers between devices: 58 us -> 80.2 us  [shifted(): return lax.ppermute(x, axis, pairs)]
    ppermute x16, starting transfers between devices: 67.3 us -> 46.3 us  [shifted(): return lax.ppermute(x, axis, pairs)]
    ppermute x1, starting transfers between devices: 5.79 us -> 1.91 us  [end_to_end(): moved = lax.ppermute(sent, 'sy', [(0, last), (last, 0)])]
where the time goes in v5:
time: 195 us
  waiting for transfers between devices  80.2 us (41%)
  Pallas kernels  54.4 us (28%)
  starting transfers between devices  48.2 us (25%)
  local copies, waits for them, and re-layouts  9.77 us (5%)
    ppermute x16, waiting for transfers between devices, shifted(): return lax.ppermute(x, axis, pairs)  80.2 us
    ppermute x16, starting transfers between devices, shifted(): return lax.ppermute(x, axis, pairs)  46.3 us
    pallas_call x1, Pallas kernels, partial_blocks(): pl.pallas_call(functools.partial(partial_kernel, members, taps), grid_spe...  24.2 us
    pallas_call x1, Pallas kernels, own_slots(): pl.pallas_call(functools.partial(own_kernel, count_y, rows, members, taps...  14.2 us
    pallas_call x4, Pallas kernels, placed(): pl.pallas_call(functools.partial(place_kernel, tuple((p[1:3] for p in pie...  10.8 us
    unnamed x12, local copies, waits for them, and re-layouts  9.67 us
    pallas_call x1, Pallas kernels, own_rows(): pl.pallas_call(functools.partial(own_rows_kernel, members), grid=(1,), in...  4.57 us
  transfers between devices with their start and end apart: 17, of which 9 were waited for; matrix products, arithmetic and copies ran while one was open for 1% of the time, Pallas kernels for 14%

profile of v5, /device:TPU:0, one launch (start us, length us, event | category | flops | bytes accessed | tf_op | source)
XLA Modules:
  0.0 194.6 jit_solution(5660040270440381312)
XLA Ops:
  0.0 0.0 copy-start.2
  0.0 1.7 copy.11
  1.7 5.0 %collective-permute-start = (bf16[32,128,128]{2,1,0:T(8,128)(2,1)S(1)}, bf16[32,128,128]{2,1,0:T(8,128)(2,1)S(1)}, u32[]{:S(2)}, u32[]{:S(2)}) collective-permute-start(bf16[32,128,128]{2,1,0:T(8,128)(2,1)S(1)} %bitcast.22), channel_id=1, source_target_pairs={{0,1},{1,2},{2,3},{4,5},{5,6},{6,7},{8,9},{9,10},{10,11},{12,13},{... | collective-permute-start | bytes 3145736 | tf_op jit(solution)/shard_map/ppermute | solution.py:42
  6.7 1.3 collective-permute-start.1
  8.0 2.5 %collective-permute-start.2 = (bf16[32,128,128]{2,1,0:T(8,128)(2,1)S(1)}, bf16[32,128,128]{2,1,0:T(8,128)(2,1)}, u32[]{:S(2)}, u32[]{:S(2)}) collective-permute-start(bf16[32,128,128]{2,1,0:T(8,128)(2,1)S(1)} %bitcast.24), channel_id=1, source_target_pairs={{0,4},{4,8},{8,12},{12,16},{16,20},{20,24},{24,28},{1,5},{5,9},{9,... | collective-permute-start | bytes 3145736 | tf_op jit(solution)/shard_map/ppermute | solution.py:42
  10.5 1.3 collective-permute-start.3
  11.8 0.8 copy.10
  12.5 0.1 reshape.12.columns
  12.6 0.1 pad_add_fusion.2.place
  12.7 0.0 copy-start.1
  12.7 1.2 copy-done.1
  14.0 0.0 copy-start.3
  14.0 0.7 copy-done.3
  14.6 14.2 %own_slots.1 = (bf16[256,4096]{1,0:T(8,128)(2,1)S(1)}, bf16[256,4096]{1,0:T(8,128)(2,1)S(1)}, s32[224]{0:T(256)S(1)}, s32[224]{0:T(256)S(1)}, s32[224]{0:T(256)S(1)}, /*index=5*/s32[8]{0:T(128)S(1)}) custom-call(s32[224]{0:T(256)S(1)} %reshape.12.columns, s32[1024]{0:T(1024)S(1)} %copy-done.3, s32[2]{0:T(128)S(1)} %pad_add_fusion.2.place, ...), custom_call_target="tpu_custom_call" | custom-call | flops 1207959552 | bytes 13631488 | tf_op jit(solution)/shard_map/own_slots/pallas_call | solution.py:104
  28.8 0.0 copy-start.4
  28.8 1.3 copy-done.4
  30.1 0.0 collective-permute-done.refs_2_
  30.1 3.2 %collective-permute-done.1.refs_3_ = bf16[32,128,128]{2,1,0:T(8,128)(2,1)} collective-permute-done((bf16[32,128,128]{2,1,0:T(8,128)(2,1)S(1)}, bf16[32,128,128]{2,1,0:T(8,128)(2,1)}, u32[]{:S(2)}, u32[]{:S(2)}) %collective-permute-start.1) | collective-permute-done | bytes 1048608 | tf_op jit(solution)/shard_map/ppermute | solution.py:42
  33.3 0.0 collective-permute-done.2.refs_4_
  33.3 0.0 collective-permute-done.3.refs_5_
  33.3 0.0 copy-done.2
  33.3 24.2 %partial_blocks.1 = (bf16[4,2,2,128,128]{4,3,2,1,0:T(8,128)(2,1)S(1)}, bf16[4,2,2,128,128]{4,3,2,1,0:T(8,128)(2,1)S(1)}, bf16[5,2,2,128,128]{4,3,2,1,0:T(8,128)(...) custom-call(s32[224]{0:T(256)S(1)} %get-tuple-element.23.tiles, ...), custom_call_target="tpu_custom_call" | custom-call | flops 11811160064 | bytes 28311552 | tf_op jit(solution)/shard_map/partial_blocks/pallas_call | solution.py:267
  57.5 6.1 %collective-permute-start.6 = (bf16[5,2,2,128,128]{4,3,2,1,0:T(8,128)(2,1)S(1)}, bf16[5,2,2,128,128]{4,3,2,1,0:T(8,128)(2,1)S(1)}, u32[]{:S(2)}, u32[]{:S(2)}) collective-permute-start(bf16[5,2,2,128,128]{4,3,2,1,0:T(8,128)(2,1)S(1)} %get-tuple-element.30), channel_id=1, source_target_pairs={{0,4},{4,8},{8,12},{12,16},{16,20},{20,24},{24,28},{1,5},{5,9},{9,... | collective-permute-start | bytes 1966088 | tf_op jit(solution)/shard_map/ppermute | solution.py:42
  63.7 1.3 collective-permute-start.7
  65.0 4.9 %collective-permute-start.4 = (bf16[4,2,2,128,128]{4,3,2,1,0:T(8,128)(2,1)S(1)}, bf16[4,2,2,128,128]{4,3,2,1,0:T(8,128)(2,1)S(1)}, u32[]{:S(2)}, u32[]{:S(2)}) collective-permute-start(bf16[4,2,2,128,128]{4,3,2,1,0:T(8,128)(2,1)S(1)} %get-tuple-element.28), channel_id=1, source_target_pairs={{0,1},{1,2},{2,3},{4,5},{5,6},{6,7},{8,9},{9,10},{10,11},{12,13},{... | collective-permute-start | bytes 1572872 | tf_op jit(solution)/shard_map/ppermute | solution.py:42
  69.9 1.3 collective-permute-start.5
  71.2 0.0 copy-start
  71.2 4.0 %copy-done = bf16[1280,4096]{1,0:T(8,128)(2,1)S(1)} copy-done((bf16[1280,4096]{1,0:T(8,128)(2,1)S(1)}, bf16[1280,4096]{1,0:T(8,128)(2,1)}, u32[]{:S(2)}) %copy-start) | copy-done | bytes 10485784
  75.2 4.6 %own_rows.1.refs_4_ = f32[5,2,2,128,128]{4,3,2,1,0:T(8,128)S(1)} custom-call(bf16[256,4096]{1,0:T(8,128)(2,1)S(1)} %get-tuple-element.32.left_own, bf16[1280,4096]{1,0:T(8,128)(2,1)S(1)} %copy-done), custom_call_target="tpu_custom_call" | custom-call | flops 2684354560 | bytes 12582912 | tf_op jit(solution)/shard_map/own_rows/pallas_call | solution.py:314
  79.7 2.1 %collective-permute-done.4.refs_0_ = bf16[4,2,2,128,128]{4,3,2,1,0:T(8,128)(2,1)S(1)} collective-permute-done((bf16[4,2,2,128,128]{4,3,2,1,0:T(8,128)(2,1)S(1)}, bf16[4,2,2,128,128]{4,3,2,1,0:T(8,128)(2,1)S(1)}, u32[]{:S(2)}, u32[]{:S(2)}) %collective-permute-start.4) | collective-permute-done | bytes 524320 | tf_op jit(solution)/shard_map/ppermute | solution.py:42
  81.9 5.0 %collective-permute-done.5.refs_1_ = bf16[4,2,2,128,128]{4,3,2,1,0:T(8,128)(2,1)S(1)} collective-permute-done((bf16[4,2,2,128,128]{4,3,2,1,0:T(8,128)(2,1)S(1)}, bf16[4,2,2,128,128]{4,3,2,1,0:T(8,128)(2,1)S(1)}, u32[]{:S(2)}, u32[]{:S(2)}) %collective-permute-start.5) | collective-permute-done | bytes 524320 | tf_op jit(solution)/shard_map/ppermute | solution.py:42
  86.9 0.0 collective-permute-done.6.refs_2_
  86.9 0.0 collective-permute-done.7.refs_3_
  86.9 0.7 finished_window.1
  87.6 4.9 %collective-permute-start.13 = (bf16[7,2,2,128,128]{4,3,2,1,0:T(8,128)(2,1)S(1)}, bf16[7,2,2,128,128]{4,3,2,1,0:T(8,128)(2,1)}, u32[]{:S(2)}, u32[]{:S(2)}) collective-permute-start(bf16[7,2,2,128,128]{4,3,2,1,0:T(8,128)(2,1)S(1)} %get-tuple-element.37.refs_1_), channel_id=1, source_target_pairs={{0,1},{1,2},{2,3},{4,5},{5,6},{6,7},{8,9},{9,10},{10,11},{12,13},{... | collective-permute-start | bytes 2752520 | tf_op jit(solution)/shard_map/ppermute | solution.py:42
  92.5 1.3 collective-permute-start.14
  93.8 1.3 collective-permute-start.10
  95.1 6.1 %collective-permute-start.8 = (bf16[6,2,2,128,128]{4,3,2,1,0:T(8,128)(2,1)S(1)}, bf16[6,2,2,128,128]{4,3,2,1,0:T(8,128)(2,1)}, u32[]{:S(2)}, u32[]{:S(2)}) collective-permute-start(bf16[6,2,2,128,128]{4,3,2,1,0:T(8,128)(2,1)S(1)} %get-tuple-element.36.refs_0_), channel_id=1, source_target_pairs={{0,1},{1,2},{2,3},{4,5},{5,6},{6,7},{8,9},{9,10},{10,11},{12,13},{... | collective-permute-start | bytes 2359304 | tf_op jit(solution)/shard_map/ppermute | solution.py:42
  101.2 1.3 fusion
  102.5 1.9 collective-permute-start.12
  104.4 0.1 pad_add_fusion.5.row
  104.5 2.0 %placed.4.refs_4_ = bf16[4,2,13,2,128,128]{5,4,3,2,1,0:T(8,128)(2,1)} custom-call(s32[2]{0:T(128)S(1)} %pad_add_fusion.5.row, s32[2]{0:T(128)S(1)} %broadcast_1_valid.2.valid, bf16[6,2,2,128,128]{4,3,2,1,0:T(8,128)(2,1)S(1)} %get-tuple-element.36.refs_0_, bf16[7,2,2,128,128]{4,3,2,1,0:T(8,128)(2,1)S(1)} %get-tuple-element.37.refs_1_), custom_call_target="tpu_custom_call" | custom-call | bytes 5111808 | tf_op jit(solution)/shard_map/placed/pallas_call | solution.py:430
  106.5 5.8 %collective-permute-done.13.refs_2_ = bf16[7,2,2,128,128]{4,3,2,1,0:T(8,128)(2,1)} collective-permute-done((bf16[7,2,2,128,128]{4,3,2,1,0:T(8,128)(2,1)S(1)}, bf16[7,2,2,128,128]{4,3,2,1,0:T(8,128)(2,1)}, u32[]{:S(2)}, u32[]{:S(2)}) %collective-permute-start.13) | collective-permute-done | bytes 917536 | tf_op jit(solution)/shard_map/ppermute | solution.py:42
  112.3 5.5 %collective-permute-done.14.refs_3_ = bf16[7,2,2,128,128]{4,3,2,1,0:T(8,128)(2,1)} collective-permute-done((bf16[7,2,2,128,128]{4,3,2,1,0:T(8,128)(2,1)S(1)}, bf16[7,2,2,128,128]{4,3,2,1,0:T(8,128)(2,1)}, u32[]{:S(2)}, u32[]{:S(2)}) %collective-permute-start.14) | collective-permute-done | bytes 917536 | tf_op jit(solution)/shard_map/ppermute | solution.py:42
  117.8 1.9 collective-permute-start.15
  119.7 1.3 collective-permute-start.16
  121.0 36.0 %collective-permute-done.10.refs_1_ = bf16[6,2,2,128,128]{4,3,2,1,0:T(8,128)(2,1)S(1)} collective-permute-done((bf16[6,2,2,128,128]{4,3,2,1,0:T(8,128)(2,1)S(1)}, bf16[6,2,2,128,128]{4,3,2,1,0:T(8,128)(2,1)S(1)}, u32[]{:S(2)}, u32[]{:S(2)}) %collective-permute-start.10) | collective-permute-done | bytes 786464 | tf_op jit(solution)/shard_map/ppermute | solution.py:42
  157.0 1.3 collective-permute-start.11
  158.3 0.0 collective-permute-done.8.refs_0_
  158.3 4.6 %collective-permute-start.9 = (bf16[6,2,2,128,128]{4,3,2,1,0:T(8,128)(2,1)}, bf16[6,2,2,128,128]{4,3,2,1,0:T(8,128)(2,1)S(1)}, u32[]{:S(2)}, u32[]{:S(2)}) collective-permute-start(bf16[6,2,2,128,128]{4,3,2,1,0:T(8,128)(2,1)} %collective-permute-done.8.refs_0_), channel_id=1, source_target_pairs={{0,1},{1,2},{2,3},{4,5},{5,6},{6,7},{8,9},{9,10},{10,11},{12,13},{... | collective-permute-start | bytes 2359304 | tf_op jit(solution)/shard_map/ppermute | solution.py:42
  162.9 0.1 pad_add_fusion.6.row
  163.0 0.1 add_convert_fusion.valid
  163.1 0.1 pad_add_fusion
  163.2 0.1 pad_add_fusion.3
  163.2 3.4 %placed.5.refs_4_ = bf16[4,2,13,2,128,128]{5,4,3,2,1,0:T(8,128)(2,1)} custom-call(s32[4]{0:T(128)S(1)} %pad_add_fusion.6.row, s32[4]{0:T(128)S(1)} %add_convert_fusion.valid, bf16[6,2,2,128,128]{4,3,2,1,0:T(8,128)(2,1)} %collective-permute-done.8.refs_0_, ...), custom_call_target="tpu_custom_call", output_to_operand_aliasing={{}: (6, {})} | custom-call | bytes 5111808 | tf_op jit(solution)/shard_map/placed/pallas_call | solution.py:430
  166.6 0.0 collective-permute-done.12.refs_0_.refs_1_
  166.6 4.8 %collective-permute-done.15.refs_2_ = bf16[7,2,2,128,128]{4,3,2,1,0:T(8,128)(2,1)S(1)} collective-permute-done((bf16[7,2,2,128,128]{4,3,2,1,0:T(8,128)(2,1)}, bf16[7,2,2,128,128]{4,3,2,1,0:T(8,128)(2,1)S(1)}, u32[]{:S(2)}, u32[]{:S(2)}) %collective-permute-start.15) | collective-permute-done | bytes 917536 | tf_op jit(solution)/shard_map/ppermute | solution.py:42
  171.4 5.3 %collective-permute-done.16.refs_3_ = bf16[7,2,2,128,128]{4,3,2,1,0:T(8,128)(2,1)} collective-permute-done((bf16[7,2,2,128,128]{4,3,2,1,0:T(8,128)(2,1)}, bf16[7,2,2,128,128]{4,3,2,1,0:T(8,128)(2,1)}, u32[]{:S(2)}, u32[]{:S(2)}) %collective-permute-start.16) | collective-permute-done | bytes 917536 | tf_op jit(solution)/shard_map/ppermute | solution.py:42
  176.8 3.1 %placed.6.refs_2_ = bf16[4,2,13,2,128,128]{5,4,3,2,1,0:T(8,128)(2,1)} custom-call(s32[4]{0:T(128)S(1)} %get-tuple-element.41.row, s32[4]{0:T(128)S(1)} %get-tuple-element.42.valid, bf16[8,2,2,128,128]{4,3,2,1,0:T(8,128)(2,1)S(1)} %collective-permute-done.12.refs_0_.refs_1_, ...), custom_call_target="tpu_custom_call", output_to_operand_aliasing={{}: (6, {})} | custom-call | bytes 5111808 | tf_op jit(solution)/shard_map/placed/pallas_call | solution.py:430
  179.9 12.4 %collective-permute-done.11.refs_1_ = bf16[6,2,2,128,128]{4,3,2,1,0:T(8,128)(2,1)} collective-permute-done((bf16[6,2,2,128,128]{4,3,2,1,0:T(8,128)(2,1)S(1)}, bf16[6,2,2,128,128]{4,3,2,1,0:T(8,128)(2,1)}, u32[]{:S(2)}, u32[]{:S(2)}) %collective-permute-start.11) | collective-permute-done | bytes 786464 | tf_op jit(solution)/shard_map/ppermute | solution.py:42
  192.3 0.0 collective-permute-done.9.refs_0_
  192.3 2.3 %placed.7 = bf16[4,2,13,2,128,128]{5,4,3,2,1,0:T(8,128)(2,1)} custom-call(s32[2]{0:T(128)S(1)} %get-tuple-element.43.row, s32[2]{0:T(128)S(1)} %get-tuple-element.44.valid, bf16[6,2,2,128,128]{4,3,2,1,0:T(8,128)(2,1)S(1)} %collective-permute-done.9.refs_0_, ...), custom_call_target="tpu_custom_call", output_to_operand_aliasing={{}: (4, {})} | custom-call | bytes 5111808 | tf_op jit(solution)/shard_map/placed/pallas_call | solution.py:430
  (1 shorter events, 0.0 us)
Async XLA Ops:
  0.0 33.3 %copy-start.2 = (bf16[1,1,32,128,128]{4,3,2,1,0:T(8,128)(2,1)S(1)}, bf16[1,1,32,128,128]{4,3,2,1,0:T(8,128)(2,1)}, u32[]{:S(2)}) copy-start(bf16[1,1,32,128,128]{4,3,2,1,0:T(8,128)(2,1)} %param.8) | copy-start | bytes 3145732
  1.7 28.4 %collective-permute-start = (bf16[32,128,128]{2,1,0:T(8,128)(2,1)S(1)}, bf16[32,128,128]{2,1,0:T(8,128)(2,1)S(1)}, u32[]{:S(2)}, u32[]{:S(2)}) collective-permute-start(bf16[32,128,128]{2,1,0:T(8,128)(2,1)S(1)} %bitcast.22), channel_id=1, source_target_pairs={{0,1},{1,2},{2,3},{4,5},{5,6},{6,7},{8,9},{9,10},{10,11},{12,13},{... | collective-permute-start | bytes 3145736 | tf_op jit(solution)/shard_map/ppermute | solution.py:42
  6.7 26.6 %collective-permute-start.1 = (bf16[32,128,128]{2,1,0:T(8,128)(2,1)S(1)}, bf16[32,128,128]{2,1,0:T(8,128)(2,1)}, u32[]{:S(2)}, u32[]{:S(2)}) collective-permute-start(bf16[32,128,128]{2,1,0:T(8,128)(2,1)S(1)} %bitcast.23), channel_id=1, source_target_pairs={{1,0},{2,1},{3,2},{5,4},{6,5},{7,6},{9,8},{10,9},{11,10},{13,12},{... | collective-permute-start | bytes 3145736 | tf_op jit(solution)/shard_map/ppermute | solution.py:42
  8.0 25.3 %collective-permute-start.2 = (bf16[32,128,128]{2,1,0:T(8,128)(2,1)S(1)}, bf16[32,128,128]{2,1,0:T(8,128)(2,1)}, u32[]{:S(2)}, u32[]{:S(2)}) collective-permute-start(bf16[32,128,128]{2,1,0:T(8,128)(2,1)S(1)} %bitcast.24), channel_id=1, source_target_pairs={{0,4},{4,8},{8,12},{12,16},{16,20},{20,24},{24,28},{1,5},{5,9},{9,... | collective-permute-start | bytes 3145736 | tf_op jit(solution)/shard_map/ppermute | solution.py:42
  10.5 22.9 %collective-permute-start.3 = (bf16[32,128,128]{2,1,0:T(8,128)(2,1)S(1)}, bf16[32,128,128]{2,1,0:T(8,128)(2,1)}, u32[]{:S(2)}, u32[]{:S(2)}) collective-permute-start(bf16[32,128,128]{2,1,0:T(8,128)(2,1)S(1)} %bitcast.25), channel_id=1, source_target_pairs={{4,0},{8,4},{12,8},{16,12},{20,16},{24,20},{28,24},{5,1},{9,5},{13... | collective-permute-start | bytes 3145736 | tf_op jit(solution)/shard_map/ppermute | solution.py:42
  12.7 1.2 copy-start.1
  14.0 0.7 copy-start.3
  28.8 1.3 copy-start.4
  57.5 29.4 %collective-permute-start.6 = (bf16[5,2,2,128,128]{4,3,2,1,0:T(8,128)(2,1)S(1)}, bf16[5,2,2,128,128]{4,3,2,1,0:T(8,128)(2,1)S(1)}, u32[]{:S(2)}, u32[]{:S(2)}) collective-permute-start(bf16[5,2,2,128,128]{4,3,2,1,0:T(8,128)(2,1)S(1)} %get-tuple-element.30), channel_id=1, source_target_pairs={{0,4},{4,8},{8,12},{12,16},{16,20},{20,24},{24,28},{1,5},{5,9},{9,... | collective-permute-start | bytes 1966088 | tf_op jit(solution)/shard_map/ppermute | solution.py:42
  63.7 23.2 %collective-permute-start.7 = (bf16[5,2,2,128,128]{4,3,2,1,0:T(8,128)(2,1)S(1)}, bf16[5,2,2,128,128]{4,3,2,1,0:T(8,128)(2,1)S(1)}, u32[]{:S(2)}, u32[]{:S(2)}) collective-permute-start(bf16[5,2,2,128,128]{4,3,2,1,0:T(8,128)(2,1)S(1)} %get-tuple-element.31), channel_id=1, source_target_pairs={{4,0},{8,4},{12,8},{16,12},{20,16},{24,20},{28,24},{5,1},{9,5},{13... | collective-permute-start | bytes 1966088 | tf_op jit(solution)/shard_map/ppermute | solution.py:42
  65.0 16.9 %collective-permute-start.4 = (bf16[4,2,2,128,128]{4,3,2,1,0:T(8,128)(2,1)S(1)}, bf16[4,2,2,128,128]{4,3,2,1,0:T(8,128)(2,1)S(1)}, u32[]{:S(2)}, u32[]{:S(2)}) collective-permute-start(bf16[4,2,2,128,128]{4,3,2,1,0:T(8,128)(2,1)S(1)} %get-tuple-element.28), channel_id=1, source_target_pairs={{0,1},{1,2},{2,3},{4,5},{5,6},{6,7},{8,9},{9,10},{10,11},{12,13},{... | collective-permute-start | bytes 1572872 | tf_op jit(solution)/shard_map/ppermute | solution.py:42
  69.9 17.0 %collective-permute-start.5 = (bf16[4,2,2,128,128]{4,3,2,1,0:T(8,128)(2,1)S(1)}, bf16[4,2,2,128,128]{4,3,2,1,0:T(8,128)(2,1)S(1)}, u32[]{:S(2)}, u32[]{:S(2)}) collective-permute-start(bf16[4,2,2,128,128]{4,3,2,1,0:T(8,128)(2,1)S(1)} %get-tuple-element.29), channel_id=1, source_target_pairs={{1,0},{2,1},{3,2},{5,4},{6,5},{7,6},{9,8},{10,9},{11,10},{13,12},{... | collective-permute-start | bytes 1572872 | tf_op jit(solution)/shard_map/ppermute | solution.py:42
  71.2 4.0 %copy-start = (bf16[1280,4096]{1,0:T(8,128)(2,1)S(1)}, bf16[1280,4096]{1,0:T(8,128)(2,1)}, u32[]{:S(2)}) copy-start(bf16[1280,4096]{1,0:T(8,128)(2,1)} %get-tuple-element.33.right_all) | copy-start | bytes 31457284
  87.6 24.7 %collective-permute-start.13 = (bf16[7,2,2,128,128]{4,3,2,1,0:T(8,128)(2,1)S(1)}, bf16[7,2,2,128,128]{4,3,2,1,0:T(8,128)(2,1)}, u32[]{:S(2)}, u32[]{:S(2)}) collective-permute-start(bf16[7,2,2,128,128]{4,3,2,1,0:T(8,128)(2,1)S(1)} %get-tuple-element.37.refs_1_), channel_id=1, source_target_pairs={{0,1},{1,2},{2,3},{4,5},{5,6},{6,7},{8,9},{9,10},{10,11},{12,13},{... | collective-permute-start | bytes 2752520 | tf_op jit(solution)/shard_map/ppermute | solution.py:42
  92.5 25.2 %collective-permute-start.14 = (bf16[7,2,2,128,128]{4,3,2,1,0:T(8,128)(2,1)S(1)}, bf16[7,2,2,128,128]{4,3,2,1,0:T(8,128)(2,1)}, u32[]{:S(2)}, u32[]{:S(2)}) collective-permute-start(bf16[7,2,2,128,128]{4,3,2,1,0:T(8,128)(2,1)S(1)} %get-tuple-element.37.refs_1_), channel_id=1, source_target_pairs={{1,0},{2,1},{3,2},{5,4},{6,5},{7,6},{9,8},{10,9},{11,10},{13,12},{... | collective-permute-start | bytes 2752520 | tf_op jit(solution)/shard_map/ppermute | solution.py:42
  93.8 63.2 %collective-permute-start.10 = (bf16[6,2,2,128,128]{4,3,2,1,0:T(8,128)(2,1)S(1)}, bf16[6,2,2,128,128]{4,3,2,1,0:T(8,128)(2,1)S(1)}, u32[]{:S(2)}, u32[]{:S(2)}) collective-permute-start(bf16[6,2,2,128,128]{4,3,2,1,0:T(8,128)(2,1)S(1)} %get-tuple-element.36.refs_0_), channel_id=1, source_target_pairs={{1,0},{2,1},{3,2},{5,4},{6,5},{7,6},{9,8},{10,9},{11,10},{13,12},{... | collective-permute-start | bytes 2359304 | tf_op jit(solution)/shard_map/ppermute | solution.py:42
  95.1 63.2 %collective-permute-start.8 = (bf16[6,2,2,128,128]{4,3,2,1,0:T(8,128)(2,1)S(1)}, bf16[6,2,2,128,128]{4,3,2,1,0:T(8,128)(2,1)}, u32[]{:S(2)}, u32[]{:S(2)}) collective-permute-start(bf16[6,2,2,128,128]{4,3,2,1,0:T(8,128)(2,1)S(1)} %get-tuple-element.36.refs_0_), channel_id=1, source_target_pairs={{0,1},{1,2},{2,3},{4,5},{5,6},{6,7},{8,9},{9,10},{10,11},{12,13},{... | collective-permute-start | bytes 2359304 | tf_op jit(solution)/shard_map/ppermute | solution.py:42
  102.5 64.1 %collective-permute-start.12 = (bf16[8,2,2,128,128]{4,3,2,1,0:T(8,128)(2,1)}, bf16[8,2,2,128,128]{4,3,2,1,0:T(8,128)(2,1)S(1)}, u32[]{:S(2)}, u32[]{:S(2)}) collective-permute-start(bf16[8,2,2,128,128]{4,3,2,1,0:T(8,128)(2,1)} %fusion), channel_id=1, source_target_pairs={{0,3},{3,0},{4,7},{7,4},{8,11},{11,8},{12,15},{15,12},{16,19},{19,... | collective-permute-start | bytes 3145736 | tf_op jit(solution)/shard_map/ppermute | solution.py:456
  117.8 53.7 %collective-permute-start.15 = (bf16[7,2,2,128,128]{4,3,2,1,0:T(8,128)(2,1)}, bf16[7,2,2,128,128]{4,3,2,1,0:T(8,128)(2,1)S(1)}, u32[]{:S(2)}, u32[]{:S(2)}) collective-permute-start(bf16[7,2,2,128,128]{4,3,2,1,0:T(8,128)(2,1)} %collective-permute-done.13.refs_2_), channel_id=1, source_target_pairs={{0,1},{1,2},{2,3},{4,5},{5,6},{6,7},{8,9},{9,10},{10,11},{12,13},{... | collective-permute-start | bytes 2752520 | tf_op jit(solution)/shard_map/ppermute | solution.py:42
  119.7 57.0 %collective-permute-start.16 = (bf16[7,2,2,128,128]{4,3,2,1,0:T(8,128)(2,1)}, bf16[7,2,2,128,128]{4,3,2,1,0:T(8,128)(2,1)}, u32[]{:S(2)}, u32[]{:S(2)}) collective-permute-start(bf16[7,2,2,128,128]{4,3,2,1,0:T(8,128)(2,1)} %collective-permute-done.14.refs_3_), channel_id=1, source_target_pairs={{1,0},{2,1},{3,2},{5,4},{6,5},{7,6},{9,8},{10,9},{11,10},{13,12},{... | collective-permute-start | bytes 2752520 | tf_op jit(solution)/shard_map/ppermute | solution.py:42
  157.0 35.3 %collective-permute-start.11 = (bf16[6,2,2,128,128]{4,3,2,1,0:T(8,128)(2,1)S(1)}, bf16[6,2,2,128,128]{4,3,2,1,0:T(8,128)(2,1)}, u32[]{:S(2)}, u32[]{:S(2)}) collective-permute-start(bf16[6,2,2,128,128]{4,3,2,1,0:T(8,128)(2,1)S(1)} %collective-permute-done.10.refs_1_), channel_id=1, source_target_pairs={{1,0},{2,1},{3,2},{5,4},{6,5},{7,6},{9,8},{10,9},{11,10},{13,12},{... | collective-permute-start | bytes 2359304 | tf_op jit(solution)/shard_map/ppermute | solution.py:42
  158.3 34.0 %collective-permute-start.9 = (bf16[6,2,2,128,128]{4,3,2,1,0:T(8,128)(2,1)}, bf16[6,2,2,128,128]{4,3,2,1,0:T(8,128)(2,1)S(1)}, u32[]{:S(2)}, u32[]{:S(2)}) collective-permute-start(bf16[6,2,2,128,128]{4,3,2,1,0:T(8,128)(2,1)} %collective-permute-done.8.refs_0_), channel_id=1, source_target_pairs={{0,1},{1,2},{2,3},{4,5},{5,6},{6,7},{8,9},{9,10},{10,11},{12,13},{... | collective-permute-start | bytes 2359304 | tf_op jit(solution)/shard_map/ppermute | solution.py:42

commit v6 on v5

--- a/solution.py
+++ b/solution.py
@@ -10,6 +10,7 @@
 CROSS_SHIFTS = ((0, -1), (0, 1), (-1, 0), (1, 0), (0, 0))
 OWN = 4
 DOWN, UP = CROSS_SHIFTS[:2]
+HALO_ORDER = (2, 0, 1, 3)
 WINDOW_SHIFTS = (
     (-2, 0),
     (-1, -1),
@@ -195,7 +196,7 @@
 
     tent_copies = [
         pltpu.make_async_copy(source, tent.at[pl.ds(d * rows, rows)], sems.at[chunks + d])
-        for d, source in enumerate(tents)
+        for d, source in zip(HALO_ORDER, tents)
     ]
     dinv_copy = pltpu.make_async_copy(dinv_hbm, dinv, sems.at[chunks + 4])
     own_part = (pl.ds(outer * tile, members * tile), slice(None))
@@ -490,9 +491,9 @@
     inverse = dinv.reshape(rows, tile, tile)
     tent = jnp.swapaxes(ptent.reshape(rows, tile, tile), 1, 2)
     tents = (
+        shifted(tent, "sx", 1),
         shifted(tent, "sy", 1),
         shifted(tent, "sy", -1),
-        shifted(tent, "sx", 1),
         shifted(tent, "sx", -1),
     )
     own_right, own_left, *lists = own_slots(

time: 195 us -> 194 us (level)
  starting transfers between devices: 48.2 us -> 42.7 us
  waiting for transfers between devices: 80.2 us -> 83 us
    ppermute x16, starting transfers between devices: 46.3 us -> 40.8 us  [shifted(): return lax.ppermute(x, axis, pairs)]
    ppermute x16, waiting for transfers between devices: 80.2 us -> 83 us  [shifted(): return lax.ppermute(x, axis, pairs)]
  transfers between devices with their start and end apart: 17 -> 17, of which waited for: 9 -> 10; matrix products, arithmetic and copies ran while one was open for 1% -> 1% of each run, Pallas kernels for 14% -> 14%
where the time goes in v6:
time: 194 us; the launch traced here: 192 us
  waiting for transfers between devices  83 us (43%)
  Pallas kernels  54.7 us (28%)
  starting transfers between devices  42.7 us (22%)
  local copies, waits for them, and re-layouts  9.77 us (5%)
    ppermute x16, waiting for transfers between devices, shifted(): return lax.ppermute(x, axis, pairs)  83 us
    ppermute x16, starting transfers between devices, shifted(): return lax.ppermute(x, axis, pairs)  40.8 us
    pallas_call x1, Pallas kernels, partial_blocks(): pl.pallas_call(functools.partial(partial_kernel, members, taps), grid_spe...  24.5 us
    pallas_call x1, Pallas kernels, own_slots(): pl.pallas_call(functools.partial(own_kernel, count_y, rows, members, taps...  14.2 us
    pallas_call x4, Pallas kernels, placed(): pl.pallas_call(functools.partial(place_kernel, tuple((p[1:3] for p in pie...  10.8 us
    unnamed x12, local copies, waits for them, and re-layouts  9.67 us
    pallas_call x1, Pallas kernels, own_rows(): pl.pallas_call(functools.partial(own_rows_kernel, members), grid=(1,), in...  4.56 us
  transfers between devices with their start and end apart: 17, of which 10 were waited for; matrix products, arithmetic and copies ran while one was open for 1% of the time, Pallas kernels for 14%

profile of v6, /device:TPU:0, one launch (start us, length us, event | category | flops | bytes accessed | tf_op | source)
XLA Modules:
  0.0 192.2 jit_solution(10619497516295176090)
XLA Ops:
  0.0 0.0 copy-start.2
  0.0 1.7 copy.11
  1.7 2.4 %collective-permute-start = (bf16[32,128,128]{2,1,0:T(8,128)(2,1)S(1)}, bf16[32,128,128]{2,1,0:T(8,128)(2,1)S(1)}, u32[]{:S(2)}, u32[]{:S(2)}) collective-permute-start(bf16[32,128,128]{2,1,0:T(8,128)(2,1)S(1)} %bitcast.22), channel_id=1, source_target_pairs={{0,4},{4,8},{8,12},{12,16},{16,20},{20,24},{24,28},{1,5},{5,9},{9,... | collective-permute-start | bytes 3145736 | tf_op jit(solution)/shard_map/ppermute | solution.py:43
  4.1 5.3 %collective-permute-start.1 = (bf16[32,128,128]{2,1,0:T(8,128)(2,1)S(1)}, bf16[32,128,128]{2,1,0:T(8,128)(2,1)}, u32[]{:S(2)}, u32[]{:S(2)}) collective-permute-start(bf16[32,128,128]{2,1,0:T(8,128)(2,1)S(1)} %bitcast.23), channel_id=1, source_target_pairs={{0,1},{1,2},{2,3},{4,5},{5,6},{6,7},{8,9},{9,10},{10,11},{12,13},{... | collective-permute-start | bytes 3145736 | tf_op jit(solution)/shard_map/ppermute | solution.py:43
  9.4 1.3 collective-permute-start.2
  10.7 1.3 collective-permute-start.3
  12.0 0.8 copy.10
  12.8 0.1 reshape.12.columns
  12.9 0.1 pad_add_fusion.2.place
  13.0 0.0 copy-start.1
  13.0 1.2 copy-done.1
  14.2 0.0 copy-start.3
  14.2 0.7 copy-done.3
  14.9 14.2 %own_slots.1 = (bf16[256,4096]{1,0:T(8,128)(2,1)S(1)}, bf16[256,4096]{1,0:T(8,128)(2,1)S(1)}, s32[224]{0:T(256)S(1)}, s32[224]{0:T(256)S(1)}, s32[224]{0:T(256)S(1)}, /*index=5*/s32[8]{0:T(128)S(1)}) custom-call(s32[224]{0:T(256)S(1)} %reshape.12.columns, s32[1024]{0:T(1024)S(1)} %copy-done.3, s32[2]{0:T(128)S(1)} %pad_add_fusion.2.place, ...), custom_call_target="tpu_custom_call" | custom-call | flops 1207959552 | bytes 13631488 | tf_op jit(solution)/shard_map/own_slots/pallas_call | solution.py:105
  29.1 0.0 copy-start.4
  29.1 1.3 copy-done.4
  30.4 0.0 collective-permute-done.refs_2_
  30.4 0.9 collective-permute-done.1.refs_3_
  31.3 5.8 %collective-permute-done.2.refs_4_ = bf16[32,128,128]{2,1,0:T(8,128)(2,1)} collective-permute-done((bf16[32,128,128]{2,1,0:T(8,128)(2,1)S(1)}, bf16[32,128,128]{2,1,0:T(8,128)(2,1)}, u32[]{:S(2)}, u32[]{:S(2)}) %collective-permute-start.2) | collective-permute-done | bytes 1048608 | tf_op jit(solution)/shard_map/ppermute | solution.py:43
  37.1 0.0 collective-permute-done.3.refs_5_
  37.1 0.0 copy-done.2
  37.1 24.5 %partial_blocks.1 = (bf16[4,2,2,128,128]{4,3,2,1,0:T(8,128)(2,1)S(1)}, bf16[4,2,2,128,128]{4,3,2,1,0:T(8,128)(2,1)S(1)}, bf16[5,2,2,128,128]{4,3,2,1,0:T(8,128)(...) custom-call(s32[224]{0:T(256)S(1)} %get-tuple-element.23.tiles, ...), custom_call_target="tpu_custom_call" | custom-call | flops 11811160064 | bytes 28311552 | tf_op jit(solution)/shard_map/partial_blocks/pallas_call | solution.py:268
  61.6 3.5 %collective-permute-start.6 = (bf16[5,2,2,128,128]{4,3,2,1,0:T(8,128)(2,1)S(1)}, bf16[5,2,2,128,128]{4,3,2,1,0:T(8,128)(2,1)S(1)}, u32[]{:S(2)}, u32[]{:S(2)}) collective-permute-start(bf16[5,2,2,128,128]{4,3,2,1,0:T(8,128)(2,1)S(1)} %get-tuple-element.30), channel_id=1, source_target_pairs={{0,4},{4,8},{8,12},{12,16},{16,20},{20,24},{24,28},{1,5},{5,9},{9,... | collective-permute-start | bytes 1966088 | tf_op jit(solution)/shard_map/ppermute | solution.py:43
  65.1 1.3 collective-permute-start.7
  66.4 2.2 %collective-permute-start.4 = (bf16[4,2,2,128,128]{4,3,2,1,0:T(8,128)(2,1)S(1)}, bf16[4,2,2,128,128]{4,3,2,1,0:T(8,128)(2,1)S(1)}, u32[]{:S(2)}, u32[]{:S(2)}) collective-permute-start(bf16[4,2,2,128,128]{4,3,2,1,0:T(8,128)(2,1)S(1)} %get-tuple-element.28), channel_id=1, source_target_pairs={{0,1},{1,2},{2,3},{4,5},{5,6},{6,7},{8,9},{9,10},{10,11},{12,13},{... | collective-permute-start | bytes 1572872 | tf_op jit(solution)/shard_map/ppermute | solution.py:43
  68.6 1.3 collective-permute-start.5
  69.9 0.0 copy-start
  69.9 4.0 %copy-done = bf16[1280,4096]{1,0:T(8,128)(2,1)S(1)} copy-done((bf16[1280,4096]{1,0:T(8,128)(2,1)S(1)}, bf16[1280,4096]{1,0:T(8,128)(2,1)}, u32[]{:S(2)}) %copy-start) | copy-done | bytes 10485784
  73.9 4.6 %own_rows.1.refs_4_ = f32[5,2,2,128,128]{4,3,2,1,0:T(8,128)S(1)} custom-call(bf16[256,4096]{1,0:T(8,128)(2,1)S(1)} %get-tuple-element.32.left_own, bf16[1280,4096]{1,0:T(8,128)(2,1)S(1)} %copy-done), custom_call_target="tpu_custom_call" | custom-call | flops 2684354560 | bytes 12582912 | tf_op jit(solution)/shard_map/own_rows/pallas_call | solution.py:315
  78.5 0.2 collective-permute-done.4.refs_0_
  78.6 4.7 %collective-permute-done.5.refs_1_ = bf16[4,2,2,128,128]{4,3,2,1,0:T(8,128)(2,1)S(1)} collective-permute-done((bf16[4,2,2,128,128]{4,3,2,1,0:T(8,128)(2,1)S(1)}, bf16[4,2,2,128,128]{4,3,2,1,0:T(8,128)(2,1)S(1)}, u32[]{:S(2)}, u32[]{:S(2)}) %collective-permute-start.5) | collective-permute-done | bytes 524320 | tf_op jit(solution)/shard_map/ppermute | solution.py:43
  83.3 0.0 collective-permute-done.6.refs_2_
  83.4 0.0 collective-permute-done.7.refs_3_
  83.4 0.7 finished_window.1
  84.1 5.0 %collective-permute-start.13 = (bf16[7,2,2,128,128]{4,3,2,1,0:T(8,128)(2,1)S(1)}, bf16[7,2,2,128,128]{4,3,2,1,0:T(8,128)(2,1)}, u32[]{:S(2)}, u32[]{:S(2)}) collective-permute-start(bf16[7,2,2,128,128]{4,3,2,1,0:T(8,128)(2,1)S(1)} %get-tuple-element.37.refs_1_), channel_id=1, source_target_pairs={{0,1},{1,2},{2,3},{4,5},{5,6},{6,7},{8,9},{9,10},{10,11},{12,13},{... | collective-permute-start | bytes 2752520 | tf_op jit(solution)/shard_map/ppermute | solution.py:43
  89.1 1.3 collective-permute-start.14
  90.3 1.3 collective-permute-start.10
  91.6 6.1 %collective-permute-start.8 = (bf16[6,2,2,128,128]{4,3,2,1,0:T(8,128)(2,1)S(1)}, bf16[6,2,2,128,128]{4,3,2,1,0:T(8,128)(2,1)}, u32[]{:S(2)}, u32[]{:S(2)}) collective-permute-start(bf16[6,2,2,128,128]{4,3,2,1,0:T(8,128)(2,1)S(1)} %get-tuple-element.36.refs_0_), channel_id=1, source_target_pairs={{0,1},{1,2},{2,3},{4,5},{5,6},{6,7},{8,9},{9,10},{10,11},{12,13},{... | collective-permute-start | bytes 2359304 | tf_op jit(solution)/shard_map/ppermute | solution.py:43
  97.7 1.3 fusion
  99.0 1.9 collective-permute-start.12
  101.0 0.1 pad_add_fusion.5.row
  101.0 2.0 %placed.4.refs_4_ = bf16[4,2,13,2,128,128]{5,4,3,2,1,0:T(8,128)(2,1)} custom-call(s32[2]{0:T(128)S(1)} %pad_add_fusion.5.row, s32[2]{0:T(128)S(1)} %broadcast_1_valid.2.valid, bf16[6,2,2,128,128]{4,3,2,1,0:T(8,128)(2,1)S(1)} %get-tuple-element.36.refs_0_, bf16[7,2,2,128,128]{4,3,2,1,0:T(8,128)(2,1)S(1)} %get-tuple-element.37.refs_1_), custom_call_target="tpu_custom_call" | custom-call | bytes 5111808 | tf_op jit(solution)/shard_map/placed/pallas_call | solution.py:431
  103.0 5.4 %collective-permute-done.13.refs_2_ = bf16[7,2,2,128,128]{4,3,2,1,0:T(8,128)(2,1)} collective-permute-done((bf16[7,2,2,128,128]{4,3,2,1,0:T(8,128)(2,1)S(1)}, bf16[7,2,2,128,128]{4,3,2,1,0:T(8,128)(2,1)}, u32[]{:S(2)}, u32[]{:S(2)}) %collective-permute-start.13) | collective-permute-done | bytes 917536 | tf_op jit(solution)/shard_map/ppermute | solution.py:43
  108.4 5.6 %collective-permute-done.14.refs_3_ = bf16[7,2,2,128,128]{4,3,2,1,0:T(8,128)(2,1)} collective-permute-done((bf16[7,2,2,128,128]{4,3,2,1,0:T(8,128)(2,1)S(1)}, bf16[7,2,2,128,128]{4,3,2,1,0:T(8,128)(2,1)}, u32[]{:S(2)}, u32[]{:S(2)}) %collective-permute-start.14) | collective-permute-done | bytes 917536 | tf_op jit(solution)/shard_map/ppermute | solution.py:43
  114.1 1.4 collective-permute-start.15
  115.5 1.3 collective-permute-start.16
  116.8 36.5 %collective-permute-done.10.refs_1_ = bf16[6,2,2,128,128]{4,3,2,1,0:T(8,128)(2,1)S(1)} collective-permute-done((bf16[6,2,2,128,128]{4,3,2,1,0:T(8,128)(2,1)S(1)}, bf16[6,2,2,128,128]{4,3,2,1,0:T(8,128)(2,1)S(1)}, u32[]{:S(2)}, u32[]{:S(2)}) %collective-permute-start.10) | collective-permute-done | bytes 786464 | tf_op jit(solution)/shard_map/ppermute | solution.py:43
  153.3 1.3 collective-permute-start.11
  154.6 0.0 collective-permute-done.8.refs_0_
  154.6 4.6 %collective-permute-start.9 = (bf16[6,2,2,128,128]{4,3,2,1,0:T(8,128)(2,1)}, bf16[6,2,2,128,128]{4,3,2,1,0:T(8,128)(2,1)S(1)}, u32[]{:S(2)}, u32[]{:S(2)}) collective-permute-start(bf16[6,2,2,128,128]{4,3,2,1,0:T(8,128)(2,1)} %collective-permute-done.8.refs_0_), channel_id=1, source_target_pairs={{0,1},{1,2},{2,3},{4,5},{5,6},{6,7},{8,9},{9,10},{10,11},{12,13},{... | collective-permute-start | bytes 2359304 | tf_op jit(solution)/shard_map/ppermute | solution.py:43
  159.2 0.1 pad_add_fusion.6.row
  159.3 0.1 add_convert_fusion.valid
  159.4 0.1 pad_add_fusion
  159.5 0.1 pad_add_fusion.3
  159.5 3.4 %placed.5.refs_4_ = bf16[4,2,13,2,128,128]{5,4,3,2,1,0:T(8,128)(2,1)} custom-call(s32[4]{0:T(128)S(1)} %pad_add_fusion.6.row, s32[4]{0:T(128)S(1)} %add_convert_fusion.valid, bf16[6,2,2,128,128]{4,3,2,1,0:T(8,128)(2,1)} %collective-permute-done.8.refs_0_, ...), custom_call_target="tpu_custom_call", output_to_operand_aliasing={{}: (6, {})} | custom-call | bytes 5111808 | tf_op jit(solution)/shard_map/placed/pallas_call | solution.py:431
  162.9 0.0 collective-permute-done.12.refs_0_.refs_1_
  162.9 4.6 %collective-permute-done.15.refs_2_ = bf16[7,2,2,128,128]{4,3,2,1,0:T(8,128)(2,1)S(1)} collective-permute-done((bf16[7,2,2,128,128]{4,3,2,1,0:T(8,128)(2,1)}, bf16[7,2,2,128,128]{4,3,2,1,0:T(8,128)(2,1)S(1)}, u32[]{:S(2)}, u32[]{:S(2)}) %collective-permute-start.15) | collective-permute-done | bytes 917536 | tf_op jit(solution)/shard_map/ppermute | solution.py:43
  167.6 5.5 %collective-permute-done.16.refs_3_ = bf16[7,2,2,128,128]{4,3,2,1,0:T(8,128)(2,1)} collective-permute-done((bf16[7,2,2,128,128]{4,3,2,1,0:T(8,128)(2,1)}, bf16[7,2,2,128,128]{4,3,2,1,0:T(8,128)(2,1)}, u32[]{:S(2)}, u32[]{:S(2)}) %collective-permute-start.16) | collective-permute-done | bytes 917536 | tf_op jit(solution)/shard_map/ppermute | solution.py:43
  173.0 3.1 %placed.6.refs_2_ = bf16[4,2,13,2,128,128]{5,4,3,2,1,0:T(8,128)(2,1)} custom-call(s32[4]{0:T(128)S(1)} %get-tuple-element.41.row, s32[4]{0:T(128)S(1)} %get-tuple-element.42.valid, bf16[8,2,2,128,128]{4,3,2,1,0:T(8,128)(2,1)S(1)} %collective-permute-done.12.refs_0_.refs_1_, ...), custom_call_target="tpu_custom_call", output_to_operand_aliasing={{}: (6, {})} | custom-call | bytes 5111808 | tf_op jit(solution)/shard_map/placed/pallas_call | solution.py:431
  176.2 13.7 %collective-permute-done.11.refs_1_ = bf16[6,2,2,128,128]{4,3,2,1,0:T(8,128)(2,1)} collective-permute-done((bf16[6,2,2,128,128]{4,3,2,1,0:T(8,128)(2,1)S(1)}, bf16[6,2,2,128,128]{4,3,2,1,0:T(8,128)(2,1)}, u32[]{:S(2)}, u32[]{:S(2)}) %collective-permute-start.11) | collective-permute-done | bytes 786464 | tf_op jit(solution)/shard_map/ppermute | solution.py:43
  189.9 0.0 collective-permute-done.9.refs_0_
  189.9 2.3 %placed.7 = bf16[4,2,13,2,128,128]{5,4,3,2,1,0:T(8,128)(2,1)} custom-call(s32[2]{0:T(128)S(1)} %get-tuple-element.43.row, s32[2]{0:T(128)S(1)} %get-tuple-element.44.valid, bf16[6,2,2,128,128]{4,3,2,1,0:T(8,128)(2,1)S(1)} %collective-permute-done.9.refs_0_, ...), custom_call_target="tpu_custom_call", output_to_operand_aliasing={{}: (4, {})} | custom-call | bytes 5111808 | tf_op jit(solution)/shard_map/placed/pallas_call | solution.py:431
  (1 shorter events, 0.0 us)
Async XLA Ops:
  0.0 37.1 %copy-start.2 = (bf16[1,1,32,128,128]{4,3,2,1,0:T(8,128)(2,1)S(1)}, bf16[1,1,32,128,128]{4,3,2,1,0:T(8,128)(2,1)}, u32[]{:S(2)}) copy-start(bf16[1,1,32,128,128]{4,3,2,1,0:T(8,128)(2,1)} %param.8) | copy-start | bytes 3145732
  1.7 28.7 %collective-permute-start = (bf16[32,128,128]{2,1,0:T(8,128)(2,1)S(1)}, bf16[32,128,128]{2,1,0:T(8,128)(2,1)S(1)}, u32[]{:S(2)}, u32[]{:S(2)}) collective-permute-start(bf16[32,128,128]{2,1,0:T(8,128)(2,1)S(1)} %bitcast.22), channel_id=1, source_target_pairs={{0,4},{4,8},{8,12},{12,16},{16,20},{20,24},{24,28},{1,5},{5,9},{9,... | collective-permute-start | bytes 3145736 | tf_op jit(solution)/shard_map/ppermute | solution.py:43
  4.1 27.2 %collective-permute-start.1 = (bf16[32,128,128]{2,1,0:T(8,128)(2,1)S(1)}, bf16[32,128,128]{2,1,0:T(8,128)(2,1)}, u32[]{:S(2)}, u32[]{:S(2)}) collective-permute-start(bf16[32,128,128]{2,1,0:T(8,128)(2,1)S(1)} %bitcast.23), channel_id=1, source_target_pairs={{0,1},{1,2},{2,3},{4,5},{5,6},{6,7},{8,9},{9,10},{10,11},{12,13},{... | collective-permute-start | bytes 3145736 | tf_op jit(solution)/shard_map/ppermute | solution.py:43
  9.4 27.6 %collective-permute-start.2 = (bf16[32,128,128]{2,1,0:T(8,128)(2,1)S(1)}, bf16[32,128,128]{2,1,0:T(8,128)(2,1)}, u32[]{:S(2)}, u32[]{:S(2)}) collective-permute-start(bf16[32,128,128]{2,1,0:T(8,128)(2,1)S(1)} %bitcast.24), channel_id=1, source_target_pairs={{1,0},{2,1},{3,2},{5,4},{6,5},{7,6},{9,8},{10,9},{11,10},{13,12},{... | collective-permute-start | bytes 3145736 | tf_op jit(solution)/shard_map/ppermute | solution.py:43
  10.7 26.4 %collective-permute-start.3 = (bf16[32,128,128]{2,1,0:T(8,128)(2,1)S(1)}, bf16[32,128,128]{2,1,0:T(8,128)(2,1)}, u32[]{:S(2)}, u32[]{:S(2)}) collective-permute-start(bf16[32,128,128]{2,1,0:T(8,128)(2,1)S(1)} %bitcast.25), channel_id=1, source_target_pairs={{4,0},{8,4},{12,8},{16,12},{20,16},{24,20},{28,24},{5,1},{9,5},{13... | collective-permute-start | bytes 3145736 | tf_op jit(solution)/shard_map/ppermute | solution.py:43
  13.0 1.2 copy-start.1
  14.2 0.7 copy-start.3
  29.1 1.3 copy-start.4
  61.6 21.8 %collective-permute-start.6 = (bf16[5,2,2,128,128]{4,3,2,1,0:T(8,128)(2,1)S(1)}, bf16[5,2,2,128,128]{4,3,2,1,0:T(8,128)(2,1)S(1)}, u32[]{:S(2)}, u32[]{:S(2)}) collective-permute-start(bf16[5,2,2,128,128]{4,3,2,1,0:T(8,128)(2,1)S(1)} %get-tuple-element.30), channel_id=1, source_target_pairs={{0,4},{4,8},{8,12},{12,16},{16,20},{20,24},{24,28},{1,5},{5,9},{9,... | collective-permute-start | bytes 1966088 | tf_op jit(solution)/shard_map/ppermute | solution.py:43
  65.1 18.3 %collective-permute-start.7 = (bf16[5,2,2,128,128]{4,3,2,1,0:T(8,128)(2,1)S(1)}, bf16[5,2,2,128,128]{4,3,2,1,0:T(8,128)(2,1)S(1)}, u32[]{:S(2)}, u32[]{:S(2)}) collective-permute-start(bf16[5,2,2,128,128]{4,3,2,1,0:T(8,128)(2,1)S(1)} %get-tuple-element.31), channel_id=1, source_target_pairs={{4,0},{8,4},{12,8},{16,12},{20,16},{24,20},{28,24},{5,1},{9,5},{13... | collective-permute-start | bytes 1966088 | tf_op jit(solution)/shard_map/ppermute | solution.py:43
  66.4 12.3 %collective-permute-start.4 = (bf16[4,2,2,128,128]{4,3,2,1,0:T(8,128)(2,1)S(1)}, bf16[4,2,2,128,128]{4,3,2,1,0:T(8,128)(2,1)S(1)}, u32[]{:S(2)}, u32[]{:S(2)}) collective-permute-start(bf16[4,2,2,128,128]{4,3,2,1,0:T(8,128)(2,1)S(1)} %get-tuple-element.28), channel_id=1, source_target_pairs={{0,1},{1,2},{2,3},{4,5},{5,6},{6,7},{8,9},{9,10},{10,11},{12,13},{... | collective-permute-start | bytes 1572872 | tf_op jit(solution)/shard_map/ppermute | solution.py:43
  68.6 14.8 %collective-permute-start.5 = (bf16[4,2,2,128,128]{4,3,2,1,0:T(8,128)(2,1)S(1)}, bf16[4,2,2,128,128]{4,3,2,1,0:T(8,128)(2,1)S(1)}, u32[]{:S(2)}, u32[]{:S(2)}) collective-permute-start(bf16[4,2,2,128,128]{4,3,2,1,0:T(8,128)(2,1)S(1)} %get-tuple-element.29), channel_id=1, source_target_pairs={{1,0},{2,1},{3,2},{5,4},{6,5},{7,6},{9,8},{10,9},{11,10},{13,12},{... | collective-permute-start | bytes 1572872 | tf_op jit(solution)/shard_map/ppermute | solution.py:43
  69.9 4.0 %copy-start = (bf16[1280,4096]{1,0:T(8,128)(2,1)S(1)}, bf16[1280,4096]{1,0:T(8,128)(2,1)}, u32[]{:S(2)}) copy-start(bf16[1280,4096]{1,0:T(8,128)(2,1)} %get-tuple-element.33.right_all) | copy-start | bytes 31457284
  84.1 24.4 %collective-permute-start.13 = (bf16[7,2,2,128,128]{4,3,2,1,0:T(8,128)(2,1)S(1)}, bf16[7,2,2,128,128]{4,3,2,1,0:T(8,128)(2,1)}, u32[]{:S(2)}, u32[]{:S(2)}) collective-permute-start(bf16[7,2,2,128,128]{4,3,2,1,0:T(8,128)(2,1)S(1)} %get-tuple-element.37.refs_1_), channel_id=1, source_target_pairs={{0,1},{1,2},{2,3},{4,5},{5,6},{6,7},{8,9},{9,10},{10,11},{12,13},{... | collective-permute-start | bytes 2752520 | tf_op jit(solution)/shard_map/ppermute | solution.py:43
  89.1 25.0 %collective-permute-start.14 = (bf16[7,2,2,128,128]{4,3,2,1,0:T(8,128)(2,1)S(1)}, bf16[7,2,2,128,128]{4,3,2,1,0:T(8,128)(2,1)}, u32[]{:S(2)}, u32[]{:S(2)}) collective-permute-start(bf16[7,2,2,128,128]{4,3,2,1,0:T(8,128)(2,1)S(1)} %get-tuple-element.37.refs_1_), channel_id=1, source_target_pairs={{1,0},{2,1},{3,2},{5,4},{6,5},{7,6},{9,8},{10,9},{11,10},{13,12},{... | collective-permute-start | bytes 2752520 | tf_op jit(solution)/shard_map/ppermute | solution.py:43
  90.3 62.9 %collective-permute-start.10 = (bf16[6,2,2,128,128]{4,3,2,1,0:T(8,128)(2,1)S(1)}, bf16[6,2,2,128,128]{4,3,2,1,0:T(8,128)(2,1)S(1)}, u32[]{:S(2)}, u32[]{:S(2)}) collective-permute-start(bf16[6,2,2,128,128]{4,3,2,1,0:T(8,128)(2,1)S(1)} %get-tuple-element.36.refs_0_), channel_id=1, source_target_pairs={{1,0},{2,1},{3,2},{5,4},{6,5},{7,6},{9,8},{10,9},{11,10},{13,12},{... | collective-permute-start | bytes 2359304 | tf_op jit(solution)/shard_map/ppermute | solution.py:43
  91.6 62.9 %collective-permute-start.8 = (bf16[6,2,2,128,128]{4,3,2,1,0:T(8,128)(2,1)S(1)}, bf16[6,2,2,128,128]{4,3,2,1,0:T(8,128)(2,1)}, u32[]{:S(2)}, u32[]{:S(2)}) collective-permute-start(bf16[6,2,2,128,128]{4,3,2,1,0:T(8,128)(2,1)S(1)} %get-tuple-element.36.refs_0_), channel_id=1, source_target_pairs={{0,1},{1,2},{2,3},{4,5},{5,6},{6,7},{8,9},{9,10},{10,11},{12,13},{... | collective-permute-start | bytes 2359304 | tf_op jit(solution)/shard_map/ppermute | solution.py:43
  99.0 63.9 %collective-permute-start.12 = (bf16[8,2,2,128,128]{4,3,2,1,0:T(8,128)(2,1)}, bf16[8,2,2,128,128]{4,3,2,1,0:T(8,128)(2,1)S(1)}, u32[]{:S(2)}, u32[]{:S(2)}) collective-permute-start(bf16[8,2,2,128,128]{4,3,2,1,0:T(8,128)(2,1)} %fusion), channel_id=1, source_target_pairs={{0,3},{3,0},{4,7},{7,4},{8,11},{11,8},{12,15},{15,12},{16,19},{19,... | collective-permute-start | bytes 3145736 | tf_op jit(solution)/shard_map/ppermute | solution.py:457
  114.1 53.5 %collective-permute-start.15 = (bf16[7,2,2,128,128]{4,3,2,1,0:T(8,128)(2,1)}, bf16[7,2,2,128,128]{4,3,2,1,0:T(8,128)(2,1)S(1)}, u32[]{:S(2)}, u32[]{:S(2)}) collective-permute-start(bf16[7,2,2,128,128]{4,3,2,1,0:T(8,128)(2,1)} %collective-permute-done.13.refs_2_), channel_id=1, source_target_pairs={{0,1},{1,2},{2,3},{4,5},{5,6},{6,7},{8,9},{9,10},{10,11},{12,13},{... | collective-permute-start | bytes 2752520 | tf_op jit(solution)/shard_map/ppermute | solution.py:43
  115.5 57.6 %collective-permute-start.16 = (bf16[7,2,2,128,128]{4,3,2,1,0:T(8,128)(2,1)}, bf16[7,2,2,128,128]{4,3,2,1,0:T(8,128)(2,1)}, u32[]{:S(2)}, u32[]{:S(2)}) collective-permute-start(bf16[7,2,2,128,128]{4,3,2,1,0:T(8,128)(2,1)} %collective-permute-done.14.refs_3_), channel_id=1, source_target_pairs={{1,0},{2,1},{3,2},{5,4},{6,5},{7,6},{9,8},{10,9},{11,10},{13,12},{... | collective-permute-start | bytes 2752520 | tf_op jit(solution)/shard_map/ppermute | solution.py:43
  153.3 36.6 %collective-permute-start.11 = (bf16[6,2,2,128,128]{4,3,2,1,0:T(8,128)(2,1)S(1)}, bf16[6,2,2,128,128]{4,3,2,1,0:T(8,128)(2,1)}, u32[]{:S(2)}, u32[]{:S(2)}) collective-permute-start(bf16[6,2,2,128,128]{4,3,2,1,0:T(8,128)(2,1)S(1)} %collective-permute-done.10.refs_1_), channel_id=1, source_target_pairs={{1,0},{2,1},{3,2},{5,4},{6,5},{7,6},{9,8},{10,9},{11,10},{13,12},{... | collective-permute-start | bytes 2359304 | tf_op jit(solution)/shard_map/ppermute | solution.py:43
  154.6 35.3 %collective-permute-start.9 = (bf16[6,2,2,128,128]{4,3,2,1,0:T(8,128)(2,1)}, bf16[6,2,2,128,128]{4,3,2,1,0:T(8,128)(2,1)S(1)}, u32[]{:S(2)}, u32[]{:S(2)}) collective-permute-start(bf16[6,2,2,128,128]{4,3,2,1,0:T(8,128)(2,1)} %collective-permute-done.8.refs_0_), channel_id=1, source_target_pairs={{0,1},{1,2},{2,3},{4,5},{5,6},{6,7},{8,9},{9,10},{10,11},{12,13},{... | collective-permute-start | bytes 2359304 | tf_op jit(solution)/shard_map/ppermute | solution.py:43

commit v7 on v6

--- a/solution.py
+++ b/solution.py
@@ -136,48 +136,18 @@
 
 
 def product(left, right, outs, lone, members, tile):
-    width = members * tile
-
-    def one(d2, carry):
-        value = lax.dot_general(
-            left[...],
-            right[lane_tiles(d2, width), :],
-            NT,
-            preferred_element_type=jnp.float32,
-        )
-
-        def write(out, at, d1):
+    value = lax.dot_general(left[...], right[...], NT, preferred_element_type=jnp.float32)
+    for d1, out in enumerate(outs):
+        for d2 in range(5):
+            target, at = out, d2
+            if d1 in lone:
+                direction, single = lone[d1]
+                target, at = (single, 0) if d2 == direction else (out, (d2 + 4 - direction) % 5)
             for m in range(members):
                 for m2 in range(members):
-                    row = (d1 * members + m) * tile
-                    block = value[row : row + tile, m2 * tile : (m2 + 1) * tile]
-                    out[at, m, m2] = block.astype(out.dtype)
-
-        for d1, out in enumerate(outs):
-            if d1 not in lone:
-                write(out, d2, d1)
-                continue
-            direction, single = lone[d1]
-
-            @pl.when(d2 == direction)
-            def _():
-                write(single, 0, d1)
-
-            @pl.when(d2 != direction)
-            def _():
-                write(out, (d2 + 4 - direction) % 5, d1)
-
-        return carry
-
-    lax.fori_loop(0, 5, one, 0)
-
-
-def smoothed_rows(left, right, first, count, dinv, g, tile):
-    lanes = lane_tiles(g, tile)
-    smooth = lax.dot_general(
-        right[first : first + count, lanes], dinv[g], NT, preferred_element_type=jnp.float32
-    )
-    left[:count, lanes] = (-smoothing * smooth).astype(jnp.bfloat16)
+                    row, column = (d1 * members + m) * tile, (d2 * members + m2) * tile
+                    block = value[row : row + tile, column : column + tile]
+                    target[at, m, m2] = block.astype(target.dtype)
 
 
 def partial_kernel(members, taps, tiles, sources, slots, ends, *refs):

time: 194 us -> 193 us (level)
  Pallas kernels: 54.7 us -> 52.1 us
where the time goes in v7:
time: 193 us; the launch traced here: 192 us
  waiting for transfers between devices  84.7 us (44%)
  Pallas kernels  52.1 us (27%)
  starting transfers between devices  43.1 us (22%)
  local copies, waits for them, and re-layouts  9.77 us (5%)
    ppermute x16, waiting for transfers between devices, shifted(): return lax.ppermute(x, axis, pairs)  84.7 us
    ppermute x16, starting transfers between devices, shifted(): return lax.ppermute(x, axis, pairs)  41.2 us
    pallas_call x1, Pallas kernels, partial_blocks(): pl.pallas_call(functools.partial(partial_kernel, members, taps), grid_spe...  22.7 us
    pallas_call x1, Pallas kernels, own_slots(): pl.pallas_call(functools.partial(own_kernel, count_y, rows, members, taps...  14.2 us
    pallas_call x4, Pallas kernels, placed(): pl.pallas_call(functools.partial(place_kernel, tuple((p[1:3] for p in pie...  10.8 us
    unnamed x12, local copies, waits for them, and re-layouts  9.67 us
  transfers between devices with their start and end apart: 17, of which 10 were waited for; matrix products, arithmetic and copies ran while one was open for 1% of the time, Pallas kernels for 14%

profile of v7, /device:TPU:0, one launch (start us, length us, event | category | flops | bytes accessed | tf_op | source)
XLA Modules:
  0.0 191.9 jit_solution(3588246124103498911)
XLA Ops:
  0.0 0.0 copy-start.2
  0.0 1.7 copy.11
  1.7 2.4 %collective-permute-start = (bf16[32,128,128]{2,1,0:T(8,128)(2,1)S(1)}, bf16[32,128,128]{2,1,0:T(8,128)(2,1)S(1)}, u32[]{:S(2)}, u32[]{:S(2)}) collective-permute-start(bf16[32,128,128]{2,1,0:T(8,128)(2,1)S(1)} %bitcast.22), channel_id=1, source_target_pairs={{0,4},{4,8},{8,12},{12,16},{16,20},{20,24},{24,28},{1,5},{5,9},{9,... | collective-permute-start | bytes 3145736 | tf_op jit(solution)/shard_map/ppermute | solution.py:43
  4.1 5.3 %collective-permute-start.1 = (bf16[32,128,128]{2,1,0:T(8,128)(2,1)S(1)}, bf16[32,128,128]{2,1,0:T(8,128)(2,1)}, u32[]{:S(2)}, u32[]{:S(2)}) collective-permute-start(bf16[32,128,128]{2,1,0:T(8,128)(2,1)S(1)} %bitcast.23), channel_id=1, source_target_pairs={{0,1},{1,2},{2,3},{4,5},{5,6},{6,7},{8,9},{9,10},{10,11},{12,13},{... | collective-permute-start | bytes 3145736 | tf_op jit(solution)/shard_map/ppermute | solution.py:43
  9.4 1.3 collective-permute-start.2
  10.7 1.3 collective-permute-start.3
  12.0 0.8 copy.10
  12.8 0.1 reshape.12.columns
  12.9 0.1 pad_add_fusion.2.place
  13.0 0.0 copy-start.1
  13.0 1.2 copy-done.1
  14.2 0.0 copy-start.3
  14.2 0.7 copy-done.3
  14.9 14.2 %own_slots.1 = (bf16[256,4096]{1,0:T(8,128)(2,1)S(1)}, bf16[256,4096]{1,0:T(8,128)(2,1)S(1)}, s32[224]{0:T(256)S(1)}, s32[224]{0:T(256)S(1)}, s32[224]{0:T(256)S(1)}, /*index=5*/s32[8]{0:T(128)S(1)}) custom-call(s32[224]{0:T(256)S(1)} %reshape.12.columns, s32[1024]{0:T(1024)S(1)} %copy-done.3, s32[2]{0:T(128)S(1)} %pad_add_fusion.2.place, ...), custom_call_target="tpu_custom_call" | custom-call | flops 1207959552 | bytes 13631488 | tf_op jit(solution)/shard_map/own_slots/pallas_call | solution.py:105
  29.1 0.0 copy-start.4
  29.1 1.3 copy-done.4
  30.4 0.0 collective-permute-done.refs_2_
  30.4 0.9 collective-permute-done.1.refs_3_
  31.3 5.8 %collective-permute-done.2.refs_4_ = bf16[32,128,128]{2,1,0:T(8,128)(2,1)} collective-permute-done((bf16[32,128,128]{2,1,0:T(8,128)(2,1)S(1)}, bf16[32,128,128]{2,1,0:T(8,128)(2,1)}, u32[]{:S(2)}, u32[]{:S(2)}) %collective-permute-start.2) | collective-permute-done | bytes 1048608 | tf_op jit(solution)/shard_map/ppermute | solution.py:43
  37.1 0.0 collective-permute-done.3.refs_5_
  37.1 0.0 copy-done.2
  37.1 22.7 %partial_blocks.1 = (bf16[4,2,2,128,128]{4,3,2,1,0:T(8,128)(2,1)S(1)}, bf16[4,2,2,128,128]{4,3,2,1,0:T(8,128)(2,1)S(1)}, bf16[5,2,2,128,128]{4,3,2,1,0:T(8,128)(...) custom-call(s32[224]{0:T(256)S(1)} %get-tuple-element.23.tiles, ...), custom_call_target="tpu_custom_call" | custom-call | flops 11811160064 | bytes 28311552 | tf_op jit(solution)/shard_map/partial_blocks/pallas_call | solution.py:238
  59.8 4.1 %collective-permute-start.6 = (bf16[5,2,2,128,128]{4,3,2,1,0:T(8,128)(2,1)S(1)}, bf16[5,2,2,128,128]{4,3,2,1,0:T(8,128)(2,1)S(1)}, u32[]{:S(2)}, u32[]{:S(2)}) collective-permute-start(bf16[5,2,2,128,128]{4,3,2,1,0:T(8,128)(2,1)S(1)} %get-tuple-element.30), channel_id=1, source_target_pairs={{0,4},{4,8},{8,12},{12,16},{16,20},{20,24},{24,28},{1,5},{5,9},{9,... | collective-permute-start | bytes 1966088 | tf_op jit(solution)/shard_map/ppermute | solution.py:43
  63.9 1.3 collective-permute-start.7
  65.2 3.2 %collective-permute-start.4 = (bf16[4,2,2,128,128]{4,3,2,1,0:T(8,128)(2,1)S(1)}, bf16[4,2,2,128,128]{4,3,2,1,0:T(8,128)(2,1)S(1)}, u32[]{:S(2)}, u32[]{:S(2)}) collective-permute-start(bf16[4,2,2,128,128]{4,3,2,1,0:T(8,128)(2,1)S(1)} %get-tuple-element.28), channel_id=1, source_target_pairs={{0,1},{1,2},{2,3},{4,5},{5,6},{6,7},{8,9},{9,10},{10,11},{12,13},{... | collective-permute-start | bytes 1572872 | tf_op jit(solution)/shard_map/ppermute | solution.py:43
  68.4 1.5 collective-permute-start.5
  69.9 0.0 copy-start
  69.9 4.0 %copy-done = bf16[1280,4096]{1,0:T(8,128)(2,1)S(1)} copy-done((bf16[1280,4096]{1,0:T(8,128)(2,1)S(1)}, bf16[1280,4096]{1,0:T(8,128)(2,1)}, u32[]{:S(2)}) %copy-start) | copy-done | bytes 10485784
  73.9 3.8 %own_rows.1.refs_4_ = f32[5,2,2,128,128]{4,3,2,1,0:T(8,128)S(1)} custom-call(bf16[256,4096]{1,0:T(8,128)(2,1)S(1)} %get-tuple-element.32.left_own, bf16[1280,4096]{1,0:T(8,128)(2,1)S(1)} %copy-done), custom_call_target="tpu_custom_call" | custom-call | flops 2684354560 | bytes 12582912 | tf_op jit(solution)/shard_map/own_rows/pallas_call | solution.py:285
  77.6 1.8 collective-permute-done.4.refs_0_
  79.5 4.7 %collective-permute-done.5.refs_1_ = bf16[4,2,2,128,128]{4,3,2,1,0:T(8,128)(2,1)S(1)} collective-permute-done((bf16[4,2,2,128,128]{4,3,2,1,0:T(8,128)(2,1)S(1)}, bf16[4,2,2,128,128]{4,3,2,1,0:T(8,128)(2,1)S(1)}, u32[]{:S(2)}, u32[]{:S(2)}) %collective-permute-start.5) | collective-permute-done | bytes 524320 | tf_op jit(solution)/shard_map/ppermute | solution.py:43
  84.2 0.0 collective-permute-done.6.refs_2_
  84.2 0.0 collective-permute-done.7.refs_3_
  84.2 0.7 finished_window.1
  84.9 3.6 %collective-permute-start.13 = (bf16[7,2,2,128,128]{4,3,2,1,0:T(8,128)(2,1)S(1)}, bf16[7,2,2,128,128]{4,3,2,1,0:T(8,128)(2,1)}, u32[]{:S(2)}, u32[]{:S(2)}) collective-permute-start(bf16[7,2,2,128,128]{4,3,2,1,0:T(8,128)(2,1)S(1)} %get-tuple-element.37.refs_1_), channel_id=1, source_target_pairs={{0,1},{1,2},{2,3},{4,5},{5,6},{6,7},{8,9},{9,10},{10,11},{12,13},{... | collective-permute-start | bytes 2752520 | tf_op jit(solution)/shard_map/ppermute | solution.py:43
  88.6 1.3 collective-permute-start.14
  89.9 1.3 collective-permute-start.10
  91.2 6.1 %collective-permute-start.8 = (bf16[6,2,2,128,128]{4,3,2,1,0:T(8,128)(2,1)S(1)}, bf16[6,2,2,128,128]{4,3,2,1,0:T(8,128)(2,1)}, u32[]{:S(2)}, u32[]{:S(2)}) collective-permute-start(bf16[6,2,2,128,128]{4,3,2,1,0:T(8,128)(2,1)S(1)} %get-tuple-element.36.refs_0_), channel_id=1, source_target_pairs={{0,1},{1,2},{2,3},{4,5},{5,6},{6,7},{8,9},{9,10},{10,11},{12,13},{... | collective-permute-start | bytes 2359304 | tf_op jit(solution)/shard_map/ppermute | solution.py:43
  97.2 1.3 fusion
  98.6 1.9 collective-permute-start.12
  100.5 0.1 pad_add_fusion.5.row
  100.6 2.0 %placed.4.refs_4_ = bf16[4,2,13,2,128,128]{5,4,3,2,1,0:T(8,128)(2,1)} custom-call(s32[2]{0:T(128)S(1)} %pad_add_fusion.5.row, s32[2]{0:T(128)S(1)} %broadcast_1_valid.2.valid, bf16[6,2,2,128,128]{4,3,2,1,0:T(8,128)(2,1)S(1)} %get-tuple-element.36.refs_0_, bf16[7,2,2,128,128]{4,3,2,1,0:T(8,128)(2,1)S(1)} %get-tuple-element.37.refs_1_), custom_call_target="tpu_custom_call" | custom-call | bytes 5111808 | tf_op jit(solution)/shard_map/placed/pallas_call | solution.py:401
  102.6 5.7 %collective-permute-done.13.refs_2_ = bf16[7,2,2,128,128]{4,3,2,1,0:T(8,128)(2,1)} collective-permute-done((bf16[7,2,2,128,128]{4,3,2,1,0:T(8,128)(2,1)S(1)}, bf16[7,2,2,128,128]{4,3,2,1,0:T(8,128)(2,1)}, u32[]{:S(2)}, u32[]{:S(2)}) %collective-permute-start.13) | collective-permute-done | bytes 917536 | tf_op jit(solution)/shard_map/ppermute | solution.py:43
  108.2 5.5 %collective-permute-done.14.refs_3_ = bf16[7,2,2,128,128]{4,3,2,1,0:T(8,128)(2,1)} collective-permute-done((bf16[7,2,2,128,128]{4,3,2,1,0:T(8,128)(2,1)S(1)}, bf16[7,2,2,128,128]{4,3,2,1,0:T(8,128)(2,1)}, u32[]{:S(2)}, u32[]{:S(2)}) %collective-permute-start.14) | collective-permute-done | bytes 917536 | tf_op jit(solution)/shard_map/ppermute | solution.py:43
  113.8 1.4 collective-permute-start.15
  115.2 1.3 collective-permute-start.16
  116.5 36.5 %collective-permute-done.10.refs_1_ = bf16[6,2,2,128,128]{4,3,2,1,0:T(8,128)(2,1)S(1)} collective-permute-done((bf16[6,2,2,128,128]{4,3,2,1,0:T(8,128)(2,1)S(1)}, bf16[6,2,2,128,128]{4,3,2,1,0:T(8,128)(2,1)S(1)}, u32[]{:S(2)}, u32[]{:S(2)}) %collective-permute-start.10) | collective-permute-done | bytes 786464 | tf_op jit(solution)/shard_map/ppermute | solution.py:43
  153.0 1.3 collective-permute-start.11
  154.3 0.0 collective-permute-done.8.refs_0_
  154.3 4.6 %collective-permute-start.9 = (bf16[6,2,2,128,128]{4,3,2,1,0:T(8,128)(2,1)}, bf16[6,2,2,128,128]{4,3,2,1,0:T(8,128)(2,1)S(1)}, u32[]{:S(2)}, u32[]{:S(2)}) collective-permute-start(bf16[6,2,2,128,128]{4,3,2,1,0:T(8,128)(2,1)} %collective-permute-done.8.refs_0_), channel_id=1, source_target_pairs={{0,1},{1,2},{2,3},{4,5},{5,6},{6,7},{8,9},{9,10},{10,11},{12,13},{... | collective-permute-start | bytes 2359304 | tf_op jit(solution)/shard_map/ppermute | solution.py:43
  159.0 0.1 pad_add_fusion.6.row
  159.0 0.1 add_convert_fusion.valid
  159.1 0.1 pad_add_fusion
  159.2 0.1 pad_add_fusion.3
  159.3 3.4 %placed.5.refs_4_ = bf16[4,2,13,2,128,128]{5,4,3,2,1,0:T(8,128)(2,1)} custom-call(s32[4]{0:T(128)S(1)} %pad_add_fusion.6.row, s32[4]{0:T(128)S(1)} %add_convert_fusion.valid, bf16[6,2,2,128,128]{4,3,2,1,0:T(8,128)(2,1)} %collective-permute-done.8.refs_0_, ...), custom_call_target="tpu_custom_call", output_to_operand_aliasing={{}: (6, {})} | custom-call | bytes 5111808 | tf_op jit(solution)/shard_map/placed/pallas_call | solution.py:401
  162.6 0.0 collective-permute-done.12.refs_0_.refs_1_
  162.6 4.7 %collective-permute-done.15.refs_2_ = bf16[7,2,2,128,128]{4,3,2,1,0:T(8,128)(2,1)S(1)} collective-permute-done((bf16[7,2,2,128,128]{4,3,2,1,0:T(8,128)(2,1)}, bf16[7,2,2,128,128]{4,3,2,1,0:T(8,128)(2,1)S(1)}, u32[]{:S(2)}, u32[]{:S(2)}) %collective-permute-start.15) | collective-permute-done | bytes 917536 | tf_op jit(solution)/shard_map/ppermute | solution.py:43
  167.4 5.4 %collective-permute-done.16.refs_3_ = bf16[7,2,2,128,128]{4,3,2,1,0:T(8,128)(2,1)} collective-permute-done((bf16[7,2,2,128,128]{4,3,2,1,0:T(8,128)(2,1)}, bf16[7,2,2,128,128]{4,3,2,1,0:T(8,128)(2,1)}, u32[]{:S(2)}, u32[]{:S(2)}) %collective-permute-start.16) | collective-permute-done | bytes 917536 | tf_op jit(solution)/shard_map/ppermute | solution.py:43
  172.8 3.1 %placed.6.refs_2_ = bf16[4,2,13,2,128,128]{5,4,3,2,1,0:T(8,128)(2,1)} custom-call(s32[4]{0:T(128)S(1)} %get-tuple-element.41.row, s32[4]{0:T(128)S(1)} %get-tuple-element.42.valid, bf16[8,2,2,128,128]{4,3,2,1,0:T(8,128)(2,1)S(1)} %collective-permute-done.12.refs_0_.refs_1_, ...), custom_call_target="tpu_custom_call", output_to_operand_aliasing={{}: (6, {})} | custom-call | bytes 5111808 | tf_op jit(solution)/shard_map/placed/pallas_call | solution.py:401
  175.9 13.6 %collective-permute-done.11.refs_1_ = bf16[6,2,2,128,128]{4,3,2,1,0:T(8,128)(2,1)} collective-permute-done((bf16[6,2,2,128,128]{4,3,2,1,0:T(8,128)(2,1)S(1)}, bf16[6,2,2,128,128]{4,3,2,1,0:T(8,128)(2,1)}, u32[]{:S(2)}, u32[]{:S(2)}) %collective-permute-start.11) | collective-permute-done | bytes 786464 | tf_op jit(solution)/shard_map/ppermute | solution.py:43
  189.5 0.0 collective-permute-done.9.refs_0_
  189.5 2.3 %placed.7 = bf16[4,2,13,2,128,128]{5,4,3,2,1,0:T(8,128)(2,1)} custom-call(s32[2]{0:T(128)S(1)} %get-tuple-element.43.row, s32[2]{0:T(128)S(1)} %get-tuple-element.44.valid, bf16[6,2,2,128,128]{4,3,2,1,0:T(8,128)(2,1)S(1)} %collective-permute-done.9.refs_0_, ...), custom_call_target="tpu_custom_call", output_to_operand_aliasing={{}: (4, {})} | custom-call | bytes 5111808 | tf_op jit(solution)/shard_map/placed/pallas_call | solution.py:401
  (1 shorter events, 0.0 us)
Async XLA Ops:
  0.0 37.1 %copy-start.2 = (bf16[1,1,32,128,128]{4,3,2,1,0:T(8,128)(2,1)S(1)}, bf16[1,1,32,128,128]{4,3,2,1,0:T(8,128)(2,1)}, u32[]{:S(2)}) copy-start(bf16[1,1,32,128,128]{4,3,2,1,0:T(8,128)(2,1)} %param.8) | copy-start | bytes 3145732
  1.7 28.7 %collective-permute-start = (bf16[32,128,128]{2,1,0:T(8,128)(2,1)S(1)}, bf16[32,128,128]{2,1,0:T(8,128)(2,1)S(1)}, u32[]{:S(2)}, u32[]{:S(2)}) collective-permute-start(bf16[32,128,128]{2,1,0:T(8,128)(2,1)S(1)} %bitcast.22), channel_id=1, source_target_pairs={{0,4},{4,8},{8,12},{12,16},{16,20},{20,24},{24,28},{1,5},{5,9},{9,... | collective-permute-start | bytes 3145736 | tf_op jit(solution)/shard_map/ppermute | solution.py:43
  4.1 27.2 %collective-permute-start.1 = (bf16[32,128,128]{2,1,0:T(8,128)(2,1)S(1)}, bf16[32,128,128]{2,1,0:T(8,128)(2,1)}, u32[]{:S(2)}, u32[]{:S(2)}) collective-permute-start(bf16[32,128,128]{2,1,0:T(8,128)(2,1)S(1)} %bitcast.23), channel_id=1, source_target_pairs={{0,1},{1,2},{2,3},{4,5},{5,6},{6,7},{8,9},{9,10},{10,11},{12,13},{... | collective-permute-start | bytes 3145736 | tf_op jit(solution)/shard_map/ppermute | solution.py:43
  9.4 27.6 %collective-permute-start.2 = (bf16[32,128,128]{2,1,0:T(8,128)(2,1)S(1)}, bf16[32,128,128]{2,1,0:T(8,128)(2,1)}, u32[]{:S(2)}, u32[]{:S(2)}) collective-permute-start(bf16[32,128,128]{2,1,0:T(8,128)(2,1)S(1)} %bitcast.24), channel_id=1, source_target_pairs={{1,0},{2,1},{3,2},{5,4},{6,5},{7,6},{9,8},{10,9},{11,10},{13,12},{... | collective-permute-start | bytes 3145736 | tf_op jit(solution)/shard_map/ppermute | solution.py:43
  10.7 26.4 %collective-permute-start.3 = (bf16[32,128,128]{2,1,0:T(8,128)(2,1)S(1)}, bf16[32,128,128]{2,1,0:T(8,128)(2,1)}, u32[]{:S(2)}, u32[]{:S(2)}) collective-permute-start(bf16[32,128,128]{2,1,0:T(8,128)(2,1)S(1)} %bitcast.25), channel_id=1, source_target_pairs={{4,0},{8,4},{12,8},{16,12},{20,16},{24,20},{28,24},{5,1},{9,5},{13... | collective-permute-start | bytes 3145736 | tf_op jit(solution)/shard_map/ppermute | solution.py:43
  13.0 1.2 copy-start.1
  14.2 0.7 copy-start.3
  29.1 1.3 copy-start.4
  59.8 24.5 %collective-permute-start.6 = (bf16[5,2,2,128,128]{4,3,2,1,0:T(8,128)(2,1)S(1)}, bf16[5,2,2,128,128]{4,3,2,1,0:T(8,128)(2,1)S(1)}, u32[]{:S(2)}, u32[]{:S(2)}) collective-permute-start(bf16[5,2,2,128,128]{4,3,2,1,0:T(8,128)(2,1)S(1)} %get-tuple-element.30), channel_id=1, source_target_pairs={{0,4},{4,8},{8,12},{12,16},{16,20},{20,24},{24,28},{1,5},{5,9},{9,... | collective-permute-start | bytes 1966088 | tf_op jit(solution)/shard_map/ppermute | solution.py:43
  63.9 20.3 %collective-permute-start.7 = (bf16[5,2,2,128,128]{4,3,2,1,0:T(8,128)(2,1)S(1)}, bf16[5,2,2,128,128]{4,3,2,1,0:T(8,128)(2,1)S(1)}, u32[]{:S(2)}, u32[]{:S(2)}) collective-permute-start(bf16[5,2,2,128,128]{4,3,2,1,0:T(8,128)(2,1)S(1)} %get-tuple-element.31), channel_id=1, source_target_pairs={{4,0},{8,4},{12,8},{16,12},{20,16},{24,20},{28,24},{5,1},{9,5},{13... | collective-permute-start | bytes 1966088 | tf_op jit(solution)/shard_map/ppermute | solution.py:43
  65.2 14.3 %collective-permute-start.4 = (bf16[4,2,2,128,128]{4,3,2,1,0:T(8,128)(2,1)S(1)}, bf16[4,2,2,128,128]{4,3,2,1,0:T(8,128)(2,1)S(1)}, u32[]{:S(2)}, u32[]{:S(2)}) collective-permute-start(bf16[4,2,2,128,128]{4,3,2,1,0:T(8,128)(2,1)S(1)} %get-tuple-element.28), channel_id=1, source_target_pairs={{0,1},{1,2},{2,3},{4,5},{5,6},{6,7},{8,9},{9,10},{10,11},{12,13},{... | collective-permute-start | bytes 1572872 | tf_op jit(solution)/shard_map/ppermute | solution.py:43
  68.4 15.8 %collective-permute-start.5 = (bf16[4,2,2,128,128]{4,3,2,1,0:T(8,128)(2,1)S(1)}, bf16[4,2,2,128,128]{4,3,2,1,0:T(8,128)(2,1)S(1)}, u32[]{:S(2)}, u32[]{:S(2)}) collective-permute-start(bf16[4,2,2,128,128]{4,3,2,1,0:T(8,128)(2,1)S(1)} %get-tuple-element.29), channel_id=1, source_target_pairs={{1,0},{2,1},{3,2},{5,4},{6,5},{7,6},{9,8},{10,9},{11,10},{13,12},{... | collective-permute-start | bytes 1572872 | tf_op jit(solution)/shard_map/ppermute | solution.py:43
  69.9 4.0 %copy-start = (bf16[1280,4096]{1,0:T(8,128)(2,1)S(1)}, bf16[1280,4096]{1,0:T(8,128)(2,1)}, u32[]{:S(2)}) copy-start(bf16[1280,4096]{1,0:T(8,128)(2,1)} %get-tuple-element.33.right_all) | copy-start | bytes 31457284
  84.9 23.3 %collective-permute-start.13 = (bf16[7,2,2,128,128]{4,3,2,1,0:T(8,128)(2,1)S(1)}, bf16[7,2,2,128,128]{4,3,2,1,0:T(8,128)(2,1)}, u32[]{:S(2)}, u32[]{:S(2)}) collective-permute-start(bf16[7,2,2,128,128]{4,3,2,1,0:T(8,128)(2,1)S(1)} %get-tuple-element.37.refs_1_), channel_id=1, source_target_pairs={{0,1},{1,2},{2,3},{4,5},{5,6},{6,7},{8,9},{9,10},{10,11},{12,13},{... | collective-permute-start | bytes 2752520 | tf_op jit(solution)/shard_map/ppermute | solution.py:43
  88.6 25.2 %collective-permute-start.14 = (bf16[7,2,2,128,128]{4,3,2,1,0:T(8,128)(2,1)S(1)}, bf16[7,2,2,128,128]{4,3,2,1,0:T(8,128)(2,1)}, u32[]{:S(2)}, u32[]{:S(2)}) collective-permute-start(bf16[7,2,2,128,128]{4,3,2,1,0:T(8,128)(2,1)S(1)} %get-tuple-element.37.refs_1_), channel_id=1, source_target_pairs={{1,0},{2,1},{3,2},{5,4},{6,5},{7,6},{9,8},{10,9},{11,10},{13,12},{... | collective-permute-start | bytes 2752520 | tf_op jit(solution)/shard_map/ppermute | solution.py:43
  89.9 63.1 %collective-permute-start.10 = (bf16[6,2,2,128,128]{4,3,2,1,0:T(8,128)(2,1)S(1)}, bf16[6,2,2,128,128]{4,3,2,1,0:T(8,128)(2,1)S(1)}, u32[]{:S(2)}, u32[]{:S(2)}) collective-permute-start(bf16[6,2,2,128,128]{4,3,2,1,0:T(8,128)(2,1)S(1)} %get-tuple-element.36.refs_0_), channel_id=1, source_target_pairs={{1,0},{2,1},{3,2},{5,4},{6,5},{7,6},{9,8},{10,9},{11,10},{13,12},{... | collective-permute-start | bytes 2359304 | tf_op jit(solution)/shard_map/ppermute | solution.py:43
  91.2 63.1 %collective-permute-start.8 = (bf16[6,2,2,128,128]{4,3,2,1,0:T(8,128)(2,1)S(1)}, bf16[6,2,2,128,128]{4,3,2,1,0:T(8,128)(2,1)}, u32[]{:S(2)}, u32[]{:S(2)}) collective-permute-start(bf16[6,2,2,128,128]{4,3,2,1,0:T(8,128)(2,1)S(1)} %get-tuple-element.36.refs_0_), channel_id=1, source_target_pairs={{0,1},{1,2},{2,3},{4,5},{5,6},{6,7},{8,9},{9,10},{10,11},{12,13},{... | collective-permute-start | bytes 2359304 | tf_op jit(solution)/shard_map/ppermute | solution.py:43
  98.6 64.1 %collective-permute-start.12 = (bf16[8,2,2,128,128]{4,3,2,1,0:T(8,128)(2,1)}, bf16[8,2,2,128,128]{4,3,2,1,0:T(8,128)(2,1)S(1)}, u32[]{:S(2)}, u32[]{:S(2)}) collective-permute-start(bf16[8,2,2,128,128]{4,3,2,1,0:T(8,128)(2,1)} %fusion), channel_id=1, source_target_pairs={{0,3},{3,0},{4,7},{7,4},{8,11},{11,8},{12,15},{15,12},{16,19},{19,... | collective-permute-start | bytes 3145736 | tf_op jit(solution)/shard_map/ppermute | solution.py:427
  113.8 53.6 %collective-permute-start.15 = (bf16[7,2,2,128,128]{4,3,2,1,0:T(8,128)(2,1)}, bf16[7,2,2,128,128]{4,3,2,1,0:T(8,128)(2,1)S(1)}, u32[]{:S(2)}, u32[]{:S(2)}) collective-permute-start(bf16[7,2,2,128,128]{4,3,2,1,0:T(8,128)(2,1)} %collective-permute-done.13.refs_2_), channel_id=1, source_target_pairs={{0,1},{1,2},{2,3},{4,5},{5,6},{6,7},{8,9},{9,10},{10,11},{12,13},{... | collective-permute-start | bytes 2752520 | tf_op jit(solution)/shard_map/ppermute | solution.py:43
  115.2 57.6 %collective-permute-start.16 = (bf16[7,2,2,128,128]{4,3,2,1,0:T(8,128)(2,1)}, bf16[7,2,2,128,128]{4,3,2,1,0:T(8,128)(2,1)}, u32[]{:S(2)}, u32[]{:S(2)}) collective-permute-start(bf16[7,2,2,128,128]{4,3,2,1,0:T(8,128)(2,1)} %collective-permute-done.14.refs_3_), channel_id=1, source_target_pairs={{1,0},{2,1},{3,2},{5,4},{6,5},{7,6},{9,8},{10,9},{11,10},{13,12},{... | collective-permute-start | bytes 2752520 | tf_op jit(solution)/shard_map/ppermute | solution.py:43
  153.0 36.5 %collective-permute-start.11 = (bf16[6,2,2,128,128]{4,3,2,1,0:T(8,128)(2,1)S(1)}, bf16[6,2,2,128,128]{4,3,2,1,0:T(8,128)(2,1)}, u32[]{:S(2)}, u32[]{:S(2)}) collective-permute-start(bf16[6,2,2,128,128]{4,3,2,1,0:T(8,128)(2,1)S(1)} %collective-permute-done.10.refs_1_), channel_id=1, source_target_pairs={{1,0},{2,1},{3,2},{5,4},{6,5},{7,6},{9,8},{10,9},{11,10},{13,12},{... | collective-permute-start | bytes 2359304 | tf_op jit(solution)/shard_map/ppermute | solution.py:43
  154.3 35.2 %collective-permute-start.9 = (bf16[6,2,2,128,128]{4,3,2,1,0:T(8,128)(2,1)}, bf16[6,2,2,128,128]{4,3,2,1,0:T(8,128)(2,1)S(1)}, u32[]{:S(2)}, u32[]{:S(2)}) collective-permute-start(bf16[6,2,2,128,128]{4,3,2,1,0:T(8,128)(2,1)} %collective-permute-done.8.refs_0_), channel_id=1, source_target_pairs={{0,1},{1,2},{2,3},{4,5},{5,6},{6,7},{8,9},{9,10},{10,11},{12,13},{... | collective-permute-start | bytes 2359304 | tf_op jit(solution)/shard_map/ppermute | solution.py:43

commit v8 on v7

--- a/solution.py
+++ b/solution.py
@@ -136,7 +136,7 @@
 
 
 def product(left, right, outs, lone, members, tile):
-    value = lax.dot_general(left[...], right[...], NT, preferred_element_type=jnp.float32)
+    value = lax.dot_general(left, right, NT, preferred_element_type=jnp.float32)
     for d1, out in enumerate(outs):
         for d2 in range(5):
             target, at = out, d2
@@ -153,12 +153,13 @@
 def partial_kernel(members, taps, tiles, sources, slots, ends, *refs):
     a_tiles, dinv_hbm, *tents = refs[:6]
     right_own, *outs, behind, ahead, right_out = refs[6:14]
-    a_held, dinv, tent, right, left, sums, sems = refs[14:]
+    a_held, dinv, tent, right, left, sems = refs[14:]
     tile = dinv.shape[-1]
     rows = dinv.shape[0]
     chunks = rows // ROWS_PER_CHUNK
     outer = 4 * members
     per = ROWS_PER_CHUNK * taps
+    depth = rows * tile
 
     def a_copy(c):
         part = pl.ds(c * per, per)
@@ -169,19 +170,22 @@
         for d, source in zip(HALO_ORDER, tents)
     ]
     dinv_copy = pltpu.make_async_copy(dinv_hbm, dinv, sems.at[chunks + 4])
-    own_part = (pl.ds(outer * tile, members * tile), slice(None))
+    own_part = (pl.ds(outer * tile, members * tile), pl.ds(0, depth))
     own_copy = pltpu.make_async_copy(right_own, right.at[own_part], sems.at[chunks + 5])
-    out_copy = pltpu.make_async_copy(right, right_out, sems.at[chunks + 6])
+    out_copy = pltpu.make_async_copy(
+        right.at[:, pl.ds(0, depth)], right_out, sems.at[chunks + 6]
+    )
     for copy in tent_copies:
         copy.start()
-    a_copy(0).start()
-    sums[...] = jnp.zeros_like(sums)
+    dinv_copy.start()
+    for c in range(chunks):
+        a_copy(c).start()
+    own_copy.start()
+    right[: outer * tile, :] = jnp.zeros((outer * tile, right.shape[1]), right.dtype)
+    left[...] = jnp.zeros_like(left)
     for copy in tent_copies:
         copy.wait()
-    dinv_copy.start()
-    for c in range(1, chunks):
-        a_copy(c).start()
-    own_copy.start()
+    dinv_copy.wait()
 
     def one_chunk(c, first):
         a_copy(c).wait()
@@ -193,39 +197,28 @@
                 at = first + UNROLL * n + u
                 index = jnp.minimum(at, last - 1)
                 number = tiles[index]
-                slot = jnp.where(at < last, slots[index], outer)
+                row = number // taps
                 z = lax.dot_general(
                     tent[sources[index]], a_held[number], NT, preferred_element_type=jnp.float32
+                ).astype(jnp.bfloat16)
+                smooth = lax.dot_general(z, dinv[row], NT, preferred_element_type=jnp.float32)
+                lanes = lane_tiles(jnp.where(at < last, row, rows), tile)
+                found.append(((lane_tiles(slots[index], tile), lanes), z, smooth))
+            for at, z, smooth in found:
+                right[at] = (right[at].astype(jnp.float32) + z.astype(jnp.float32)).astype(
+                    jnp.bfloat16
                 )
-                found.append((slot, number // taps - c * ROWS_PER_CHUNK, z))
-            for slot, row, z in found:
-                at = (lane_tiles(slot, tile), lane_tiles(row, tile))
-                sums[at] += z.astype(jnp.bfloat16).astype(jnp.float32)
+                left[at] = (left[at].astype(jnp.float32) - smoothing * smooth).astype(jnp.bfloat16)
             return carry
 
         lax.fori_loop(0, (last - first + UNROLL - 1) // UNROLL, some, 0)
-        lanes = lane_tiles(c, ROWS_PER_CHUNK * tile)
-        right[: outer * tile, lanes] = sums[: outer * tile, :].astype(jnp.bfloat16)
-        sums[...] = jnp.zeros_like(sums)
-
-        @pl.when(c == 0)
-        def _():
-            dinv_copy.wait()
-
-        for u in range(ROWS_PER_CHUNK):
-            g = c * ROWS_PER_CHUNK + u
-            lanes = lane_tiles(g, tile)
-            smooth = lax.dot_general(
-                right[: outer * tile, lanes], dinv[g], NT, preferred_element_type=jnp.float32
-            )
-            left[: outer * tile, lanes] = (-smoothing * smooth).astype(jnp.bfloat16)
         return last
 
     lax.fori_loop(0, chunks, one_chunk, 0)
     own_copy.wait()
     out_copy.start()
     lone = {d: (CROSS_SHIFTS.index(t), out) for d, t, out in ((0, UP, behind), (1, DOWN, ahead))}
-    product(left, right, outs, lone, members, tile)
+    product(left[:, :depth], right[:, :depth], outs, lone, members, tile)
     out_copy.wait()
 
 
@@ -246,9 +239,8 @@
                 pltpu.VMEM((rows * taps, tile, tile), jnp.bfloat16),
                 pltpu.VMEM((rows, tile, tile), jnp.bfloat16),
                 pltpu.VMEM((4 * rows, tile, tile), jnp.bfloat16),
-                pltpu.VMEM((slots, rows * tile), jnp.bfloat16),
-                pltpu.VMEM((outer, rows * tile), jnp.bfloat16),
-                pltpu.VMEM((outer + tile, ROWS_PER_CHUNK * tile), jnp.float32),
+                pltpu.VMEM((slots, (rows + 1) * tile), jnp.bfloat16),
+                pltpu.VMEM((outer, (rows + 1) * tile), jnp.bfloat16),
                 pltpu.SemaphoreType.DMA((rows // ROWS_PER_CHUNK + 7,)),
             ],
         ),
@@ -259,7 +251,7 @@
         + [jax.ShapeDtypeStruct((slots, rows * tile), jnp.bfloat16)],
         compiler_params=pltpu.CompilerParams(vmem_limit_bytes=48 * 1024 * 1024),
         cost_estimate=pl.CostEstimate(
-            flops=2 * tile**3 * rows * members * (4 + 20 * members),
+            flops=2 * tile**3 * rows * (taps + 20 * members * members),
             bytes_accessed=2 * (a_tiles.size + 20 * dinv.size),
             transcendentals=0,
         ),
@@ -276,7 +268,7 @@
         copy.start()
     for copy in copies:
         copy.wait()
-    product(left, right, (own,), {}, members, own.shape[-1])
+    product(left[...], right[...], (own,), {}, members, own.shape[-1])
 
 
 def own_rows(left, right, members):

time: 193 us -> 194 us (level)
  starting transfers between devices: 43.1 us -> 45.5 us
    ppermute x16, starting transfers between devices: 41.2 us -> 43.6 us  [shifted(): return lax.ppermute(x, axis, pairs)]
where the time goes in v8:
time: 194 us; the launch traced here: 193 us
  waiting for transfers between devices  83.9 us (43%)
  Pallas kernels  51.9 us (27%)
  starting transfers between devices  45.5 us (23%)
  local copies, waits for them, and re-layouts  9.77 us (5%)
    ppermute x16, waiting for transfers between devices, shifted(): return lax.ppermute(x, axis, pairs)  83.9 us
    ppermute x16, starting transfers between devices, shifted(): return lax.ppermute(x, axis, pairs)  43.6 us
    pallas_call x1, Pallas kernels, partial_blocks(): pl.pallas_call(functools.partial(partial_kernel, members, taps), grid_spe...  22.5 us
    pallas_call x1, Pallas kernels, own_slots(): pl.pallas_call(functools.partial(own_kernel, count_y, rows, members, taps...  14.2 us
    pallas_call x4, Pallas kernels, placed(): pl.pallas_call(functools.partial(place_kernel, tuple((p[1:3] for p in pie...  10.8 us
    unnamed x12, local copies, waits for them, and re-layouts  9.67 us
  transfers between devices with their start and end apart: 17, of which 10 were waited for; matrix products, arithmetic and copies ran while one was open for 1% of the time, Pallas kernels for 14%

profile of v8, /device:TPU:0, one launch (start us, length us, event | category | flops | bytes accessed | tf_op | source)
XLA Modules:
  0.0 193.2 jit_solution(17984693735364712682)
XLA Ops:
  0.0 0.0 copy-start.2
  0.0 1.7 copy.11
  1.7 2.4 %collective-permute-start = (bf16[32,128,128]{2,1,0:T(8,128)(2,1)S(1)}, bf16[32,128,128]{2,1,0:T(8,128)(2,1)S(1)}, u32[]{:S(2)}, u32[]{:S(2)}) collective-permute-start(bf16[32,128,128]{2,1,0:T(8,128)(2,1)S(1)} %bitcast.22), channel_id=1, source_target_pairs={{0,4},{4,8},{8,12},{12,16},{16,20},{20,24},{24,28},{1,5},{5,9},{9,... | collective-permute-start | bytes 3145736 | tf_op jit(solution)/shard_map/ppermute | solution.py:43
  4.1 5.3 %collective-permute-start.1 = (bf16[32,128,128]{2,1,0:T(8,128)(2,1)S(1)}, bf16[32,128,128]{2,1,0:T(8,128)(2,1)}, u32[]{:S(2)}, u32[]{:S(2)}) collective-permute-start(bf16[32,128,128]{2,1,0:T(8,128)(2,1)S(1)} %bitcast.23), channel_id=1, source_target_pairs={{0,1},{1,2},{2,3},{4,5},{5,6},{6,7},{8,9},{9,10},{10,11},{12,13},{... | collective-permute-start | bytes 3145736 | tf_op jit(solution)/shard_map/ppermute | solution.py:43
  9.4 1.3 collective-permute-start.2
  10.7 1.3 collective-permute-start.3
  12.0 0.8 copy.10
  12.8 0.1 reshape.12.columns
  12.9 0.1 pad_add_fusion.2.place
  13.0 0.0 copy-start.1
  13.0 1.2 copy-done.1
  14.2 0.0 copy-start.3
  14.2 0.7 copy-done.3
  14.9 14.2 %own_slots.1 = (bf16[256,4096]{1,0:T(8,128)(2,1)S(1)}, bf16[256,4096]{1,0:T(8,128)(2,1)S(1)}, s32[224]{0:T(256)S(1)}, s32[224]{0:T(256)S(1)}, s32[224]{0:T(256)S(1)}, /*index=5*/s32[8]{0:T(128)S(1)}) custom-call(s32[224]{0:T(256)S(1)} %reshape.12.columns, s32[1024]{0:T(1024)S(1)} %copy-done.3, s32[2]{0:T(128)S(1)} %pad_add_fusion.2.place, ...), custom_call_target="tpu_custom_call" | custom-call | flops 1207959552 | bytes 13631488 | tf_op jit(solution)/shard_map/own_slots/pallas_call | solution.py:105
  29.1 0.0 copy-start.4
  29.1 1.3 copy-done.4
  30.4 0.0 collective-permute-done.refs_2_
  30.4 0.9 collective-permute-done.1.refs_3_
  31.3 5.8 %collective-permute-done.2.refs_4_ = bf16[32,128,128]{2,1,0:T(8,128)(2,1)} collective-permute-done((bf16[32,128,128]{2,1,0:T(8,128)(2,1)S(1)}, bf16[32,128,128]{2,1,0:T(8,128)(2,1)}, u32[]{:S(2)}, u32[]{:S(2)}) %collective-permute-start.2) | collective-permute-done | bytes 1048608 | tf_op jit(solution)/shard_map/ppermute | solution.py:43
  37.1 0.0 collective-permute-done.3.refs_5_
  37.1 0.0 copy-done.2
  37.1 22.5 %partial_blocks.1 = (bf16[4,2,2,128,128]{4,3,2,1,0:T(8,128)(2,1)S(1)}, bf16[4,2,2,128,128]{4,3,2,1,0:T(8,128)(2,1)S(1)}, bf16[5,2,2,128,128]{4,3,2,1,0:T(8,128)(...) custom-call(s32[224]{0:T(256)S(1)} %get-tuple-element.23.tiles, ...), custom_call_target="tpu_custom_call" | custom-call | flops 11676942336 | bytes 28311552 | tf_op jit(solution)/shard_map/partial_blocks/pallas_call | solution.py:231
  59.6 4.3 %collective-permute-start.6 = (bf16[5,2,2,128,128]{4,3,2,1,0:T(8,128)(2,1)S(1)}, bf16[5,2,2,128,128]{4,3,2,1,0:T(8,128)(2,1)S(1)}, u32[]{:S(2)}, u32[]{:S(2)}) collective-permute-start(bf16[5,2,2,128,128]{4,3,2,1,0:T(8,128)(2,1)S(1)} %get-tuple-element.30), channel_id=1, source_target_pairs={{0,4},{4,8},{8,12},{12,16},{16,20},{20,24},{24,28},{1,5},{5,9},{9,... | collective-permute-start | bytes 1966088 | tf_op jit(solution)/shard_map/ppermute | solution.py:43
  63.9 1.3 collective-permute-start.7
  65.2 3.6 %collective-permute-start.4 = (bf16[4,2,2,128,128]{4,3,2,1,0:T(8,128)(2,1)S(1)}, bf16[4,2,2,128,128]{4,3,2,1,0:T(8,128)(2,1)S(1)}, u32[]{:S(2)}, u32[]{:S(2)}) collective-permute-start(bf16[4,2,2,128,128]{4,3,2,1,0:T(8,128)(2,1)S(1)} %get-tuple-element.28), channel_id=1, source_target_pairs={{0,1},{1,2},{2,3},{4,5},{5,6},{6,7},{8,9},{9,10},{10,11},{12,13},{... | collective-permute-start | bytes 1572872 | tf_op jit(solution)/shard_map/ppermute | solution.py:43
  68.8 1.5 collective-permute-start.5
  70.3 0.0 copy-start
  70.3 4.0 %copy-done = bf16[1280,4096]{1,0:T(8,128)(2,1)S(1)} copy-done((bf16[1280,4096]{1,0:T(8,128)(2,1)S(1)}, bf16[1280,4096]{1,0:T(8,128)(2,1)}, u32[]{:S(2)}) %copy-start) | copy-done | bytes 10485784
  74.2 3.8 %own_rows.1.refs_4_ = f32[5,2,2,128,128]{4,3,2,1,0:T(8,128)S(1)} custom-call(bf16[256,4096]{1,0:T(8,128)(2,1)S(1)} %get-tuple-element.32.left_own, bf16[1280,4096]{1,0:T(8,128)(2,1)S(1)} %copy-done), custom_call_target="tpu_custom_call" | custom-call | flops 2684354560 | bytes 12582912 | tf_op jit(solution)/shard_map/own_rows/pallas_call | solution.py:277
  78.0 1.8 collective-permute-done.4.refs_0_
  79.8 4.9 %collective-permute-done.5.refs_1_ = bf16[4,2,2,128,128]{4,3,2,1,0:T(8,128)(2,1)S(1)} collective-permute-done((bf16[4,2,2,128,128]{4,3,2,1,0:T(8,128)(2,1)S(1)}, bf16[4,2,2,128,128]{4,3,2,1,0:T(8,128)(2,1)S(1)}, u32[]{:S(2)}, u32[]{:S(2)}) %collective-permute-start.5) | collective-permute-done | bytes 524320 | tf_op jit(solution)/shard_map/ppermute | solution.py:43
  84.8 0.0 collective-permute-done.6.refs_2_
  84.8 0.0 collective-permute-done.7.refs_3_
  84.8 0.7 finished_window.1
  85.5 5.4 %collective-permute-start.13 = (bf16[7,2,2,128,128]{4,3,2,1,0:T(8,128)(2,1)S(1)}, bf16[7,2,2,128,128]{4,3,2,1,0:T(8,128)(2,1)}, u32[]{:S(2)}, u32[]{:S(2)}) collective-permute-start(bf16[7,2,2,128,128]{4,3,2,1,0:T(8,128)(2,1)S(1)} %get-tuple-element.37.refs_1_), channel_id=1, source_target_pairs={{0,1},{1,2},{2,3},{4,5},{5,6},{6,7},{8,9},{9,10},{10,11},{12,13},{... | collective-permute-start | bytes 2752520 | tf_op jit(solution)/shard_map/ppermute | solution.py:43
  90.9 1.3 collective-permute-start.14
  92.2 1.3 collective-permute-start.10
  93.5 6.1 %collective-permute-start.8 = (bf16[6,2,2,128,128]{4,3,2,1,0:T(8,128)(2,1)S(1)}, bf16[6,2,2,128,128]{4,3,2,1,0:T(8,128)(2,1)}, u32[]{:S(2)}, u32[]{:S(2)}) collective-permute-start(bf16[6,2,2,128,128]{4,3,2,1,0:T(8,128)(2,1)S(1)} %get-tuple-element.36.refs_0_), channel_id=1, source_target_pairs={{0,1},{1,2},{2,3},{4,5},{5,6},{6,7},{8,9},{9,10},{10,11},{12,13},{... | collective-permute-start | bytes 2359304 | tf_op jit(solution)/shard_map/ppermute | solution.py:43
  99.5 1.3 fusion
  100.8 1.9 collective-permute-start.12
  102.8 0.1 pad_add_fusion.5.row
  102.8 2.0 %placed.4.refs_4_ = bf16[4,2,13,2,128,128]{5,4,3,2,1,0:T(8,128)(2,1)} custom-call(s32[2]{0:T(128)S(1)} %pad_add_fusion.5.row, s32[2]{0:T(128)S(1)} %broadcast_1_valid.2.valid, bf16[6,2,2,128,128]{4,3,2,1,0:T(8,128)(2,1)S(1)} %get-tuple-element.36.refs_0_, bf16[7,2,2,128,128]{4,3,2,1,0:T(8,128)(2,1)S(1)} %get-tuple-element.37.refs_1_), custom_call_target="tpu_custom_call" | custom-call | bytes 5111808 | tf_op jit(solution)/shard_map/placed/pallas_call | solution.py:393
  104.8 5.8 %collective-permute-done.13.refs_2_ = bf16[7,2,2,128,128]{4,3,2,1,0:T(8,128)(2,1)} collective-permute-done((bf16[7,2,2,128,128]{4,3,2,1,0:T(8,128)(2,1)S(1)}, bf16[7,2,2,128,128]{4,3,2,1,0:T(8,128)(2,1)}, u32[]{:S(2)}, u32[]{:S(2)}) %collective-permute-start.13) | collective-permute-done | bytes 917536 | tf_op jit(solution)/shard_map/ppermute | solution.py:43
  110.6 5.5 %collective-permute-done.14.refs_3_ = bf16[7,2,2,128,128]{4,3,2,1,0:T(8,128)(2,1)} collective-permute-done((bf16[7,2,2,128,128]{4,3,2,1,0:T(8,128)(2,1)S(1)}, bf16[7,2,2,128,128]{4,3,2,1,0:T(8,128)(2,1)}, u32[]{:S(2)}, u32[]{:S(2)}) %collective-permute-start.14) | collective-permute-done | bytes 917536 | tf_op jit(solution)/shard_map/ppermute | solution.py:43
  116.1 1.4 collective-permute-start.15
  117.5 1.3 collective-permute-start.16
  118.8 36.5 %collective-permute-done.10.refs_1_ = bf16[6,2,2,128,128]{4,3,2,1,0:T(8,128)(2,1)S(1)} collective-permute-done((bf16[6,2,2,128,128]{4,3,2,1,0:T(8,128)(2,1)S(1)}, bf16[6,2,2,128,128]{4,3,2,1,0:T(8,128)(2,1)S(1)}, u32[]{:S(2)}, u32[]{:S(2)}) %collective-permute-start.10) | collective-permute-done | bytes 786464 | tf_op jit(solution)/shard_map/ppermute | solution.py:43
  155.3 1.3 collective-permute-start.11
  156.6 0.0 collective-permute-done.8.refs_0_
  156.6 4.6 %collective-permute-start.9 = (bf16[6,2,2,128,128]{4,3,2,1,0:T(8,128)(2,1)}, bf16[6,2,2,128,128]{4,3,2,1,0:T(8,128)(2,1)S(1)}, u32[]{:S(2)}, u32[]{:S(2)}) collective-permute-start(bf16[6,2,2,128,128]{4,3,2,1,0:T(8,128)(2,1)} %collective-permute-done.8.refs_0_), channel_id=1, source_target_pairs={{0,1},{1,2},{2,3},{4,5},{5,6},{6,7},{8,9},{9,10},{10,11},{12,13},{... | collective-permute-start | bytes 2359304 | tf_op jit(solution)/shard_map/ppermute | solution.py:43
  161.2 0.1 pad_add_fusion.6.row
  161.3 0.1 add_convert_fusion.valid
  161.4 0.1 pad_add_fusion
  161.5 0.1 pad_add_fusion.3
  161.6 3.4 %placed.5.refs_4_ = bf16[4,2,13,2,128,128]{5,4,3,2,1,0:T(8,128)(2,1)} custom-call(s32[4]{0:T(128)S(1)} %pad_add_fusion.6.row, s32[4]{0:T(128)S(1)} %add_convert_fusion.valid, bf16[6,2,2,128,128]{4,3,2,1,0:T(8,128)(2,1)} %collective-permute-done.8.refs_0_, ...), custom_call_target="tpu_custom_call", output_to_operand_aliasing={{}: (6, {})} | custom-call | bytes 5111808 | tf_op jit(solution)/shard_map/placed/pallas_call | solution.py:393
  164.9 0.0 collective-permute-done.12.refs_0_.refs_1_
  164.9 4.8 %collective-permute-done.15.refs_2_ = bf16[7,2,2,128,128]{4,3,2,1,0:T(8,128)(2,1)S(1)} collective-permute-done((bf16[7,2,2,128,128]{4,3,2,1,0:T(8,128)(2,1)}, bf16[7,2,2,128,128]{4,3,2,1,0:T(8,128)(2,1)S(1)}, u32[]{:S(2)}, u32[]{:S(2)}) %collective-permute-start.15) | collective-permute-done | bytes 917536 | tf_op jit(solution)/shard_map/ppermute | solution.py:43
  169.8 5.3 %collective-permute-done.16.refs_3_ = bf16[7,2,2,128,128]{4,3,2,1,0:T(8,128)(2,1)} collective-permute-done((bf16[7,2,2,128,128]{4,3,2,1,0:T(8,128)(2,1)}, bf16[7,2,2,128,128]{4,3,2,1,0:T(8,128)(2,1)}, u32[]{:S(2)}, u32[]{:S(2)}) %collective-permute-start.16) | collective-permute-done | bytes 917536 | tf_op jit(solution)/shard_map/ppermute | solution.py:43
  175.1 3.1 %placed.6.refs_2_ = bf16[4,2,13,2,128,128]{5,4,3,2,1,0:T(8,128)(2,1)} custom-call(s32[4]{0:T(128)S(1)} %get-tuple-element.41.row, s32[4]{0:T(128)S(1)} %get-tuple-element.42.valid, bf16[8,2,2,128,128]{4,3,2,1,0:T(8,128)(2,1)S(1)} %collective-permute-done.12.refs_0_.refs_1_, ...), custom_call_target="tpu_custom_call", output_to_operand_aliasing={{}: (6, {})} | custom-call | bytes 5111808 | tf_op jit(solution)/shard_map/placed/pallas_call | solution.py:393
  178.2 12.6 %collective-permute-done.11.refs_1_ = bf16[6,2,2,128,128]{4,3,2,1,0:T(8,128)(2,1)} collective-permute-done((bf16[6,2,2,128,128]{4,3,2,1,0:T(8,128)(2,1)S(1)}, bf16[6,2,2,128,128]{4,3,2,1,0:T(8,128)(2,1)}, u32[]{:S(2)}, u32[]{:S(2)}) %collective-permute-start.11) | collective-permute-done | bytes 786464 | tf_op jit(solution)/shard_map/ppermute | solution.py:43
  190.8 0.0 collective-permute-done.9.refs_0_
  190.8 2.3 %placed.7 = bf16[4,2,13,2,128,128]{5,4,3,2,1,0:T(8,128)(2,1)} custom-call(s32[2]{0:T(128)S(1)} %get-tuple-element.43.row, s32[2]{0:T(128)S(1)} %get-tuple-element.44.valid, bf16[6,2,2,128,128]{4,3,2,1,0:T(8,128)(2,1)S(1)} %collective-permute-done.9.refs_0_, ...), custom_call_target="tpu_custom_call", output_to_operand_aliasing={{}: (4, {})} | custom-call | bytes 5111808 | tf_op jit(solution)/shard_map/placed/pallas_call | solution.py:393
  (1 shorter events, 0.0 us)
Async XLA Ops:
  0.0 37.1 %copy-start.2 = (bf16[1,1,32,128,128]{4,3,2,1,0:T(8,128)(2,1)S(1)}, bf16[1,1,32,128,128]{4,3,2,1,0:T(8,128)(2,1)}, u32[]{:S(2)}) copy-start(bf16[1,1,32,128,128]{4,3,2,1,0:T(8,128)(2,1)} %param.8) | copy-start | bytes 3145732
  1.7 28.7 %collective-permute-start = (bf16[32,128,128]{2,1,0:T(8,128)(2,1)S(1)}, bf16[32,128,128]{2,1,0:T(8,128)(2,1)S(1)}, u32[]{:S(2)}, u32[]{:S(2)}) collective-permute-start(bf16[32,128,128]{2,1,0:T(8,128)(2,1)S(1)} %bitcast.22), channel_id=1, source_target_pairs={{0,4},{4,8},{8,12},{12,16},{16,20},{20,24},{24,28},{1,5},{5,9},{9,... | collective-permute-start | bytes 3145736 | tf_op jit(solution)/shard_map/ppermute | solution.py:43
  4.1 27.2 %collective-permute-start.1 = (bf16[32,128,128]{2,1,0:T(8,128)(2,1)S(1)}, bf16[32,128,128]{2,1,0:T(8,128)(2,1)}, u32[]{:S(2)}, u32[]{:S(2)}) collective-permute-start(bf16[32,128,128]{2,1,0:T(8,128)(2,1)S(1)} %bitcast.23), channel_id=1, source_target_pairs={{0,1},{1,2},{2,3},{4,5},{5,6},{6,7},{8,9},{9,10},{10,11},{12,13},{... | collective-permute-start | bytes 3145736 | tf_op jit(solution)/shard_map/ppermute | solution.py:43
  9.4 27.6 %collective-permute-start.2 = (bf16[32,128,128]{2,1,0:T(8,128)(2,1)S(1)}, bf16[32,128,128]{2,1,0:T(8,128)(2,1)}, u32[]{:S(2)}, u32[]{:S(2)}) collective-permute-start(bf16[32,128,128]{2,1,0:T(8,128)(2,1)S(1)} %bitcast.24), channel_id=1, source_target_pairs={{1,0},{2,1},{3,2},{5,4},{6,5},{7,6},{9,8},{10,9},{11,10},{13,12},{... | collective-permute-start | bytes 3145736 | tf_op jit(solution)/shard_map/ppermute | solution.py:43
  10.7 26.4 %collective-permute-start.3 = (bf16[32,128,128]{2,1,0:T(8,128)(2,1)S(1)}, bf16[32,128,128]{2,1,0:T(8,128)(2,1)}, u32[]{:S(2)}, u32[]{:S(2)}) collective-permute-start(bf16[32,128,128]{2,1,0:T(8,128)(2,1)S(1)} %bitcast.25), channel_id=1, source_target_pairs={{4,0},{8,4},{12,8},{16,12},{20,16},{24,20},{28,24},{5,1},{9,5},{13... | collective-permute-start | bytes 3145736 | tf_op jit(solution)/shard_map/ppermute | solution.py:43
  13.0 1.2 copy-start.1
  14.2 0.7 copy-start.3
  29.1 1.3 copy-start.4
  59.6 25.2 %collective-permute-start.6 = (bf16[5,2,2,128,128]{4,3,2,1,0:T(8,128)(2,1)S(1)}, bf16[5,2,2,128,128]{4,3,2,1,0:T(8,128)(2,1)S(1)}, u32[]{:S(2)}, u32[]{:S(2)}) collective-permute-start(bf16[5,2,2,128,128]{4,3,2,1,0:T(8,128)(2,1)S(1)} %get-tuple-element.30), channel_id=1, source_target_pairs={{0,4},{4,8},{8,12},{12,16},{16,20},{20,24},{24,28},{1,5},{5,9},{9,... | collective-permute-start | bytes 1966088 | tf_op jit(solution)/shard_map/ppermute | solution.py:43
  63.9 20.9 %collective-permute-start.7 = (bf16[5,2,2,128,128]{4,3,2,1,0:T(8,128)(2,1)S(1)}, bf16[5,2,2,128,128]{4,3,2,1,0:T(8,128)(2,1)S(1)}, u32[]{:S(2)}, u32[]{:S(2)}) collective-permute-start(bf16[5,2,2,128,128]{4,3,2,1,0:T(8,128)(2,1)S(1)} %get-tuple-element.31), channel_id=1, source_target_pairs={{4,0},{8,4},{12,8},{16,12},{20,16},{24,20},{28,24},{5,1},{9,5},{13... | collective-permute-start | bytes 1966088 | tf_op jit(solution)/shard_map/ppermute | solution.py:43
  65.2 14.7 %collective-permute-start.4 = (bf16[4,2,2,128,128]{4,3,2,1,0:T(8,128)(2,1)S(1)}, bf16[4,2,2,128,128]{4,3,2,1,0:T(8,128)(2,1)S(1)}, u32[]{:S(2)}, u32[]{:S(2)}) collective-permute-start(bf16[4,2,2,128,128]{4,3,2,1,0:T(8,128)(2,1)S(1)} %get-tuple-element.28), channel_id=1, source_target_pairs={{0,1},{1,2},{2,3},{4,5},{5,6},{6,7},{8,9},{9,10},{10,11},{12,13},{... | collective-permute-start | bytes 1572872 | tf_op jit(solution)/shard_map/ppermute | solution.py:43
  68.8 16.0 %collective-permute-start.5 = (bf16[4,2,2,128,128]{4,3,2,1,0:T(8,128)(2,1)S(1)}, bf16[4,2,2,128,128]{4,3,2,1,0:T(8,128)(2,1)S(1)}, u32[]{:S(2)}, u32[]{:S(2)}) collective-permute-start(bf16[4,2,2,128,128]{4,3,2,1,0:T(8,128)(2,1)S(1)} %get-tuple-element.29), channel_id=1, source_target_pairs={{1,0},{2,1},{3,2},{5,4},{6,5},{7,6},{9,8},{10,9},{11,10},{13,12},{... | collective-permute-start | bytes 1572872 | tf_op jit(solution)/shard_map/ppermute | solution.py:43
  70.3 4.0 %copy-start = (bf16[1280,4096]{1,0:T(8,128)(2,1)S(1)}, bf16[1280,4096]{1,0:T(8,128)(2,1)}, u32[]{:S(2)}) copy-start(bf16[1280,4096]{1,0:T(8,128)(2,1)} %get-tuple-element.33.right_all) | copy-start | bytes 31457284
  85.5 25.1 %collective-permute-start.13 = (bf16[7,2,2,128,128]{4,3,2,1,0:T(8,128)(2,1)S(1)}, bf16[7,2,2,128,128]{4,3,2,1,0:T(8,128)(2,1)}, u32[]{:S(2)}, u32[]{:S(2)}) collective-permute-start(bf16[7,2,2,128,128]{4,3,2,1,0:T(8,128)(2,1)S(1)} %get-tuple-element.37.refs_1_), channel_id=1, source_target_pairs={{0,1},{1,2},{2,3},{4,5},{5,6},{6,7},{8,9},{9,10},{10,11},{12,13},{... | collective-permute-start | bytes 2752520 | tf_op jit(solution)/shard_map/ppermute | solution.py:43
  90.9 25.2 %collective-permute-start.14 = (bf16[7,2,2,128,128]{4,3,2,1,0:T(8,128)(2,1)S(1)}, bf16[7,2,2,128,128]{4,3,2,1,0:T(8,128)(2,1)}, u32[]{:S(2)}, u32[]{:S(2)}) collective-permute-start(bf16[7,2,2,128,128]{4,3,2,1,0:T(8,128)(2,1)S(1)} %get-tuple-element.37.refs_1_), channel_id=1, source_target_pairs={{1,0},{2,1},{3,2},{5,4},{6,5},{7,6},{9,8},{10,9},{11,10},{13,12},{... | collective-permute-start | bytes 2752520 | tf_op jit(solution)/shard_map/ppermute | solution.py:43
  92.2 63.2 %collective-permute-start.10 = (bf16[6,2,2,128,128]{4,3,2,1,0:T(8,128)(2,1)S(1)}, bf16[6,2,2,128,128]{4,3,2,1,0:T(8,128)(2,1)S(1)}, u32[]{:S(2)}, u32[]{:S(2)}) collective-permute-start(bf16[6,2,2,128,128]{4,3,2,1,0:T(8,128)(2,1)S(1)} %get-tuple-element.36.refs_0_), channel_id=1, source_target_pairs={{1,0},{2,1},{3,2},{5,4},{6,5},{7,6},{9,8},{10,9},{11,10},{13,12},{... | collective-permute-start | bytes 2359304 | tf_op jit(solution)/shard_map/ppermute | solution.py:43
  93.5 63.1 %collective-permute-start.8 = (bf16[6,2,2,128,128]{4,3,2,1,0:T(8,128)(2,1)S(1)}, bf16[6,2,2,128,128]{4,3,2,1,0:T(8,128)(2,1)}, u32[]{:S(2)}, u32[]{:S(2)}) collective-permute-start(bf16[6,2,2,128,128]{4,3,2,1,0:T(8,128)(2,1)S(1)} %get-tuple-element.36.refs_0_), channel_id=1, source_target_pairs={{0,1},{1,2},{2,3},{4,5},{5,6},{6,7},{8,9},{9,10},{10,11},{12,13},{... | collective-permute-start | bytes 2359304 | tf_op jit(solution)/shard_map/ppermute | solution.py:43
  100.8 64.1 %collective-permute-start.12 = (bf16[8,2,2,128,128]{4,3,2,1,0:T(8,128)(2,1)}, bf16[8,2,2,128,128]{4,3,2,1,0:T(8,128)(2,1)S(1)}, u32[]{:S(2)}, u32[]{:S(2)}) collective-permute-start(bf16[8,2,2,128,128]{4,3,2,1,0:T(8,128)(2,1)} %fusion), channel_id=1, source_target_pairs={{0,3},{3,0},{4,7},{7,4},{8,11},{11,8},{12,15},{15,12},{16,19},{19,... | collective-permute-start | bytes 3145736 | tf_op jit(solution)/shard_map/ppermute | solution.py:419
  116.1 53.7 %collective-permute-start.15 = (bf16[7,2,2,128,128]{4,3,2,1,0:T(8,128)(2,1)}, bf16[7,2,2,128,128]{4,3,2,1,0:T(8,128)(2,1)S(1)}, u32[]{:S(2)}, u32[]{:S(2)}) collective-permute-start(bf16[7,2,2,128,128]{4,3,2,1,0:T(8,128)(2,1)} %collective-permute-done.13.refs_2_), channel_id=1, source_target_pairs={{0,1},{1,2},{2,3},{4,5},{5,6},{6,7},{8,9},{9,10},{10,11},{12,13},{... | collective-permute-start | bytes 2752520 | tf_op jit(solution)/shard_map/ppermute | solution.py:43
  117.5 57.6 %collective-permute-start.16 = (bf16[7,2,2,128,128]{4,3,2,1,0:T(8,128)(2,1)}, bf16[7,2,2,128,128]{4,3,2,1,0:T(8,128)(2,1)}, u32[]{:S(2)}, u32[]{:S(2)}) collective-permute-start(bf16[7,2,2,128,128]{4,3,2,1,0:T(8,128)(2,1)} %collective-permute-done.14.refs_3_), channel_id=1, source_target_pairs={{1,0},{2,1},{3,2},{5,4},{6,5},{7,6},{9,8},{10,9},{11,10},{13,12},{... | collective-permute-start | bytes 2752520 | tf_op jit(solution)/shard_map/ppermute | solution.py:43
  155.3 35.5 %collective-permute-start.11 = (bf16[6,2,2,128,128]{4,3,2,1,0:T(8,128)(2,1)S(1)}, bf16[6,2,2,128,128]{4,3,2,1,0:T(8,128)(2,1)}, u32[]{:S(2)}, u32[]{:S(2)}) collective-permute-start(bf16[6,2,2,128,128]{4,3,2,1,0:T(8,128)(2,1)S(1)} %collective-permute-done.10.refs_1_), channel_id=1, source_target_pairs={{1,0},{2,1},{3,2},{5,4},{6,5},{7,6},{9,8},{10,9},{11,10},{13,12},{... | collective-permute-start | bytes 2359304 | tf_op jit(solution)/shard_map/ppermute | solution.py:43
  156.6 34.2 %collective-permute-start.9 = (bf16[6,2,2,128,128]{4,3,2,1,0:T(8,128)(2,1)}, bf16[6,2,2,128,128]{4,3,2,1,0:T(8,128)(2,1)S(1)}, u32[]{:S(2)}, u32[]{:S(2)}) collective-permute-start(bf16[6,2,2,128,128]{4,3,2,1,0:T(8,128)(2,1)} %collective-permute-done.8.refs_0_), channel_id=1, source_target_pairs={{0,1},{1,2},{2,3},{4,5},{5,6},{6,7},{8,9},{9,10},{10,11},{12,13},{... | collective-permute-start | bytes 2359304 | tf_op jit(solution)/shard_map/ppermute | solution.py:43

commit v9 on v8

--- a/solution.py
+++ b/solution.py
@@ -32,7 +32,7 @@
 smoothing = 2.0 / 3.0
 MEMBERS = 2
 ROWS_PER_STEP = 4
-ROWS_PER_CHUNK = 8
+ROWS_PER_CHUNK = 16
 UNROLL = 8
 NT = (((1,), (1,)), ((), ()))
 
@@ -153,7 +153,7 @@
 def partial_kernel(members, taps, tiles, sources, slots, ends, *refs):
     a_tiles, dinv_hbm, *tents = refs[:6]
     right_own, *outs, behind, ahead, right_out = refs[6:14]
-    a_held, dinv, tent, right, left, sems = refs[14:]
+    a_held, dinv, tent, right, left, held, sems = refs[14:]
     tile = dinv.shape[-1]
     rows = dinv.shape[0]
     chunks = rows // ROWS_PER_CHUNK
@@ -177,41 +177,56 @@
     )
     for copy in tent_copies:
         copy.start()
+    a_copy(0).start()
     dinv_copy.start()
-    for c in range(chunks):
+    right[: outer * tile, :] = jnp.zeros((outer * tile, right.shape[1]), right.dtype)
+    left[...] = jnp.zeros_like(left)
+    held[...] = jnp.zeros_like(held)
+    for copy in tent_copies:
+        copy.wait()
+    for c in range(1, chunks):
         a_copy(c).start()
     own_copy.start()
-    right[: outer * tile, :] = jnp.zeros((outer * tile, right.shape[1]), right.dtype)
-    left[...] = jnp.zeros_like(left)
-    for copy in tent_copies:
-        copy.wait()
     dinv_copy.wait()
 
     def one_chunk(c, first):
         a_copy(c).wait()
         last = ends[(c + 1) * (ROWS_PER_CHUNK // ROWS_PER_STEP) - 1]
+        batches = (last - first + UNROLL - 1) // UNROLL
+
+        def entry(at):
+            index = jnp.clip(at, first, last - 1)
+            row = tiles[index] // taps
+            lanes = lane_tiles(jnp.where((at >= first) & (at < last), row, rows), tile)
+            return index, row, (lane_tiles(slots[index], tile), lanes)
 
         def some(n, carry):
-            found = []
+            fresh, older = [], []
             for u in range(UNROLL):
-                at = first + UNROLL * n + u
-                index = jnp.minimum(at, last - 1)
-                number = tiles[index]
-                row = number // taps
+                index, _, at = entry(first + UNROLL * n + u)
                 z = lax.dot_general(
-                    tent[sources[index]], a_held[number], NT, preferred_element_type=jnp.float32
+                    tent[sources[index]],
+                    a_held[tiles[index]],
+                    NT,
+                    preferred_element_type=jnp.float32,
                 ).astype(jnp.bfloat16)
-                smooth = lax.dot_general(z, dinv[row], NT, preferred_element_type=jnp.float32)
-                lanes = lane_tiles(jnp.where(at < last, row, rows), tile)
-                found.append(((lane_tiles(slots[index], tile), lanes), z, smooth))
-            for at, z, smooth in found:
+                fresh.append((at, z))
+                _, row, at = entry(first + UNROLL * (n - 1) + u)
+                smooth = lax.dot_general(
+                    held[(n + 1) % 2, u], dinv[row], NT, preferred_element_type=jnp.float32
+                )
+                older.append((at, smooth))
+            for u, ((at, z), (old_at, smooth)) in enumerate(zip(fresh, older)):
+                held[n % 2, u] = z
                 right[at] = (right[at].astype(jnp.float32) + z.astype(jnp.float32)).astype(
                     jnp.bfloat16
                 )
-                left[at] = (left[at].astype(jnp.float32) - smoothing * smooth).astype(jnp.bfloat16)
+                left[old_at] = (left[old_at].astype(jnp.float32) - smoothing * smooth).astype(
+                    jnp.bfloat16
+                )
             return carry
 
-        lax.fori_loop(0, (last - first + UNROLL - 1) // UNROLL, some, 0)
+        lax.fori_loop(0, jnp.where(batches > 0, batches + 1, 0), some, 0)
         return last
 
     lax.fori_loop(0, chunks, one_chunk, 0)
@@ -241,6 +256,7 @@
                 pltpu.VMEM((4 * rows, tile, tile), jnp.bfloat16),
                 pltpu.VMEM((slots, (rows + 1) * tile), jnp.bfloat16),
                 pltpu.VMEM((outer, (rows + 1) * tile), jnp.bfloat16),
+                pltpu.VMEM((2, UNROLL, tile, tile), jnp.bfloat16),
                 pltpu.SemaphoreType.DMA((rows // ROWS_PER_CHUNK + 7,)),
             ],
         ),

time: 194 us -> 193 us (level)
  starting transfers between devices: 45.5 us -> 42.9 us
    ppermute x16, starting transfers between devices: 43.6 us -> 41 us  [shifted(): return lax.ppermute(x, axis, pairs)]
where the time goes in v9:
time: 193 us; the launch traced here: 191 us
  waiting for transfers between devices  84.2 us (44%)
  Pallas kernels  52.2 us (27%)
  starting transfers between devices  42.9 us (22%)
  local copies, waits for them, and re-layouts  9.77 us (5%)
    ppermute x16, waiting for transfers between devices, shifted(): return lax.ppermute(x, axis, pairs)  84.2 us
    ppermute x16, starting transfers between devices, shifted(): return lax.ppermute(x, axis, pairs)  41 us
    pallas_call x1, Pallas kernels, partial_blocks(): pl.pallas_call(functools.partial(partial_kernel, members, taps), grid_spe...  22.8 us
    pallas_call x1, Pallas kernels, own_slots(): pl.pallas_call(functools.partial(own_kernel, count_y, rows, members, taps...  14.2 us
    pallas_call x4, Pallas kernels, placed(): pl.pallas_call(functools.partial(place_kernel, tuple((p[1:3] for p in pie...  10.8 us
    unnamed x12, local copies, waits for them, and re-layouts  9.67 us
  transfers between devices with their start and end apart: 17, of which 10 were waited for; matrix products, arithmetic and copies ran while one was open for 1% of the time, Pallas kernels for 14%

profile of v9, /device:TPU:0, one launch (start us, length us, event | category | flops | bytes accessed | tf_op | source)
XLA Modules:
  0.0 191.2 jit_solution(12367742641986958227)
XLA Ops:
  0.0 0.0 copy-start.2
  0.0 1.7 copy.11
  1.7 2.4 %collective-permute-start = (bf16[32,128,128]{2,1,0:T(8,128)(2,1)S(1)}, bf16[32,128,128]{2,1,0:T(8,128)(2,1)S(1)}, u32[]{:S(2)}, u32[]{:S(2)}) collective-permute-start(bf16[32,128,128]{2,1,0:T(8,128)(2,1)S(1)} %bitcast.22), channel_id=1, source_target_pairs={{0,4},{4,8},{8,12},{12,16},{16,20},{20,24},{24,28},{1,5},{5,9},{9,... | collective-permute-start | bytes 3145736 | tf_op jit(solution)/shard_map/ppermute | solution.py:43
  4.1 5.3 %collective-permute-start.1 = (bf16[32,128,128]{2,1,0:T(8,128)(2,1)S(1)}, bf16[32,128,128]{2,1,0:T(8,128)(2,1)}, u32[]{:S(2)}, u32[]{:S(2)}) collective-permute-start(bf16[32,128,128]{2,1,0:T(8,128)(2,1)S(1)} %bitcast.23), channel_id=1, source_target_pairs={{0,1},{1,2},{2,3},{4,5},{5,6},{6,7},{8,9},{9,10},{10,11},{12,13},{... | collective-permute-start | bytes 3145736 | tf_op jit(solution)/shard_map/ppermute | solution.py:43
  9.4 1.3 collective-permute-start.2
  10.7 1.3 collective-permute-start.3
  12.0 0.8 copy.10
  12.8 0.1 reshape.12.columns
  12.9 0.1 pad_add_fusion.2.place
  13.0 0.0 copy-start.1
  13.0 1.2 copy-done.1
  14.2 0.0 copy-start.3
  14.2 0.7 copy-done.3
  14.9 14.2 %own_slots.1 = (bf16[256,4096]{1,0:T(8,128)(2,1)S(1)}, bf16[256,4096]{1,0:T(8,128)(2,1)S(1)}, s32[224]{0:T(256)S(1)}, s32[224]{0:T(256)S(1)}, s32[224]{0:T(256)S(1)}, /*index=5*/s32[8]{0:T(128)S(1)}) custom-call(s32[224]{0:T(256)S(1)} %reshape.12.columns, s32[1024]{0:T(1024)S(1)} %copy-done.3, s32[2]{0:T(128)S(1)} %pad_add_fusion.2.place, ...), custom_call_target="tpu_custom_call" | custom-call | flops 1207959552 | bytes 13631488 | tf_op jit(solution)/shard_map/own_slots/pallas_call | solution.py:105
  29.1 0.0 copy-start.4
  29.1 1.3 copy-done.4
  30.4 0.0 collective-permute-done.refs_2_
  30.4 0.9 collective-permute-done.1.refs_3_
  31.3 5.8 %collective-permute-done.2.refs_4_ = bf16[32,128,128]{2,1,0:T(8,128)(2,1)} collective-permute-done((bf16[32,128,128]{2,1,0:T(8,128)(2,1)S(1)}, bf16[32,128,128]{2,1,0:T(8,128)(2,1)}, u32[]{:S(2)}, u32[]{:S(2)}) %collective-permute-start.2) | collective-permute-done | bytes 1048608 | tf_op jit(solution)/shard_map/ppermute | solution.py:43
  37.1 0.0 collective-permute-done.3.refs_5_
  37.1 0.0 copy-done.2
  37.1 22.8 %partial_blocks.1 = (bf16[4,2,2,128,128]{4,3,2,1,0:T(8,128)(2,1)S(1)}, bf16[4,2,2,128,128]{4,3,2,1,0:T(8,128)(2,1)S(1)}, bf16[5,2,2,128,128]{4,3,2,1,0:T(8,128)(...) custom-call(s32[224]{0:T(256)S(1)} %get-tuple-element.23.tiles, ...), custom_call_target="tpu_custom_call" | custom-call | flops 11676942336 | bytes 28311552 | tf_op jit(solution)/shard_map/partial_blocks/pallas_call | solution.py:246
  59.9 3.6 %collective-permute-start.6 = (bf16[5,2,2,128,128]{4,3,2,1,0:T(8,128)(2,1)S(1)}, bf16[5,2,2,128,128]{4,3,2,1,0:T(8,128)(2,1)S(1)}, u32[]{:S(2)}, u32[]{:S(2)}) collective-permute-start(bf16[5,2,2,128,128]{4,3,2,1,0:T(8,128)(2,1)S(1)} %get-tuple-element.30), channel_id=1, source_target_pairs={{0,4},{4,8},{8,12},{12,16},{16,20},{20,24},{24,28},{1,5},{5,9},{9,... | collective-permute-start | bytes 1966088 | tf_op jit(solution)/shard_map/ppermute | solution.py:43
  63.4 1.3 collective-permute-start.7
  64.7 3.9 %collective-permute-start.4 = (bf16[4,2,2,128,128]{4,3,2,1,0:T(8,128)(2,1)S(1)}, bf16[4,2,2,128,128]{4,3,2,1,0:T(8,128)(2,1)S(1)}, u32[]{:S(2)}, u32[]{:S(2)}) collective-permute-start(bf16[4,2,2,128,128]{4,3,2,1,0:T(8,128)(2,1)S(1)} %get-tuple-element.28), channel_id=1, source_target_pairs={{0,1},{1,2},{2,3},{4,5},{5,6},{6,7},{8,9},{9,10},{10,11},{12,13},{... | collective-permute-start | bytes 1572872 | tf_op jit(solution)/shard_map/ppermute | solution.py:43
  68.7 1.5 collective-permute-start.5
  70.2 0.0 copy-start
  70.2 4.0 %copy-done = bf16[1280,4096]{1,0:T(8,128)(2,1)S(1)} copy-done((bf16[1280,4096]{1,0:T(8,128)(2,1)S(1)}, bf16[1280,4096]{1,0:T(8,128)(2,1)}, u32[]{:S(2)}) %copy-start) | copy-done | bytes 10485784
  74.1 3.8 %own_rows.1.refs_4_ = f32[5,2,2,128,128]{4,3,2,1,0:T(8,128)S(1)} custom-call(bf16[256,4096]{1,0:T(8,128)(2,1)S(1)} %get-tuple-element.32.left_own, bf16[1280,4096]{1,0:T(8,128)(2,1)S(1)} %copy-done), custom_call_target="tpu_custom_call" | custom-call | flops 2684354560 | bytes 12582912 | tf_op jit(solution)/shard_map/own_rows/pallas_call | solution.py:293
  77.9 2.8 %collective-permute-done.4.refs_0_ = bf16[4,2,2,128,128]{4,3,2,1,0:T(8,128)(2,1)S(1)} collective-permute-done((bf16[4,2,2,128,128]{4,3,2,1,0:T(8,128)(2,1)S(1)}, bf16[4,2,2,128,128]{4,3,2,1,0:T(8,128)(2,1)S(1)}, u32[]{:S(2)}, u32[]{:S(2)}) %collective-permute-start.4) | collective-permute-done | bytes 524320 | tf_op jit(solution)/shard_map/ppermute | solution.py:43
  80.7 3.5 %collective-permute-done.5.refs_1_ = bf16[4,2,2,128,128]{4,3,2,1,0:T(8,128)(2,1)S(1)} collective-permute-done((bf16[4,2,2,128,128]{4,3,2,1,0:T(8,128)(2,1)S(1)}, bf16[4,2,2,128,128]{4,3,2,1,0:T(8,128)(2,1)S(1)}, u32[]{:S(2)}, u32[]{:S(2)}) %collective-permute-start.5) | collective-permute-done | bytes 524320 | tf_op jit(solution)/shard_map/ppermute | solution.py:43
  84.2 0.0 collective-permute-done.6.refs_2_
  84.2 0.0 collective-permute-done.7.refs_3_
  84.2 0.7 finished_window.1
  84.9 3.2 %collective-permute-start.13 = (bf16[7,2,2,128,128]{4,3,2,1,0:T(8,128)(2,1)S(1)}, bf16[7,2,2,128,128]{4,3,2,1,0:T(8,128)(2,1)}, u32[]{:S(2)}, u32[]{:S(2)}) collective-permute-start(bf16[7,2,2,128,128]{4,3,2,1,0:T(8,128)(2,1)S(1)} %get-tuple-element.37.refs_1_), channel_id=1, source_target_pairs={{0,1},{1,2},{2,3},{4,5},{5,6},{6,7},{8,9},{9,10},{10,11},{12,13},{... | collective-permute-start | bytes 2752520 | tf_op jit(solution)/shard_map/ppermute | solution.py:43
  88.1 1.3 collective-permute-start.14
  89.4 1.3 collective-permute-start.10
  90.7 6.1 %collective-permute-start.8 = (bf16[6,2,2,128,128]{4,3,2,1,0:T(8,128)(2,1)S(1)}, bf16[6,2,2,128,128]{4,3,2,1,0:T(8,128)(2,1)}, u32[]{:S(2)}, u32[]{:S(2)}) collective-permute-start(bf16[6,2,2,128,128]{4,3,2,1,0:T(8,128)(2,1)S(1)} %get-tuple-element.36.refs_0_), channel_id=1, source_target_pairs={{0,1},{1,2},{2,3},{4,5},{5,6},{6,7},{8,9},{9,10},{10,11},{12,13},{... | collective-permute-start | bytes 2359304 | tf_op jit(solution)/shard_map/ppermute | solution.py:43
  96.8 1.3 fusion
  98.1 1.9 collective-permute-start.12
  100.0 0.1 pad_add_fusion.5.row
  100.1 2.0 %placed.4.refs_4_ = bf16[4,2,13,2,128,128]{5,4,3,2,1,0:T(8,128)(2,1)} custom-call(s32[2]{0:T(128)S(1)} %pad_add_fusion.5.row, s32[2]{0:T(128)S(1)} %broadcast_1_valid.2.valid, bf16[6,2,2,128,128]{4,3,2,1,0:T(8,128)(2,1)S(1)} %get-tuple-element.36.refs_0_, bf16[7,2,2,128,128]{4,3,2,1,0:T(8,128)(2,1)S(1)} %get-tuple-element.37.refs_1_), custom_call_target="tpu_custom_call" | custom-call | bytes 5111808 | tf_op jit(solution)/shard_map/placed/pallas_call | solution.py:409
  102.1 5.1 %collective-permute-done.13.refs_2_ = bf16[7,2,2,128,128]{4,3,2,1,0:T(8,128)(2,1)} collective-permute-done((bf16[7,2,2,128,128]{4,3,2,1,0:T(8,128)(2,1)S(1)}, bf16[7,2,2,128,128]{4,3,2,1,0:T(8,128)(2,1)}, u32[]{:S(2)}, u32[]{:S(2)}) %collective-permute-start.13) | collective-permute-done | bytes 917536 | tf_op jit(solution)/shard_map/ppermute | solution.py:43
  107.2 5.7 %collective-permute-done.14.refs_3_ = bf16[7,2,2,128,128]{4,3,2,1,0:T(8,128)(2,1)} collective-permute-done((bf16[7,2,2,128,128]{4,3,2,1,0:T(8,128)(2,1)S(1)}, bf16[7,2,2,128,128]{4,3,2,1,0:T(8,128)(2,1)}, u32[]{:S(2)}, u32[]{:S(2)}) %collective-permute-start.14) | collective-permute-done | bytes 917536 | tf_op jit(solution)/shard_map/ppermute | solution.py:43
  112.9 1.4 collective-permute-start.15
  114.3 1.3 collective-permute-start.16
  115.6 36.5 %collective-permute-done.10.refs_1_ = bf16[6,2,2,128,128]{4,3,2,1,0:T(8,128)(2,1)S(1)} collective-permute-done((bf16[6,2,2,128,128]{4,3,2,1,0:T(8,128)(2,1)S(1)}, bf16[6,2,2,128,128]{4,3,2,1,0:T(8,128)(2,1)S(1)}, u32[]{:S(2)}, u32[]{:S(2)}) %collective-permute-start.10) | collective-permute-done | bytes 786464 | tf_op jit(solution)/shard_map/ppermute | solution.py:43
  152.2 1.3 collective-permute-start.11
  153.5 0.0 collective-permute-done.8.refs_0_
  153.5 4.6 %collective-permute-start.9 = (bf16[6,2,2,128,128]{4,3,2,1,0:T(8,128)(2,1)}, bf16[6,2,2,128,128]{4,3,2,1,0:T(8,128)(2,1)S(1)}, u32[]{:S(2)}, u32[]{:S(2)}) collective-permute-start(bf16[6,2,2,128,128]{4,3,2,1,0:T(8,128)(2,1)} %collective-permute-done.8.refs_0_), channel_id=1, source_target_pairs={{0,1},{1,2},{2,3},{4,5},{5,6},{6,7},{8,9},{9,10},{10,11},{12,13},{... | collective-permute-start | bytes 2359304 | tf_op jit(solution)/shard_map/ppermute | solution.py:43
  158.1 0.1 pad_add_fusion.6.row
  158.2 0.1 add_convert_fusion.valid
  158.3 0.1 pad_add_fusion
  158.3 0.1 pad_add_fusion.3
  158.4 3.4 %placed.5.refs_4_ = bf16[4,2,13,2,128,128]{5,4,3,2,1,0:T(8,128)(2,1)} custom-call(s32[4]{0:T(128)S(1)} %pad_add_fusion.6.row, s32[4]{0:T(128)S(1)} %add_convert_fusion.valid, bf16[6,2,2,128,128]{4,3,2,1,0:T(8,128)(2,1)} %collective-permute-done.8.refs_0_, ...), custom_call_target="tpu_custom_call", output_to_operand_aliasing={{}: (6, {})} | custom-call | bytes 5111808 | tf_op jit(solution)/shard_map/placed/pallas_call | solution.py:409
  161.8 0.0 collective-permute-done.12.refs_0_.refs_1_
  161.8 4.5 %collective-permute-done.15.refs_2_ = bf16[7,2,2,128,128]{4,3,2,1,0:T(8,128)(2,1)S(1)} collective-permute-done((bf16[7,2,2,128,128]{4,3,2,1,0:T(8,128)(2,1)}, bf16[7,2,2,128,128]{4,3,2,1,0:T(8,128)(2,1)S(1)}, u32[]{:S(2)}, u32[]{:S(2)}) %collective-permute-start.15) | collective-permute-done | bytes 917536 | tf_op jit(solution)/shard_map/ppermute | solution.py:43
  166.3 5.6 %collective-permute-done.16.refs_3_ = bf16[7,2,2,128,128]{4,3,2,1,0:T(8,128)(2,1)} collective-permute-done((bf16[7,2,2,128,128]{4,3,2,1,0:T(8,128)(2,1)}, bf16[7,2,2,128,128]{4,3,2,1,0:T(8,128)(2,1)}, u32[]{:S(2)}, u32[]{:S(2)}) %collective-permute-start.16) | collective-permute-done | bytes 917536 | tf_op jit(solution)/shard_map/ppermute | solution.py:43
  171.9 3.1 %placed.6.refs_2_ = bf16[4,2,13,2,128,128]{5,4,3,2,1,0:T(8,128)(2,1)} custom-call(s32[4]{0:T(128)S(1)} %get-tuple-element.41.row, s32[4]{0:T(128)S(1)} %get-tuple-element.42.valid, bf16[8,2,2,128,128]{4,3,2,1,0:T(8,128)(2,1)S(1)} %collective-permute-done.12.refs_0_.refs_1_, ...), custom_call_target="tpu_custom_call", output_to_operand_aliasing={{}: (6, {})} | custom-call | bytes 5111808 | tf_op jit(solution)/shard_map/placed/pallas_call | solution.py:409
  175.1 13.7 %collective-permute-done.11.refs_1_ = bf16[6,2,2,128,128]{4,3,2,1,0:T(8,128)(2,1)} collective-permute-done((bf16[6,2,2,128,128]{4,3,2,1,0:T(8,128)(2,1)S(1)}, bf16[6,2,2,128,128]{4,3,2,1,0:T(8,128)(2,1)}, u32[]{:S(2)}, u32[]{:S(2)}) %collective-permute-start.11) | collective-permute-done | bytes 786464 | tf_op jit(solution)/shard_map/ppermute | solution.py:43
  188.8 0.0 collective-permute-done.9.refs_0_
  188.8 2.3 %placed.7 = bf16[4,2,13,2,128,128]{5,4,3,2,1,0:T(8,128)(2,1)} custom-call(s32[2]{0:T(128)S(1)} %get-tuple-element.43.row, s32[2]{0:T(128)S(1)} %get-tuple-element.44.valid, bf16[6,2,2,128,128]{4,3,2,1,0:T(8,128)(2,1)S(1)} %collective-permute-done.9.refs_0_, ...), custom_call_target="tpu_custom_call", output_to_operand_aliasing={{}: (4, {})} | custom-call | bytes 5111808 | tf_op jit(solution)/shard_map/placed/pallas_call | solution.py:409
  (1 shorter events, 0.0 us)
Async XLA Ops:
  0.0 37.1 %copy-start.2 = (bf16[1,1,32,128,128]{4,3,2,1,0:T(8,128)(2,1)S(1)}, bf16[1,1,32,128,128]{4,3,2,1,0:T(8,128)(2,1)}, u32[]{:S(2)}) copy-start(bf16[1,1,32,128,128]{4,3,2,1,0:T(8,128)(2,1)} %param.8) | copy-start | bytes 3145732
  1.7 28.7 %collective-permute-start = (bf16[32,128,128]{2,1,0:T(8,128)(2,1)S(1)}, bf16[32,128,128]{2,1,0:T(8,128)(2,1)S(1)}, u32[]{:S(2)}, u32[]{:S(2)}) collective-permute-start(bf16[32,128,128]{2,1,0:T(8,128)(2,1)S(1)} %bitcast.22), channel_id=1, source_target_pairs={{0,4},{4,8},{8,12},{12,16},{16,20},{20,24},{24,28},{1,5},{5,9},{9,... | collective-permute-start | bytes 3145736 | tf_op jit(solution)/shard_map/ppermute | solution.py:43
  4.1 27.2 %collective-permute-start.1 = (bf16[32,128,128]{2,1,0:T(8,128)(2,1)S(1)}, bf16[32,128,128]{2,1,0:T(8,128)(2,1)}, u32[]{:S(2)}, u32[]{:S(2)}) collective-permute-start(bf16[32,128,128]{2,1,0:T(8,128)(2,1)S(1)} %bitcast.23), channel_id=1, source_target_pairs={{0,1},{1,2},{2,3},{4,5},{5,6},{6,7},{8,9},{9,10},{10,11},{12,13},{... | collective-permute-start | bytes 3145736 | tf_op jit(solution)/shard_map/ppermute | solution.py:43
  9.4 27.6 %collective-permute-start.2 = (bf16[32,128,128]{2,1,0:T(8,128)(2,1)S(1)}, bf16[32,128,128]{2,1,0:T(8,128)(2,1)}, u32[]{:S(2)}, u32[]{:S(2)}) collective-permute-start(bf16[32,128,128]{2,1,0:T(8,128)(2,1)S(1)} %bitcast.24), channel_id=1, source_target_pairs={{1,0},{2,1},{3,2},{5,4},{6,5},{7,6},{9,8},{10,9},{11,10},{13,12},{... | collective-permute-start | bytes 3145736 | tf_op jit(solution)/shard_map/ppermute | solution.py:43
  10.7 26.4 %collective-permute-start.3 = (bf16[32,128,128]{2,1,0:T(8,128)(2,1)S(1)}, bf16[32,128,128]{2,1,0:T(8,128)(2,1)}, u32[]{:S(2)}, u32[]{:S(2)}) collective-permute-start(bf16[32,128,128]{2,1,0:T(8,128)(2,1)S(1)} %bitcast.25), channel_id=1, source_target_pairs={{4,0},{8,4},{12,8},{16,12},{20,16},{24,20},{28,24},{5,1},{9,5},{13... | collective-permute-start | bytes 3145736 | tf_op jit(solution)/shard_map/ppermute | solution.py:43
  13.0 1.2 copy-start.1
  14.2 0.7 copy-start.3
  29.1 1.3 copy-start.4
  59.9 24.3 %collective-permute-start.6 = (bf16[5,2,2,128,128]{4,3,2,1,0:T(8,128)(2,1)S(1)}, bf16[5,2,2,128,128]{4,3,2,1,0:T(8,128)(2,1)S(1)}, u32[]{:S(2)}, u32[]{:S(2)}) collective-permute-start(bf16[5,2,2,128,128]{4,3,2,1,0:T(8,128)(2,1)S(1)} %get-tuple-element.30), channel_id=1, source_target_pairs={{0,4},{4,8},{8,12},{12,16},{16,20},{20,24},{24,28},{1,5},{5,9},{9,... | collective-permute-start | bytes 1966088 | tf_op jit(solution)/shard_map/ppermute | solution.py:43
  63.4 20.8 %collective-permute-start.7 = (bf16[5,2,2,128,128]{4,3,2,1,0:T(8,128)(2,1)S(1)}, bf16[5,2,2,128,128]{4,3,2,1,0:T(8,128)(2,1)S(1)}, u32[]{:S(2)}, u32[]{:S(2)}) collective-permute-start(bf16[5,2,2,128,128]{4,3,2,1,0:T(8,128)(2,1)S(1)} %get-tuple-element.31), channel_id=1, source_target_pairs={{4,0},{8,4},{12,8},{16,12},{20,16},{24,20},{28,24},{5,1},{9,5},{13... | collective-permute-start | bytes 1966088 | tf_op jit(solution)/shard_map/ppermute | solution.py:43
  64.7 16.0 %collective-permute-start.4 = (bf16[4,2,2,128,128]{4,3,2,1,0:T(8,128)(2,1)S(1)}, bf16[4,2,2,128,128]{4,3,2,1,0:T(8,128)(2,1)S(1)}, u32[]{:S(2)}, u32[]{:S(2)}) collective-permute-start(bf16[4,2,2,128,128]{4,3,2,1,0:T(8,128)(2,1)S(1)} %get-tuple-element.28), channel_id=1, source_target_pairs={{0,1},{1,2},{2,3},{4,5},{5,6},{6,7},{8,9},{9,10},{10,11},{12,13},{... | collective-permute-start | bytes 1572872 | tf_op jit(solution)/shard_map/ppermute | solution.py:43
  68.7 15.5 %collective-permute-start.5 = (bf16[4,2,2,128,128]{4,3,2,1,0:T(8,128)(2,1)S(1)}, bf16[4,2,2,128,128]{4,3,2,1,0:T(8,128)(2,1)S(1)}, u32[]{:S(2)}, u32[]{:S(2)}) collective-permute-start(bf16[4,2,2,128,128]{4,3,2,1,0:T(8,128)(2,1)S(1)} %get-tuple-element.29), channel_id=1, source_target_pairs={{1,0},{2,1},{3,2},{5,4},{6,5},{7,6},{9,8},{10,9},{11,10},{13,12},{... | collective-permute-start | bytes 1572872 | tf_op jit(solution)/shard_map/ppermute | solution.py:43
  70.2 4.0 %copy-start = (bf16[1280,4096]{1,0:T(8,128)(2,1)S(1)}, bf16[1280,4096]{1,0:T(8,128)(2,1)}, u32[]{:S(2)}) copy-start(bf16[1280,4096]{1,0:T(8,128)(2,1)} %get-tuple-element.33.right_all) | copy-start | bytes 31457284
  84.9 22.3 %collective-permute-start.13 = (bf16[7,2,2,128,128]{4,3,2,1,0:T(8,128)(2,1)S(1)}, bf16[7,2,2,128,128]{4,3,2,1,0:T(8,128)(2,1)}, u32[]{:S(2)}, u32[]{:S(2)}) collective-permute-start(bf16[7,2,2,128,128]{4,3,2,1,0:T(8,128)(2,1)S(1)} %get-tuple-element.37.refs_1_), channel_id=1, source_target_pairs={{0,1},{1,2},{2,3},{4,5},{5,6},{6,7},{8,9},{9,10},{10,11},{12,13},{... | collective-permute-start | bytes 2752520 | tf_op jit(solution)/shard_map/ppermute | solution.py:43
  88.1 24.8 %collective-permute-start.14 = (bf16[7,2,2,128,128]{4,3,2,1,0:T(8,128)(2,1)S(1)}, bf16[7,2,2,128,128]{4,3,2,1,0:T(8,128)(2,1)}, u32[]{:S(2)}, u32[]{:S(2)}) collective-permute-start(bf16[7,2,2,128,128]{4,3,2,1,0:T(8,128)(2,1)S(1)} %get-tuple-element.37.refs_1_), channel_id=1, source_target_pairs={{1,0},{2,1},{3,2},{5,4},{6,5},{7,6},{9,8},{10,9},{11,10},{13,12},{... | collective-permute-start | bytes 2752520 | tf_op jit(solution)/shard_map/ppermute | solution.py:43
  89.4 62.8 %collective-permute-start.10 = (bf16[6,2,2,128,128]{4,3,2,1,0:T(8,128)(2,1)S(1)}, bf16[6,2,2,128,128]{4,3,2,1,0:T(8,128)(2,1)S(1)}, u32[]{:S(2)}, u32[]{:S(2)}) collective-permute-start(bf16[6,2,2,128,128]{4,3,2,1,0:T(8,128)(2,1)S(1)} %get-tuple-element.36.refs_0_), channel_id=1, source_target_pairs={{1,0},{2,1},{3,2},{5,4},{6,5},{7,6},{9,8},{10,9},{11,10},{13,12},{... | collective-permute-start | bytes 2359304 | tf_op jit(solution)/shard_map/ppermute | solution.py:43
  90.7 62.7 %collective-permute-start.8 = (bf16[6,2,2,128,128]{4,3,2,1,0:T(8,128)(2,1)S(1)}, bf16[6,2,2,128,128]{4,3,2,1,0:T(8,128)(2,1)}, u32[]{:S(2)}, u32[]{:S(2)}) collective-permute-start(bf16[6,2,2,128,128]{4,3,2,1,0:T(8,128)(2,1)S(1)} %get-tuple-element.36.refs_0_), channel_id=1, source_target_pairs={{0,1},{1,2},{2,3},{4,5},{5,6},{6,7},{8,9},{9,10},{10,11},{12,13},{... | collective-permute-start | bytes 2359304 | tf_op jit(solution)/shard_map/ppermute | solution.py:43
  98.1 63.7 %collective-permute-start.12 = (bf16[8,2,2,128,128]{4,3,2,1,0:T(8,128)(2,1)}, bf16[8,2,2,128,128]{4,3,2,1,0:T(8,128)(2,1)S(1)}, u32[]{:S(2)}, u32[]{:S(2)}) collective-permute-start(bf16[8,2,2,128,128]{4,3,2,1,0:T(8,128)(2,1)} %fusion), channel_id=1, source_target_pairs={{0,3},{3,0},{4,7},{7,4},{8,11},{11,8},{12,15},{15,12},{16,19},{19,... | collective-permute-start | bytes 3145736 | tf_op jit(solution)/shard_map/ppermute | solution.py:435
  112.9 53.4 %collective-permute-start.15 = (bf16[7,2,2,128,128]{4,3,2,1,0:T(8,128)(2,1)}, bf16[7,2,2,128,128]{4,3,2,1,0:T(8,128)(2,1)S(1)}, u32[]{:S(2)}, u32[]{:S(2)}) collective-permute-start(bf16[7,2,2,128,128]{4,3,2,1,0:T(8,128)(2,1)} %collective-permute-done.13.refs_2_), channel_id=1, source_target_pairs={{0,1},{1,2},{2,3},{4,5},{5,6},{6,7},{8,9},{9,10},{10,11},{12,13},{... | collective-permute-start | bytes 2752520 | tf_op jit(solution)/shard_map/ppermute | solution.py:43
  114.3 57.6 %collective-permute-start.16 = (bf16[7,2,2,128,128]{4,3,2,1,0:T(8,128)(2,1)}, bf16[7,2,2,128,128]{4,3,2,1,0:T(8,128)(2,1)}, u32[]{:S(2)}, u32[]{:S(2)}) collective-permute-start(bf16[7,2,2,128,128]{4,3,2,1,0:T(8,128)(2,1)} %collective-permute-done.14.refs_3_), channel_id=1, source_target_pairs={{1,0},{2,1},{3,2},{5,4},{6,5},{7,6},{9,8},{10,9},{11,10},{13,12},{... | collective-permute-start | bytes 2752520 | tf_op jit(solution)/shard_map/ppermute | solution.py:43
  152.2 36.6 %collective-permute-start.11 = (bf16[6,2,2,128,128]{4,3,2,1,0:T(8,128)(2,1)S(1)}, bf16[6,2,2,128,128]{4,3,2,1,0:T(8,128)(2,1)}, u32[]{:S(2)}, u32[]{:S(2)}) collective-permute-start(bf16[6,2,2,128,128]{4,3,2,1,0:T(8,128)(2,1)S(1)} %collective-permute-done.10.refs_1_), channel_id=1, source_target_pairs={{1,0},{2,1},{3,2},{5,4},{6,5},{7,6},{9,8},{10,9},{11,10},{13,12},{... | collective-permute-start | bytes 2359304 | tf_op jit(solution)/shard_map/ppermute | solution.py:43
  153.5 35.3 %collective-permute-start.9 = (bf16[6,2,2,128,128]{4,3,2,1,0:T(8,128)(2,1)}, bf16[6,2,2,128,128]{4,3,2,1,0:T(8,128)(2,1)S(1)}, u32[]{:S(2)}, u32[]{:S(2)}) collective-permute-start(bf16[6,2,2,128,128]{4,3,2,1,0:T(8,128)(2,1)} %collective-permute-done.8.refs_0_), channel_id=1, source_target_pairs={{0,1},{1,2},{2,3},{4,5},{5,6},{6,7},{8,9},{9,10},{10,11},{12,13},{... | collective-permute-start | bytes 2359304 | tf_op jit(solution)/shard_map/ppermute | solution.py:43

commit v10 on v8

--- a/solution.py
+++ b/solution.py
@@ -32,7 +32,6 @@
 smoothing = 2.0 / 3.0
 MEMBERS = 2
 ROWS_PER_STEP = 4
-ROWS_PER_CHUNK = 8
 UNROLL = 8
 NT = (((1,), (1,)), ((), ()))
 
@@ -120,7 +119,7 @@
         out_shape=[jax.ShapeDtypeStruct((members * tile, rows * tile), jnp.bfloat16)] * 2
         + [jax.ShapeDtypeStruct((rows * taps,), jnp.int32)] * 3
         + [jax.ShapeDtypeStruct((steps,), jnp.int32)],
-        compiler_params=pltpu.CompilerParams(vmem_limit_bytes=44 * 1024 * 1024),
+        compiler_params=pltpu.CompilerParams(vmem_limit_bytes=24 * 1024 * 1024),
         cost_estimate=pl.CostEstimate(
             flops=2 * tile**3 * rows * (taps + members),
             bytes_accessed=2 * (a_tiles.size + dinv.size * 6),
@@ -151,70 +150,66 @@
 
 
 def partial_kernel(members, taps, tiles, sources, slots, ends, *refs):
-    a_tiles, dinv_hbm, *tents = refs[:6]
+    a_tiles, dinv, *tents = refs[:6]
     right_own, *outs, behind, ahead, right_out = refs[6:14]
-    a_held, dinv, tent, right, left, sems = refs[14:]
+    tent, right, left, held, sems = refs[14:]
     tile = dinv.shape[-1]
     rows = dinv.shape[0]
-    chunks = rows // ROWS_PER_CHUNK
     outer = 4 * members
-    per = ROWS_PER_CHUNK * taps
     depth = rows * tile
 
-    def a_copy(c):
-        part = pl.ds(c * per, per)
-        return pltpu.make_async_copy(a_tiles.at[part], a_held.at[part], sems.at[c])
-
-    tent_copies = [
-        pltpu.make_async_copy(source, tent.at[pl.ds(d * rows, rows)], sems.at[chunks + d])
+    copies = [
+        pltpu.make_async_copy(source, tent.at[pl.ds(d * rows, rows)], sems.at[d])
         for d, source in zip(HALO_ORDER, tents)
     ]
-    dinv_copy = pltpu.make_async_copy(dinv_hbm, dinv, sems.at[chunks + 4])
     own_part = (pl.ds(outer * tile, members * tile), pl.ds(0, depth))
-    own_copy = pltpu.make_async_copy(right_own, right.at[own_part], sems.at[chunks + 5])
-    out_copy = pltpu.make_async_copy(
-        right.at[:, pl.ds(0, depth)], right_out, sems.at[chunks + 6]
-    )
-    for copy in tent_copies:
+    own_copy = pltpu.make_async_copy(right_own, right.at[own_part], sems.at[4])
+    out_copy = pltpu.make_async_copy(right.at[:, pl.ds(0, depth)], right_out, sems.at[5])
+    for copy in copies:
         copy.start()
-    dinv_copy.start()
-    for c in range(chunks):
-        a_copy(c).start()
     own_copy.start()
     right[: outer * tile, :] = jnp.zeros((outer * tile, right.shape[1]), right.dtype)
     left[...] = jnp.zeros_like(left)
-    for copy in tent_copies:
+    held[...] = jnp.zeros_like(held)
+    for copy in copies:
         copy.wait()
-    dinv_copy.wait()
-
-    def one_chunk(c, first):
-        a_copy(c).wait()
-        last = ends[(c + 1) * (ROWS_PER_CHUNK // ROWS_PER_STEP) - 1]
-
-        def some(n, carry):
-            found = []
-            for u in range(UNROLL):
-                at = first + UNROLL * n + u
-                index = jnp.minimum(at, last - 1)
-                number = tiles[index]
-                row = number // taps
-                z = lax.dot_general(
-                    tent[sources[index]], a_held[number], NT, preferred_element_type=jnp.float32
-                ).astype(jnp.bfloat16)
-                smooth = lax.dot_general(z, dinv[row], NT, preferred_element_type=jnp.float32)
-                lanes = lane_tiles(jnp.where(at < last, row, rows), tile)
-                found.append(((lane_tiles(slots[index], tile), lanes), z, smooth))
-            for at, z, smooth in found:
-                right[at] = (right[at].astype(jnp.float32) + z.astype(jnp.float32)).astype(
-                    jnp.bfloat16
-                )
-                left[at] = (left[at].astype(jnp.float32) - smoothing * smooth).astype(jnp.bfloat16)
-            return carry
-
-        lax.fori_loop(0, (last - first + UNROLL - 1) // UNROLL, some, 0)
-        return last
-
-    lax.fori_loop(0, chunks, one_chunk, 0)
+
+    last = ends[rows // ROWS_PER_STEP - 1]
+    batches = (last + UNROLL - 1) // UNROLL
+
+    def entry(at):
+        index = jnp.clip(at, 0, last - 1)
+        row = tiles[index] // taps
+        lanes = lane_tiles(jnp.where((at >= 0) & (at < last), row, rows), tile)
+        return index, row, (lane_tiles(slots[index], tile), lanes)
+
+    def some(n, carry):
+        fresh, older = [], []
+        for u in range(UNROLL):
+            index, _, at = entry(UNROLL * n + u)
+            z = lax.dot_general(
+                tent[sources[index]],
+                a_tiles[tiles[index]],
+                NT,
+                preferred_element_type=jnp.float32,
+            ).astype(jnp.bfloat16)
+            fresh.append((at, z))
+            _, row, at = entry(UNROLL * (n - 1) + u)
+            smooth = lax.dot_general(
+                held[(n + 1) % 2, u], dinv[row], NT, preferred_element_type=jnp.float32
+            )
+            older.append((at, smooth))
+        for u, ((at, z), (old_at, smooth)) in enumerate(zip(fresh, older)):
+            held[n % 2, u] = z
+            right[at] = (right[at].astype(jnp.float32) + z.astype(jnp.float32)).astype(
+                jnp.bfloat16
+            )
+            left[old_at] = (left[old_at].astype(jnp.float32) - smoothing * smooth).astype(
+                jnp.bfloat16
+            )
+        return carry
+
+    lax.fori_loop(0, jnp.where(batches > 0, batches + 1, 0), some, 0)
     own_copy.wait()
     out_copy.start()
     lone = {d: (CROSS_SHIFTS.index(t), out) for d, t, out in ((0, UP, behind), (1, DOWN, ahead))}
@@ -224,32 +219,29 @@
 
 def partial_blocks(a_tiles, dinv, tents, own_right, lists, members):
     rows, taps, tile = a_tiles.shape[0], a_tiles.shape[1], a_tiles.shape[-1]
-    whole = lambda lead: pl.BlockSpec((lead, members, members, tile, tile), lambda s, *_: (0,) * 5)
     leads = (4, 4, 5, 5, 1, 1)
     outer = 4 * members * tile
     slots = outer + members * tile
+    scalars, inside, anywhere = (
+        pl.BlockSpec(memory_space=space) for space in (pltpu.SMEM, pltpu.VMEM, pl.ANY)
+    )
     return pl.pallas_call(
         functools.partial(partial_kernel, members, taps),
-        grid_spec=pltpu.PrefetchScalarGridSpec(
-            num_scalar_prefetch=4,
-            grid=(1,),
-            in_specs=[pl.BlockSpec(memory_space=pl.ANY)] * 7,
-            out_specs=[whole(lead) for lead in leads] + [pl.BlockSpec(memory_space=pl.ANY)],
-            scratch_shapes=[
-                pltpu.VMEM((rows * taps, tile, tile), jnp.bfloat16),
-                pltpu.VMEM((rows, tile, tile), jnp.bfloat16),
-                pltpu.VMEM((4 * rows, tile, tile), jnp.bfloat16),
-                pltpu.VMEM((slots, (rows + 1) * tile), jnp.bfloat16),
-                pltpu.VMEM((outer, (rows + 1) * tile), jnp.bfloat16),
-                pltpu.SemaphoreType.DMA((rows // ROWS_PER_CHUNK + 7,)),
-            ],
-        ),
+        in_specs=[scalars] * 4 + [inside] * 6 + [anywhere],
+        out_specs=[inside] * 6 + [anywhere],
+        scratch_shapes=[
+            pltpu.VMEM((4 * rows, tile, tile), jnp.bfloat16),
+            pltpu.VMEM((slots, (rows + 1) * tile), jnp.bfloat16),
+            pltpu.VMEM((outer, (rows + 1) * tile), jnp.bfloat16),
+            pltpu.VMEM((2, UNROLL, tile, tile), jnp.bfloat16),
+            pltpu.SemaphoreType.DMA((6,)),
+        ],
         out_shape=[
             jax.ShapeDtypeStruct((lead, members, members, tile, tile), jnp.bfloat16)
             for lead in leads
         ]
         + [jax.ShapeDtypeStruct((slots, rows * tile), jnp.bfloat16)],
-        compiler_params=pltpu.CompilerParams(vmem_limit_bytes=48 * 1024 * 1024),
+        compiler_params=pltpu.CompilerParams(vmem_limit_bytes=36 * 1024 * 1024),
         cost_estimate=pl.CostEstimate(
             flops=2 * tile**3 * rows * (taps + 20 * members * members),
             bytes_accessed=2 * (a_tiles.size + 20 * dinv.size),

time: 194 us -> 193 us (level)
  transfers between devices with their start and end apart: 17 -> 17, of which waited for: 10 -> 10; matrix products, arithmetic and copies ran while one was open for 1% -> 1% of each run, Pallas kernels for 14% -> 13%
where the time goes in v10:
time: 193 us
  waiting for transfers between devices  83.5 us (43%)
  Pallas kernels  50.6 us (26%)
  starting transfers between devices  45 us (23%)
  local copies, waits for them, and re-layouts  11.5 us (6%)
    ppermute x16, waiting for transfers between devices, shifted(): return lax.ppermute(x, axis, pairs)  83.5 us
    ppermute x16, starting transfers between devices, shifted(): return lax.ppermute(x, axis, pairs)  43.1 us
    pallas_call x1, Pallas kernels, partial_blocks(): pl.pallas_call(functools.partial(partial_kernel, members, taps), in_specs...  22.4 us
    pallas_call x1, Pallas kernels, own_slots(): pl.pallas_call(functools.partial(own_kernel, count_y, rows, members, taps...  12.9 us
    unnamed x12, local copies, waits for them, and re-layouts  11.4 us
    pallas_call x4, Pallas kernels, placed(): pl.pallas_call(functools.partial(place_kernel, tuple((p[1:3] for p in pie...  10.8 us
  transfers between devices with their start and end apart: 17, of which 10 were waited for; matrix products, arithmetic and copies ran while one was open for 1% of the time, Pallas kernels for 13%

profile of v10, /device:TPU:0, one launch (start us, length us, event | category | flops | bytes accessed | tf_op | source)
XLA Modules:
  0.0 192.7 jit_solution(14125628157708468520)
XLA Ops:
  0.0 1.6 copy.11
  1.6 3.4 %collective-permute-start = (bf16[32,128,128]{2,1,0:T(8,128)(2,1)S(1)}, bf16[32,128,128]{2,1,0:T(8,128)(2,1)}, u32[]{:S(2)}, u32[]{:S(2)}) collective-permute-start(bf16[32,128,128]{2,1,0:T(8,128)(2,1)S(1)} %bitcast.24), channel_id=1, source_target_pairs={{0,4},{4,8},{8,12},{12,16},{16,20},{20,24},{24,28},{1,5},{5,9},{9,... | collective-permute-start | bytes 3145736 | tf_op jit(solution)/shard_map/ppermute | solution.py:42
  5.0 5.3 %collective-permute-start.1 = (bf16[32,128,128]{2,1,0:T(8,128)(2,1)S(1)}, bf16[32,128,128]{2,1,0:T(8,128)(2,1)}, u32[]{:S(2)}, u32[]{:S(2)}) collective-permute-start(bf16[32,128,128]{2,1,0:T(8,128)(2,1)S(1)} %bitcast.25), channel_id=1, source_target_pairs={{0,1},{1,2},{2,3},{4,5},{5,6},{6,7},{8,9},{9,10},{10,11},{12,13},{... | collective-permute-start | bytes 3145736 | tf_op jit(solution)/shard_map/ppermute | solution.py:42
  10.3 1.3 collective-permute-start.2
  11.6 1.3 collective-permute-start.3
  12.9 0.8 copy.10
  13.6 0.1 reshape.12.columns
  13.7 0.1 pad_add_fusion.2.place
  13.8 0.0 copy-start.1
  13.8 3.1 %copy-done.1 = bf16[1,1,32,7,128,128]{5,4,3,2,1,0:T(8,128)(2,1)S(1)} copy-done((bf16[1,1,32,7,128,128]{5,4,3,2,1,0:T(8,128)(2,1)S(1)}, bf16[1,1,32,7,128,128]{5,4,3,2,1,0:T(8,128)(2,1)}, u32[]{:S(2)}) %copy-start.1) | copy-done | bytes 7340056
  16.9 0.0 copy-start.3
  16.9 1.2 copy-done.3
  18.2 0.0 copy-start.4
  18.2 0.7 copy-done.4
  18.8 0.0 copy-start.2
  18.8 12.9 %own_slots.1 = (bf16[256,4096]{1,0:T(8,128)(2,1)S(1)}, bf16[256,4096]{1,0:T(8,128)(2,1)S(1)}, s32[224]{0:T(256)S(1)}, s32[224]{0:T(256)S(1)}, s32[224]{0:T(256)S(1)}, /*index=5*/s32[8]{0:T(128)S(1)}) custom-call(s32[224]{0:T(256)S(1)} %reshape.12.columns, s32[1024]{0:T(1024)S(1)} %copy-done.4, s32[2]{0:T(128)S(1)} %pad_add_fusion.2.place, ...), custom_call_target="tpu_custom_call" | custom-call | flops 1207959552 | bytes 13631488 | tf_op jit(solution)/shard_map/own_slots/pallas_call | solution.py:104
  31.8 0.0 collective-permute-done.refs_2_
  31.8 0.8 collective-permute-done.1.refs_3_
  32.6 5.2 %collective-permute-done.2.refs_4_ = bf16[32,128,128]{2,1,0:T(8,128)(2,1)} collective-permute-done((bf16[32,128,128]{2,1,0:T(8,128)(2,1)S(1)}, bf16[32,128,128]{2,1,0:T(8,128)(2,1)}, u32[]{:S(2)}, u32[]{:S(2)}) %collective-permute-start.2) | collective-permute-done | bytes 1048608 | tf_op jit(solution)/shard_map/ppermute | solution.py:42
  37.9 0.0 collective-permute-done.3.refs_5_
  37.9 0.0 copy-done.2
  37.9 22.4 %partial_blocks.1 = (bf16[4,2,2,128,128]{4,3,2,1,0:T(8,128)(2,1)S(1)}, bf16[4,2,2,128,128]{4,3,2,1,0:T(8,128)(2,1)S(1)}, bf16[5,2,2,128,128]{4,3,2,1,0:T(8,128)(...) custom-call(s32[224]{0:T(256)S(1)} %get-tuple-element.23.tiles, ...), custom_call_target="tpu_custom_call" | custom-call | flops 11676942336 | bytes 28311552 | tf_op jit(solution)/shard_map/partial_blocks/pallas_call | solution.py:228
  60.3 2.6 %collective-permute-start.6 = (bf16[5,2,2,128,128]{4,3,2,1,0:T(8,128)(2,1)S(1)}, bf16[5,2,2,128,128]{4,3,2,1,0:T(8,128)(2,1)S(1)}, u32[]{:S(2)}, u32[]{:S(2)}) collective-permute-start(bf16[5,2,2,128,128]{4,3,2,1,0:T(8,128)(2,1)S(1)} %get-tuple-element.30), channel_id=1, source_target_pairs={{0,4},{4,8},{8,12},{12,16},{16,20},{20,24},{24,28},{1,5},{5,9},{9,... | collective-permute-start | bytes 1966088 | tf_op jit(solution)/shard_map/ppermute | solution.py:42
  62.9 1.3 collective-permute-start.7
  64.2 3.5 %collective-permute-start.4 = (bf16[4,2,2,128,128]{4,3,2,1,0:T(8,128)(2,1)S(1)}, bf16[4,2,2,128,128]{4,3,2,1,0:T(8,128)(2,1)S(1)}, u32[]{:S(2)}, u32[]{:S(2)}) collective-permute-start(bf16[4,2,2,128,128]{4,3,2,1,0:T(8,128)(2,1)S(1)} %get-tuple-element.28), channel_id=1, source_target_pairs={{0,1},{1,2},{2,3},{4,5},{5,6},{6,7},{8,9},{9,10},{10,11},{12,13},{... | collective-permute-start | bytes 1572872 | tf_op jit(solution)/shard_map/ppermute | solution.py:42
  67.7 1.5 collective-permute-start.5
  69.2 0.0 copy-start
  69.2 4.0 %copy-done = bf16[1280,4096]{1,0:T(8,128)(2,1)S(1)} copy-done((bf16[1280,4096]{1,0:T(8,128)(2,1)S(1)}, bf16[1280,4096]{1,0:T(8,128)(2,1)}, u32[]{:S(2)}) %copy-start) | copy-done | bytes 10485784
  73.1 3.8 %own_rows.1.refs_4_ = f32[5,2,2,128,128]{4,3,2,1,0:T(8,128)S(1)} custom-call(bf16[256,4096]{1,0:T(8,128)(2,1)S(1)} %get-tuple-element.32.left_own, bf16[1280,4096]{1,0:T(8,128)(2,1)S(1)} %copy-done), custom_call_target="tpu_custom_call" | custom-call | flops 2684354560 | bytes 12582912 | tf_op jit(solution)/shard_map/own_rows/pallas_call | solution.py:269
  76.9 1.3 collective-permute-done.4.refs_0_
  78.2 5.7 %collective-permute-done.5.refs_1_ = bf16[4,2,2,128,128]{4,3,2,1,0:T(8,128)(2,1)S(1)} collective-permute-done((bf16[4,2,2,128,128]{4,3,2,1,0:T(8,128)(2,1)S(1)}, bf16[4,2,2,128,128]{4,3,2,1,0:T(8,128)(2,1)S(1)}, u32[]{:S(2)}, u32[]{:S(2)}) %collective-permute-start.5) | collective-permute-done | bytes 524320 | tf_op jit(solution)/shard_map/ppermute | solution.py:42
  83.9 0.0 collective-permute-done.6.refs_2_
  83.9 0.0 collective-permute-done.7.refs_3_
  83.9 0.7 finished_window.1
  84.6 5.8 %collective-permute-start.13 = (bf16[7,2,2,128,128]{4,3,2,1,0:T(8,128)(2,1)S(1)}, bf16[7,2,2,128,128]{4,3,2,1,0:T(8,128)(2,1)}, u32[]{:S(2)}, u32[]{:S(2)}) collective-permute-start(bf16[7,2,2,128,128]{4,3,2,1,0:T(8,128)(2,1)S(1)} %get-tuple-element.37.refs_1_), channel_id=1, source_target_pairs={{0,1},{1,2},{2,3},{4,5},{5,6},{6,7},{8,9},{9,10},{10,11},{12,13},{... | collective-permute-start | bytes 2752520 | tf_op jit(solution)/shard_map/ppermute | solution.py:42
  90.4 1.3 collective-permute-start.14
  91.7 1.3 collective-permute-start.10
  93.0 6.1 %collective-permute-start.8 = (bf16[6,2,2,128,128]{4,3,2,1,0:T(8,128)(2,1)S(1)}, bf16[6,2,2,128,128]{4,3,2,1,0:T(8,128)(2,1)}, u32[]{:S(2)}, u32[]{:S(2)}) collective-permute-start(bf16[6,2,2,128,128]{4,3,2,1,0:T(8,128)(2,1)S(1)} %get-tuple-element.36.refs_0_), channel_id=1, source_target_pairs={{0,1},{1,2},{2,3},{4,5},{5,6},{6,7},{8,9},{9,10},{10,11},{12,13},{... | collective-permute-start | bytes 2359304 | tf_op jit(solution)/shard_map/ppermute | solution.py:42
  99.0 1.3 fusion
  100.3 1.9 collective-permute-start.12
  102.3 0.1 pad_add_fusion.5.row
  102.3 2.0 %placed.4.refs_4_ = bf16[4,2,13,2,128,128]{5,4,3,2,1,0:T(8,128)(2,1)} custom-call(s32[2]{0:T(128)S(1)} %pad_add_fusion.5.row, s32[2]{0:T(128)S(1)} %broadcast_1_valid.2.valid, bf16[6,2,2,128,128]{4,3,2,1,0:T(8,128)(2,1)S(1)} %get-tuple-element.36.refs_0_, bf16[7,2,2,128,128]{4,3,2,1,0:T(8,128)(2,1)S(1)} %get-tuple-element.37.refs_1_), custom_call_target="tpu_custom_call" | custom-call | bytes 5111808 | tf_op jit(solution)/shard_map/placed/pallas_call | solution.py:385
  104.4 5.8 %collective-permute-done.13.refs_2_ = bf16[7,2,2,128,128]{4,3,2,1,0:T(8,128)(2,1)} collective-permute-done((bf16[7,2,2,128,128]{4,3,2,1,0:T(8,128)(2,1)S(1)}, bf16[7,2,2,128,128]{4,3,2,1,0:T(8,128)(2,1)}, u32[]{:S(2)}, u32[]{:S(2)}) %collective-permute-start.13) | collective-permute-done | bytes 917536 | tf_op jit(solution)/shard_map/ppermute | solution.py:42
  110.1 5.5 %collective-permute-done.14.refs_3_ = bf16[7,2,2,128,128]{4,3,2,1,0:T(8,128)(2,1)} collective-permute-done((bf16[7,2,2,128,128]{4,3,2,1,0:T(8,128)(2,1)S(1)}, bf16[7,2,2,128,128]{4,3,2,1,0:T(8,128)(2,1)}, u32[]{:S(2)}, u32[]{:S(2)}) %collective-permute-start.14) | collective-permute-done | bytes 917536 | tf_op jit(solution)/shard_map/ppermute | solution.py:42
  115.6 1.4 collective-permute-start.15
  117.0 1.3 collective-permute-start.16
  118.3 36.5 %collective-permute-done.10.refs_1_ = bf16[6,2,2,128,128]{4,3,2,1,0:T(8,128)(2,1)S(1)} collective-permute-done((bf16[6,2,2,128,128]{4,3,2,1,0:T(8,128)(2,1)S(1)}, bf16[6,2,2,128,128]{4,3,2,1,0:T(8,128)(2,1)S(1)}, u32[]{:S(2)}, u32[]{:S(2)}) %collective-permute-start.10) | collective-permute-done | bytes 786464 | tf_op jit(solution)/shard_map/ppermute | solution.py:42
  154.8 1.3 collective-permute-start.11
  156.1 0.0 collective-permute-done.8.refs_0_
  156.1 4.6 %collective-permute-start.9 = (bf16[6,2,2,128,128]{4,3,2,1,0:T(8,128)(2,1)}, bf16[6,2,2,128,128]{4,3,2,1,0:T(8,128)(2,1)S(1)}, u32[]{:S(2)}, u32[]{:S(2)}) collective-permute-start(bf16[6,2,2,128,128]{4,3,2,1,0:T(8,128)(2,1)} %collective-permute-done.8.refs_0_), channel_id=1, source_target_pairs={{0,1},{1,2},{2,3},{4,5},{5,6},{6,7},{8,9},{9,10},{10,11},{12,13},{... | collective-permute-start | bytes 2359304 | tf_op jit(solution)/shard_map/ppermute | solution.py:42
  160.7 0.1 pad_add_fusion.6.row
  160.8 0.1 add_convert_fusion.valid
  160.9 0.1 pad_add_fusion
  161.0 0.1 pad_add_fusion.3
  161.1 3.4 %placed.5.refs_4_ = bf16[4,2,13,2,128,128]{5,4,3,2,1,0:T(8,128)(2,1)} custom-call(s32[4]{0:T(128)S(1)} %pad_add_fusion.6.row, s32[4]{0:T(128)S(1)} %add_convert_fusion.valid, bf16[6,2,2,128,128]{4,3,2,1,0:T(8,128)(2,1)} %collective-permute-done.8.refs_0_, ...), custom_call_target="tpu_custom_call", output_to_operand_aliasing={{}: (6, {})} | custom-call | bytes 5111808 | tf_op jit(solution)/shard_map/placed/pallas_call | solution.py:385
  164.4 0.0 collective-permute-done.12.refs_0_.refs_1_
  164.4 4.8 %collective-permute-done.15.refs_2_ = bf16[7,2,2,128,128]{4,3,2,1,0:T(8,128)(2,1)S(1)} collective-permute-done((bf16[7,2,2,128,128]{4,3,2,1,0:T(8,128)(2,1)}, bf16[7,2,2,128,128]{4,3,2,1,0:T(8,128)(2,1)S(1)}, u32[]{:S(2)}, u32[]{:S(2)}) %collective-permute-start.15) | collective-permute-done | bytes 917536 | tf_op jit(solution)/shard_map/ppermute | solution.py:42
  169.3 5.3 %collective-permute-done.16.refs_3_ = bf16[7,2,2,128,128]{4,3,2,1,0:T(8,128)(2,1)} collective-permute-done((bf16[7,2,2,128,128]{4,3,2,1,0:T(8,128)(2,1)}, bf16[7,2,2,128,128]{4,3,2,1,0:T(8,128)(2,1)}, u32[]{:S(2)}, u32[]{:S(2)}) %collective-permute-start.16) | collective-permute-done | bytes 917536 | tf_op jit(solution)/shard_map/ppermute | solution.py:42
  174.6 3.1 %placed.6.refs_2_ = bf16[4,2,13,2,128,128]{5,4,3,2,1,0:T(8,128)(2,1)} custom-call(s32[4]{0:T(128)S(1)} %get-tuple-element.41.row, s32[4]{0:T(128)S(1)} %get-tuple-element.42.valid, bf16[8,2,2,128,128]{4,3,2,1,0:T(8,128)(2,1)S(1)} %collective-permute-done.12.refs_0_.refs_1_, ...), custom_call_target="tpu_custom_call", output_to_operand_aliasing={{}: (6, {})} | custom-call | bytes 5111808 | tf_op jit(solution)/shard_map/placed/pallas_call | solution.py:385
  177.7 12.6 %collective-permute-done.11.refs_1_ = bf16[6,2,2,128,128]{4,3,2,1,0:T(8,128)(2,1)} collective-permute-done((bf16[6,2,2,128,128]{4,3,2,1,0:T(8,128)(2,1)S(1)}, bf16[6,2,2,128,128]{4,3,2,1,0:T(8,128)(2,1)}, u32[]{:S(2)}, u32[]{:S(2)}) %collective-permute-start.11) | collective-permute-done | bytes 786464 | tf_op jit(solution)/shard_map/ppermute | solution.py:42
  190.3 0.0 collective-permute-done.9.refs_0_
  190.3 2.3 %placed.7 = bf16[4,2,13,2,128,128]{5,4,3,2,1,0:T(8,128)(2,1)} custom-call(s32[2]{0:T(128)S(1)} %get-tuple-element.43.row, s32[2]{0:T(128)S(1)} %get-tuple-element.44.valid, bf16[6,2,2,128,128]{4,3,2,1,0:T(8,128)(2,1)S(1)} %collective-permute-done.9.refs_0_, ...), custom_call_target="tpu_custom_call", output_to_operand_aliasing={{}: (4, {})} | custom-call | bytes 5111808 | tf_op jit(solution)/shard_map/placed/pallas_call | solution.py:385
  (1 shorter events, 0.0 us)
Async XLA Ops:
  1.6 30.2 %collective-permute-start = (bf16[32,128,128]{2,1,0:T(8,128)(2,1)S(1)}, bf16[32,128,128]{2,1,0:T(8,128)(2,1)}, u32[]{:S(2)}, u32[]{:S(2)}) collective-permute-start(bf16[32,128,128]{2,1,0:T(8,128)(2,1)S(1)} %bitcast.24), channel_id=1, source_target_pairs={{0,4},{4,8},{8,12},{12,16},{16,20},{20,24},{24,28},{1,5},{5,9},{9,... | collective-permute-start | bytes 3145736 | tf_op jit(solution)/shard_map/ppermute | solution.py:42
  5.0 27.7 %collective-permute-start.1 = (bf16[32,128,128]{2,1,0:T(8,128)(2,1)S(1)}, bf16[32,128,128]{2,1,0:T(8,128)(2,1)}, u32[]{:S(2)}, u32[]{:S(2)}) collective-permute-start(bf16[32,128,128]{2,1,0:T(8,128)(2,1)S(1)} %bitcast.25), channel_id=1, source_target_pairs={{0,1},{1,2},{2,3},{4,5},{5,6},{6,7},{8,9},{9,10},{10,11},{12,13},{... | collective-permute-start | bytes 3145736 | tf_op jit(solution)/shard_map/ppermute | solution.py:42
  10.3 27.6 %collective-permute-start.2 = (bf16[32,128,128]{2,1,0:T(8,128)(2,1)S(1)}, bf16[32,128,128]{2,1,0:T(8,128)(2,1)}, u32[]{:S(2)}, u32[]{:S(2)}) collective-permute-start(bf16[32,128,128]{2,1,0:T(8,128)(2,1)S(1)} %bitcast.26), channel_id=1, source_target_pairs={{1,0},{2,1},{3,2},{5,4},{6,5},{7,6},{9,8},{10,9},{11,10},{13,12},{... | collective-permute-start | bytes 3145736 | tf_op jit(solution)/shard_map/ppermute | solution.py:42
  11.6 26.3 %collective-permute-start.3 = (bf16[32,128,128]{2,1,0:T(8,128)(2,1)S(1)}, bf16[32,128,128]{2,1,0:T(8,128)(2,1)}, u32[]{:S(2)}, u32[]{:S(2)}) collective-permute-start(bf16[32,128,128]{2,1,0:T(8,128)(2,1)S(1)} %bitcast.27), channel_id=1, source_target_pairs={{4,0},{8,4},{12,8},{16,12},{20,16},{24,20},{28,24},{5,1},{9,5},{13... | collective-permute-start | bytes 3145736 | tf_op jit(solution)/shard_map/ppermute | solution.py:42
  13.8 3.1 %copy-start.1 = (bf16[1,1,32,7,128,128]{5,4,3,2,1,0:T(8,128)(2,1)S(1)}, bf16[1,1,32,7,128,128]{5,4,3,2,1,0:T(8,128)(2,1)}, u32[]{:S(2)}) copy-start(bf16[1,1,32,7,128,128]{5,4,3,2,1,0:T(8,128)(2,1)} %param.5) | copy-start | bytes 22020100
  16.9 1.2 copy-start.3
  18.2 0.7 copy-start.4
  18.8 19.0 %copy-start.2 = (bf16[1,1,32,7,128,128]{5,4,3,2,1,0:T(8,128)(2,1)S(1)}, bf16[1,1,32,7,128,128]{5,4,3,2,1,0:T(8,128)(2,1)}, u32[]{:S(2)}) copy-start(bf16[1,1,32,7,128,128]{5,4,3,2,1,0:T(8,128)(2,1)} %param.5) | copy-start | bytes 22020100
  60.3 23.6 %collective-permute-start.6 = (bf16[5,2,2,128,128]{4,3,2,1,0:T(8,128)(2,1)S(1)}, bf16[5,2,2,128,128]{4,3,2,1,0:T(8,128)(2,1)S(1)}, u32[]{:S(2)}, u32[]{:S(2)}) collective-permute-start(bf16[5,2,2,128,128]{4,3,2,1,0:T(8,128)(2,1)S(1)} %get-tuple-element.30), channel_id=1, source_target_pairs={{0,4},{4,8},{8,12},{12,16},{16,20},{20,24},{24,28},{1,5},{5,9},{9,... | collective-permute-start | bytes 1966088 | tf_op jit(solution)/shard_map/ppermute | solution.py:42
  62.9 21.0 %collective-permute-start.7 = (bf16[5,2,2,128,128]{4,3,2,1,0:T(8,128)(2,1)S(1)}, bf16[5,2,2,128,128]{4,3,2,1,0:T(8,128)(2,1)S(1)}, u32[]{:S(2)}, u32[]{:S(2)}) collective-permute-start(bf16[5,2,2,128,128]{4,3,2,1,0:T(8,128)(2,1)S(1)} %get-tuple-element.31), channel_id=1, source_target_pairs={{4,0},{8,4},{12,8},{16,12},{20,16},{24,20},{28,24},{5,1},{9,5},{13... | collective-permute-start | bytes 1966088 | tf_op jit(solution)/shard_map/ppermute | solution.py:42
  64.2 13.9 %collective-permute-start.4 = (bf16[4,2,2,128,128]{4,3,2,1,0:T(8,128)(2,1)S(1)}, bf16[4,2,2,128,128]{4,3,2,1,0:T(8,128)(2,1)S(1)}, u32[]{:S(2)}, u32[]{:S(2)}) collective-permute-start(bf16[4,2,2,128,128]{4,3,2,1,0:T(8,128)(2,1)S(1)} %get-tuple-element.28), channel_id=1, source_target_pairs={{0,1},{1,2},{2,3},{4,5},{5,6},{6,7},{8,9},{9,10},{10,11},{12,13},{... | collective-permute-start | bytes 1572872 | tf_op jit(solution)/shard_map/ppermute | solution.py:42
  67.7 16.2 %collective-permute-start.5 = (bf16[4,2,2,128,128]{4,3,2,1,0:T(8,128)(2,1)S(1)}, bf16[4,2,2,128,128]{4,3,2,1,0:T(8,128)(2,1)S(1)}, u32[]{:S(2)}, u32[]{:S(2)}) collective-permute-start(bf16[4,2,2,128,128]{4,3,2,1,0:T(8,128)(2,1)S(1)} %get-tuple-element.29), channel_id=1, source_target_pairs={{1,0},{2,1},{3,2},{5,4},{6,5},{7,6},{9,8},{10,9},{11,10},{13,12},{... | collective-permute-start | bytes 1572872 | tf_op jit(solution)/shard_map/ppermute | solution.py:42
  69.2 4.0 %copy-start = (bf16[1280,4096]{1,0:T(8,128)(2,1)S(1)}, bf16[1280,4096]{1,0:T(8,128)(2,1)}, u32[]{:S(2)}) copy-start(bf16[1280,4096]{1,0:T(8,128)(2,1)} %get-tuple-element.33.right_all) | copy-start | bytes 31457284
  84.6 25.6 %collective-permute-start.13 = (bf16[7,2,2,128,128]{4,3,2,1,0:T(8,128)(2,1)S(1)}, bf16[7,2,2,128,128]{4,3,2,1,0:T(8,128)(2,1)}, u32[]{:S(2)}, u32[]{:S(2)}) collective-permute-start(bf16[7,2,2,128,128]{4,3,2,1,0:T(8,128)(2,1)S(1)} %get-tuple-element.37.refs_1_), channel_id=1, source_target_pairs={{0,1},{1,2},{2,3},{4,5},{5,6},{6,7},{8,9},{9,10},{10,11},{12,13},{... | collective-permute-start | bytes 2752520 | tf_op jit(solution)/shard_map/ppermute | solution.py:42
  90.4 25.2 %collective-permute-start.14 = (bf16[7,2,2,128,128]{4,3,2,1,0:T(8,128)(2,1)S(1)}, bf16[7,2,2,128,128]{4,3,2,1,0:T(8,128)(2,1)}, u32[]{:S(2)}, u32[]{:S(2)}) collective-permute-start(bf16[7,2,2,128,128]{4,3,2,1,0:T(8,128)(2,1)S(1)} %get-tuple-element.37.refs_1_), channel_id=1, source_target_pairs={{1,0},{2,1},{3,2},{5,4},{6,5},{7,6},{9,8},{10,9},{11,10},{13,12},{... | collective-permute-start | bytes 2752520 | tf_op jit(solution)/shard_map/ppermute | solution.py:42
  91.7 63.2 %collective-permute-start.10 = (bf16[6,2,2,128,128]{4,3,2,1,0:T(8,128)(2,1)S(1)}, bf16[6,2,2,128,128]{4,3,2,1,0:T(8,128)(2,1)S(1)}, u32[]{:S(2)}, u32[]{:S(2)}) collective-permute-start(bf16[6,2,2,128,128]{4,3,2,1,0:T(8,128)(2,1)S(1)} %get-tuple-element.36.refs_0_), channel_id=1, source_target_pairs={{1,0},{2,1},{3,2},{5,4},{6,5},{7,6},{9,8},{10,9},{11,10},{13,12},{... | collective-permute-start | bytes 2359304 | tf_op jit(solution)/shard_map/ppermute | solution.py:42
  93.0 63.1 %collective-permute-start.8 = (bf16[6,2,2,128,128]{4,3,2,1,0:T(8,128)(2,1)S(1)}, bf16[6,2,2,128,128]{4,3,2,1,0:T(8,128)(2,1)}, u32[]{:S(2)}, u32[]{:S(2)}) collective-permute-start(bf16[6,2,2,128,128]{4,3,2,1,0:T(8,128)(2,1)S(1)} %get-tuple-element.36.refs_0_), channel_id=1, source_target_pairs={{0,1},{1,2},{2,3},{4,5},{5,6},{6,7},{8,9},{9,10},{10,11},{12,13},{... | collective-permute-start | bytes 2359304 | tf_op jit(solution)/shard_map/ppermute | solution.py:42
  100.3 64.1 %collective-permute-start.12 = (bf16[8,2,2,128,128]{4,3,2,1,0:T(8,128)(2,1)}, bf16[8,2,2,128,128]{4,3,2,1,0:T(8,128)(2,1)S(1)}, u32[]{:S(2)}, u32[]{:S(2)}) collective-permute-start(bf16[8,2,2,128,128]{4,3,2,1,0:T(8,128)(2,1)} %fusion), channel_id=1, source_target_pairs={{0,3},{3,0},{4,7},{7,4},{8,11},{11,8},{12,15},{15,12},{16,19},{19,... | collective-permute-start | bytes 3145736 | tf_op jit(solution)/shard_map/ppermute | solution.py:411
  115.6 53.7 %collective-permute-start.15 = (bf16[7,2,2,128,128]{4,3,2,1,0:T(8,128)(2,1)}, bf16[7,2,2,128,128]{4,3,2,1,0:T(8,128)(2,1)S(1)}, u32[]{:S(2)}, u32[]{:S(2)}) collective-permute-start(bf16[7,2,2,128,128]{4,3,2,1,0:T(8,128)(2,1)} %collective-permute-done.13.refs_2_), channel_id=1, source_target_pairs={{0,1},{1,2},{2,3},{4,5},{5,6},{6,7},{8,9},{9,10},{10,11},{12,13},{... | collective-permute-start | bytes 2752520 | tf_op jit(solution)/shard_map/ppermute | solution.py:42
  117.0 57.6 %collective-permute-start.16 = (bf16[7,2,2,128,128]{4,3,2,1,0:T(8,128)(2,1)}, bf16[7,2,2,128,128]{4,3,2,1,0:T(8,128)(2,1)}, u32[]{:S(2)}, u32[]{:S(2)}) collective-permute-start(bf16[7,2,2,128,128]{4,3,2,1,0:T(8,128)(2,1)} %collective-permute-done.14.refs_3_), channel_id=1, source_target_pairs={{1,0},{2,1},{3,2},{5,4},{6,5},{7,6},{9,8},{10,9},{11,10},{13,12},{... | collective-permute-start | bytes 2752520 | tf_op jit(solution)/shard_map/ppermute | solution.py:42
  154.8 35.5 %collective-permute-start.11 = (bf16[6,2,2,128,128]{4,3,2,1,0:T(8,128)(2,1)S(1)}, bf16[6,2,2,128,128]{4,3,2,1,0:T(8,128)(2,1)}, u32[]{:S(2)}, u32[]{:S(2)}) collective-permute-start(bf16[6,2,2,128,128]{4,3,2,1,0:T(8,128)(2,1)S(1)} %collective-permute-done.10.refs_1_), channel_id=1, source_target_pairs={{1,0},{2,1},{3,2},{5,4},{6,5},{7,6},{9,8},{10,9},{11,10},{13,12},{... | collective-permute-start | bytes 2359304 | tf_op jit(solution)/shard_map/ppermute | solution.py:42
  156.1 34.2 %collective-permute-start.9 = (bf16[6,2,2,128,128]{4,3,2,1,0:T(8,128)(2,1)}, bf16[6,2,2,128,128]{4,3,2,1,0:T(8,128)(2,1)S(1)}, u32[]{:S(2)}, u32[]{:S(2)}) collective-permute-start(bf16[6,2,2,128,128]{4,3,2,1,0:T(8,128)(2,1)} %collective-permute-done.8.refs_0_), channel_id=1, source_target_pairs={{0,1},{1,2},{2,3},{4,5},{5,6},{6,7},{8,9},{9,10},{10,11},{12,13},{... | collective-permute-start | bytes 2359304 | tf_op jit(solution)/shard_map/ppermute | solution.py:42

commit v11 on v10

--- a/solution.py
+++ b/solution.py
@@ -10,7 +10,7 @@
 CROSS_SHIFTS = ((0, -1), (0, 1), (-1, 0), (1, 0), (0, 0))
 OWN = 4
 DOWN, UP = CROSS_SHIFTS[:2]
-HALO_ORDER = (2, 0, 1, 3)
+HALO_ORDER = (0, 1, 3, 2)
 WINDOW_SHIFTS = (
     (-2, 0),
     (-1, -1),
@@ -46,6 +46,11 @@
     return pl.ds(pl.multiple_of(g * tile, tile), tile)
 
 
+def swapped(x, axis, first):
+    lows = range(first, lax.axis_size(axis) - 1, 2)
+    return lax.ppermute(x, axis, [(i + a, i + 1 - a) for i in lows for a in (0, 1)])
+
+
 def own_kernel(count_y, rows, members, taps, columns, agg, place, a_ref, dinv_ref, tent, *refs):
     right, left, tiles, sources, slots, ends, found = refs[:7]
     sums = refs[7:]
@@ -77,7 +82,8 @@
                 own_member = member
             else:
                 tiles[listed] = g * taps + k
-                sources[listed] = direction * rows + target % rows
+                seat = jnp.where(direction < 2, direction, 2 + (direction + place[0] + 1) % 2)
+                sources[listed] = seat * rows + target % rows
                 slots[listed] = direction * members + member
                 listed += jnp.where(direction == OWN, 0, 1)
             z = lax.dot_general(
@@ -445,10 +451,10 @@
     inverse = dinv.reshape(rows, tile, tile)
     tent = jnp.swapaxes(ptent.reshape(rows, tile, tile), 1, 2)
     tents = (
-        shifted(tent, "sx", 1),
         shifted(tent, "sy", 1),
         shifted(tent, "sy", -1),
-        shifted(tent, "sx", -1),
+        swapped(tent, "sx", 1),
+        swapped(tent, "sx", 0),
     )
     own_right, own_left, *lists = own_slots(
         coupling,

time: 193 us -> 192 us (level)
  waiting for transfers between devices: 83.5 us -> 80.1 us
    ppermute x0 -> x2, starting transfers between devices: none -> 3.59 us  [swapped(): lax.ppermute(x, axis, [(i + a, i + 1 - a) for i in lows for a in (0, 1)])]
    ppermute x16 -> x14, waiting for transfers between devices: 83.5 us -> 80.1 us  [shifted(): return lax.ppermute(x, axis, pairs)]
    ppermute x16 -> x14, starting transfers between devices: 43.1 us -> 41.4 us  [shifted(): return lax.ppermute(x, axis, pairs)]
  transfers between devices with their start and end apart: 17 -> 17, of which waited for: 10 -> 9; matrix products, arithmetic and copies ran while one was open for 1% -> 1% of each run, Pallas kernels for 13% -> 13%
where the time goes in v11:
time: 192 us; the launch traced here: 191 us
  waiting for transfers between devices  80.1 us (42%)
  Pallas kernels  50.9 us (27%)
  starting transfers between devices  46.9 us (24%)
  local copies, waits for them, and re-layouts  11.5 us (6%)
    ppermute x14, waiting for transfers between devices, shifted(): return lax.ppermute(x, axis, pairs)  80.1 us
    ppermute x14, starting transfers between devices, shifted(): return lax.ppermute(x, axis, pairs)  41.4 us
    pallas_call x1, Pallas kernels, partial_blocks(): pl.pallas_call(functools.partial(partial_kernel, members, taps), in_specs...  22.4 us
    pallas_call x1, Pallas kernels, own_slots(): pl.pallas_call(functools.partial(own_kernel, count_y, rows, members, taps...  13.2 us
    unnamed x12, local copies, waits for them, and re-layouts  11.4 us
    pallas_call x4, Pallas kernels, placed(): pl.pallas_call(functools.partial(place_kernel, tuple((p[1:3] for p in pie...  10.8 us
  transfers between devices with their start and end apart: 17, of which 9 were waited for; matrix products, arithmetic and copies ran while one was open for 1% of the time, Pallas kernels for 13%

profile of v11, /device:TPU:0, one launch (start us, length us, event | category | flops | bytes accessed | tf_op | source)
XLA Modules:
  0.0 191.5 jit_solution(10369551943382475846)
XLA Ops:
  0.0 1.6 copy.11
  1.6 5.9 %collective-permute-start = (bf16[32,128,128]{2,1,0:T(8,128)(2,1)S(1)}, bf16[32,128,128]{2,1,0:T(8,128)(2,1)}, u32[]{:S(2)}, u32[]{:S(2)}) collective-permute-start(bf16[32,128,128]{2,1,0:T(8,128)(2,1)S(1)} %bitcast.24), channel_id=1, source_target_pairs={{0,1},{1,2},{2,3},{4,5},{5,6},{6,7},{8,9},{9,10},{10,11},{12,13},{... | collective-permute-start | bytes 3145736 | tf_op jit(solution)/shard_map/ppermute | solution.py:42
  7.5 1.3 collective-permute-start.1
  8.8 1.7 collective-permute-start.2
  10.5 1.9 collective-permute-start.3
  12.4 0.8 copy.10
  13.2 0.1 reshape.12.columns
  13.3 0.1 pad_add_fusion.2.place
  13.4 0.0 copy-start.1
  13.4 3.1 %copy-done.1 = bf16[1,1,32,7,128,128]{5,4,3,2,1,0:T(8,128)(2,1)S(1)} copy-done((bf16[1,1,32,7,128,128]{5,4,3,2,1,0:T(8,128)(2,1)S(1)}, bf16[1,1,32,7,128,128]{5,4,3,2,1,0:T(8,128)(2,1)}, u32[]{:S(2)}) %copy-start.1) | copy-done | bytes 7340056
  16.5 0.0 copy-start.3
  16.5 1.2 copy-done.3
  17.7 0.0 copy-start.4
  17.7 0.7 copy-done.4
  18.4 0.0 copy-start.2
  18.4 13.2 %own_slots.1 = (bf16[256,4096]{1,0:T(8,128)(2,1)S(1)}, bf16[256,4096]{1,0:T(8,128)(2,1)S(1)}, s32[224]{0:T(256)S(1)}, s32[224]{0:T(256)S(1)}, s32[224]{0:T(256)S(1)}, /*index=5*/s32[8]{0:T(128)S(1)}) custom-call(s32[224]{0:T(256)S(1)} %reshape.12.columns, s32[1024]{0:T(1024)S(1)} %copy-done.4, s32[2]{0:T(128)S(1)} %pad_add_fusion.2.place, ...), custom_call_target="tpu_custom_call" | custom-call | flops 1207959552 | bytes 13631488 | tf_op jit(solution)/shard_map/own_slots/pallas_call | solution.py:110
  31.6 0.0 collective-permute-done.refs_2_
  31.7 2.5 %collective-permute-done.1.refs_3_ = bf16[32,128,128]{2,1,0:T(8,128)(2,1)} collective-permute-done((bf16[32,128,128]{2,1,0:T(8,128)(2,1)S(1)}, bf16[32,128,128]{2,1,0:T(8,128)(2,1)}, u32[]{:S(2)}, u32[]{:S(2)}) %collective-permute-start.1) | collective-permute-done | bytes 1048608 | tf_op jit(solution)/shard_map/ppermute | solution.py:42
  34.2 0.0 collective-permute-done.2.refs_4_
  34.2 0.0 collective-permute-done.3.refs_5_
  34.2 0.0 copy-done.2
  34.2 22.4 %partial_blocks.1 = (bf16[4,2,2,128,128]{4,3,2,1,0:T(8,128)(2,1)S(1)}, bf16[4,2,2,128,128]{4,3,2,1,0:T(8,128)(2,1)S(1)}, bf16[5,2,2,128,128]{4,3,2,1,0:T(8,128)(...) custom-call(s32[224]{0:T(256)S(1)} %get-tuple-element.23.tiles, ...), custom_call_target="tpu_custom_call" | custom-call | flops 11676942336 | bytes 28311552 | tf_op jit(solution)/shard_map/partial_blocks/pallas_call | solution.py:234
  56.6 4.4 %collective-permute-start.6 = (bf16[5,2,2,128,128]{4,3,2,1,0:T(8,128)(2,1)S(1)}, bf16[5,2,2,128,128]{4,3,2,1,0:T(8,128)(2,1)S(1)}, u32[]{:S(2)}, u32[]{:S(2)}) collective-permute-start(bf16[5,2,2,128,128]{4,3,2,1,0:T(8,128)(2,1)S(1)} %get-tuple-element.30), channel_id=1, source_target_pairs={{0,4},{4,8},{8,12},{12,16},{16,20},{20,24},{24,28},{1,5},{5,9},{9,... | collective-permute-start | bytes 1966088 | tf_op jit(solution)/shard_map/ppermute | solution.py:42
  61.1 1.3 collective-permute-start.7
  62.4 6.5 %collective-permute-start.4 = (bf16[4,2,2,128,128]{4,3,2,1,0:T(8,128)(2,1)S(1)}, bf16[4,2,2,128,128]{4,3,2,1,0:T(8,128)(2,1)S(1)}, u32[]{:S(2)}, u32[]{:S(2)}) collective-permute-start(bf16[4,2,2,128,128]{4,3,2,1,0:T(8,128)(2,1)S(1)} %get-tuple-element.28), channel_id=1, source_target_pairs={{0,1},{1,2},{2,3},{4,5},{5,6},{6,7},{8,9},{9,10},{10,11},{12,13},{... | collective-permute-start | bytes 1572872 | tf_op jit(solution)/shard_map/ppermute | solution.py:42
  68.8 1.5 collective-permute-start.5
  70.3 0.0 copy-start
  70.3 4.0 %copy-done = bf16[1280,4096]{1,0:T(8,128)(2,1)S(1)} copy-done((bf16[1280,4096]{1,0:T(8,128)(2,1)S(1)}, bf16[1280,4096]{1,0:T(8,128)(2,1)}, u32[]{:S(2)}) %copy-start) | copy-done | bytes 10485784
  74.3 3.8 %own_rows.1.refs_4_ = f32[5,2,2,128,128]{4,3,2,1,0:T(8,128)S(1)} custom-call(bf16[256,4096]{1,0:T(8,128)(2,1)S(1)} %get-tuple-element.32.left_own, bf16[1280,4096]{1,0:T(8,128)(2,1)S(1)} %copy-done), custom_call_target="tpu_custom_call" | custom-call | flops 2684354560 | bytes 12582912 | tf_op jit(solution)/shard_map/own_rows/pallas_call | solution.py:275
  78.0 2.9 %collective-permute-done.4.refs_0_ = bf16[4,2,2,128,128]{4,3,2,1,0:T(8,128)(2,1)S(1)} collective-permute-done((bf16[4,2,2,128,128]{4,3,2,1,0:T(8,128)(2,1)S(1)}, bf16[4,2,2,128,128]{4,3,2,1,0:T(8,128)(2,1)S(1)}, u32[]{:S(2)}, u32[]{:S(2)}) %collective-permute-start.4) | collective-permute-done | bytes 524320 | tf_op jit(solution)/shard_map/ppermute | solution.py:42
  80.9 4.5 %collective-permute-done.5.refs_1_ = bf16[4,2,2,128,128]{4,3,2,1,0:T(8,128)(2,1)S(1)} collective-permute-done((bf16[4,2,2,128,128]{4,3,2,1,0:T(8,128)(2,1)S(1)}, bf16[4,2,2,128,128]{4,3,2,1,0:T(8,128)(2,1)S(1)}, u32[]{:S(2)}, u32[]{:S(2)}) %collective-permute-start.5) | collective-permute-done | bytes 524320 | tf_op jit(solution)/shard_map/ppermute | solution.py:42
  85.4 0.0 collective-permute-done.6.refs_2_
  85.4 0.0 collective-permute-done.7.refs_3_
  85.4 0.7 finished_window.1
  86.1 3.0 %collective-permute-start.13 = (bf16[7,2,2,128,128]{4,3,2,1,0:T(8,128)(2,1)S(1)}, bf16[7,2,2,128,128]{4,3,2,1,0:T(8,128)(2,1)}, u32[]{:S(2)}, u32[]{:S(2)}) collective-permute-start(bf16[7,2,2,128,128]{4,3,2,1,0:T(8,128)(2,1)S(1)} %get-tuple-element.37.refs_1_), channel_id=1, source_target_pairs={{0,1},{1,2},{2,3},{4,5},{5,6},{6,7},{8,9},{9,10},{10,11},{12,13},{... | collective-permute-start | bytes 2752520 | tf_op jit(solution)/shard_map/ppermute | solution.py:42
  89.1 1.3 collective-permute-start.14
  90.4 1.3 collective-permute-start.10
  91.7 6.1 %collective-permute-start.8 = (bf16[6,2,2,128,128]{4,3,2,1,0:T(8,128)(2,1)S(1)}, bf16[6,2,2,128,128]{4,3,2,1,0:T(8,128)(2,1)}, u32[]{:S(2)}, u32[]{:S(2)}) collective-permute-start(bf16[6,2,2,128,128]{4,3,2,1,0:T(8,128)(2,1)S(1)} %get-tuple-element.36.refs_0_), channel_id=1, source_target_pairs={{0,1},{1,2},{2,3},{4,5},{5,6},{6,7},{8,9},{9,10},{10,11},{12,13},{... | collective-permute-start | bytes 2359304 | tf_op jit(solution)/shard_map/ppermute | solution.py:42
  97.8 1.3 fusion
  99.1 1.9 collective-permute-start.12
  101.0 0.1 pad_add_fusion.5.row
  101.1 2.0 %placed.4.refs_4_ = bf16[4,2,13,2,128,128]{5,4,3,2,1,0:T(8,128)(2,1)} custom-call(s32[2]{0:T(128)S(1)} %pad_add_fusion.5.row, s32[2]{0:T(128)S(1)} %broadcast_1_valid.2.valid, bf16[6,2,2,128,128]{4,3,2,1,0:T(8,128)(2,1)S(1)} %get-tuple-element.36.refs_0_, bf16[7,2,2,128,128]{4,3,2,1,0:T(8,128)(2,1)S(1)} %get-tuple-element.37.refs_1_), custom_call_target="tpu_custom_call" | custom-call | bytes 5111808 | tf_op jit(solution)/shard_map/placed/pallas_call | solution.py:391
  103.1 5.8 %collective-permute-done.13.refs_2_ = bf16[7,2,2,128,128]{4,3,2,1,0:T(8,128)(2,1)} collective-permute-done((bf16[7,2,2,128,128]{4,3,2,1,0:T(8,128)(2,1)S(1)}, bf16[7,2,2,128,128]{4,3,2,1,0:T(8,128)(2,1)}, u32[]{:S(2)}, u32[]{:S(2)}) %collective-permute-start.13) | collective-permute-done | bytes 917536 | tf_op jit(solution)/shard_map/ppermute | solution.py:42
  108.9 5.5 %collective-permute-done.14.refs_3_ = bf16[7,2,2,128,128]{4,3,2,1,0:T(8,128)(2,1)} collective-permute-done((bf16[7,2,2,128,128]{4,3,2,1,0:T(8,128)(2,1)S(1)}, bf16[7,2,2,128,128]{4,3,2,1,0:T(8,128)(2,1)}, u32[]{:S(2)}, u32[]{:S(2)}) %collective-permute-start.14) | collective-permute-done | bytes 917536 | tf_op jit(solution)/shard_map/ppermute | solution.py:42
  114.4 1.7 collective-permute-start.15
  116.0 1.3 collective-permute-start.16
  117.3 36.3 %collective-permute-done.10.refs_1_ = bf16[6,2,2,128,128]{4,3,2,1,0:T(8,128)(2,1)S(1)} collective-permute-done((bf16[6,2,2,128,128]{4,3,2,1,0:T(8,128)(2,1)S(1)}, bf16[6,2,2,128,128]{4,3,2,1,0:T(8,128)(2,1)S(1)}, u32[]{:S(2)}, u32[]{:S(2)}) %collective-permute-start.10) | collective-permute-done | bytes 786464 | tf_op jit(solution)/shard_map/ppermute | solution.py:42
  153.6 1.3 collective-permute-start.11
  154.9 0.0 collective-permute-done.8.refs_0_
  154.9 4.6 %collective-permute-start.9 = (bf16[6,2,2,128,128]{4,3,2,1,0:T(8,128)(2,1)}, bf16[6,2,2,128,128]{4,3,2,1,0:T(8,128)(2,1)S(1)}, u32[]{:S(2)}, u32[]{:S(2)}) collective-permute-start(bf16[6,2,2,128,128]{4,3,2,1,0:T(8,128)(2,1)} %collective-permute-done.8.refs_0_), channel_id=1, source_target_pairs={{0,1},{1,2},{2,3},{4,5},{5,6},{6,7},{8,9},{9,10},{10,11},{12,13},{... | collective-permute-start | bytes 2359304 | tf_op jit(solution)/shard_map/ppermute | solution.py:42
  159.5 0.1 pad_add_fusion.6.row
  159.6 0.1 add_convert_fusion.valid
  159.7 0.1 pad_add_fusion
  159.7 0.1 pad_add_fusion.3
  159.8 3.4 %placed.5.refs_4_ = bf16[4,2,13,2,128,128]{5,4,3,2,1,0:T(8,128)(2,1)} custom-call(s32[4]{0:T(128)S(1)} %pad_add_fusion.6.row, s32[4]{0:T(128)S(1)} %add_convert_fusion.valid, bf16[6,2,2,128,128]{4,3,2,1,0:T(8,128)(2,1)} %collective-permute-done.8.refs_0_, ...), custom_call_target="tpu_custom_call", output_to_operand_aliasing={{}: (6, {})} | custom-call | bytes 5111808 | tf_op jit(solution)/shard_map/placed/pallas_call | solution.py:391
  163.2 0.0 collective-permute-done.12.refs_0_.refs_1_
  163.2 4.8 %collective-permute-done.15.refs_2_ = bf16[7,2,2,128,128]{4,3,2,1,0:T(8,128)(2,1)S(1)} collective-permute-done((bf16[7,2,2,128,128]{4,3,2,1,0:T(8,128)(2,1)}, bf16[7,2,2,128,128]{4,3,2,1,0:T(8,128)(2,1)S(1)}, u32[]{:S(2)}, u32[]{:S(2)}) %collective-permute-start.15) | collective-permute-done | bytes 917536 | tf_op jit(solution)/shard_map/ppermute | solution.py:42
  168.0 5.3 %collective-permute-done.16.refs_3_ = bf16[7,2,2,128,128]{4,3,2,1,0:T(8,128)(2,1)} collective-permute-done((bf16[7,2,2,128,128]{4,3,2,1,0:T(8,128)(2,1)}, bf16[7,2,2,128,128]{4,3,2,1,0:T(8,128)(2,1)}, u32[]{:S(2)}, u32[]{:S(2)}) %collective-permute-start.16) | collective-permute-done | bytes 917536 | tf_op jit(solution)/shard_map/ppermute | solution.py:42
  173.3 3.1 %placed.6.refs_2_ = bf16[4,2,13,2,128,128]{5,4,3,2,1,0:T(8,128)(2,1)} custom-call(s32[4]{0:T(128)S(1)} %get-tuple-element.41.row, s32[4]{0:T(128)S(1)} %get-tuple-element.42.valid, bf16[8,2,2,128,128]{4,3,2,1,0:T(8,128)(2,1)S(1)} %collective-permute-done.12.refs_0_.refs_1_, ...), custom_call_target="tpu_custom_call", output_to_operand_aliasing={{}: (6, {})} | custom-call | bytes 5111808 | tf_op jit(solution)/shard_map/placed/pallas_call | solution.py:391
  176.5 12.6 %collective-permute-done.11.refs_1_ = bf16[6,2,2,128,128]{4,3,2,1,0:T(8,128)(2,1)} collective-permute-done((bf16[6,2,2,128,128]{4,3,2,1,0:T(8,128)(2,1)S(1)}, bf16[6,2,2,128,128]{4,3,2,1,0:T(8,128)(2,1)}, u32[]{:S(2)}, u32[]{:S(2)}) %collective-permute-start.11) | collective-permute-done | bytes 786464 | tf_op jit(solution)/shard_map/ppermute | solution.py:42
  189.1 0.0 collective-permute-done.9.refs_0_
  189.1 2.3 %placed.7 = bf16[4,2,13,2,128,128]{5,4,3,2,1,0:T(8,128)(2,1)} custom-call(s32[2]{0:T(128)S(1)} %get-tuple-element.43.row, s32[2]{0:T(128)S(1)} %get-tuple-element.44.valid, bf16[6,2,2,128,128]{4,3,2,1,0:T(8,128)(2,1)S(1)} %collective-permute-done.9.refs_0_, ...), custom_call_target="tpu_custom_call", output_to_operand_aliasing={{}: (4, {})} | custom-call | bytes 5111808 | tf_op jit(solution)/shard_map/placed/pallas_call | solution.py:391
  (1 shorter events, 0.0 us)
Async XLA Ops:
  1.6 30.0 %collective-permute-start = (bf16[32,128,128]{2,1,0:T(8,128)(2,1)S(1)}, bf16[32,128,128]{2,1,0:T(8,128)(2,1)}, u32[]{:S(2)}, u32[]{:S(2)}) collective-permute-start(bf16[32,128,128]{2,1,0:T(8,128)(2,1)S(1)} %bitcast.24), channel_id=1, source_target_pairs={{0,1},{1,2},{2,3},{4,5},{5,6},{6,7},{8,9},{9,10},{10,11},{12,13},{... | collective-permute-start | bytes 3145736 | tf_op jit(solution)/shard_map/ppermute | solution.py:42
  7.5 26.6 %collective-permute-start.1 = (bf16[32,128,128]{2,1,0:T(8,128)(2,1)S(1)}, bf16[32,128,128]{2,1,0:T(8,128)(2,1)}, u32[]{:S(2)}, u32[]{:S(2)}) collective-permute-start(bf16[32,128,128]{2,1,0:T(8,128)(2,1)S(1)} %bitcast.25), channel_id=1, source_target_pairs={{1,0},{2,1},{3,2},{5,4},{6,5},{7,6},{9,8},{10,9},{11,10},{13,12},{... | collective-permute-start | bytes 3145736 | tf_op jit(solution)/shard_map/ppermute | solution.py:42
  8.8 25.3 %collective-permute-start.2 = (bf16[32,128,128]{2,1,0:T(8,128)(2,1)S(1)}, bf16[32,128,128]{2,1,0:T(8,128)(2,1)}, u32[]{:S(2)}, u32[]{:S(2)}) collective-permute-start(bf16[32,128,128]{2,1,0:T(8,128)(2,1)S(1)} %bitcast.26), channel_id=1, source_target_pairs={{4,8},{8,4},{12,16},{16,12},{20,24},{24,20},{5,9},{9,5},{13,17},{1... | collective-permute-start | bytes 3145736 | tf_op jit(solution)/shard_map/ppermute | solution.py:51
  10.5 23.6 %collective-permute-start.3 = (bf16[32,128,128]{2,1,0:T(8,128)(2,1)S(1)}, bf16[32,128,128]{2,1,0:T(8,128)(2,1)}, u32[]{:S(2)}, u32[]{:S(2)}) collective-permute-start(bf16[32,128,128]{2,1,0:T(8,128)(2,1)S(1)} %bitcast.27), channel_id=1, source_target_pairs={{0,4},{4,0},{8,12},{12,8},{16,20},{20,16},{24,28},{28,24},{1,5},{5... | collective-permute-start | bytes 3145736 | tf_op jit(solution)/shard_map/ppermute | solution.py:51
  13.4 3.1 %copy-start.1 = (bf16[1,1,32,7,128,128]{5,4,3,2,1,0:T(8,128)(2,1)S(1)}, bf16[1,1,32,7,128,128]{5,4,3,2,1,0:T(8,128)(2,1)}, u32[]{:S(2)}) copy-start(bf16[1,1,32,7,128,128]{5,4,3,2,1,0:T(8,128)(2,1)} %param.5) | copy-start | bytes 22020100
  16.5 1.2 copy-start.3
  17.7 0.7 copy-start.4
  18.4 15.8 %copy-start.2 = (bf16[1,1,32,7,128,128]{5,4,3,2,1,0:T(8,128)(2,1)S(1)}, bf16[1,1,32,7,128,128]{5,4,3,2,1,0:T(8,128)(2,1)}, u32[]{:S(2)}) copy-start(bf16[1,1,32,7,128,128]{5,4,3,2,1,0:T(8,128)(2,1)} %param.5) | copy-start | bytes 22020100
  56.6 28.8 %collective-permute-start.6 = (bf16[5,2,2,128,128]{4,3,2,1,0:T(8,128)(2,1)S(1)}, bf16[5,2,2,128,128]{4,3,2,1,0:T(8,128)(2,1)S(1)}, u32[]{:S(2)}, u32[]{:S(2)}) collective-permute-start(bf16[5,2,2,128,128]{4,3,2,1,0:T(8,128)(2,1)S(1)} %get-tuple-element.30), channel_id=1, source_target_pairs={{0,4},{4,8},{8,12},{12,16},{16,20},{20,24},{24,28},{1,5},{5,9},{9,... | collective-permute-start | bytes 1966088 | tf_op jit(solution)/shard_map/ppermute | solution.py:42
  61.1 24.3 %collective-permute-start.7 = (bf16[5,2,2,128,128]{4,3,2,1,0:T(8,128)(2,1)S(1)}, bf16[5,2,2,128,128]{4,3,2,1,0:T(8,128)(2,1)S(1)}, u32[]{:S(2)}, u32[]{:S(2)}) collective-permute-start(bf16[5,2,2,128,128]{4,3,2,1,0:T(8,128)(2,1)S(1)} %get-tuple-element.31), channel_id=1, source_target_pairs={{4,0},{8,4},{12,8},{16,12},{20,16},{24,20},{28,24},{5,1},{9,5},{13... | collective-permute-start | bytes 1966088 | tf_op jit(solution)/shard_map/ppermute | solution.py:42
  62.4 18.6 %collective-permute-start.4 = (bf16[4,2,2,128,128]{4,3,2,1,0:T(8,128)(2,1)S(1)}, bf16[4,2,2,128,128]{4,3,2,1,0:T(8,128)(2,1)S(1)}, u32[]{:S(2)}, u32[]{:S(2)}) collective-permute-start(bf16[4,2,2,128,128]{4,3,2,1,0:T(8,128)(2,1)S(1)} %get-tuple-element.28), channel_id=1, source_target_pairs={{0,1},{1,2},{2,3},{4,5},{5,6},{6,7},{8,9},{9,10},{10,11},{12,13},{... | collective-permute-start | bytes 1572872 | tf_op jit(solution)/shard_map/ppermute | solution.py:42
  68.8 16.6 %collective-permute-start.5 = (bf16[4,2,2,128,128]{4,3,2,1,0:T(8,128)(2,1)S(1)}, bf16[4,2,2,128,128]{4,3,2,1,0:T(8,128)(2,1)S(1)}, u32[]{:S(2)}, u32[]{:S(2)}) collective-permute-start(bf16[4,2,2,128,128]{4,3,2,1,0:T(8,128)(2,1)S(1)} %get-tuple-element.29), channel_id=1, source_target_pairs={{1,0},{2,1},{3,2},{5,4},{6,5},{7,6},{9,8},{10,9},{11,10},{13,12},{... | collective-permute-start | bytes 1572872 | tf_op jit(solution)/shard_map/ppermute | solution.py:42
  70.3 4.0 %copy-start = (bf16[1280,4096]{1,0:T(8,128)(2,1)S(1)}, bf16[1280,4096]{1,0:T(8,128)(2,1)}, u32[]{:S(2)}) copy-start(bf16[1280,4096]{1,0:T(8,128)(2,1)} %get-tuple-element.33.right_all) | copy-start | bytes 31457284
  86.1 22.8 %collective-permute-start.13 = (bf16[7,2,2,128,128]{4,3,2,1,0:T(8,128)(2,1)S(1)}, bf16[7,2,2,128,128]{4,3,2,1,0:T(8,128)(2,1)}, u32[]{:S(2)}, u32[]{:S(2)}) collective-permute-start(bf16[7,2,2,128,128]{4,3,2,1,0:T(8,128)(2,1)S(1)} %get-tuple-element.37.refs_1_), channel_id=1, source_target_pairs={{0,1},{1,2},{2,3},{4,5},{5,6},{6,7},{8,9},{9,10},{10,11},{12,13},{... | collective-permute-start | bytes 2752520 | tf_op jit(solution)/shard_map/ppermute | solution.py:42
  89.1 25.2 %collective-permute-start.14 = (bf16[7,2,2,128,128]{4,3,2,1,0:T(8,128)(2,1)S(1)}, bf16[7,2,2,128,128]{4,3,2,1,0:T(8,128)(2,1)}, u32[]{:S(2)}, u32[]{:S(2)}) collective-permute-start(bf16[7,2,2,128,128]{4,3,2,1,0:T(8,128)(2,1)S(1)} %get-tuple-element.37.refs_1_), channel_id=1, source_target_pairs={{1,0},{2,1},{3,2},{5,4},{6,5},{7,6},{9,8},{10,9},{11,10},{13,12},{... | collective-permute-start | bytes 2752520 | tf_op jit(solution)/shard_map/ppermute | solution.py:42
  90.4 63.2 %collective-permute-start.10 = (bf16[6,2,2,128,128]{4,3,2,1,0:T(8,128)(2,1)S(1)}, bf16[6,2,2,128,128]{4,3,2,1,0:T(8,128)(2,1)S(1)}, u32[]{:S(2)}, u32[]{:S(2)}) collective-permute-start(bf16[6,2,2,128,128]{4,3,2,1,0:T(8,128)(2,1)S(1)} %get-tuple-element.36.refs_0_), channel_id=1, source_target_pairs={{1,0},{2,1},{3,2},{5,4},{6,5},{7,6},{9,8},{10,9},{11,10},{13,12},{... | collective-permute-start | bytes 2359304 | tf_op jit(solution)/shard_map/ppermute | solution.py:42
  91.7 63.1 %collective-permute-start.8 = (bf16[6,2,2,128,128]{4,3,2,1,0:T(8,128)(2,1)S(1)}, bf16[6,2,2,128,128]{4,3,2,1,0:T(8,128)(2,1)}, u32[]{:S(2)}, u32[]{:S(2)}) collective-permute-start(bf16[6,2,2,128,128]{4,3,2,1,0:T(8,128)(2,1)S(1)} %get-tuple-element.36.refs_0_), channel_id=1, source_target_pairs={{0,1},{1,2},{2,3},{4,5},{5,6},{6,7},{8,9},{9,10},{10,11},{12,13},{... | collective-permute-start | bytes 2359304 | tf_op jit(solution)/shard_map/ppermute | solution.py:42
  99.1 64.1 %collective-permute-start.12 = (bf16[8,2,2,128,128]{4,3,2,1,0:T(8,128)(2,1)}, bf16[8,2,2,128,128]{4,3,2,1,0:T(8,128)(2,1)S(1)}, u32[]{:S(2)}, u32[]{:S(2)}) collective-permute-start(bf16[8,2,2,128,128]{4,3,2,1,0:T(8,128)(2,1)} %fusion), channel_id=1, source_target_pairs={{0,3},{3,0},{4,7},{7,4},{8,11},{11,8},{12,15},{15,12},{16,19},{19,... | collective-permute-start | bytes 3145736 | tf_op jit(solution)/shard_map/ppermute | solution.py:417
  114.4 53.7 %collective-permute-start.15 = (bf16[7,2,2,128,128]{4,3,2,1,0:T(8,128)(2,1)}, bf16[7,2,2,128,128]{4,3,2,1,0:T(8,128)(2,1)S(1)}, u32[]{:S(2)}, u32[]{:S(2)}) collective-permute-start(bf16[7,2,2,128,128]{4,3,2,1,0:T(8,128)(2,1)} %collective-permute-done.13.refs_2_), channel_id=1, source_target_pairs={{0,1},{1,2},{2,3},{4,5},{5,6},{6,7},{8,9},{9,10},{10,11},{12,13},{... | collective-permute-start | bytes 2752520 | tf_op jit(solution)/shard_map/ppermute | solution.py:42
  116.0 57.3 %collective-permute-start.16 = (bf16[7,2,2,128,128]{4,3,2,1,0:T(8,128)(2,1)}, bf16[7,2,2,128,128]{4,3,2,1,0:T(8,128)(2,1)}, u32[]{:S(2)}, u32[]{:S(2)}) collective-permute-start(bf16[7,2,2,128,128]{4,3,2,1,0:T(8,128)(2,1)} %collective-permute-done.14.refs_3_), channel_id=1, source_target_pairs={{1,0},{2,1},{3,2},{5,4},{6,5},{7,6},{9,8},{10,9},{11,10},{13,12},{... | collective-permute-start | bytes 2752520 | tf_op jit(solution)/shard_map/ppermute | solution.py:42
  153.6 35.5 %collective-permute-start.11 = (bf16[6,2,2,128,128]{4,3,2,1,0:T(8,128)(2,1)S(1)}, bf16[6,2,2,128,128]{4,3,2,1,0:T(8,128)(2,1)}, u32[]{:S(2)}, u32[]{:S(2)}) collective-permute-start(bf16[6,2,2,128,128]{4,3,2,1,0:T(8,128)(2,1)S(1)} %collective-permute-done.10.refs_1_), channel_id=1, source_target_pairs={{1,0},{2,1},{3,2},{5,4},{6,5},{7,6},{9,8},{10,9},{11,10},{13,12},{... | collective-permute-start | bytes 2359304 | tf_op jit(solution)/shard_map/ppermute | solution.py:42
  154.9 34.2 %collective-permute-start.9 = (bf16[6,2,2,128,128]{4,3,2,1,0:T(8,128)(2,1)}, bf16[6,2,2,128,128]{4,3,2,1,0:T(8,128)(2,1)S(1)}, u32[]{:S(2)}, u32[]{:S(2)}) collective-permute-start(bf16[6,2,2,128,128]{4,3,2,1,0:T(8,128)(2,1)} %collective-permute-done.8.refs_0_), channel_id=1, source_target_pairs={{0,1},{1,2},{2,3},{4,5},{5,6},{6,7},{8,9},{9,10},{10,11},{12,13},{... | collective-permute-start | bytes 2359304 | tf_op jit(solution)/shard_map/ppermute | solution.py:42

commit v12 on v11

--- a/solution.py
+++ b/solution.py
@@ -141,8 +141,14 @@
 
 
 def product(left, right, outs, lone, members, tile):
-    value = lax.dot_general(left, right, NT, preferred_element_type=jnp.float32)
+    width = members * tile
     for d1, out in enumerate(outs):
+        value = lax.dot_general(
+            left[d1 * width : (d1 + 1) * width],
+            right,
+            NT,
+            preferred_element_type=jnp.float32,
+        )
         for d2 in range(5):
             target, at = out, d2
             if d1 in lone:
@@ -150,7 +156,7 @@
                 target, at = (single, 0) if d2 == direction else (out, (d2 + 4 - direction) % 5)
             for m in range(members):
                 for m2 in range(members):
-                    row, column = (d1 * members + m) * tile, (d2 * members + m2) * tile
+                    row, column = m * tile, (d2 * members + m2) * tile
                     block = value[row : row + tile, column : column + tile]
                     target[at, m, m2] = block.astype(target.dtype)
 

time: 192 us -> 189 us (0.984)
  Pallas kernels: 50.9 us -> 47.3 us
    pallas_call x1, Pallas kernels: 22.4 us -> 18.8 us  [partial_blocks(): pl.pallas_call(functools.partial(partial_kernel, members, taps), in_specs...]
  transfers between devices with their start and end apart: 17 -> 17, of which waited for: 9 -> 9; matrix products, arithmetic and copies ran while one was open for 1% -> 1% of each run, Pallas kernels for 13% -> 14%
where the time goes in v12:
time: 189 us; the launch traced here: 187 us
  waiting for transfers between devices  79.5 us (42%)
  Pallas kernels  47.3 us (25%)
  starting transfers between devices  46.7 us (25%)
  local copies, waits for them, and re-layouts  11.5 us (6%)
    ppermute x14, waiting for transfers between devices, shifted(): return lax.ppermute(x, axis, pairs)  79.5 us
    ppermute x14, starting transfers between devices, shifted(): return lax.ppermute(x, axis, pairs)  41.2 us
    pallas_call x1, Pallas kernels, partial_blocks(): pl.pallas_call(functools.partial(partial_kernel, members, taps), in_specs...  18.8 us
    pallas_call x1, Pallas kernels, own_slots(): pl.pallas_call(functools.partial(own_kernel, count_y, rows, members, taps...  13.2 us
    unnamed x12, local copies, waits for them, and re-layouts  11.4 us
    pallas_call x4, Pallas kernels, placed(): pl.pallas_call(functools.partial(place_kernel, tuple((p[1:3] for p in pie...  10.8 us
  transfers between devices with their start and end apart: 17, of which 9 were waited for; matrix products, arithmetic and copies ran while one was open for 1% of the time, Pallas kernels for 14%

profile of v12, /device:TPU:0, one launch (start us, length us, event | category | flops | bytes accessed | tf_op | source)
XLA Modules:
  0.0 187.2 jit_solution(17162306167515178348)
XLA Ops:
  0.0 1.6 copy.11
  1.6 5.9 %collective-permute-start = (bf16[32,128,128]{2,1,0:T(8,128)(2,1)S(1)}, bf16[32,128,128]{2,1,0:T(8,128)(2,1)}, u32[]{:S(2)}, u32[]{:S(2)}) collective-permute-start(bf16[32,128,128]{2,1,0:T(8,128)(2,1)S(1)} %bitcast.24), channel_id=1, source_target_pairs={{0,1},{1,2},{2,3},{4,5},{5,6},{6,7},{8,9},{9,10},{10,11},{12,13},{... | collective-permute-start | bytes 3145736 | tf_op jit(solution)/shard_map/ppermute | solution.py:42
  7.5 1.3 collective-permute-start.1
  8.8 1.7 collective-permute-start.2
  10.5 1.9 %collective-permute-start.3 = (bf16[32,128,128]{2,1,0:T(8,128)(2,1)S(1)}, bf16[32,128,128]{2,1,0:T(8,128)(2,1)}, u32[]{:S(2)}, u32[]{:S(2)}) collective-permute-start(bf16[32,128,128]{2,1,0:T(8,128)(2,1)S(1)} %bitcast.27), channel_id=1, source_target_pairs={{0,4},{4,0},{8,12},{12,8},{16,20},{20,16},{24,28},{28,24},{1,5},{5... | collective-permute-start | bytes 3145736 | tf_op jit(solution)/shard_map/ppermute | solution.py:51
  12.4 0.8 copy.10
  13.2 0.1 reshape.12.columns
  13.3 0.1 pad_add_fusion.2.place
  13.4 0.0 copy-start.1
  13.4 3.1 %copy-done.1 = bf16[1,1,32,7,128,128]{5,4,3,2,1,0:T(8,128)(2,1)S(1)} copy-done((bf16[1,1,32,7,128,128]{5,4,3,2,1,0:T(8,128)(2,1)S(1)}, bf16[1,1,32,7,128,128]{5,4,3,2,1,0:T(8,128)(2,1)}, u32[]{:S(2)}) %copy-start.1) | copy-done | bytes 7340056
  16.5 0.0 copy-start.3
  16.5 1.2 copy-done.3
  17.7 0.0 copy-start.4
  17.7 0.7 copy-done.4
  18.4 0.0 copy-start.2
  18.4 13.2 %own_slots.1 = (bf16[256,4096]{1,0:T(8,128)(2,1)S(1)}, bf16[256,4096]{1,0:T(8,128)(2,1)S(1)}, s32[224]{0:T(256)S(1)}, s32[224]{0:T(256)S(1)}, s32[224]{0:T(256)S(1)}, /*index=5*/s32[8]{0:T(128)S(1)}) custom-call(s32[224]{0:T(256)S(1)} %reshape.12.columns, s32[1024]{0:T(1024)S(1)} %copy-done.4, s32[2]{0:T(128)S(1)} %pad_add_fusion.2.place, ...), custom_call_target="tpu_custom_call" | custom-call | flops 1207959552 | bytes 13631488 | tf_op jit(solution)/shard_map/own_slots/pallas_call | solution.py:110
  31.6 0.0 collective-permute-done.refs_2_
  31.6 2.5 %collective-permute-done.1.refs_3_ = bf16[32,128,128]{2,1,0:T(8,128)(2,1)} collective-permute-done((bf16[32,128,128]{2,1,0:T(8,128)(2,1)S(1)}, bf16[32,128,128]{2,1,0:T(8,128)(2,1)}, u32[]{:S(2)}, u32[]{:S(2)}) %collective-permute-start.1) | collective-permute-done | bytes 1048608 | tf_op jit(solution)/shard_map/ppermute | solution.py:42
  34.2 0.0 collective-permute-done.2.refs_4_
  34.2 0.0 collective-permute-done.3.refs_5_
  34.2 0.0 copy-done.2
  34.2 18.8 %partial_blocks.1 = (bf16[4,2,2,128,128]{4,3,2,1,0:T(8,128)(2,1)S(1)}, bf16[4,2,2,128,128]{4,3,2,1,0:T(8,128)(2,1)S(1)}, bf16[5,2,2,128,128]{4,3,2,1,0:T(8,128)(...) custom-call(s32[224]{0:T(256)S(1)} %get-tuple-element.23.tiles, ...), custom_call_target="tpu_custom_call" | custom-call | flops 11676942336 | bytes 28311552 | tf_op jit(solution)/shard_map/partial_blocks/pallas_call | solution.py:240
  53.0 4.4 %collective-permute-start.6 = (bf16[5,2,2,128,128]{4,3,2,1,0:T(8,128)(2,1)S(1)}, bf16[5,2,2,128,128]{4,3,2,1,0:T(8,128)(2,1)S(1)}, u32[]{:S(2)}, u32[]{:S(2)}) collective-permute-start(bf16[5,2,2,128,128]{4,3,2,1,0:T(8,128)(2,1)S(1)} %get-tuple-element.30), channel_id=1, source_target_pairs={{0,4},{4,8},{8,12},{12,16},{16,20},{20,24},{24,28},{1,5},{5,9},{9,... | collective-permute-start | bytes 1966088 | tf_op jit(solution)/shard_map/ppermute | solution.py:42
  57.4 1.3 collective-permute-start.7
  58.7 6.0 %collective-permute-start.4 = (bf16[4,2,2,128,128]{4,3,2,1,0:T(8,128)(2,1)S(1)}, bf16[4,2,2,128,128]{4,3,2,1,0:T(8,128)(2,1)S(1)}, u32[]{:S(2)}, u32[]{:S(2)}) collective-permute-start(bf16[4,2,2,128,128]{4,3,2,1,0:T(8,128)(2,1)S(1)} %get-tuple-element.28), channel_id=1, source_target_pairs={{0,1},{1,2},{2,3},{4,5},{5,6},{6,7},{8,9},{9,10},{10,11},{12,13},{... | collective-permute-start | bytes 1572872 | tf_op jit(solution)/shard_map/ppermute | solution.py:42
  64.7 1.3 collective-permute-start.5
  66.0 0.0 copy-start
  66.0 4.0 %copy-done = bf16[1280,4096]{1,0:T(8,128)(2,1)S(1)} copy-done((bf16[1280,4096]{1,0:T(8,128)(2,1)S(1)}, bf16[1280,4096]{1,0:T(8,128)(2,1)}, u32[]{:S(2)}) %copy-start) | copy-done | bytes 10485784
  70.0 3.8 %own_rows.1.refs_4_ = f32[5,2,2,128,128]{4,3,2,1,0:T(8,128)S(1)} custom-call(bf16[256,4096]{1,0:T(8,128)(2,1)S(1)} %get-tuple-element.32.left_own, bf16[1280,4096]{1,0:T(8,128)(2,1)S(1)} %copy-done), custom_call_target="tpu_custom_call" | custom-call | flops 2684354560 | bytes 12582912 | tf_op jit(solution)/shard_map/own_rows/pallas_call | solution.py:281
  73.8 3.1 %collective-permute-done.4.refs_0_ = bf16[4,2,2,128,128]{4,3,2,1,0:T(8,128)(2,1)S(1)} collective-permute-done((bf16[4,2,2,128,128]{4,3,2,1,0:T(8,128)(2,1)S(1)}, bf16[4,2,2,128,128]{4,3,2,1,0:T(8,128)(2,1)S(1)}, u32[]{:S(2)}, u32[]{:S(2)}) %collective-permute-start.4) | collective-permute-done | bytes 524320 | tf_op jit(solution)/shard_map/ppermute | solution.py:42
  76.8 4.5 %collective-permute-done.5.refs_1_ = bf16[4,2,2,128,128]{4,3,2,1,0:T(8,128)(2,1)S(1)} collective-permute-done((bf16[4,2,2,128,128]{4,3,2,1,0:T(8,128)(2,1)S(1)}, bf16[4,2,2,128,128]{4,3,2,1,0:T(8,128)(2,1)S(1)}, u32[]{:S(2)}, u32[]{:S(2)}) %collective-permute-start.5) | collective-permute-done | bytes 524320 | tf_op jit(solution)/shard_map/ppermute | solution.py:42
  81.3 0.0 collective-permute-done.6.refs_2_
  81.3 0.0 collective-permute-done.7.refs_3_
  81.3 0.7 finished_window.1
  82.0 2.8 %collective-permute-start.13 = (bf16[7,2,2,128,128]{4,3,2,1,0:T(8,128)(2,1)S(1)}, bf16[7,2,2,128,128]{4,3,2,1,0:T(8,128)(2,1)}, u32[]{:S(2)}, u32[]{:S(2)}) collective-permute-start(bf16[7,2,2,128,128]{4,3,2,1,0:T(8,128)(2,1)S(1)} %get-tuple-element.37.refs_1_), channel_id=1, source_target_pairs={{0,1},{1,2},{2,3},{4,5},{5,6},{6,7},{8,9},{9,10},{10,11},{12,13},{... | collective-permute-start | bytes 2752520 | tf_op jit(solution)/shard_map/ppermute | solution.py:42
  84.8 1.3 collective-permute-start.14
  86.1 1.3 collective-permute-start.10
  87.4 6.1 %collective-permute-start.8 = (bf16[6,2,2,128,128]{4,3,2,1,0:T(8,128)(2,1)S(1)}, bf16[6,2,2,128,128]{4,3,2,1,0:T(8,128)(2,1)}, u32[]{:S(2)}, u32[]{:S(2)}) collective-permute-start(bf16[6,2,2,128,128]{4,3,2,1,0:T(8,128)(2,1)S(1)} %get-tuple-element.36.refs_0_), channel_id=1, source_target_pairs={{0,1},{1,2},{2,3},{4,5},{5,6},{6,7},{8,9},{9,10},{10,11},{12,13},{... | collective-permute-start | bytes 2359304 | tf_op jit(solution)/shard_map/ppermute | solution.py:42
  93.5 1.3 fusion
  94.8 1.9 %collective-permute-start.12 = (bf16[8,2,2,128,128]{4,3,2,1,0:T(8,128)(2,1)}, bf16[8,2,2,128,128]{4,3,2,1,0:T(8,128)(2,1)S(1)}, u32[]{:S(2)}, u32[]{:S(2)}) collective-permute-start(bf16[8,2,2,128,128]{4,3,2,1,0:T(8,128)(2,1)} %fusion), channel_id=1, source_target_pairs={{0,3},{3,0},{4,7},{7,4},{8,11},{11,8},{12,15},{15,12},{16,19},{19,... | collective-permute-start | bytes 3145736 | tf_op jit(solution)/shard_map/ppermute | solution.py:423
  96.7 0.1 pad_add_fusion.5.row
  96.8 2.0 %placed.4.refs_4_ = bf16[4,2,13,2,128,128]{5,4,3,2,1,0:T(8,128)(2,1)} custom-call(s32[2]{0:T(128)S(1)} %pad_add_fusion.5.row, s32[2]{0:T(128)S(1)} %broadcast_1_valid.2.valid, bf16[6,2,2,128,128]{4,3,2,1,0:T(8,128)(2,1)S(1)} %get-tuple-element.36.refs_0_, bf16[7,2,2,128,128]{4,3,2,1,0:T(8,128)(2,1)S(1)} %get-tuple-element.37.refs_1_), custom_call_target="tpu_custom_call" | custom-call | bytes 5111808 | tf_op jit(solution)/shard_map/placed/pallas_call | solution.py:397
  98.8 5.8 %collective-permute-done.13.refs_2_ = bf16[7,2,2,128,128]{4,3,2,1,0:T(8,128)(2,1)} collective-permute-done((bf16[7,2,2,128,128]{4,3,2,1,0:T(8,128)(2,1)S(1)}, bf16[7,2,2,128,128]{4,3,2,1,0:T(8,128)(2,1)}, u32[]{:S(2)}, u32[]{:S(2)}) %collective-permute-start.13) | collective-permute-done | bytes 917536 | tf_op jit(solution)/shard_map/ppermute | solution.py:42
  104.6 5.5 %collective-permute-done.14.refs_3_ = bf16[7,2,2,128,128]{4,3,2,1,0:T(8,128)(2,1)} collective-permute-done((bf16[7,2,2,128,128]{4,3,2,1,0:T(8,128)(2,1)S(1)}, bf16[7,2,2,128,128]{4,3,2,1,0:T(8,128)(2,1)}, u32[]{:S(2)}, u32[]{:S(2)}) %collective-permute-start.14) | collective-permute-done | bytes 917536 | tf_op jit(solution)/shard_map/ppermute | solution.py:42
  110.0 2.4 %collective-permute-start.15 = (bf16[7,2,2,128,128]{4,3,2,1,0:T(8,128)(2,1)}, bf16[7,2,2,128,128]{4,3,2,1,0:T(8,128)(2,1)S(1)}, u32[]{:S(2)}, u32[]{:S(2)}) collective-permute-start(bf16[7,2,2,128,128]{4,3,2,1,0:T(8,128)(2,1)} %collective-permute-done.13.refs_2_), channel_id=1, source_target_pairs={{0,1},{1,2},{2,3},{4,5},{5,6},{6,7},{8,9},{9,10},{10,11},{12,13},{... | collective-permute-start | bytes 2752520 | tf_op jit(solution)/shard_map/ppermute | solution.py:42
  112.4 1.3 collective-permute-start.16
  113.7 35.5 %collective-permute-done.10.refs_1_ = bf16[6,2,2,128,128]{4,3,2,1,0:T(8,128)(2,1)S(1)} collective-permute-done((bf16[6,2,2,128,128]{4,3,2,1,0:T(8,128)(2,1)S(1)}, bf16[6,2,2,128,128]{4,3,2,1,0:T(8,128)(2,1)S(1)}, u32[]{:S(2)}, u32[]{:S(2)}) %collective-permute-start.10) | collective-permute-done | bytes 786464 | tf_op jit(solution)/shard_map/ppermute | solution.py:42
  149.2 1.3 collective-permute-start.11
  150.5 0.0 collective-permute-done.8.refs_0_
  150.5 4.6 %collective-permute-start.9 = (bf16[6,2,2,128,128]{4,3,2,1,0:T(8,128)(2,1)}, bf16[6,2,2,128,128]{4,3,2,1,0:T(8,128)(2,1)S(1)}, u32[]{:S(2)}, u32[]{:S(2)}) collective-permute-start(bf16[6,2,2,128,128]{4,3,2,1,0:T(8,128)(2,1)} %collective-permute-done.8.refs_0_), channel_id=1, source_target_pairs={{0,1},{1,2},{2,3},{4,5},{5,6},{6,7},{8,9},{9,10},{10,11},{12,13},{... | collective-permute-start | bytes 2359304 | tf_op jit(solution)/shard_map/ppermute | solution.py:42
  155.2 0.1 pad_add_fusion.6.row
  155.3 0.1 add_convert_fusion.valid
  155.3 0.1 pad_add_fusion
  155.4 0.1 pad_add_fusion.3
  155.5 3.4 %placed.5.refs_4_ = bf16[4,2,13,2,128,128]{5,4,3,2,1,0:T(8,128)(2,1)} custom-call(s32[4]{0:T(128)S(1)} %pad_add_fusion.6.row, s32[4]{0:T(128)S(1)} %add_convert_fusion.valid, bf16[6,2,2,128,128]{4,3,2,1,0:T(8,128)(2,1)} %collective-permute-done.8.refs_0_, ...), custom_call_target="tpu_custom_call", output_to_operand_aliasing={{}: (6, {})} | custom-call | bytes 5111808 | tf_op jit(solution)/shard_map/placed/pallas_call | solution.py:397
  158.9 0.0 collective-permute-done.12.refs_0_.refs_1_
  158.9 4.8 %collective-permute-done.15.refs_2_ = bf16[7,2,2,128,128]{4,3,2,1,0:T(8,128)(2,1)S(1)} collective-permute-done((bf16[7,2,2,128,128]{4,3,2,1,0:T(8,128)(2,1)}, bf16[7,2,2,128,128]{4,3,2,1,0:T(8,128)(2,1)S(1)}, u32[]{:S(2)}, u32[]{:S(2)}) %collective-permute-start.15) | collective-permute-done | bytes 917536 | tf_op jit(solution)/shard_map/ppermute | solution.py:42
  163.7 5.3 %collective-permute-done.16.refs_3_ = bf16[7,2,2,128,128]{4,3,2,1,0:T(8,128)(2,1)} collective-permute-done((bf16[7,2,2,128,128]{4,3,2,1,0:T(8,128)(2,1)}, bf16[7,2,2,128,128]{4,3,2,1,0:T(8,128)(2,1)}, u32[]{:S(2)}, u32[]{:S(2)}) %collective-permute-start.16) | collective-permute-done | bytes 917536 | tf_op jit(solution)/shard_map/ppermute | solution.py:42
  169.0 3.1 %placed.6.refs_2_ = bf16[4,2,13,2,128,128]{5,4,3,2,1,0:T(8,128)(2,1)} custom-call(s32[4]{0:T(128)S(1)} %get-tuple-element.41.row, s32[4]{0:T(128)S(1)} %get-tuple-element.42.valid, bf16[8,2,2,128,128]{4,3,2,1,0:T(8,128)(2,1)S(1)} %collective-permute-done.12.refs_0_.refs_1_, ...), custom_call_target="tpu_custom_call", output_to_operand_aliasing={{}: (6, {})} | custom-call | bytes 5111808 | tf_op jit(solution)/shard_map/placed/pallas_call | solution.py:397
  172.1 12.6 %collective-permute-done.11.refs_1_ = bf16[6,2,2,128,128]{4,3,2,1,0:T(8,128)(2,1)} collective-permute-done((bf16[6,2,2,128,128]{4,3,2,1,0:T(8,128)(2,1)S(1)}, bf16[6,2,2,128,128]{4,3,2,1,0:T(8,128)(2,1)}, u32[]{:S(2)}, u32[]{:S(2)}) %collective-permute-start.11) | collective-permute-done | bytes 786464 | tf_op jit(solution)/shard_map/ppermute | solution.py:42
  184.7 0.0 collective-permute-done.9.refs_0_
  184.7 2.3 %placed.7 = bf16[4,2,13,2,128,128]{5,4,3,2,1,0:T(8,128)(2,1)} custom-call(s32[2]{0:T(128)S(1)} %get-tuple-element.43.row, s32[2]{0:T(128)S(1)} %get-tuple-element.44.valid, bf16[6,2,2,128,128]{4,3,2,1,0:T(8,128)(2,1)S(1)} %collective-permute-done.9.refs_0_, ...), custom_call_target="tpu_custom_call", output_to_operand_aliasing={{}: (4, {})} | custom-call | bytes 5111808 | tf_op jit(solution)/shard_map/placed/pallas_call | solution.py:397
  (1 shorter events, 0.0 us)
Async XLA Ops:
  1.6 30.0 %collective-permute-start = (bf16[32,128,128]{2,1,0:T(8,128)(2,1)S(1)}, bf16[32,128,128]{2,1,0:T(8,128)(2,1)}, u32[]{:S(2)}, u32[]{:S(2)}) collective-permute-start(bf16[32,128,128]{2,1,0:T(8,128)(2,1)S(1)} %bitcast.24), channel_id=1, source_target_pairs={{0,1},{1,2},{2,3},{4,5},{5,6},{6,7},{8,9},{9,10},{10,11},{12,13},{... | collective-permute-start | bytes 3145736 | tf_op jit(solution)/shard_map/ppermute | solution.py:42
  7.5 26.6 %collective-permute-start.1 = (bf16[32,128,128]{2,1,0:T(8,128)(2,1)S(1)}, bf16[32,128,128]{2,1,0:T(8,128)(2,1)}, u32[]{:S(2)}, u32[]{:S(2)}) collective-permute-start(bf16[32,128,128]{2,1,0:T(8,128)(2,1)S(1)} %bitcast.25), channel_id=1, source_target_pairs={{1,0},{2,1},{3,2},{5,4},{6,5},{7,6},{9,8},{10,9},{11,10},{13,12},{... | collective-permute-start | bytes 3145736 | tf_op jit(solution)/shard_map/ppermute | solution.py:42
  8.8 25.3 %collective-permute-start.2 = (bf16[32,128,128]{2,1,0:T(8,128)(2,1)S(1)}, bf16[32,128,128]{2,1,0:T(8,128)(2,1)}, u32[]{:S(2)}, u32[]{:S(2)}) collective-permute-start(bf16[32,128,128]{2,1,0:T(8,128)(2,1)S(1)} %bitcast.26), channel_id=1, source_target_pairs={{4,8},{8,4},{12,16},{16,12},{20,24},{24,20},{5,9},{9,5},{13,17},{1... | collective-permute-start | bytes 3145736 | tf_op jit(solution)/shard_map/ppermute | solution.py:51
  10.5 23.6 %collective-permute-start.3 = (bf16[32,128,128]{2,1,0:T(8,128)(2,1)S(1)}, bf16[32,128,128]{2,1,0:T(8,128)(2,1)}, u32[]{:S(2)}, u32[]{:S(2)}) collective-permute-start(bf16[32,128,128]{2,1,0:T(8,128)(2,1)S(1)} %bitcast.27), channel_id=1, source_target_pairs={{0,4},{4,0},{8,12},{12,8},{16,20},{20,16},{24,28},{28,24},{1,5},{5... | collective-permute-start | bytes 3145736 | tf_op jit(solution)/shard_map/ppermute | solution.py:51
  13.4 3.1 %copy-start.1 = (bf16[1,1,32,7,128,128]{5,4,3,2,1,0:T(8,128)(2,1)S(1)}, bf16[1,1,32,7,128,128]{5,4,3,2,1,0:T(8,128)(2,1)}, u32[]{:S(2)}) copy-start(bf16[1,1,32,7,128,128]{5,4,3,2,1,0:T(8,128)(2,1)} %param.5) | copy-start | bytes 22020100
  16.5 1.2 copy-start.3
  17.7 0.7 copy-start.4
  18.4 15.8 %copy-start.2 = (bf16[1,1,32,7,128,128]{5,4,3,2,1,0:T(8,128)(2,1)S(1)}, bf16[1,1,32,7,128,128]{5,4,3,2,1,0:T(8,128)(2,1)}, u32[]{:S(2)}) copy-start(bf16[1,1,32,7,128,128]{5,4,3,2,1,0:T(8,128)(2,1)} %param.5) | copy-start | bytes 22020100
  53.0 28.3 %collective-permute-start.6 = (bf16[5,2,2,128,128]{4,3,2,1,0:T(8,128)(2,1)S(1)}, bf16[5,2,2,128,128]{4,3,2,1,0:T(8,128)(2,1)S(1)}, u32[]{:S(2)}, u32[]{:S(2)}) collective-permute-start(bf16[5,2,2,128,128]{4,3,2,1,0:T(8,128)(2,1)S(1)} %get-tuple-element.30), channel_id=1, source_target_pairs={{0,4},{4,8},{8,12},{12,16},{16,20},{20,24},{24,28},{1,5},{5,9},{9,... | collective-permute-start | bytes 1966088 | tf_op jit(solution)/shard_map/ppermute | solution.py:42
  57.4 23.9 %collective-permute-start.7 = (bf16[5,2,2,128,128]{4,3,2,1,0:T(8,128)(2,1)S(1)}, bf16[5,2,2,128,128]{4,3,2,1,0:T(8,128)(2,1)S(1)}, u32[]{:S(2)}, u32[]{:S(2)}) collective-permute-start(bf16[5,2,2,128,128]{4,3,2,1,0:T(8,128)(2,1)S(1)} %get-tuple-element.31), channel_id=1, source_target_pairs={{4,0},{8,4},{12,8},{16,12},{20,16},{24,20},{28,24},{5,1},{9,5},{13... | collective-permute-start | bytes 1966088 | tf_op jit(solution)/shard_map/ppermute | solution.py:42
  58.7 18.1 %collective-permute-start.4 = (bf16[4,2,2,128,128]{4,3,2,1,0:T(8,128)(2,1)S(1)}, bf16[4,2,2,128,128]{4,3,2,1,0:T(8,128)(2,1)S(1)}, u32[]{:S(2)}, u32[]{:S(2)}) collective-permute-start(bf16[4,2,2,128,128]{4,3,2,1,0:T(8,128)(2,1)S(1)} %get-tuple-element.28), channel_id=1, source_target_pairs={{0,1},{1,2},{2,3},{4,5},{5,6},{6,7},{8,9},{9,10},{10,11},{12,13},{... | collective-permute-start | bytes 1572872 | tf_op jit(solution)/shard_map/ppermute | solution.py:42
  64.7 16.6 %collective-permute-start.5 = (bf16[4,2,2,128,128]{4,3,2,1,0:T(8,128)(2,1)S(1)}, bf16[4,2,2,128,128]{4,3,2,1,0:T(8,128)(2,1)S(1)}, u32[]{:S(2)}, u32[]{:S(2)}) collective-permute-start(bf16[4,2,2,128,128]{4,3,2,1,0:T(8,128)(2,1)S(1)} %get-tuple-element.29), channel_id=1, source_target_pairs={{1,0},{2,1},{3,2},{5,4},{6,5},{7,6},{9,8},{10,9},{11,10},{13,12},{... | collective-permute-start | bytes 1572872 | tf_op jit(solution)/shard_map/ppermute | solution.py:42
  66.0 4.0 %copy-start = (bf16[1280,4096]{1,0:T(8,128)(2,1)S(1)}, bf16[1280,4096]{1,0:T(8,128)(2,1)}, u32[]{:S(2)}) copy-start(bf16[1280,4096]{1,0:T(8,128)(2,1)} %get-tuple-element.33.right_all) | copy-start | bytes 31457284
  82.0 22.6 %collective-permute-start.13 = (bf16[7,2,2,128,128]{4,3,2,1,0:T(8,128)(2,1)S(1)}, bf16[7,2,2,128,128]{4,3,2,1,0:T(8,128)(2,1)}, u32[]{:S(2)}, u32[]{:S(2)}) collective-permute-start(bf16[7,2,2,128,128]{4,3,2,1,0:T(8,128)(2,1)S(1)} %get-tuple-element.37.refs_1_), channel_id=1, source_target_pairs={{0,1},{1,2},{2,3},{4,5},{5,6},{6,7},{8,9},{9,10},{10,11},{12,13},{... | collective-permute-start | bytes 2752520 | tf_op jit(solution)/shard_map/ppermute | solution.py:42
  84.8 25.2 %collective-permute-start.14 = (bf16[7,2,2,128,128]{4,3,2,1,0:T(8,128)(2,1)S(1)}, bf16[7,2,2,128,128]{4,3,2,1,0:T(8,128)(2,1)}, u32[]{:S(2)}, u32[]{:S(2)}) collective-permute-start(bf16[7,2,2,128,128]{4,3,2,1,0:T(8,128)(2,1)S(1)} %get-tuple-element.37.refs_1_), channel_id=1, source_target_pairs={{1,0},{2,1},{3,2},{5,4},{6,5},{7,6},{9,8},{10,9},{11,10},{13,12},{... | collective-permute-start | bytes 2752520 | tf_op jit(solution)/shard_map/ppermute | solution.py:42
  86.1 63.2 %collective-permute-start.10 = (bf16[6,2,2,128,128]{4,3,2,1,0:T(8,128)(2,1)S(1)}, bf16[6,2,2,128,128]{4,3,2,1,0:T(8,128)(2,1)S(1)}, u32[]{:S(2)}, u32[]{:S(2)}) collective-permute-start(bf16[6,2,2,128,128]{4,3,2,1,0:T(8,128)(2,1)S(1)} %get-tuple-element.36.refs_0_), channel_id=1, source_target_pairs={{1,0},{2,1},{3,2},{5,4},{6,5},{7,6},{9,8},{10,9},{11,10},{13,12},{... | collective-permute-start | bytes 2359304 | tf_op jit(solution)/shard_map/ppermute | solution.py:42
  87.4 63.1 %collective-permute-start.8 = (bf16[6,2,2,128,128]{4,3,2,1,0:T(8,128)(2,1)S(1)}, bf16[6,2,2,128,128]{4,3,2,1,0:T(8,128)(2,1)}, u32[]{:S(2)}, u32[]{:S(2)}) collective-permute-start(bf16[6,2,2,128,128]{4,3,2,1,0:T(8,128)(2,1)S(1)} %get-tuple-element.36.refs_0_), channel_id=1, source_target_pairs={{0,1},{1,2},{2,3},{4,5},{5,6},{6,7},{8,9},{9,10},{10,11},{12,13},{... | collective-permute-start | bytes 2359304 | tf_op jit(solution)/shard_map/ppermute | solution.py:42
  94.8 64.1 %collective-permute-start.12 = (bf16[8,2,2,128,128]{4,3,2,1,0:T(8,128)(2,1)}, bf16[8,2,2,128,128]{4,3,2,1,0:T(8,128)(2,1)S(1)}, u32[]{:S(2)}, u32[]{:S(2)}) collective-permute-start(bf16[8,2,2,128,128]{4,3,2,1,0:T(8,128)(2,1)} %fusion), channel_id=1, source_target_pairs={{0,3},{3,0},{4,7},{7,4},{8,11},{11,8},{12,15},{15,12},{16,19},{19,... | collective-permute-start | bytes 3145736 | tf_op jit(solution)/shard_map/ppermute | solution.py:423
  110.0 53.7 %collective-permute-start.15 = (bf16[7,2,2,128,128]{4,3,2,1,0:T(8,128)(2,1)}, bf16[7,2,2,128,128]{4,3,2,1,0:T(8,128)(2,1)S(1)}, u32[]{:S(2)}, u32[]{:S(2)}) collective-permute-start(bf16[7,2,2,128,128]{4,3,2,1,0:T(8,128)(2,1)} %collective-permute-done.13.refs_2_), channel_id=1, source_target_pairs={{0,1},{1,2},{2,3},{4,5},{5,6},{6,7},{8,9},{9,10},{10,11},{12,13},{... | collective-permute-start | bytes 2752520 | tf_op jit(solution)/shard_map/ppermute | solution.py:42
  112.4 56.6 %collective-permute-start.16 = (bf16[7,2,2,128,128]{4,3,2,1,0:T(8,128)(2,1)}, bf16[7,2,2,128,128]{4,3,2,1,0:T(8,128)(2,1)}, u32[]{:S(2)}, u32[]{:S(2)}) collective-permute-start(bf16[7,2,2,128,128]{4,3,2,1,0:T(8,128)(2,1)} %collective-permute-done.14.refs_3_), channel_id=1, source_target_pairs={{1,0},{2,1},{3,2},{5,4},{6,5},{7,6},{9,8},{10,9},{11,10},{13,12},{... | collective-permute-start | bytes 2752520 | tf_op jit(solution)/shard_map/ppermute | solution.py:42
  149.2 35.5 %collective-permute-start.11 = (bf16[6,2,2,128,128]{4,3,2,1,0:T(8,128)(2,1)S(1)}, bf16[6,2,2,128,128]{4,3,2,1,0:T(8,128)(2,1)}, u32[]{:S(2)}, u32[]{:S(2)}) collective-permute-start(bf16[6,2,2,128,128]{4,3,2,1,0:T(8,128)(2,1)S(1)} %collective-permute-done.10.refs_1_), channel_id=1, source_target_pairs={{1,0},{2,1},{3,2},{5,4},{6,5},{7,6},{9,8},{10,9},{11,10},{13,12},{... | collective-permute-start | bytes 2359304 | tf_op jit(solution)/shard_map/ppermute | solution.py:42
  150.5 34.2 %collective-permute-start.9 = (bf16[6,2,2,128,128]{4,3,2,1,0:T(8,128)(2,1)}, bf16[6,2,2,128,128]{4,3,2,1,0:T(8,128)(2,1)S(1)}, u32[]{:S(2)}, u32[]{:S(2)}) collective-permute-start(bf16[6,2,2,128,128]{4,3,2,1,0:T(8,128)(2,1)} %collective-permute-done.8.refs_0_), channel_id=1, source_target_pairs={{0,1},{1,2},{2,3},{4,5},{5,6},{6,7},{8,9},{9,10},{10,11},{12,13},{... | collective-permute-start | bytes 2359304 | tf_op jit(solution)/shard_map/ppermute | solution.py:42

commit v13 on v12

--- a/solution.py
+++ b/solution.py
@@ -32,7 +32,7 @@
 smoothing = 2.0 / 3.0
 MEMBERS = 2
 ROWS_PER_STEP = 4
-UNROLL = 8
+UNROLL = 16
 NT = (((1,), (1,)), ((), ()))
 
 

time: 189 us -> 188 us (level)
  no operation moved by 1% of the time
where the time goes in v13:
time: 188 us
  waiting for transfers between devices  79.8 us (42%)
  Pallas kernels  47.6 us (25%)
  starting transfers between devices  46.5 us (25%)
  local copies, waits for them, and re-layouts  11.5 us (6%)
    ppermute x14, waiting for transfers between devices, shifted(): return lax.ppermute(x, axis, pairs)  79.8 us
    ppermute x14, starting transfers between devices, shifted(): return lax.ppermute(x, axis, pairs)  41 us
    pallas_call x1, Pallas kernels, partial_blocks(): pl.pallas_call(functools.partial(partial_kernel, members, taps), in_specs...  19.1 us
    pallas_call x1, Pallas kernels, own_slots(): pl.pallas_call(functools.partial(own_kernel, count_y, rows, members, taps...  13.2 us
    unnamed x12, local copies, waits for them, and re-layouts  11.4 us
    pallas_call x4, Pallas kernels, placed(): pl.pallas_call(functools.partial(place_kernel, tuple((p[1:3] for p in pie...  10.8 us
  transfers between devices with their start and end apart: 17, of which 9 were waited for; matrix products, arithmetic and copies ran while one was open for 1% of the time, Pallas kernels for 14%

profile of v13, /device:TPU:0, one launch (start us, length us, event | category | flops | bytes accessed | tf_op | source)
XLA Modules:
  0.0 187.5 jit_solution(1171568478956517998)
XLA Ops:
  0.0 1.6 copy.11
  1.6 5.9 %collective-permute-start = (bf16[32,128,128]{2,1,0:T(8,128)(2,1)S(1)}, bf16[32,128,128]{2,1,0:T(8,128)(2,1)}, u32[]{:S(2)}, u32[]{:S(2)}) collective-permute-start(bf16[32,128,128]{2,1,0:T(8,128)(2,1)S(1)} %bitcast.24), channel_id=1, source_target_pairs={{0,1},{1,2},{2,3},{4,5},{5,6},{6,7},{8,9},{9,10},{10,11},{12,13},{... | collective-permute-start | bytes 3145736 | tf_op jit(solution)/shard_map/ppermute | solution.py:42
  7.5 1.3 collective-permute-start.1
  8.8 1.7 collective-permute-start.2
  10.5 1.9 %collective-permute-start.3 = (bf16[32,128,128]{2,1,0:T(8,128)(2,1)S(1)}, bf16[32,128,128]{2,1,0:T(8,128)(2,1)}, u32[]{:S(2)}, u32[]{:S(2)}) collective-permute-start(bf16[32,128,128]{2,1,0:T(8,128)(2,1)S(1)} %bitcast.27), channel_id=1, source_target_pairs={{0,4},{4,0},{8,12},{12,8},{16,20},{20,16},{24,28},{28,24},{1,5},{5... | collective-permute-start | bytes 3145736 | tf_op jit(solution)/shard_map/ppermute | solution.py:51
  12.4 0.8 copy.10
  13.2 0.1 reshape.12.columns
  13.3 0.1 pad_add_fusion.2.place
  13.4 0.0 copy-start.1
  13.4 3.1 %copy-done.1 = bf16[1,1,32,7,128,128]{5,4,3,2,1,0:T(8,128)(2,1)S(1)} copy-done((bf16[1,1,32,7,128,128]{5,4,3,2,1,0:T(8,128)(2,1)S(1)}, bf16[1,1,32,7,128,128]{5,4,3,2,1,0:T(8,128)(2,1)}, u32[]{:S(2)}) %copy-start.1) | copy-done | bytes 7340056
  16.5 0.0 copy-start.3
  16.5 1.2 copy-done.3
  17.7 0.0 copy-start.4
  17.7 0.7 copy-done.4
  18.4 0.0 copy-start.2
  18.4 13.2 %own_slots.1 = (bf16[256,4096]{1,0:T(8,128)(2,1)S(1)}, bf16[256,4096]{1,0:T(8,128)(2,1)S(1)}, s32[224]{0:T(256)S(1)}, s32[224]{0:T(256)S(1)}, s32[224]{0:T(256)S(1)}, /*index=5*/s32[8]{0:T(128)S(1)}) custom-call(s32[224]{0:T(256)S(1)} %reshape.12.columns, s32[1024]{0:T(1024)S(1)} %copy-done.4, s32[2]{0:T(128)S(1)} %pad_add_fusion.2.place, ...), custom_call_target="tpu_custom_call" | custom-call | flops 1207959552 | bytes 13631488 | tf_op jit(solution)/shard_map/own_slots/pallas_call | solution.py:110
  31.6 0.0 collective-permute-done.refs_2_
  31.6 2.5 %collective-permute-done.1.refs_3_ = bf16[32,128,128]{2,1,0:T(8,128)(2,1)} collective-permute-done((bf16[32,128,128]{2,1,0:T(8,128)(2,1)S(1)}, bf16[32,128,128]{2,1,0:T(8,128)(2,1)}, u32[]{:S(2)}, u32[]{:S(2)}) %collective-permute-start.1) | collective-permute-done | bytes 1048608 | tf_op jit(solution)/shard_map/ppermute | solution.py:42
  34.2 0.0 collective-permute-done.2.refs_4_
  34.2 0.0 collective-permute-done.3.refs_5_
  34.2 0.0 copy-done.2
  34.2 19.1 %partial_blocks.1 = (bf16[4,2,2,128,128]{4,3,2,1,0:T(8,128)(2,1)S(1)}, bf16[4,2,2,128,128]{4,3,2,1,0:T(8,128)(2,1)S(1)}, bf16[5,2,2,128,128]{4,3,2,1,0:T(8,128)(...) custom-call(s32[224]{0:T(256)S(1)} %get-tuple-element.23.tiles, ...), custom_call_target="tpu_custom_call" | custom-call | flops 11676942336 | bytes 28311552 | tf_op jit(solution)/shard_map/partial_blocks/pallas_call | solution.py:240
  53.3 3.8 %collective-permute-start.6 = (bf16[5,2,2,128,128]{4,3,2,1,0:T(8,128)(2,1)S(1)}, bf16[5,2,2,128,128]{4,3,2,1,0:T(8,128)(2,1)S(1)}, u32[]{:S(2)}, u32[]{:S(2)}) collective-permute-start(bf16[5,2,2,128,128]{4,3,2,1,0:T(8,128)(2,1)S(1)} %get-tuple-element.30), channel_id=1, source_target_pairs={{0,4},{4,8},{8,12},{12,16},{16,20},{20,24},{24,28},{1,5},{5,9},{9,... | collective-permute-start | bytes 1966088 | tf_op jit(solution)/shard_map/ppermute | solution.py:42
  57.1 1.3 collective-permute-start.7
  58.4 5.4 %collective-permute-start.4 = (bf16[4,2,2,128,128]{4,3,2,1,0:T(8,128)(2,1)S(1)}, bf16[4,2,2,128,128]{4,3,2,1,0:T(8,128)(2,1)S(1)}, u32[]{:S(2)}, u32[]{:S(2)}) collective-permute-start(bf16[4,2,2,128,128]{4,3,2,1,0:T(8,128)(2,1)S(1)} %get-tuple-element.28), channel_id=1, source_target_pairs={{0,1},{1,2},{2,3},{4,5},{5,6},{6,7},{8,9},{9,10},{10,11},{12,13},{... | collective-permute-start | bytes 1572872 | tf_op jit(solution)/shard_map/ppermute | solution.py:42
  63.8 1.3 collective-permute-start.5
  65.1 0.0 copy-start
  65.1 4.0 %copy-done = bf16[1280,4096]{1,0:T(8,128)(2,1)S(1)} copy-done((bf16[1280,4096]{1,0:T(8,128)(2,1)S(1)}, bf16[1280,4096]{1,0:T(8,128)(2,1)}, u32[]{:S(2)}) %copy-start) | copy-done | bytes 10485784
  69.1 3.8 %own_rows.1.refs_4_ = f32[5,2,2,128,128]{4,3,2,1,0:T(8,128)S(1)} custom-call(bf16[256,4096]{1,0:T(8,128)(2,1)S(1)} %get-tuple-element.32.left_own, bf16[1280,4096]{1,0:T(8,128)(2,1)S(1)} %copy-done), custom_call_target="tpu_custom_call" | custom-call | flops 2684354560 | bytes 12582912 | tf_op jit(solution)/shard_map/own_rows/pallas_call | solution.py:281
  72.9 3.1 %collective-permute-done.4.refs_0_ = bf16[4,2,2,128,128]{4,3,2,1,0:T(8,128)(2,1)S(1)} collective-permute-done((bf16[4,2,2,128,128]{4,3,2,1,0:T(8,128)(2,1)S(1)}, bf16[4,2,2,128,128]{4,3,2,1,0:T(8,128)(2,1)S(1)}, u32[]{:S(2)}, u32[]{:S(2)}) %collective-permute-start.4) | collective-permute-done | bytes 524320 | tf_op jit(solution)/shard_map/ppermute | solution.py:42
  75.9 4.5 %collective-permute-done.5.refs_1_ = bf16[4,2,2,128,128]{4,3,2,1,0:T(8,128)(2,1)S(1)} collective-permute-done((bf16[4,2,2,128,128]{4,3,2,1,0:T(8,128)(2,1)S(1)}, bf16[4,2,2,128,128]{4,3,2,1,0:T(8,128)(2,1)S(1)}, u32[]{:S(2)}, u32[]{:S(2)}) %collective-permute-start.5) | collective-permute-done | bytes 524320 | tf_op jit(solution)/shard_map/ppermute | solution.py:42
  80.4 0.0 collective-permute-done.6.refs_2_
  80.4 0.0 collective-permute-done.7.refs_3_
  80.4 0.7 finished_window.1
  81.1 4.2 %collective-permute-start.13 = (bf16[7,2,2,128,128]{4,3,2,1,0:T(8,128)(2,1)S(1)}, bf16[7,2,2,128,128]{4,3,2,1,0:T(8,128)(2,1)}, u32[]{:S(2)}, u32[]{:S(2)}) collective-permute-start(bf16[7,2,2,128,128]{4,3,2,1,0:T(8,128)(2,1)S(1)} %get-tuple-element.37.refs_1_), channel_id=1, source_target_pairs={{0,1},{1,2},{2,3},{4,5},{5,6},{6,7},{8,9},{9,10},{10,11},{12,13},{... | collective-permute-start | bytes 2752520 | tf_op jit(solution)/shard_map/ppermute | solution.py:42
  85.3 1.3 collective-permute-start.14
  86.6 1.3 collective-permute-start.10
  87.9 6.1 %collective-permute-start.8 = (bf16[6,2,2,128,128]{4,3,2,1,0:T(8,128)(2,1)S(1)}, bf16[6,2,2,128,128]{4,3,2,1,0:T(8,128)(2,1)}, u32[]{:S(2)}, u32[]{:S(2)}) collective-permute-start(bf16[6,2,2,128,128]{4,3,2,1,0:T(8,128)(2,1)S(1)} %get-tuple-element.36.refs_0_), channel_id=1, source_target_pairs={{0,1},{1,2},{2,3},{4,5},{5,6},{6,7},{8,9},{9,10},{10,11},{12,13},{... | collective-permute-start | bytes 2359304 | tf_op jit(solution)/shard_map/ppermute | solution.py:42
  94.0 1.3 fusion
  95.3 1.9 %collective-permute-start.12 = (bf16[8,2,2,128,128]{4,3,2,1,0:T(8,128)(2,1)}, bf16[8,2,2,128,128]{4,3,2,1,0:T(8,128)(2,1)S(1)}, u32[]{:S(2)}, u32[]{:S(2)}) collective-permute-start(bf16[8,2,2,128,128]{4,3,2,1,0:T(8,128)(2,1)} %fusion), channel_id=1, source_target_pairs={{0,3},{3,0},{4,7},{7,4},{8,11},{11,8},{12,15},{15,12},{16,19},{19,... | collective-permute-start | bytes 3145736 | tf_op jit(solution)/shard_map/ppermute | solution.py:423
  97.2 0.1 pad_add_fusion.5.row
  97.3 2.0 %placed.4.refs_4_ = bf16[4,2,13,2,128,128]{5,4,3,2,1,0:T(8,128)(2,1)} custom-call(s32[2]{0:T(128)S(1)} %pad_add_fusion.5.row, s32[2]{0:T(128)S(1)} %broadcast_1_valid.2.valid, bf16[6,2,2,128,128]{4,3,2,1,0:T(8,128)(2,1)S(1)} %get-tuple-element.36.refs_0_, bf16[7,2,2,128,128]{4,3,2,1,0:T(8,128)(2,1)S(1)} %get-tuple-element.37.refs_1_), custom_call_target="tpu_custom_call" | custom-call | bytes 5111808 | tf_op jit(solution)/shard_map/placed/pallas_call | solution.py:397
  99.3 5.8 %collective-permute-done.13.refs_2_ = bf16[7,2,2,128,128]{4,3,2,1,0:T(8,128)(2,1)} collective-permute-done((bf16[7,2,2,128,128]{4,3,2,1,0:T(8,128)(2,1)S(1)}, bf16[7,2,2,128,128]{4,3,2,1,0:T(8,128)(2,1)}, u32[]{:S(2)}, u32[]{:S(2)}) %collective-permute-start.13) | collective-permute-done | bytes 917536 | tf_op jit(solution)/shard_map/ppermute | solution.py:42
  105.1 5.5 %collective-permute-done.14.refs_3_ = bf16[7,2,2,128,128]{4,3,2,1,0:T(8,128)(2,1)} collective-permute-done((bf16[7,2,2,128,128]{4,3,2,1,0:T(8,128)(2,1)S(1)}, bf16[7,2,2,128,128]{4,3,2,1,0:T(8,128)(2,1)}, u32[]{:S(2)}, u32[]{:S(2)}) %collective-permute-start.14) | collective-permute-done | bytes 917536 | tf_op jit(solution)/shard_map/ppermute | solution.py:42
  110.6 2.0 %collective-permute-start.15 = (bf16[7,2,2,128,128]{4,3,2,1,0:T(8,128)(2,1)}, bf16[7,2,2,128,128]{4,3,2,1,0:T(8,128)(2,1)S(1)}, u32[]{:S(2)}, u32[]{:S(2)}) collective-permute-start(bf16[7,2,2,128,128]{4,3,2,1,0:T(8,128)(2,1)} %collective-permute-done.13.refs_2_), channel_id=1, source_target_pairs={{0,1},{1,2},{2,3},{4,5},{5,6},{6,7},{8,9},{9,10},{10,11},{12,13},{... | collective-permute-start | bytes 2752520 | tf_op jit(solution)/shard_map/ppermute | solution.py:42
  112.6 1.3 collective-permute-start.16
  113.9 35.9 %collective-permute-done.10.refs_1_ = bf16[6,2,2,128,128]{4,3,2,1,0:T(8,128)(2,1)S(1)} collective-permute-done((bf16[6,2,2,128,128]{4,3,2,1,0:T(8,128)(2,1)S(1)}, bf16[6,2,2,128,128]{4,3,2,1,0:T(8,128)(2,1)S(1)}, u32[]{:S(2)}, u32[]{:S(2)}) %collective-permute-start.10) | collective-permute-done | bytes 786464 | tf_op jit(solution)/shard_map/ppermute | solution.py:42
  149.8 1.3 collective-permute-start.11
  151.1 0.0 collective-permute-done.8.refs_0_
  151.1 4.6 %collective-permute-start.9 = (bf16[6,2,2,128,128]{4,3,2,1,0:T(8,128)(2,1)}, bf16[6,2,2,128,128]{4,3,2,1,0:T(8,128)(2,1)S(1)}, u32[]{:S(2)}, u32[]{:S(2)}) collective-permute-start(bf16[6,2,2,128,128]{4,3,2,1,0:T(8,128)(2,1)} %collective-permute-done.8.refs_0_), channel_id=1, source_target_pairs={{0,1},{1,2},{2,3},{4,5},{5,6},{6,7},{8,9},{9,10},{10,11},{12,13},{... | collective-permute-start | bytes 2359304 | tf_op jit(solution)/shard_map/ppermute | solution.py:42
  155.7 0.1 pad_add_fusion.6.row
  155.8 0.1 add_convert_fusion.valid
  155.9 0.1 pad_add_fusion
  155.9 0.1 pad_add_fusion.3
  156.0 3.4 %placed.5.refs_4_ = bf16[4,2,13,2,128,128]{5,4,3,2,1,0:T(8,128)(2,1)} custom-call(s32[4]{0:T(128)S(1)} %pad_add_fusion.6.row, s32[4]{0:T(128)S(1)} %add_convert_fusion.valid, bf16[6,2,2,128,128]{4,3,2,1,0:T(8,128)(2,1)} %collective-permute-done.8.refs_0_, ...), custom_call_target="tpu_custom_call", output_to_operand_aliasing={{}: (6, {})} | custom-call | bytes 5111808 | tf_op jit(solution)/shard_map/placed/pallas_call | solution.py:397
  159.4 0.0 collective-permute-done.12.refs_0_.refs_1_
  159.4 4.8 %collective-permute-done.15.refs_2_ = bf16[7,2,2,128,128]{4,3,2,1,0:T(8,128)(2,1)S(1)} collective-permute-done((bf16[7,2,2,128,128]{4,3,2,1,0:T(8,128)(2,1)}, bf16[7,2,2,128,128]{4,3,2,1,0:T(8,128)(2,1)S(1)}, u32[]{:S(2)}, u32[]{:S(2)}) %collective-permute-start.15) | collective-permute-done | bytes 917536 | tf_op jit(solution)/shard_map/ppermute | solution.py:42
  164.2 5.3 %collective-permute-done.16.refs_3_ = bf16[7,2,2,128,128]{4,3,2,1,0:T(8,128)(2,1)} collective-permute-done((bf16[7,2,2,128,128]{4,3,2,1,0:T(8,128)(2,1)}, bf16[7,2,2,128,128]{4,3,2,1,0:T(8,128)(2,1)}, u32[]{:S(2)}, u32[]{:S(2)}) %collective-permute-start.16) | collective-permute-done | bytes 917536 | tf_op jit(solution)/shard_map/ppermute | solution.py:42
  169.5 3.1 %placed.6.refs_2_ = bf16[4,2,13,2,128,128]{5,4,3,2,1,0:T(8,128)(2,1)} custom-call(s32[4]{0:T(128)S(1)} %get-tuple-element.41.row, s32[4]{0:T(128)S(1)} %get-tuple-element.42.valid, bf16[8,2,2,128,128]{4,3,2,1,0:T(8,128)(2,1)S(1)} %collective-permute-done.12.refs_0_.refs_1_, ...), custom_call_target="tpu_custom_call", output_to_operand_aliasing={{}: (6, {})} | custom-call | bytes 5111808 | tf_op jit(solution)/shard_map/placed/pallas_call | solution.py:397
  172.7 12.4 %collective-permute-done.11.refs_1_ = bf16[6,2,2,128,128]{4,3,2,1,0:T(8,128)(2,1)} collective-permute-done((bf16[6,2,2,128,128]{4,3,2,1,0:T(8,128)(2,1)S(1)}, bf16[6,2,2,128,128]{4,3,2,1,0:T(8,128)(2,1)}, u32[]{:S(2)}, u32[]{:S(2)}) %collective-permute-start.11) | collective-permute-done | bytes 786464 | tf_op jit(solution)/shard_map/ppermute | solution.py:42
  185.1 0.0 collective-permute-done.9.refs_0_
  185.1 2.3 %placed.7 = bf16[4,2,13,2,128,128]{5,4,3,2,1,0:T(8,128)(2,1)} custom-call(s32[2]{0:T(128)S(1)} %get-tuple-element.43.row, s32[2]{0:T(128)S(1)} %get-tuple-element.44.valid, bf16[6,2,2,128,128]{4,3,2,1,0:T(8,128)(2,1)S(1)} %collective-permute-done.9.refs_0_, ...), custom_call_target="tpu_custom_call", output_to_operand_aliasing={{}: (4, {})} | custom-call | bytes 5111808 | tf_op jit(solution)/shard_map/placed/pallas_call | solution.py:397
  (1 shorter events, 0.0 us)
Async XLA Ops:
  1.6 30.0 %collective-permute-start = (bf16[32,128,128]{2,1,0:T(8,128)(2,1)S(1)}, bf16[32,128,128]{2,1,0:T(8,128)(2,1)}, u32[]{:S(2)}, u32[]{:S(2)}) collective-permute-start(bf16[32,128,128]{2,1,0:T(8,128)(2,1)S(1)} %bitcast.24), channel_id=1, source_target_pairs={{0,1},{1,2},{2,3},{4,5},{5,6},{6,7},{8,9},{9,10},{10,11},{12,13},{... | collective-permute-start | bytes 3145736 | tf_op jit(solution)/shard_map/ppermute | solution.py:42
  7.5 26.6 %collective-permute-start.1 = (bf16[32,128,128]{2,1,0:T(8,128)(2,1)S(1)}, bf16[32,128,128]{2,1,0:T(8,128)(2,1)}, u32[]{:S(2)}, u32[]{:S(2)}) collective-permute-start(bf16[32,128,128]{2,1,0:T(8,128)(2,1)S(1)} %bitcast.25), channel_id=1, source_target_pairs={{1,0},{2,1},{3,2},{5,4},{6,5},{7,6},{9,8},{10,9},{11,10},{13,12},{... | collective-permute-start | bytes 3145736 | tf_op jit(solution)/shard_map/ppermute | solution.py:42
  8.8 25.3 %collective-permute-start.2 = (bf16[32,128,128]{2,1,0:T(8,128)(2,1)S(1)}, bf16[32,128,128]{2,1,0:T(8,128)(2,1)}, u32[]{:S(2)}, u32[]{:S(2)}) collective-permute-start(bf16[32,128,128]{2,1,0:T(8,128)(2,1)S(1)} %bitcast.26), channel_id=1, source_target_pairs={{4,8},{8,4},{12,16},{16,12},{20,24},{24,20},{5,9},{9,5},{13,17},{1... | collective-permute-start | bytes 3145736 | tf_op jit(solution)/shard_map/ppermute | solution.py:51
  10.5 23.6 %collective-permute-start.3 = (bf16[32,128,128]{2,1,0:T(8,128)(2,1)S(1)}, bf16[32,128,128]{2,1,0:T(8,128)(2,1)}, u32[]{:S(2)}, u32[]{:S(2)}) collective-permute-start(bf16[32,128,128]{2,1,0:T(8,128)(2,1)S(1)} %bitcast.27), channel_id=1, source_target_pairs={{0,4},{4,0},{8,12},{12,8},{16,20},{20,16},{24,28},{28,24},{1,5},{5... | collective-permute-start | bytes 3145736 | tf_op jit(solution)/shard_map/ppermute | solution.py:51
  13.4 3.1 %copy-start.1 = (bf16[1,1,32,7,128,128]{5,4,3,2,1,0:T(8,128)(2,1)S(1)}, bf16[1,1,32,7,128,128]{5,4,3,2,1,0:T(8,128)(2,1)}, u32[]{:S(2)}) copy-start(bf16[1,1,32,7,128,128]{5,4,3,2,1,0:T(8,128)(2,1)} %param.5) | copy-start | bytes 22020100
  16.5 1.2 copy-start.3
  17.7 0.7 copy-start.4
  18.4 15.8 %copy-start.2 = (bf16[1,1,32,7,128,128]{5,4,3,2,1,0:T(8,128)(2,1)S(1)}, bf16[1,1,32,7,128,128]{5,4,3,2,1,0:T(8,128)(2,1)}, u32[]{:S(2)}) copy-start(bf16[1,1,32,7,128,128]{5,4,3,2,1,0:T(8,128)(2,1)} %param.5) | copy-start | bytes 22020100
  53.3 27.1 %collective-permute-start.6 = (bf16[5,2,2,128,128]{4,3,2,1,0:T(8,128)(2,1)S(1)}, bf16[5,2,2,128,128]{4,3,2,1,0:T(8,128)(2,1)S(1)}, u32[]{:S(2)}, u32[]{:S(2)}) collective-permute-start(bf16[5,2,2,128,128]{4,3,2,1,0:T(8,128)(2,1)S(1)} %get-tuple-element.30), channel_id=1, source_target_pairs={{0,4},{4,8},{8,12},{12,16},{16,20},{20,24},{24,28},{1,5},{5,9},{9,... | collective-permute-start | bytes 1966088 | tf_op jit(solution)/shard_map/ppermute | solution.py:42
  57.1 23.3 %collective-permute-start.7 = (bf16[5,2,2,128,128]{4,3,2,1,0:T(8,128)(2,1)S(1)}, bf16[5,2,2,128,128]{4,3,2,1,0:T(8,128)(2,1)S(1)}, u32[]{:S(2)}, u32[]{:S(2)}) collective-permute-start(bf16[5,2,2,128,128]{4,3,2,1,0:T(8,128)(2,1)S(1)} %get-tuple-element.31), channel_id=1, source_target_pairs={{4,0},{8,4},{12,8},{16,12},{20,16},{24,20},{28,24},{5,1},{9,5},{13... | collective-permute-start | bytes 1966088 | tf_op jit(solution)/shard_map/ppermute | solution.py:42
  58.4 17.5 %collective-permute-start.4 = (bf16[4,2,2,128,128]{4,3,2,1,0:T(8,128)(2,1)S(1)}, bf16[4,2,2,128,128]{4,3,2,1,0:T(8,128)(2,1)S(1)}, u32[]{:S(2)}, u32[]{:S(2)}) collective-permute-start(bf16[4,2,2,128,128]{4,3,2,1,0:T(8,128)(2,1)S(1)} %get-tuple-element.28), channel_id=1, source_target_pairs={{0,1},{1,2},{2,3},{4,5},{5,6},{6,7},{8,9},{9,10},{10,11},{12,13},{... | collective-permute-start | bytes 1572872 | tf_op jit(solution)/shard_map/ppermute | solution.py:42
  63.8 16.6 %collective-permute-start.5 = (bf16[4,2,2,128,128]{4,3,2,1,0:T(8,128)(2,1)S(1)}, bf16[4,2,2,128,128]{4,3,2,1,0:T(8,128)(2,1)S(1)}, u32[]{:S(2)}, u32[]{:S(2)}) collective-permute-start(bf16[4,2,2,128,128]{4,3,2,1,0:T(8,128)(2,1)S(1)} %get-tuple-element.29), channel_id=1, source_target_pairs={{1,0},{2,1},{3,2},{5,4},{6,5},{7,6},{9,8},{10,9},{11,10},{13,12},{... | collective-permute-start | bytes 1572872 | tf_op jit(solution)/shard_map/ppermute | solution.py:42
  65.1 4.0 %copy-start = (bf16[1280,4096]{1,0:T(8,128)(2,1)S(1)}, bf16[1280,4096]{1,0:T(8,128)(2,1)}, u32[]{:S(2)}) copy-start(bf16[1280,4096]{1,0:T(8,128)(2,1)} %get-tuple-element.33.right_all) | copy-start | bytes 31457284
  81.1 24.0 %collective-permute-start.13 = (bf16[7,2,2,128,128]{4,3,2,1,0:T(8,128)(2,1)S(1)}, bf16[7,2,2,128,128]{4,3,2,1,0:T(8,128)(2,1)}, u32[]{:S(2)}, u32[]{:S(2)}) collective-permute-start(bf16[7,2,2,128,128]{4,3,2,1,0:T(8,128)(2,1)S(1)} %get-tuple-element.37.refs_1_), channel_id=1, source_target_pairs={{0,1},{1,2},{2,3},{4,5},{5,6},{6,7},{8,9},{9,10},{10,11},{12,13},{... | collective-permute-start | bytes 2752520 | tf_op jit(solution)/shard_map/ppermute | solution.py:42
  85.3 25.2 %collective-permute-start.14 = (bf16[7,2,2,128,128]{4,3,2,1,0:T(8,128)(2,1)S(1)}, bf16[7,2,2,128,128]{4,3,2,1,0:T(8,128)(2,1)}, u32[]{:S(2)}, u32[]{:S(2)}) collective-permute-start(bf16[7,2,2,128,128]{4,3,2,1,0:T(8,128)(2,1)S(1)} %get-tuple-element.37.refs_1_), channel_id=1, source_target_pairs={{1,0},{2,1},{3,2},{5,4},{6,5},{7,6},{9,8},{10,9},{11,10},{13,12},{... | collective-permute-start | bytes 2752520 | tf_op jit(solution)/shard_map/ppermute | solution.py:42
  86.6 63.2 %collective-permute-start.10 = (bf16[6,2,2,128,128]{4,3,2,1,0:T(8,128)(2,1)S(1)}, bf16[6,2,2,128,128]{4,3,2,1,0:T(8,128)(2,1)S(1)}, u32[]{:S(2)}, u32[]{:S(2)}) collective-permute-start(bf16[6,2,2,128,128]{4,3,2,1,0:T(8,128)(2,1)S(1)} %get-tuple-element.36.refs_0_), channel_id=1, source_target_pairs={{1,0},{2,1},{3,2},{5,4},{6,5},{7,6},{9,8},{10,9},{11,10},{13,12},{... | collective-permute-start | bytes 2359304 | tf_op jit(solution)/shard_map/ppermute | solution.py:42
  87.9 63.2 %collective-permute-start.8 = (bf16[6,2,2,128,128]{4,3,2,1,0:T(8,128)(2,1)S(1)}, bf16[6,2,2,128,128]{4,3,2,1,0:T(8,128)(2,1)}, u32[]{:S(2)}, u32[]{:S(2)}) collective-permute-start(bf16[6,2,2,128,128]{4,3,2,1,0:T(8,128)(2,1)S(1)} %get-tuple-element.36.refs_0_), channel_id=1, source_target_pairs={{0,1},{1,2},{2,3},{4,5},{5,6},{6,7},{8,9},{9,10},{10,11},{12,13},{... | collective-permute-start | bytes 2359304 | tf_op jit(solution)/shard_map/ppermute | solution.py:42
  95.3 64.1 %collective-permute-start.12 = (bf16[8,2,2,128,128]{4,3,2,1,0:T(8,128)(2,1)}, bf16[8,2,2,128,128]{4,3,2,1,0:T(8,128)(2,1)S(1)}, u32[]{:S(2)}, u32[]{:S(2)}) collective-permute-start(bf16[8,2,2,128,128]{4,3,2,1,0:T(8,128)(2,1)} %fusion), channel_id=1, source_target_pairs={{0,3},{3,0},{4,7},{7,4},{8,11},{11,8},{12,15},{15,12},{16,19},{19,... | collective-permute-start | bytes 3145736 | tf_op jit(solution)/shard_map/ppermute | solution.py:423
  110.6 53.7 %collective-permute-start.15 = (bf16[7,2,2,128,128]{4,3,2,1,0:T(8,128)(2,1)}, bf16[7,2,2,128,128]{4,3,2,1,0:T(8,128)(2,1)S(1)}, u32[]{:S(2)}, u32[]{:S(2)}) collective-permute-start(bf16[7,2,2,128,128]{4,3,2,1,0:T(8,128)(2,1)} %collective-permute-done.13.refs_2_), channel_id=1, source_target_pairs={{0,1},{1,2},{2,3},{4,5},{5,6},{6,7},{8,9},{9,10},{10,11},{12,13},{... | collective-permute-start | bytes 2752520 | tf_op jit(solution)/shard_map/ppermute | solution.py:42
  112.6 57.0 %collective-permute-start.16 = (bf16[7,2,2,128,128]{4,3,2,1,0:T(8,128)(2,1)}, bf16[7,2,2,128,128]{4,3,2,1,0:T(8,128)(2,1)}, u32[]{:S(2)}, u32[]{:S(2)}) collective-permute-start(bf16[7,2,2,128,128]{4,3,2,1,0:T(8,128)(2,1)} %collective-permute-done.14.refs_3_), channel_id=1, source_target_pairs={{1,0},{2,1},{3,2},{5,4},{6,5},{7,6},{9,8},{10,9},{11,10},{13,12},{... | collective-permute-start | bytes 2752520 | tf_op jit(solution)/shard_map/ppermute | solution.py:42
  149.8 35.3 %collective-permute-start.11 = (bf16[6,2,2,128,128]{4,3,2,1,0:T(8,128)(2,1)S(1)}, bf16[6,2,2,128,128]{4,3,2,1,0:T(8,128)(2,1)}, u32[]{:S(2)}, u32[]{:S(2)}) collective-permute-start(bf16[6,2,2,128,128]{4,3,2,1,0:T(8,128)(2,1)S(1)} %collective-permute-done.10.refs_1_), channel_id=1, source_target_pairs={{1,0},{2,1},{3,2},{5,4},{6,5},{7,6},{9,8},{10,9},{11,10},{13,12},{... | collective-permute-start | bytes 2359304 | tf_op jit(solution)/shard_map/ppermute | solution.py:42
  151.1 34.0 %collective-permute-start.9 = (bf16[6,2,2,128,128]{4,3,2,1,0:T(8,128)(2,1)}, bf16[6,2,2,128,128]{4,3,2,1,0:T(8,128)(2,1)S(1)}, u32[]{:S(2)}, u32[]{:S(2)}) collective-permute-start(bf16[6,2,2,128,128]{4,3,2,1,0:T(8,128)(2,1)} %collective-permute-done.8.refs_0_), channel_id=1, source_target_pairs={{0,1},{1,2},{2,3},{4,5},{5,6},{6,7},{8,9},{9,10},{10,11},{12,13},{... | collective-permute-start | bytes 2359304 | tf_op jit(solution)/shard_map/ppermute | solution.py:42

commit v14 on v13

--- a/solution.py
+++ b/solution.py
@@ -28,7 +28,7 @@
 )
 AHEAD, BEHIND = 4, 8
 TRAVEL = (4, 1, 5, 9, 0, 2, 6, 10, 12, 3, 7, 11, 8)
-HALVES = (TRAVEL[:6], TRAVEL[6:])
+HALVES = (TRAVEL[:5], TRAVEL[5:])
 smoothing = 2.0 / 3.0
 MEMBERS = 2
 ROWS_PER_STEP = 4

time: 188 us -> 188 us (level)
  no operation moved by 1% of the time
where the time goes in v14:
time: 188 us; the launch traced here: 187 us
  waiting for transfers between devices  79.8 us (42%)
  Pallas kernels  46.8 us (25%)
  starting transfers between devices  46.5 us (25%)
  local copies, waits for them, and re-layouts  11.5 us (6%)
    ppermute x14, waiting for transfers between devices, shifted(): return lax.ppermute(x, axis, pairs)  79.8 us
    ppermute x14, starting transfers between devices, shifted(): return lax.ppermute(x, axis, pairs)  41 us
    pallas_call x1, Pallas kernels, partial_blocks(): pl.pallas_call(functools.partial(partial_kernel, members, taps), in_specs...  18.3 us
    pallas_call x1, Pallas kernels, own_slots(): pl.pallas_call(functools.partial(own_kernel, count_y, rows, members, taps...  13.3 us
    unnamed x12, local copies, waits for them, and re-layouts  11.4 us
    pallas_call x4, Pallas kernels, placed(): pl.pallas_call(functools.partial(place_kernel, tuple((p[1:3] for p in pie...  10.8 us
  transfers between devices with their start and end apart: 17, of which 9 were waited for; matrix products, arithmetic and copies ran while one was open for 1% of the time, Pallas kernels for 14%

profile of v14, /device:TPU:0, one launch (start us, length us, event | category | flops | bytes accessed | tf_op | source)
XLA Modules:
  0.0 186.7 jit_solution(11612392326680399090)
XLA Ops:
  0.0 1.6 copy.11
  1.6 5.9 %collective-permute-start = (bf16[32,128,128]{2,1,0:T(8,128)(2,1)S(1)}, bf16[32,128,128]{2,1,0:T(8,128)(2,1)}, u32[]{:S(2)}, u32[]{:S(2)}) collective-permute-start(bf16[32,128,128]{2,1,0:T(8,128)(2,1)S(1)} %bitcast.24), channel_id=1, source_target_pairs={{0,1},{1,2},{2,3},{4,5},{5,6},{6,7},{8,9},{9,10},{10,11},{12,13},{... | collective-permute-start | bytes 3145736 | tf_op jit(solution)/shard_map/ppermute | solution.py:42
  7.5 1.3 collective-permute-start.1
  8.8 1.7 collective-permute-start.2
  10.5 1.9 %collective-permute-start.3 = (bf16[32,128,128]{2,1,0:T(8,128)(2,1)S(1)}, bf16[32,128,128]{2,1,0:T(8,128)(2,1)}, u32[]{:S(2)}, u32[]{:S(2)}) collective-permute-start(bf16[32,128,128]{2,1,0:T(8,128)(2,1)S(1)} %bitcast.27), channel_id=1, source_target_pairs={{0,4},{4,0},{8,12},{12,8},{16,20},{20,16},{24,28},{28,24},{1,5},{5... | collective-permute-start | bytes 3145736 | tf_op jit(solution)/shard_map/ppermute | solution.py:51
  12.4 0.8 copy.10
  13.2 0.1 reshape.12.columns
  13.3 0.1 pad_add_fusion.2.place
  13.4 0.0 copy-start.1
  13.4 3.1 %copy-done.1 = bf16[1,1,32,7,128,128]{5,4,3,2,1,0:T(8,128)(2,1)S(1)} copy-done((bf16[1,1,32,7,128,128]{5,4,3,2,1,0:T(8,128)(2,1)S(1)}, bf16[1,1,32,7,128,128]{5,4,3,2,1,0:T(8,128)(2,1)}, u32[]{:S(2)}) %copy-start.1) | copy-done | bytes 7340056
  16.5 0.0 copy-start.3
  16.5 1.2 copy-done.3
  17.7 0.0 copy-start.4
  17.7 0.7 copy-done.4
  18.4 0.0 copy-start.2
  18.4 13.3 %own_slots.1 = (bf16[256,4096]{1,0:T(8,128)(2,1)S(1)}, bf16[256,4096]{1,0:T(8,128)(2,1)S(1)}, s32[224]{0:T(256)S(1)}, s32[224]{0:T(256)S(1)}, s32[224]{0:T(256)S(1)}, /*index=5*/s32[8]{0:T(128)S(1)}) custom-call(s32[224]{0:T(256)S(1)} %reshape.12.columns, s32[1024]{0:T(1024)S(1)} %copy-done.4, s32[2]{0:T(128)S(1)} %pad_add_fusion.2.place, ...), custom_call_target="tpu_custom_call" | custom-call | flops 1207959552 | bytes 13631488 | tf_op jit(solution)/shard_map/own_slots/pallas_call | solution.py:110
  31.7 0.0 collective-permute-done.refs_2_
  31.7 2.5 %collective-permute-done.1.refs_3_ = bf16[32,128,128]{2,1,0:T(8,128)(2,1)} collective-permute-done((bf16[32,128,128]{2,1,0:T(8,128)(2,1)S(1)}, bf16[32,128,128]{2,1,0:T(8,128)(2,1)}, u32[]{:S(2)}, u32[]{:S(2)}) %collective-permute-start.1) | collective-permute-done | bytes 1048608 | tf_op jit(solution)/shard_map/ppermute | solution.py:42
  34.2 0.0 collective-permute-done.2.refs_4_
  34.2 0.0 collective-permute-done.3.refs_5_
  34.2 0.0 copy-done.2
  34.2 18.3 %partial_blocks.1 = (bf16[4,2,2,128,128]{4,3,2,1,0:T(8,128)(2,1)S(1)}, bf16[4,2,2,128,128]{4,3,2,1,0:T(8,128)(2,1)S(1)}, bf16[5,2,2,128,128]{4,3,2,1,0:T(8,128)(...) custom-call(s32[224]{0:T(256)S(1)} %get-tuple-element.23.tiles, ...), custom_call_target="tpu_custom_call" | custom-call | flops 11676942336 | bytes 28311552 | tf_op jit(solution)/shard_map/partial_blocks/pallas_call | solution.py:240
  52.5 4.6 %collective-permute-start.6 = (bf16[5,2,2,128,128]{4,3,2,1,0:T(8,128)(2,1)S(1)}, bf16[5,2,2,128,128]{4,3,2,1,0:T(8,128)(2,1)S(1)}, u32[]{:S(2)}, u32[]{:S(2)}) collective-permute-start(bf16[5,2,2,128,128]{4,3,2,1,0:T(8,128)(2,1)S(1)} %get-tuple-element.30), channel_id=1, source_target_pairs={{0,4},{4,8},{8,12},{12,16},{16,20},{20,24},{24,28},{1,5},{5,9},{9,... | collective-permute-start | bytes 1966088 | tf_op jit(solution)/shard_map/ppermute | solution.py:42
  57.1 1.3 collective-permute-start.7
  58.4 5.4 %collective-permute-start.4 = (bf16[4,2,2,128,128]{4,3,2,1,0:T(8,128)(2,1)S(1)}, bf16[4,2,2,128,128]{4,3,2,1,0:T(8,128)(2,1)S(1)}, u32[]{:S(2)}, u32[]{:S(2)}) collective-permute-start(bf16[4,2,2,128,128]{4,3,2,1,0:T(8,128)(2,1)S(1)} %get-tuple-element.28), channel_id=1, source_target_pairs={{0,1},{1,2},{2,3},{4,5},{5,6},{6,7},{8,9},{9,10},{10,11},{12,13},{... | collective-permute-start | bytes 1572872 | tf_op jit(solution)/shard_map/ppermute | solution.py:42
  63.8 1.3 collective-permute-start.5
  65.1 0.0 copy-start
  65.1 4.0 %copy-done = bf16[1280,4096]{1,0:T(8,128)(2,1)S(1)} copy-done((bf16[1280,4096]{1,0:T(8,128)(2,1)S(1)}, bf16[1280,4096]{1,0:T(8,128)(2,1)}, u32[]{:S(2)}) %copy-start) | copy-done | bytes 10485784
  69.1 3.8 %own_rows.1.refs_4_ = f32[5,2,2,128,128]{4,3,2,1,0:T(8,128)S(1)} custom-call(bf16[256,4096]{1,0:T(8,128)(2,1)S(1)} %get-tuple-element.32.left_own, bf16[1280,4096]{1,0:T(8,128)(2,1)S(1)} %copy-done), custom_call_target="tpu_custom_call" | custom-call | flops 2684354560 | bytes 12582912 | tf_op jit(solution)/shard_map/own_rows/pallas_call | solution.py:281
  72.9 3.1 %collective-permute-done.4.refs_0_ = bf16[4,2,2,128,128]{4,3,2,1,0:T(8,128)(2,1)S(1)} collective-permute-done((bf16[4,2,2,128,128]{4,3,2,1,0:T(8,128)(2,1)S(1)}, bf16[4,2,2,128,128]{4,3,2,1,0:T(8,128)(2,1)S(1)}, u32[]{:S(2)}, u32[]{:S(2)}) %collective-permute-start.4) | collective-permute-done | bytes 524320 | tf_op jit(solution)/shard_map/ppermute | solution.py:42
  75.9 4.5 %collective-permute-done.5.refs_1_ = bf16[4,2,2,128,128]{4,3,2,1,0:T(8,128)(2,1)S(1)} collective-permute-done((bf16[4,2,2,128,128]{4,3,2,1,0:T(8,128)(2,1)S(1)}, bf16[4,2,2,128,128]{4,3,2,1,0:T(8,128)(2,1)S(1)}, u32[]{:S(2)}, u32[]{:S(2)}) %collective-permute-start.5) | collective-permute-done | bytes 524320 | tf_op jit(solution)/shard_map/ppermute | solution.py:42
  80.4 0.0 collective-permute-done.6.refs_2_
  80.4 0.0 collective-permute-done.7.refs_3_
  80.4 0.7 finished_window.1
  81.1 3.5 %collective-permute-start.13 = (bf16[8,2,2,128,128]{4,3,2,1,0:T(8,128)(2,1)S(1)}, bf16[8,2,2,128,128]{4,3,2,1,0:T(8,128)(2,1)}, u32[]{:S(2)}, u32[]{:S(2)}) collective-permute-start(bf16[8,2,2,128,128]{4,3,2,1,0:T(8,128)(2,1)S(1)} %get-tuple-element.37.refs_1_), channel_id=1, source_target_pairs={{0,1},{1,2},{2,3},{4,5},{5,6},{6,7},{8,9},{9,10},{10,11},{12,13},{... | collective-permute-start | bytes 3145736 | tf_op jit(solution)/shard_map/ppermute | solution.py:42
  84.6 1.3 collective-permute-start.14
  85.9 1.3 collective-permute-start.10
  87.2 6.0 %collective-permute-start.8 = (bf16[5,2,2,128,128]{4,3,2,1,0:T(8,128)(2,1)S(1)}, bf16[5,2,2,128,128]{4,3,2,1,0:T(8,128)(2,1)}, u32[]{:S(2)}, u32[]{:S(2)}) collective-permute-start(bf16[5,2,2,128,128]{4,3,2,1,0:T(8,128)(2,1)S(1)} %get-tuple-element.36.refs_0_), channel_id=1, source_target_pairs={{0,1},{1,2},{2,3},{4,5},{5,6},{6,7},{8,9},{9,10},{10,11},{12,13},{... | collective-permute-start | bytes 1966088 | tf_op jit(solution)/shard_map/ppermute | solution.py:42
  93.2 0.1 pad_add_fusion.5.row
  93.3 1.2 fusion
  94.5 1.9 %collective-permute-start.12 = (bf16[8,2,2,128,128]{4,3,2,1,0:T(8,128)(2,1)}, bf16[8,2,2,128,128]{4,3,2,1,0:T(8,128)(2,1)S(1)}, u32[]{:S(2)}, u32[]{:S(2)}) collective-permute-start(bf16[8,2,2,128,128]{4,3,2,1,0:T(8,128)(2,1)} %fusion), channel_id=1, source_target_pairs={{0,3},{3,0},{4,7},{7,4},{8,11},{11,8},{12,15},{15,12},{16,19},{19,... | collective-permute-start | bytes 3145736 | tf_op jit(solution)/shard_map/ppermute | solution.py:423
  96.5 2.0 %placed.4.refs_4_ = bf16[4,2,13,2,128,128]{5,4,3,2,1,0:T(8,128)(2,1)} custom-call(s32[2]{0:T(128)S(1)} %pad_add_fusion.5.row, s32[2]{0:T(128)S(1)} %broadcast_1_valid.2.valid, bf16[5,2,2,128,128]{4,3,2,1,0:T(8,128)(2,1)S(1)} %get-tuple-element.36.refs_0_, bf16[8,2,2,128,128]{4,3,2,1,0:T(8,128)(2,1)S(1)} %get-tuple-element.37.refs_1_), custom_call_target="tpu_custom_call" | custom-call | bytes 5111808 | tf_op jit(solution)/shard_map/placed/pallas_call | solution.py:397
  98.5 8.6 %collective-permute-done.13.refs_2_ = bf16[8,2,2,128,128]{4,3,2,1,0:T(8,128)(2,1)} collective-permute-done((bf16[8,2,2,128,128]{4,3,2,1,0:T(8,128)(2,1)S(1)}, bf16[8,2,2,128,128]{4,3,2,1,0:T(8,128)(2,1)}, u32[]{:S(2)}, u32[]{:S(2)}) %collective-permute-start.13) | collective-permute-done | bytes 1048608 | tf_op jit(solution)/shard_map/ppermute | solution.py:42
  107.1 5.5 %collective-permute-done.14.refs_3_ = bf16[8,2,2,128,128]{4,3,2,1,0:T(8,128)(2,1)} collective-permute-done((bf16[8,2,2,128,128]{4,3,2,1,0:T(8,128)(2,1)S(1)}, bf16[8,2,2,128,128]{4,3,2,1,0:T(8,128)(2,1)}, u32[]{:S(2)}, u32[]{:S(2)}) %collective-permute-start.14) | collective-permute-done | bytes 1048608 | tf_op jit(solution)/shard_map/ppermute | solution.py:42
  112.6 1.9 %collective-permute-start.15 = (bf16[8,2,2,128,128]{4,3,2,1,0:T(8,128)(2,1)}, bf16[8,2,2,128,128]{4,3,2,1,0:T(8,128)(2,1)S(1)}, u32[]{:S(2)}, u32[]{:S(2)}) collective-permute-start(bf16[8,2,2,128,128]{4,3,2,1,0:T(8,128)(2,1)} %collective-permute-done.13.refs_2_), channel_id=1, source_target_pairs={{0,1},{1,2},{2,3},{4,5},{5,6},{6,7},{8,9},{9,10},{10,11},{12,13},{... | collective-permute-start | bytes 3145736 | tf_op jit(solution)/shard_map/ppermute | solution.py:42
  114.6 1.3 collective-permute-start.16
  115.9 33.2 %collective-permute-done.10.refs_1_ = bf16[5,2,2,128,128]{4,3,2,1,0:T(8,128)(2,1)S(1)} collective-permute-done((bf16[5,2,2,128,128]{4,3,2,1,0:T(8,128)(2,1)S(1)}, bf16[5,2,2,128,128]{4,3,2,1,0:T(8,128)(2,1)S(1)}, u32[]{:S(2)}, u32[]{:S(2)}) %collective-permute-start.10) | collective-permute-done | bytes 655392 | tf_op jit(solution)/shard_map/ppermute | solution.py:42
  149.1 1.3 collective-permute-start.11
  150.3 0.0 collective-permute-done.8.refs_0_
  150.4 4.6 %collective-permute-start.9 = (bf16[5,2,2,128,128]{4,3,2,1,0:T(8,128)(2,1)}, bf16[5,2,2,128,128]{4,3,2,1,0:T(8,128)(2,1)S(1)}, u32[]{:S(2)}, u32[]{:S(2)}) collective-permute-start(bf16[5,2,2,128,128]{4,3,2,1,0:T(8,128)(2,1)} %collective-permute-done.8.refs_0_), channel_id=1, source_target_pairs={{0,1},{1,2},{2,3},{4,5},{5,6},{6,7},{8,9},{9,10},{10,11},{12,13},{... | collective-permute-start | bytes 1966088 | tf_op jit(solution)/shard_map/ppermute | solution.py:42
  155.0 0.1 pad_add_fusion.6.row
  155.1 0.1 add_convert_fusion.valid
  155.1 0.1 pad_add_fusion
  155.2 0.1 pad_add_fusion.3
  155.3 3.4 %placed.5.refs_4_ = bf16[4,2,13,2,128,128]{5,4,3,2,1,0:T(8,128)(2,1)} custom-call(s32[4]{0:T(128)S(1)} %pad_add_fusion.6.row, s32[4]{0:T(128)S(1)} %add_convert_fusion.valid, bf16[5,2,2,128,128]{4,3,2,1,0:T(8,128)(2,1)} %collective-permute-done.8.refs_0_, ...), custom_call_target="tpu_custom_call", output_to_operand_aliasing={{}: (6, {})} | custom-call | bytes 5111808 | tf_op jit(solution)/shard_map/placed/pallas_call | solution.py:397
  158.7 0.0 collective-permute-done.12.refs_0_.refs_1_
  158.7 7.5 %collective-permute-done.15.refs_2_ = bf16[8,2,2,128,128]{4,3,2,1,0:T(8,128)(2,1)S(1)} collective-permute-done((bf16[8,2,2,128,128]{4,3,2,1,0:T(8,128)(2,1)}, bf16[8,2,2,128,128]{4,3,2,1,0:T(8,128)(2,1)S(1)}, u32[]{:S(2)}, u32[]{:S(2)}) %collective-permute-start.15) | collective-permute-done | bytes 1048608 | tf_op jit(solution)/shard_map/ppermute | solution.py:42
  166.2 5.4 %collective-permute-done.16.refs_3_ = bf16[8,2,2,128,128]{4,3,2,1,0:T(8,128)(2,1)} collective-permute-done((bf16[8,2,2,128,128]{4,3,2,1,0:T(8,128)(2,1)}, bf16[8,2,2,128,128]{4,3,2,1,0:T(8,128)(2,1)}, u32[]{:S(2)}, u32[]{:S(2)}) %collective-permute-start.16) | collective-permute-done | bytes 1048608 | tf_op jit(solution)/shard_map/ppermute | solution.py:42
  171.6 3.2 %placed.6.refs_2_ = bf16[4,2,13,2,128,128]{5,4,3,2,1,0:T(8,128)(2,1)} custom-call(s32[4]{0:T(128)S(1)} %get-tuple-element.41.row, s32[4]{0:T(128)S(1)} %get-tuple-element.42.valid, bf16[8,2,2,128,128]{4,3,2,1,0:T(8,128)(2,1)S(1)} %collective-permute-done.12.refs_0_.refs_1_, ...), custom_call_target="tpu_custom_call", output_to_operand_aliasing={{}: (6, {})} | custom-call | bytes 5111808 | tf_op jit(solution)/shard_map/placed/pallas_call | solution.py:397
  174.8 9.5 %collective-permute-done.11.refs_1_ = bf16[5,2,2,128,128]{4,3,2,1,0:T(8,128)(2,1)} collective-permute-done((bf16[5,2,2,128,128]{4,3,2,1,0:T(8,128)(2,1)S(1)}, bf16[5,2,2,128,128]{4,3,2,1,0:T(8,128)(2,1)}, u32[]{:S(2)}, u32[]{:S(2)}) %collective-permute-start.11) | collective-permute-done | bytes 655392 | tf_op jit(solution)/shard_map/ppermute | solution.py:42
  184.4 0.0 collective-permute-done.9.refs_0_
  184.4 2.2 %placed.7 = bf16[4,2,13,2,128,128]{5,4,3,2,1,0:T(8,128)(2,1)} custom-call(s32[2]{0:T(128)S(1)} %get-tuple-element.43.row, s32[2]{0:T(128)S(1)} %get-tuple-element.44.valid, bf16[5,2,2,128,128]{4,3,2,1,0:T(8,128)(2,1)S(1)} %collective-permute-done.9.refs_0_, ...), custom_call_target="tpu_custom_call", output_to_operand_aliasing={{}: (4, {})} | custom-call | bytes 5111808 | tf_op jit(solution)/shard_map/placed/pallas_call | solution.py:397
  (1 shorter events, 0.0 us)
Async XLA Ops:
  1.6 30.0 %collective-permute-start = (bf16[32,128,128]{2,1,0:T(8,128)(2,1)S(1)}, bf16[32,128,128]{2,1,0:T(8,128)(2,1)}, u32[]{:S(2)}, u32[]{:S(2)}) collective-permute-start(bf16[32,128,128]{2,1,0:T(8,128)(2,1)S(1)} %bitcast.24), channel_id=1, source_target_pairs={{0,1},{1,2},{2,3},{4,5},{5,6},{6,7},{8,9},{9,10},{10,11},{12,13},{... | collective-permute-start | bytes 3145736 | tf_op jit(solution)/shard_map/ppermute | solution.py:42
  7.5 26.6 %collective-permute-start.1 = (bf16[32,128,128]{2,1,0:T(8,128)(2,1)S(1)}, bf16[32,128,128]{2,1,0:T(8,128)(2,1)}, u32[]{:S(2)}, u32[]{:S(2)}) collective-permute-start(bf16[32,128,128]{2,1,0:T(8,128)(2,1)S(1)} %bitcast.25), channel_id=1, source_target_pairs={{1,0},{2,1},{3,2},{5,4},{6,5},{7,6},{9,8},{10,9},{11,10},{13,12},{... | collective-permute-start | bytes 3145736 | tf_op jit(solution)/shard_map/ppermute | solution.py:42
  8.8 25.3 %collective-permute-start.2 = (bf16[32,128,128]{2,1,0:T(8,128)(2,1)S(1)}, bf16[32,128,128]{2,1,0:T(8,128)(2,1)}, u32[]{:S(2)}, u32[]{:S(2)}) collective-permute-start(bf16[32,128,128]{2,1,0:T(8,128)(2,1)S(1)} %bitcast.26), channel_id=1, source_target_pairs={{4,8},{8,4},{12,16},{16,12},{20,24},{24,20},{5,9},{9,5},{13,17},{1... | collective-permute-start | bytes 3145736 | tf_op jit(solution)/shard_map/ppermute | solution.py:51
  10.5 23.6 %collective-permute-start.3 = (bf16[32,128,128]{2,1,0:T(8,128)(2,1)S(1)}, bf16[32,128,128]{2,1,0:T(8,128)(2,1)}, u32[]{:S(2)}, u32[]{:S(2)}) collective-permute-start(bf16[32,128,128]{2,1,0:T(8,128)(2,1)S(1)} %bitcast.27), channel_id=1, source_target_pairs={{0,4},{4,0},{8,12},{12,8},{16,20},{20,16},{24,28},{28,24},{1,5},{5... | collective-permute-start | bytes 3145736 | tf_op jit(solution)/shard_map/ppermute | solution.py:51
  13.4 3.1 %copy-start.1 = (bf16[1,1,32,7,128,128]{5,4,3,2,1,0:T(8,128)(2,1)S(1)}, bf16[1,1,32,7,128,128]{5,4,3,2,1,0:T(8,128)(2,1)}, u32[]{:S(2)}) copy-start(bf16[1,1,32,7,128,128]{5,4,3,2,1,0:T(8,128)(2,1)} %param.5) | copy-start | bytes 22020100
  16.5 1.2 copy-start.3
  17.7 0.7 copy-start.4
  18.4 15.8 %copy-start.2 = (bf16[1,1,32,7,128,128]{5,4,3,2,1,0:T(8,128)(2,1)S(1)}, bf16[1,1,32,7,128,128]{5,4,3,2,1,0:T(8,128)(2,1)}, u32[]{:S(2)}) copy-start(bf16[1,1,32,7,128,128]{5,4,3,2,1,0:T(8,128)(2,1)} %param.5) | copy-start | bytes 22020100
  52.5 27.9 %collective-permute-start.6 = (bf16[5,2,2,128,128]{4,3,2,1,0:T(8,128)(2,1)S(1)}, bf16[5,2,2,128,128]{4,3,2,1,0:T(8,128)(2,1)S(1)}, u32[]{:S(2)}, u32[]{:S(2)}) collective-permute-start(bf16[5,2,2,128,128]{4,3,2,1,0:T(8,128)(2,1)S(1)} %get-tuple-element.30), channel_id=1, source_target_pairs={{0,4},{4,8},{8,12},{12,16},{16,20},{20,24},{24,28},{1,5},{5,9},{9,... | collective-permute-start | bytes 1966088 | tf_op jit(solution)/shard_map/ppermute | solution.py:42
  57.1 23.3 %collective-permute-start.7 = (bf16[5,2,2,128,128]{4,3,2,1,0:T(8,128)(2,1)S(1)}, bf16[5,2,2,128,128]{4,3,2,1,0:T(8,128)(2,1)S(1)}, u32[]{:S(2)}, u32[]{:S(2)}) collective-permute-start(bf16[5,2,2,128,128]{4,3,2,1,0:T(8,128)(2,1)S(1)} %get-tuple-element.31), channel_id=1, source_target_pairs={{4,0},{8,4},{12,8},{16,12},{20,16},{24,20},{28,24},{5,1},{9,5},{13... | collective-permute-start | bytes 1966088 | tf_op jit(solution)/shard_map/ppermute | solution.py:42
  58.4 17.5 %collective-permute-start.4 = (bf16[4,2,2,128,128]{4,3,2,1,0:T(8,128)(2,1)S(1)}, bf16[4,2,2,128,128]{4,3,2,1,0:T(8,128)(2,1)S(1)}, u32[]{:S(2)}, u32[]{:S(2)}) collective-permute-start(bf16[4,2,2,128,128]{4,3,2,1,0:T(8,128)(2,1)S(1)} %get-tuple-element.28), channel_id=1, source_target_pairs={{0,1},{1,2},{2,3},{4,5},{5,6},{6,7},{8,9},{9,10},{10,11},{12,13},{... | collective-permute-start | bytes 1572872 | tf_op jit(solution)/shard_map/ppermute | solution.py:42
  63.8 16.6 %collective-permute-start.5 = (bf16[4,2,2,128,128]{4,3,2,1,0:T(8,128)(2,1)S(1)}, bf16[4,2,2,128,128]{4,3,2,1,0:T(8,128)(2,1)S(1)}, u32[]{:S(2)}, u32[]{:S(2)}) collective-permute-start(bf16[4,2,2,128,128]{4,3,2,1,0:T(8,128)(2,1)S(1)} %get-tuple-element.29), channel_id=1, source_target_pairs={{1,0},{2,1},{3,2},{5,4},{6,5},{7,6},{9,8},{10,9},{11,10},{13,12},{... | collective-permute-start | bytes 1572872 | tf_op jit(solution)/shard_map/ppermute | solution.py:42
  65.1 4.0 %copy-start = (bf16[1280,4096]{1,0:T(8,128)(2,1)S(1)}, bf16[1280,4096]{1,0:T(8,128)(2,1)}, u32[]{:S(2)}) copy-start(bf16[1280,4096]{1,0:T(8,128)(2,1)} %get-tuple-element.33.right_all) | copy-start | bytes 31457284
  81.1 26.0 %collective-permute-start.13 = (bf16[8,2,2,128,128]{4,3,2,1,0:T(8,128)(2,1)S(1)}, bf16[8,2,2,128,128]{4,3,2,1,0:T(8,128)(2,1)}, u32[]{:S(2)}, u32[]{:S(2)}) collective-permute-start(bf16[8,2,2,128,128]{4,3,2,1,0:T(8,128)(2,1)S(1)} %get-tuple-element.37.refs_1_), channel_id=1, source_target_pairs={{0,1},{1,2},{2,3},{4,5},{5,6},{6,7},{8,9},{9,10},{10,11},{12,13},{... | collective-permute-start | bytes 3145736 | tf_op jit(solution)/shard_map/ppermute | solution.py:42
  84.6 28.1 %collective-permute-start.14 = (bf16[8,2,2,128,128]{4,3,2,1,0:T(8,128)(2,1)S(1)}, bf16[8,2,2,128,128]{4,3,2,1,0:T(8,128)(2,1)}, u32[]{:S(2)}, u32[]{:S(2)}) collective-permute-start(bf16[8,2,2,128,128]{4,3,2,1,0:T(8,128)(2,1)S(1)} %get-tuple-element.37.refs_1_), channel_id=1, source_target_pairs={{1,0},{2,1},{3,2},{5,4},{6,5},{7,6},{9,8},{10,9},{11,10},{13,12},{... | collective-permute-start | bytes 3145736 | tf_op jit(solution)/shard_map/ppermute | solution.py:42
  85.9 63.2 %collective-permute-start.10 = (bf16[5,2,2,128,128]{4,3,2,1,0:T(8,128)(2,1)S(1)}, bf16[5,2,2,128,128]{4,3,2,1,0:T(8,128)(2,1)S(1)}, u32[]{:S(2)}, u32[]{:S(2)}) collective-permute-start(bf16[5,2,2,128,128]{4,3,2,1,0:T(8,128)(2,1)S(1)} %get-tuple-element.36.refs_0_), channel_id=1, source_target_pairs={{1,0},{2,1},{3,2},{5,4},{6,5},{7,6},{9,8},{10,9},{11,10},{13,12},{... | collective-permute-start | bytes 1966088 | tf_op jit(solution)/shard_map/ppermute | solution.py:42
  87.2 63.2 %collective-permute-start.8 = (bf16[5,2,2,128,128]{4,3,2,1,0:T(8,128)(2,1)S(1)}, bf16[5,2,2,128,128]{4,3,2,1,0:T(8,128)(2,1)}, u32[]{:S(2)}, u32[]{:S(2)}) collective-permute-start(bf16[5,2,2,128,128]{4,3,2,1,0:T(8,128)(2,1)S(1)} %get-tuple-element.36.refs_0_), channel_id=1, source_target_pairs={{0,1},{1,2},{2,3},{4,5},{5,6},{6,7},{8,9},{9,10},{10,11},{12,13},{... | collective-permute-start | bytes 1966088 | tf_op jit(solution)/shard_map/ppermute | solution.py:42
  94.5 64.2 %collective-permute-start.12 = (bf16[8,2,2,128,128]{4,3,2,1,0:T(8,128)(2,1)}, bf16[8,2,2,128,128]{4,3,2,1,0:T(8,128)(2,1)S(1)}, u32[]{:S(2)}, u32[]{:S(2)}) collective-permute-start(bf16[8,2,2,128,128]{4,3,2,1,0:T(8,128)(2,1)} %fusion), channel_id=1, source_target_pairs={{0,3},{3,0},{4,7},{7,4},{8,11},{11,8},{12,15},{15,12},{16,19},{19,... | collective-permute-start | bytes 3145736 | tf_op jit(solution)/shard_map/ppermute | solution.py:423
  112.6 53.6 %collective-permute-start.15 = (bf16[8,2,2,128,128]{4,3,2,1,0:T(8,128)(2,1)}, bf16[8,2,2,128,128]{4,3,2,1,0:T(8,128)(2,1)S(1)}, u32[]{:S(2)}, u32[]{:S(2)}) collective-permute-start(bf16[8,2,2,128,128]{4,3,2,1,0:T(8,128)(2,1)} %collective-permute-done.13.refs_2_), channel_id=1, source_target_pairs={{0,1},{1,2},{2,3},{4,5},{5,6},{6,7},{8,9},{9,10},{10,11},{12,13},{... | collective-permute-start | bytes 3145736 | tf_op jit(solution)/shard_map/ppermute | solution.py:42
  114.6 57.0 %collective-permute-start.16 = (bf16[8,2,2,128,128]{4,3,2,1,0:T(8,128)(2,1)}, bf16[8,2,2,128,128]{4,3,2,1,0:T(8,128)(2,1)}, u32[]{:S(2)}, u32[]{:S(2)}) collective-permute-start(bf16[8,2,2,128,128]{4,3,2,1,0:T(8,128)(2,1)} %collective-permute-done.14.refs_3_), channel_id=1, source_target_pairs={{1,0},{2,1},{3,2},{5,4},{6,5},{7,6},{9,8},{10,9},{11,10},{13,12},{... | collective-permute-start | bytes 3145736 | tf_op jit(solution)/shard_map/ppermute | solution.py:42
  149.1 35.3 %collective-permute-start.11 = (bf16[5,2,2,128,128]{4,3,2,1,0:T(8,128)(2,1)S(1)}, bf16[5,2,2,128,128]{4,3,2,1,0:T(8,128)(2,1)}, u32[]{:S(2)}, u32[]{:S(2)}) collective-permute-start(bf16[5,2,2,128,128]{4,3,2,1,0:T(8,128)(2,1)S(1)} %collective-permute-done.10.refs_1_), channel_id=1, source_target_pairs={{1,0},{2,1},{3,2},{5,4},{6,5},{7,6},{9,8},{10,9},{11,10},{13,12},{... | collective-permute-start | bytes 1966088 | tf_op jit(solution)/shard_map/ppermute | solution.py:42
  150.4 34.0 %collective-permute-start.9 = (bf16[5,2,2,128,128]{4,3,2,1,0:T(8,128)(2,1)}, bf16[5,2,2,128,128]{4,3,2,1,0:T(8,128)(2,1)S(1)}, u32[]{:S(2)}, u32[]{:S(2)}) collective-permute-start(bf16[5,2,2,128,128]{4,3,2,1,0:T(8,128)(2,1)} %collective-permute-done.8.refs_0_), channel_id=1, source_target_pairs={{0,1},{1,2},{2,3},{4,5},{5,6},{6,7},{8,9},{9,10},{10,11},{12,13},{... | collective-permute-start | bytes 1966088 | tf_op jit(solution)/shard_map/ppermute | solution.py:42
